TPU v7x, 768 devices: a whole 4x8x12 slice. The times are simulated.
768 devices in a mesh: dp: 16 (over y, core), expert: 48 (over x, z).
Axes of the slice: x: 4, y: 8, z: 12, core: 2. Of those that a mesh axis runs over, the one named last changes fastest.
Arguments:
- layer_input: bfloat16 [36864, 2048], P(('dp', 'expert')), may hold values from -60 to 60
- out_grad: bfloat16 [36864, 2048], P(('dp', 'expert')), may hold values from -4 to 4
- router_weight: bfloat16 [96, 2048], replicated, may hold values from -1 to 1
- routes: int32 [36864, 8], P(('dp', 'expert')), may hold values from 0 to 95, all different within a row; in each aligned block of 48 rows (0 to 47, 48 to 95, ...) at most 5 rows name the same one
- hidden_act: bfloat16 [16, 96, 240, 768], P('dp', 'expert'), may hold values from -6 to 6
- down_weight: bfloat16 [96, 768, 2048], P('expert'), may hold values from -0.21875 to 0.21875
Outputs:
- down_grad: float32 [96, 768, 2048], P('expert', None, 'dp')
- hidden_grad: bfloat16 [16, 96, 240, 768], P('dp', 'expert')
- router_grad: float32 [96, 2048], P('expert')
- input_grad: bfloat16 [36864, 2048], P(('dp', 'expert'))
Inputs may be any that keep to these rules, and one draw needn't show every extreme that they name: `routes`: each row names 8 different experts; among the rows of one device no expert is named more than 5 times.
All inputs are finite; a program needn't handle non-finite values.
Results may differ from a plain program's by a relative error of at most 0.02.
Values may be sent and summed in bfloat16 or wider, within the bound.
No kernel may reach another device: no remote copies, remote signals or barrier semaphores. Data moves between devices by JAX's collectives and lax.ppermute only.
A program may use at most 128 MiB of HBM per device.

v0:
```python
import jax
import jax.numpy as jnp
from jax import lax
from jax.sharding import PartitionSpec as P


def slot_positions(route_blocks, experts):
    blocks, row_count, top_count = route_blocks.shape
    onehot_int = (route_blocks[..., None] == jnp.arange(experts, dtype=jnp.int32)).astype(jnp.int32)
    flat_int = onehot_int.reshape(blocks, row_count * top_count, experts)
    earlier = jnp.cumsum(flat_int, axis=1) - flat_int
    position = jnp.sum(earlier * flat_int, axis=2)
    return (onehot_int, position)


def on_device(layer_input, out_grad, router_weight, routes, hidden_act, down_weight):
    n_expert = lax.axis_size("expert")
    experts = router_weight.shape[0]
    exp_dev = experts // n_expert
    slots_all = hidden_act.shape[2]
    capacity = slots_all // n_expert
    tok_rows, top_count = routes.shape
    width = out_grad.shape[1]
    logits = jnp.einsum("td,ed->te", layer_input, router_weight, preferred_element_type=jnp.float32)
    onehot_int, position = slot_positions(routes[None], experts)
    onehot = onehot_int[0].astype(jnp.float32)
    picked = jnp.sum(onehot * logits[:, None, :], axis=2)
    highest = jnp.max(picked, axis=1, keepdims=True)
    weights = jnp.exp(picked - highest)
    gate_probs = weights / jnp.sum(weights, axis=1, keepdims=True)
    gate_wire = gate_probs.astype(jnp.bfloat16)
    target = routes.reshape(-1) * capacity + position[0]
    token_ids = jnp.repeat(jnp.arange(tok_rows, dtype=jnp.int32), top_count)
    slot_token = jnp.full((experts * capacity,), -1, jnp.int32).at[target].set(token_ids)
    is_filled = slot_token >= 0
    send_rows = jnp.where(
        is_filled[:, None], out_grad[jnp.maximum(slot_token, 0)], jnp.zeros((), jnp.bfloat16)
    )
    send_gate = jnp.zeros((experts * capacity,), jnp.bfloat16).at[target].set(gate_wire.reshape(-1))
    arrived, arrived_gate = (
        lax.all_to_all(
            send_rows.reshape(n_expert, exp_dev, capacity, width),
            "expert",
            split_axis=0,
            concat_axis=2,
            tiled=True,
        ),
        lax.all_to_all(
            send_gate.reshape(n_expert, exp_dev, capacity),
            "expert",
            split_axis=0,
            concat_axis=2,
            tiled=True,
        ),
    )
    arrived = arrived[0]
    arrived_gate = arrived_gate[0]
    hidden = hidden_act[0]
    gate_wide = arrived_gate.astype(jnp.float32)[:, :, None]
    scaled = (gate_wide * arrived.astype(jnp.float32)).astype(jnp.bfloat16)
    recomputed = jnp.einsum("esf,efd->esd", hidden, down_weight, preferred_element_type=jnp.float32)
    slot_grad = jnp.sum(recomputed * arrived.astype(jnp.float32), axis=2)
    hidden_grad = jnp.einsum(
        "esd,efd->esf", scaled, down_weight, preferred_element_type=jnp.float32
    ).astype(jnp.bfloat16)[None]
    partial_value = jnp.einsum("esf,esd->efd", hidden, scaled, preferred_element_type=jnp.float32)
    down_grad = lax.psum_scatter(
        partial_value.astype(jnp.bfloat16), "dp", scatter_dimension=2, tiled=True
    ).astype(jnp.float32)
    returned = lax.all_to_all(
        slot_grad.reshape(1, exp_dev, n_expert, capacity),
        "expert",
        split_axis=2,
        concat_axis=0,
        tiled=True,
    ).reshape(-1)
    gate_grad = returned[target].reshape(tok_rows, top_count)
    weighted = jnp.sum(gate_probs * gate_grad, axis=1, keepdims=True)
    picked_grad = gate_probs * (gate_grad - weighted)
    logit_grad = jnp.einsum("tke,tk->te", onehot, picked_grad)
    input_grad = jnp.dot(
        logit_grad.astype(jnp.bfloat16), router_weight, preferred_element_type=jnp.float32
    ).astype(jnp.bfloat16)
    router_term = jnp.einsum(
        "te,td->ed", logit_grad, layer_input.astype(jnp.float32), precision=lax.Precision.HIGHEST
    )
    summed = lax.psum(router_term, ("dp", "expert"))
    router_grad = lax.dynamic_slice_in_dim(summed, lax.axis_index("expert") * exp_dev, exp_dev, 0)
    return (down_grad, hidden_grad, router_grad, input_grad)


def solution(mesh):
    in_specs = (
        P(("dp", "expert"), None),
        P(("dp", "expert"), None),
        P(),
        P(("dp", "expert"), None),
        P("dp", "expert", None, None),
        P("expert", None, None),
    )
    out_specs = (
        P("expert", None, "dp"),
        P("dp", "expert", None, None),
        P("expert", None),
        P(("dp", "expert"), None),
    )
    return jax.shard_map(
        on_device, mesh=mesh, in_specs=in_specs, out_specs=out_specs, check_vma=False
    )
```

profile of v0, /device:TPU:1, one launch (start us, length us, event | category | flops | bytes accessed | tf_op | source)
XLA Modules:
  0.0 645.6 jit_solution(4615610391455551243)
XLA Ops:
  8.0 0.0 copy-start
  8.0 0.0 copy-start.1
  8.0 0.8 broadcast_multiply_fusion
  8.8 0.8 copy.70
  9.6 0.1 copy.69
  9.7 0.1 mul.49
  9.7 0.1 eq.34
  9.9 1.0 reduce-window.6
  10.8 0.2 slice_reduce_fusion
  11.1 0.1 copy.83
  11.2 0.2 broadcast.84
  11.3 0.1 reshape.189
  11.4 0.1 fusion.7
  11.5 0.1 reshape.227
  11.6 2.9 scatter_custom_fusion.1
  14.6 0.0 copy-done.1
  14.6 2.5 gather_fusion
  17.1 2.5 gather.9
  19.5 0.2 broadcast_in_dim.42
  19.7 2.2 broadcast_select_fusion
  22.0 0.0 copy-start.3
  22.0 0.0 copy-start.4
  22.0 3.6 copy.76
  25.7 19.0 %all-to-all-start.1 = ((bf16[48,2,5,2048]{3,1,2,0:T(2,128)(2,1)}), bf16[48,2,5,2048]{3,1,2,0:T(2,128)(2,1)S(1)}, u32[]{:S(2)}, u32[]{:S(2)}) async-start(bf16[48,2,5,2048]{3,1,2,0:T(2,128)(2,1)} %copy.76), calls=%async_computation.1 | async-start | bytes 3932160 | tf_op jit(solution)/shard_map/all_to_all | solution.py:41
  44.7 0.0 copy-done.3
  44.7 0.0 copy-done.4
  44.7 0.3 fusion.20
  45.0 0.2 multiply_reduce_fusion.1
  45.2 0.1 reduce_max.9
  45.3 0.2 fusion.11
  45.5 65.8 %all-to-all-done.1 = bf16[48,2,5,2048]{3,1,2,0:T(2,128)(2,1)S(1)} async-done(((bf16[48,2,5,2048]{3,1,2,0:T(2,128)(2,1)}), bf16[48,2,5,2048]{3,1,2,0:T(2,128)(2,1)S(1)}, u32[]{:S(2)}, u32[]{:S(2)}) %all-to-all-start.1) | async-done | bytes 1966112 | tf_op jit(solution)/shard_map/all_to_all | solution.py:41
  111.3 2.3 bitcast_convert_fusion
  113.6 0.0 copy-start.2
  113.6 1.9 copy-done.2
  115.5 0.0 copy-done
  115.5 6.4 multiply_reduce_fusion
  121.9 0.1 reshape.192
  122.1 0.6 copy.79
  122.7 9.4 %all-to-all-start.2 = ((f32[1,2,48,5]{3,1,0,2:T(2,128)}), f32[1,2,48,5]{3,1,0,2:T(2,128)S(1)}, u32[]{:S(2)}, u32[]{:S(2)}) async-start(f32[1,2,48,5]{3,1,0,2:T(2,128)} %copy.79), calls=%async_computation.3 | async-start | bytes 98304 | tf_op jit(solution)/shard_map/all_to_all | solution.py:70
  132.2 11.4 %all-to-all-done.2 = f32[1,2,48,5]{3,1,0,2:T(2,128)S(1)} async-done(((f32[1,2,48,5]{3,1,0,2:T(2,128)}), f32[1,2,48,5]{3,1,0,2:T(2,128)S(1)}, u32[]{:S(2)}, u32[]{:S(2)}) %all-to-all-start.2) | async-done | bytes 1952 | tf_op jit(solution)/shard_map/all_to_all | solution.py:70
  143.5 0.2 reshape.193
  143.7 2.8 gather_fusion.1
  146.5 0.1 reshape.194
  146.6 0.2 multiply_reduce_fusion.2
  146.8 0.1 subtract_multiply_fusion
  146.9 0.1 reshape.219
  147.0 3.0 scatter_custom_fusion
  150.0 0.8 reshape.190
  150.8 4.5 all-to-all-start
  155.3 0.0 all-reduce.2.cloned.1.call-start
  155.3 0.3 fusion.3
  155.6 1.4 fusion.21
  157.0 0.0 all-reduce.2.cloned.1.call-update
  157.0 0.3 reduce-scatter.2.cloned.1.call-start
  157.3 9.1 %all-to-all-done = bf16[48,2,5]{2,1,0:T(2,128)(2,1)S(1)} async-done(((bf16[48,2,5]{2,1,0:T(2,128)(2,1)}), bf16[48,2,5]{2,1,0:T(2,128)(2,1)S(1)}, u32[]{:S(2)}, u32[]{:S(2)}) %all-to-all-start) | async-done | bytes 992 | tf_op jit(solution)/shard_map/all_to_all | solution.py:48
  166.4 0.1 reshape.195
  166.5 8.2 %convert_bitcast_fusion = bf16[2,768,2048]{1,2,0:T(8,128)(2,1)} fusion(bf16[1,2,240,768]{3,2,1,0:T(8,128)(2,1)S(1)} %copy-done, f32[2,240,2048]{2,0,1:T(2,128)} %bitcast.64, f32[2,240]{1,0:T(2,128)S(1)} %reshape.195), kind=kOutput, calls=%fused_computation.4 | convolution fusion | flops 1515061248 | bytes 10962816 | tf_op jit(solution)/shard_map/esf,esd->efd/dot_general | solution.py:66
  174.7 0.0 reduce-scatter.2.cloned.1.call-update
  174.7 0.9 convolution_convert_fusion
  175.6 8.2 %fusion = bf16[1,2,240,768]{3,2,1,0:T(8,128)(2,1)} fusion(bf16[2,768,2048]{2,1,0:T(8,128)(2,1)} %param.11, f32[2,240,2048]{2,0,1:T(2,128)} %bitcast.65, f32[2,240]{1,0:T(2,128)S(1)} %reshape.195), kind=kOutput, calls=%fused_computation.11 | convolution fusion | flops 1512284160 | bytes 10962816 | tf_op jit(solution)/shard_map/esd,efd->esf/dot_general | solution.py:63
  183.9 450.8 %all-reduce.2.cloned.1.call-done = f32[96,2048]{1,0:T(8,128)} async-done(((f32[96,2048]{1,0:T(8,128)}), f32[96,2048]{1,0:T(8,128)}) %all-reduce.2.cloned.1.call-update) | async-done | bytes 786448 | tf_op jit(solution)/shard_map/psum | solution.py:87
  634.6 1.5 constant_dynamic-slice_fusion
  636.1 0.0 reduce-scatter.2.cloned.1.call-done
  636.1 2.0 copy.80
  (12 shorter events, 0.1 us)
Async XLA Ops:
  8.0 107.5 %copy-start = (bf16[1,2,240,768]{3,2,1,0:T(8,128)(2,1)S(1)}, bf16[1,2,240,768]{3,2,1,0:T(8,128)(2,1)}, u32[]{:S(2)}) copy-start(bf16[1,2,240,768]{3,2,1,0:T(8,128)(2,1)} %param.10) | copy-start | bytes 2211844
  8.0 6.6 %copy-start.1 = (bf16[48,2048]{1,0:T(8,128)(2,1)S(1)}, bf16[48,2048]{1,0:T(8,128)(2,1)}, u32[]{:S(2)}) copy-start(bf16[48,2048]{1,0:T(8,128)(2,1)} %param.7) | copy-start | bytes 589828
  22.0 22.7 %copy-start.3 = (bf16[96,2048]{1,0:T(8,128)(2,1)S(1)}, bf16[96,2048]{1,0:T(8,128)(2,1)}, u32[]{:S(2)}) copy-start(bf16[96,2048]{1,0:T(8,128)(2,1)} %param.8) | copy-start | bytes 1179652
  22.0 22.7 %copy-start.4 = (bf16[48,2048]{1,0:T(8,128)(2,1)S(1)}, bf16[48,2048]{1,0:T(8,128)(2,1)}, u32[]{:S(2)}) copy-start(bf16[48,2048]{1,0:T(8,128)(2,1)} %param.6) | copy-start | bytes 589828
  25.7 85.6 %all-to-all-start.1 = ((bf16[48,2,5,2048]{3,1,2,0:T(2,128)(2,1)}), bf16[48,2,5,2048]{3,1,2,0:T(2,128)(2,1)S(1)}, u32[]{:S(2)}, u32[]{:S(2)}) async-start(bf16[48,2,5,2048]{3,1,2,0:T(2,128)(2,1)} %copy.76), calls=%async_computation.1 | async-start | bytes 3932160 | tf_op jit(solution)/shard_map/all_to_all | solution.py:41
  113.6 1.9 copy-start.2
  122.7 20.8 %all-to-all-start.2 = ((f32[1,2,48,5]{3,1,0,2:T(2,128)}), f32[1,2,48,5]{3,1,0,2:T(2,128)S(1)}, u32[]{:S(2)}, u32[]{:S(2)}) async-start(f32[1,2,48,5]{3,1,0,2:T(2,128)} %copy.79), calls=%async_computation.3 | async-start | bytes 98304 | tf_op jit(solution)/shard_map/all_to_all | solution.py:70
  150.8 15.6 %all-to-all-start = ((bf16[48,2,5]{2,1,0:T(2,128)(2,1)}), bf16[48,2,5]{2,1,0:T(2,128)(2,1)S(1)}, u32[]{:S(2)}, u32[]{:S(2)}) async-start(bf16[48,2,5]{2,1,0:T(2,128)(2,1)} %reshape.190), calls=%async_computation | async-start | bytes 49152 | tf_op jit(solution)/shard_map/all_to_all | solution.py:48
  155.3 479.4 %all-reduce.2.cloned.1.call-start = ((), (), s32[]{:S(2)}) async-start(), calls=%async_computation.5 | async-start | bytes 1572864 | tf_op jit(solution)/shard_map/psum | solution.py:87
  157.0 479.1 %reduce-scatter.2.cloned.1.call-start = ((), (), s32[]{:S(2)}) async-start(), calls=%async_computation.4 | async-start | bytes 6684672 | tf_op jit(solution)/shard_map/reduce_scatter | solution.py:67
Sparse Core Ops, SparseCore 0:
  162.0 472.5 all-reduce.1
Sparse Core Ops, SparseCore 1:
  174.8 67.0 reduce-scatter.1
where the time goes:
time: 646 us
  waiting for transfers between devices  537 us (83%)
  starting transfers between devices  33.3 us (5%)
  local copies, waits for them, and re-layouts  26.6 us (4%)
  matrix products  25.6 us (4%)
  between operations  15.8 us (2%)
  other arithmetic  7.18 us (1%)
    psum x1, waiting for transfers between devices, on_device(): summed = lax.psum(router_term, ('dp', 'expert'))  451 us
    all_to_all x1, waiting for transfers between devices, on_device(): lax.all_to_all(send_rows.reshape(n_expert, exp_dev, capacity, width), 'ex...  65.8 us
    all_to_all x1, starting transfers between devices, on_device(): lax.all_to_all(send_rows.reshape(n_expert, exp_dev, capacity, width), 'ex...  19 us
  transfers between devices with their start and end apart: 5, of which 4 were waited for; matrix products, arithmetic and copies ran while one was open for 3% of the time, Pallas kernels for 0%

commit v1 on v0

v1 whole, which is shorter than its diff:
```python
import jax
import jax.numpy as jnp
from jax import lax
from jax.sharding import PartitionSpec as P

F32 = jnp.float32
BF16 = jnp.bfloat16


def on_device(layer_input, out_grad, router_weight, routes, hidden_act, down_weight):
    n_expert = lax.axis_size("expert")
    n_dp = lax.axis_size("dp")
    n_y = n_dp // 2
    experts = router_weight.shape[0]
    exp_dev = experts // n_expert
    slots_all = hidden_act.shape[2]
    capacity = slots_all // n_expert
    tok_rows, top_count = routes.shape
    width = out_grad.shape[1]
    send_slots = experts * capacity
    dp_index = lax.axis_index("dp")
    core = dp_index % 2
    y_index = dp_index // 2

    expert_ids = jnp.arange(experts, dtype=jnp.int32)
    chosen = jnp.any(routes[:, :, None] == expert_ids, axis=1)
    logits = jnp.einsum("td,ed->te", layer_input, router_weight, preferred_element_type=F32)
    highest = jnp.max(jnp.where(chosen, logits, -jnp.inf), axis=1, keepdims=True)
    weights = jnp.where(chosen, jnp.exp(jnp.where(chosen, logits - highest, 0.0)), 0.0)
    probs = weights / jnp.sum(weights, axis=1, keepdims=True)
    tok = jnp.arange(tok_rows, dtype=jnp.int32)
    before = (tok[:, None] > tok[None, :]).astype(BF16)
    position = jnp.dot(before, chosen.astype(BF16), preferred_element_type=F32)
    code = jnp.where(chosen, position, -1.0).astype(BF16)
    slot_ids = jnp.arange(send_slots, dtype=jnp.int32)
    spread = (slot_ids[:, None] // capacity == expert_ids[None, :]).astype(BF16)
    code_slot = jnp.einsum("ie,te->it", spread, code, preferred_element_type=F32)
    select = code_slot == (slot_ids % capacity).astype(F32)[:, None]
    select_b = select.astype(BF16)
    send_rows = jnp.dot(select_b, out_grad, preferred_element_type=F32).astype(BF16)
    prob_slot = jnp.einsum("ie,te->it", spread, probs.astype(BF16), preferred_element_type=F32)
    send_gate = jnp.sum(jnp.where(select, prob_slot, 0.0), axis=1).astype(BF16)

    arrived = lax.all_to_all(
        send_rows.reshape(n_expert, exp_dev, capacity, width), "expert", split_axis=0, concat_axis=2, tiled=True
    )[0]
    arrived_gate = lax.all_to_all(
        send_gate.reshape(n_expert, exp_dev, capacity), "expert", split_axis=0, concat_axis=2, tiled=True
    )[0]
    hidden = hidden_act[0]
    gate_wide = arrived_gate.astype(F32)[:, :, None]
    gated_hidden = (gate_wide * hidden.astype(F32)).astype(BF16)

    by_core = arrived.reshape(exp_dev, slots_all, n_y, 2, width // n_dp)
    even, odd = by_core[:, :, :, 0], by_core[:, :, :, 1]
    mine = jnp.where(core == 0, even, odd).reshape(exp_dev, slots_all, width // 2)
    other = jnp.where(core == 0, odd, even).reshape(exp_dev, slots_all, width // 2)
    swap = [(i, i ^ 1) for i in range(n_dp)]
    got_rows = lax.ppermute(other, "dp", swap)
    got_hidden = lax.ppermute(gated_hidden, "dp", swap)

    product = jnp.einsum("esd,efd->esf", arrived, down_weight, preferred_element_type=F32)
    slot_grad = jnp.sum(product * hidden.astype(F32), axis=2)
    hidden_grad = (gate_wide * product).astype(BF16)[None]

    pair_hidden = jnp.concatenate([gated_hidden, got_hidden], axis=1)
    pair_rows = jnp.concatenate([mine, got_rows], axis=1)
    partial_sum = jnp.einsum("esf,esd->efd", pair_hidden, pair_rows, preferred_element_type=F32).astype(BF16)
    blocks = partial_sum.reshape(exp_dev, -1, n_y, width // n_dp).transpose(2, 0, 1, 3)

    def block_at(offset):
        return lax.dynamic_index_in_dim(blocks, (y_index + offset) % n_y, 0, keepdims=False)

    up = [(i, (i + 2) % n_dp) for i in range(n_dp)]
    down = [(i, (i - 2) % n_dp) for i in range(n_dp)]
    half = n_y // 2
    far = block_at(half)
    going_up = lax.ppermute(far[0], "dp", up)
    going_down = lax.ppermute(far[1], "dp", down)
    for step in range(half - 1, 0, -1):
        next_up, next_down = block_at(step), block_at(n_y - step)
        if step == half - 1:
            next_up = jnp.stack([(next_up[0].astype(F32) + going_up.astype(F32)).astype(BF16), next_up[1]])
            next_down = jnp.stack([next_down[0], (next_down[1].astype(F32) + going_down.astype(F32)).astype(BF16)])
        else:
            next_up = (next_up.astype(F32) + going_up.astype(F32)).astype(BF16)
            next_down = (next_down.astype(F32) + going_down.astype(F32)).astype(BF16)
        going_up = lax.ppermute(next_up, "dp", up)
        going_down = lax.ppermute(next_down, "dp", down)
    if half == 1:
        down_grad = block_at(0).astype(F32) + jnp.stack([going_up, going_down]).astype(F32)
    else:
        down_grad = block_at(0).astype(F32) + going_up.astype(F32) + going_down.astype(F32)

    returned = lax.all_to_all(
        slot_grad.reshape(1, exp_dev, n_expert, capacity), "expert", split_axis=2, concat_axis=0, tiled=True
    ).reshape(-1)
    placed = jnp.where(select, returned[:, None], 0.0)
    gate_grad = jnp.einsum("it,ie->te", placed, spread.astype(F32), precision=lax.Precision.HIGHEST)
    weighted = jnp.sum(probs * gate_grad, axis=1, keepdims=True)
    logit_grad = probs * (gate_grad - weighted)
    input_grad = jnp.dot(logit_grad.astype(BF16), router_weight, preferred_element_type=F32).astype(BF16)
    router_term = jnp.einsum(
        "te,td->ed", logit_grad, layer_input.astype(F32), precision=lax.Precision.HIGHEST
    ).astype(BF16)
    shares = lax.all_to_all(
        router_term.reshape(n_expert, exp_dev, width), "expert", split_axis=0, concat_axis=0, tiled=True
    )
    replica_sum = jnp.sum(shares.astype(F32), axis=0)
    copies = jnp.broadcast_to(replica_sum[None], (n_dp, exp_dev, width))
    gathered = lax.all_to_all(copies, "dp", split_axis=0, concat_axis=0, tiled=True)
    router_grad = jnp.sum(gathered, axis=0)
    return (down_grad, hidden_grad, router_grad, input_grad)


def solution(mesh):
    in_specs = (
        P(("dp", "expert"), None),
        P(("dp", "expert"), None),
        P(),
        P(("dp", "expert"), None),
        P("dp", "expert", None, None),
        P("expert", None, None),
    )
    out_specs = (
        P("expert", None, "dp"),
        P("dp", "expert", None, None),
        P("expert", None),
        P(("dp", "expert"), None),
    )
    return jax.shard_map(
        on_device, mesh=mesh, in_specs=in_specs, out_specs=out_specs, check_vma=False
    )
```

time: 646 us -> 252 us (0.39)
  waiting for transfers between devices: 537 us -> 87.8 us
  starting transfers between devices: 33.3 us -> 89 us
  between operations: 15.8 us -> 1.31 us
  other arithmetic: 7.18 us -> 21.2 us
  matrix products: 25.6 us -> 16.6 us
    psum x1 -> x0, waiting for transfers between devices: 451 us -> none  [on_device(): summed = lax.psum(router_term, ('dp', 'expert'))]
    ppermute x0 -> x10, starting transfers between devices: none -> 36.2 us  [the longest x3 12.3 us: on_device(): going_down = lax.ppermute(next_down, 'dp', down)]
    all_to_all x0 -> x2, starting transfers between devices: none -> 15.3 us  [the longest x1 10.7 us: on_device(): lax.all_to_all(copies, 'dp', split_axis=0, concat_axis=0, tiled=True)]
    all_to_all x1, starting transfers between devices: 4.5 us -> 19 us  [on_device(): lax.all_to_all(send_gate.reshape(n_expert, exp_dev, capacity), 'expert',...]
    ppermute x0 -> x10, waiting for transfers between devices: none -> 12.1 us  [the longest x3 9.64 us: on_device(): going_up = lax.ppermute(next_up, 'dp', up)]
    another operation x5 -> x2, local copies, waits for them, and re-layouts: 0.35 us -> 12.4 us
    select_n x2, other arithmetic: 2.26 us -> 12.6 us  [the longest x1 12.6 us: on_device(): jnp.where(core == 0, even, odd).reshape(exp_dev, slots_all, width // 2)]
    dot_general x6 -> x8, matrix products: 25.4 us -> 15.3 us  [the longest x1 6.31 us: on_device(): jnp.einsum('esd,efd->esf', arrived, down_weight, preferred_element_type=F32)]
  transfers between devices with their start and end apart: 5 -> 15, of which waited for: 4 -> 8; matrix products, arithmetic and copies ran while one was open for 3% -> 16% of each run, Pallas kernels for 0% -> 0%
where the time goes in v1:
time: 252 us; the launch traced here: 249 us
  starting transfers between devices  89 us (35%)
  waiting for transfers between devices  87.8 us (35%)
  local copies, waits for them, and re-layouts  33 us (13%)
  other arithmetic  21.2 us (8%)
  matrix products  16.6 us (7%)
    all_to_all x1, waiting for transfers between devices, on_device(): lax.all_to_all(send_rows.reshape(n_expert, exp_dev, capacity, width), 'ex...  63 us
    all_to_all x1, starting transfers between devices, on_device(): lax.all_to_all(send_gate.reshape(n_expert, exp_dev, capacity), 'expert',...  19 us
    select_n x1, other arithmetic, on_device(): jnp.where(core == 0, even, odd).reshape(exp_dev, slots_all, width // 2)  12.6 us
    ppermute x3, starting transfers between devices, on_device(): going_down = lax.ppermute(next_down, 'dp', down)  12.3 us
    all_to_all x1, starting transfers between devices, on_device(): lax.all_to_all(copies, 'dp', split_axis=0, concat_axis=0, tiled=True)  10.7 us
    all_to_all x1, starting transfers between devices, on_device(): lax.all_to_all(send_rows.reshape(n_expert, exp_dev, capacity, width), 'ex...  10.4 us
    all_to_all x1, waiting for transfers between devices, on_device(): lax.all_to_all(slot_grad.reshape(1, exp_dev, n_expert, capacity), 'expert...  10.2 us
    ppermute x3, waiting for transfers between devices, on_device(): going_up = lax.ppermute(next_up, 'dp', up)  9.64 us
  transfers between devices with their start and end apart: 15, of which 8 were waited for; matrix products, arithmetic and copies ran while one was open for 16% of the time, Pallas kernels for 0%

profile of v1, /device:TPU:1, one launch (start us, length us, event | category | flops | bytes accessed | tf_op | source)
XLA Modules:
  0.0 248.9 jit_solution(9495675082565005627)
XLA Ops:
  0.7 0.8 copy.63
  1.5 0.1 fusion.25
  1.6 0.3 convolution_compare_fusion
  1.9 1.3 select_reduce_fusion
  3.2 0.2 fusion.33
  3.4 0.4 copy-done.4
  3.8 0.3 fusion.12
  4.1 0.8 convert_element_type.161
  4.9 19.0 %all-to-all-start = ((bf16[48,2,5]{2,1,0:T(2,128)(2,1)}), bf16[48,2,5]{2,1,0:T(2,128)(2,1)}, u32[]{:S(2)}, u32[]{:S(2)}) async-start(bf16[48,2,5]{2,1,0:T(2,128)(2,1)} %convert_element_type.161), calls=%async_computation | async-start | bytes 49152 | tf_op jit(solution)/shard_map/all_to_all | solution.py:47
  24.0 3.0 %convolution_convert_fusion = bf16[480,2048]{1,0:T(8,128)(2,1)} fusion(pred[480,48]{0,1:T(8,128)(4,1)S(1)} %convolution_compare_fusion, bf16[48,2048]{1,0:T(8,128)(2,1)} %param.7), kind=kOutput, calls=%fused_computation.2 | convolution fusion | flops 95354880 | bytes 2185728 | tf_op jit(solution)/shard_map/dot_general | solution.py:40
  27.0 2.7 %reshape.121 = bf16[48,2,5,2048]{3,2,1,0:T(8,128)(2,1)S(1)} reshape(bf16[480,2048]{1,0:T(8,128)(2,1)} %convolution_convert_fusion) | data formatting | bytes 3932160 | tf_op jit(solution)/shard_map/reshape | solution.py:45
  29.7 3.7 %copy.65 = bf16[48,2,5,2048]{3,1,2,0:T(2,128)(2,1)} copy(bf16[48,2,5,2048]{3,2,1,0:T(8,128)(2,1)S(1)} %reshape.121) | data formatting | bytes 3932160 | tf_op jit(solution)/shard_map/reshape | solution.py:45
  33.3 1.6 all-to-all-done
  35.0 10.4 %all-to-all-start.1 = ((bf16[48,2,5,2048]{3,1,2,0:T(2,128)(2,1)}), bf16[48,2,5,2048]{3,1,2,0:T(2,128)(2,1)S(1)}, u32[]{:S(2)}, u32[]{:S(2)}) async-start(bf16[48,2,5,2048]{3,1,2,0:T(2,128)(2,1)} %copy.65), calls=%async_computation.1 | async-start | bytes 3932160 | tf_op jit(solution)/shard_map/all_to_all | solution.py:44
  45.4 0.8 convert_bitcast_fusion
  46.1 0.1 reshape.125
  46.3 63.0 %all-to-all-done.1 = bf16[48,2,5,2048]{3,1,2,0:T(2,128)(2,1)S(1)} async-done(((bf16[48,2,5,2048]{3,1,2,0:T(2,128)(2,1)}), bf16[48,2,5,2048]{3,1,2,0:T(2,128)(2,1)S(1)}, u32[]{:S(2)}, u32[]{:S(2)}) %all-to-all-start.1) | async-done | bytes 1966112 | tf_op jit(solution)/shard_map/all_to_all | solution.py:44
  109.3 1.3 copy-done.1
  110.6 5.9 %reshape_squeeze.3 = bf16[2,240,8,2,128]{4,3,2,0,1:T(2,128)(2,1)S(1)} reshape(bf16[1,2,48,5,2048]{4,1,3,2,0:T(2,128)(2,1)} %bitcast.102) | data formatting | bytes 3932160 | tf_op jit(solution)/shard_map/reshape;squeeze | solution.py:54
  116.5 12.6 %fusion = (bf16[2,240,8,128]{3,2,0,1:T(8,128)(2,1)S(1)}, bf16[2,240,8,128]{3,2,0,1:T(8,128)(2,1)}) fusion(pred[]{:T(512)S(6)} %eq.70, bf16[2,240,8,2,128]{4,3,2,0,1:T(2,128)(2,1)S(1)} %reshape_squeeze.3), kind=kLoop, calls=%fused_computation.6 | loop fusion | flops 983040 | bytes 3932161 | tf_op jit(solution)/shard_map/jit(_where)/select_n | solution.py:56
  129.1 3.1 %reshape.136 = bf16[2,240,1024]{2,0,1:T(2,128)(2,1)} reshape(bf16[2,240,8,128]{3,2,0,1:T(8,128)(2,1)} %get-tuple-element.5) | data formatting | bytes 1966080 | tf_op jit(solution)/shard_map/jit(_where)/select_n | solution.py:57
  132.2 2.5 %copy.80 = bf16[2,240,1024]{2,1,0:T(8,128)(2,1)} copy(bf16[2,240,1024]{2,0,1:T(2,128)(2,1)} %reshape.136) | data formatting | bytes 1966080 | tf_op jit(solution)/shard_map/jit(_where)/select_n | solution.py:57
  134.7 7.8 %collective-permute-start.1 = (bf16[2,240,1024]{2,1,0:T(8,128)(2,1)}, bf16[2,240,1024]{2,1,0:T(8,128)(2,1)}, u32[]{:S(2)}, u32[]{:S(2)}) collective-permute-start(bf16[2,240,1024]{2,1,0:T(8,128)(2,1)} %copy.80), channel_id=1, source_target_pairs={{0,48},{48,0},{96,144},{144,96},{192,240},{240,192},{288,336},{336... | collective-permute-start | bytes 2949128 | tf_op jit(solution)/shard_map/ppermute | solution.py:59
  142.5 6.3 %fusion.8 = (f32[2,240]{1,0:T(2,128)S(1)}, bf16[1,2,240,768]{3,2,1,0:T(8,128)(2,1)}, bf16[2,240,768]{2,1,0:T(8,128)(2,1)}) fusion(bf16[1,2,240,768]{3,2,1,0:T(8,128)(2,1)S(1)} %copy-done.10, f32[2,240]{1,0:T(2,128)S(1)} %reshape.125, bf16[2,768,2048]{2,1,0:T(8,128)(2,1)} %param.11, bf16[2,240,2048]{2,0,1:T(2,128)(2,1)S(1)} %bitcast.103), kind=kOutput, calls=%fused_computation.16 | convolution fusion | flops 1512529408 | bytes 10473216 | tf_op jit(solution)/shard_map/esd,efd->esf/dot_general | solution.py:62
  148.8 1.9 collective-permute-start
  150.8 0.1 reshape.123
  150.9 0.6 copy.77
  151.6 8.1 %all-to-all-start.2 = ((f32[1,2,48,5]{3,1,0,2:T(2,128)}), f32[1,2,48,5]{3,1,0,2:T(2,128)}, u32[]{:S(2)}, u32[]{:S(2)}) async-start(f32[1,2,48,5]{3,1,0,2:T(2,128)} %copy.77), calls=%async_computation.2 | async-start | bytes 98304 | tf_op jit(solution)/shard_map/all_to_all | solution.py:95
  159.8 0.2 reshape.135
  160.1 0.3 copy.79
  160.4 10.2 %all-to-all-done.2 = f32[1,2,48,5]{3,1,0,2:T(2,128)} async-done(((f32[1,2,48,5]{3,1,0,2:T(2,128)}), f32[1,2,48,5]{3,1,0,2:T(2,128)}, u32[]{:S(2)}, u32[]{:S(2)}) %all-to-all-start.2) | async-done | bytes 1952 | tf_op jit(solution)/shard_map/all_to_all | solution.py:95
  170.6 1.0 broadcast_in_dim.52
  171.6 0.4 multiply_reduce_fusion
  172.0 0.6 convolution_convert_fusion.1
  172.6 1.0 reshape.124
  173.6 4.5 %all-to-all-start.3 = ((bf16[48,2,2048]{2,1,0:T(2,128)(2,1)}), bf16[48,2,2048]{2,1,0:T(2,128)(2,1)S(1)}, u32[]{:S(2)}, u32[]{:S(2)}) async-start(bf16[48,2,2048]{2,1,0:T(2,128)(2,1)} %reshape.124), calls=%async_computation.3 | async-start | bytes 786432 | tf_op jit(solution)/shard_map/all_to_all | solution.py:106
  178.2 3.5 %convolution_convert_fusion.2 = bf16[2,768,1024]{2,1,0:T(8,128)(2,1)S(1)} fusion(bf16[2,240,1024]{2,1,0:T(8,128)(2,1)} %collective-permute-done.1, bf16[2,240,1024]{2,1,0:T(8,128)(2,1)S(1)} %copy.79, bf16[2,240,768]{2,1,0:T(8,128)(2,1)} %collective-permute-done, bf16[2,240,768]{2,1,0:T(8,128)(2,1)} %get-tuple-element.16), kind=kOutput, calls=%fused_computation.4 | convolution fusion | flops 1518403584 | bytes 6586368 | tf_op jit(solution)/shard_map/esf,esd->efd/dot_general | solution.py:68
  181.7 0.8 copy.90
  182.5 6.5 %constant_dynamic-slice_fusion.7 = (bf16[2,768,1,128]{3,2,1,0:T(2,128)(2,1)S(1)}, bf16[2,768,1,128]{3,2,1,0:T(2,128)(2,1)S(1)}, bf16[2,768,1,128]{3,2,1,0:T(2,12...) fusion(bf16[2,768,8,128]{3,2,1,0:T(8,128)(2,1)S(1)} %bitcast.10, ...), kind=kLoop, calls=%fused_computation.98 | loop fusion | bytes 6291488 | tf_op jit(solution)/shard_map/dynamic-slice
  189.2 3.2 %collective-permute-start.2 = (bf16[768,128]{1,0:T(8,128)(2,1)S(1)}, bf16[768,128]{1,0:T(8,128)(2,1)S(1)}, u32[]{:S(2)}, u32[]{:S(2)}) collective-permute-start(bf16[768,128]{1,0:T(8,128)(2,1)S(1)} %get-tuple-element.17), channel_id=1, source_target_pairs={{0,96},{48,144},{96,192},{144,240},{192,288},{240,336},{288,384},{... | collective-permute-start | bytes 589832 | tf_op jit(solution)/shard_map/ppermute | solution.py:78
  192.5 3.8 %collective-permute-start.6 = (bf16[768,128]{1,0:T(8,128)(2,1)S(1)}, bf16[768,128]{1,0:T(8,128)(2,1)S(1)}, u32[]{:S(2)}, u32[]{:S(2)}) collective-permute-start(bf16[768,128]{1,0:T(8,128)(2,1)S(1)} %get-tuple-element.18), channel_id=1, source_target_pairs={{0,672},{48,720},{96,0},{144,48},{192,96},{240,144},{288,192},{336... | collective-permute-start | bytes 589832 | tf_op jit(solution)/shard_map/ppermute | solution.py:79
  196.4 1.2 collective-permute-done.2
  197.6 0.1 fusion.23
  197.7 1.9 collective-permute-start.3
  199.7 0.1 fusion.24
  199.8 4.6 %collective-permute-start.7 = (bf16[2,768,128]{2,1,0:T(8,128)(2,1)S(1)}, bf16[2,768,128]{2,1,0:T(8,128)(2,1)S(1)}, u32[]{:S(2)}, u32[]{:S(2)}) collective-permute-start(bf16[2,768,128]{2,1,0:T(8,128)(2,1)S(1)} %pad_maximum_fusion.1), channel_id=1, source_target_pairs={{0,672},{48,720},{96,0},{144,48},{192,96},{240,144},{288,192},{336... | collective-permute-start | bytes 1179656 | tf_op jit(solution)/shard_map/ppermute | solution.py:89
  204.4 4.4 %collective-permute-done.3 = bf16[2,768,128]{2,1,0:T(8,128)(2,1)S(1)} collective-permute-done((bf16[2,768,128]{2,1,0:T(8,128)(2,1)S(1)}, bf16[2,768,128]{2,1,0:T(8,128)(2,1)S(1)}, u32[]{:S(2)}, u32[]{:S(2)}) %collective-permute-start.3) | collective-permute-done | bytes 393248 | tf_op jit(solution)/shard_map/ppermute | solution.py:88
  208.8 0.8 fusion.16
  209.6 1.9 collective-permute-start.4
  211.6 0.8 fusion.14
  212.4 4.6 %collective-permute-start.8 = (bf16[2,768,128]{2,1,0:T(8,128)(2,1)}, bf16[2,768,128]{2,1,0:T(8,128)(2,1)}, u32[]{:S(2)}, u32[]{:S(2)}) collective-permute-start(bf16[2,768,128]{2,1,0:T(8,128)(2,1)} %fusion.14), channel_id=1, source_target_pairs={{0,672},{48,720},{96,0},{144,48},{192,96},{240,144},{288,192},{336... | collective-permute-start | bytes 1179656 | tf_op jit(solution)/shard_map/ppermute | solution.py:89
  217.0 0.3 convert_reduce_fusion
  217.3 0.8 broadcast_in_dim.54
  218.1 10.7 %all-to-all-start.4 = ((f32[16,2,2048]{2,1,0:T(2,128)}), f32[16,2,2048]{2,1,0:T(2,128)S(1)}, u32[]{:S(2)}, u32[]{:S(2)}) async-start(f32[16,2,2048]{2,1,0:T(2,128)} %broadcast_in_dim.54), calls=%async_computation.4 | async-start | bytes 524288 | tf_op jit(solution)/shard_map/all_to_all | solution.py:111
  228.8 1.8 fusion.17
  230.7 3.3 %collective-permute-start.5 = (bf16[2,768,128]{2,1,0:T(8,128)(2,1)}, bf16[2,768,128]{2,1,0:T(8,128)(2,1)S(1)}, u32[]{:S(2)}, u32[]{:S(2)}) collective-permute-start(bf16[2,768,128]{2,1,0:T(8,128)(2,1)} %fusion.17), channel_id=1, source_target_pairs={{0,96},{48,144},{96,192},{144,240},{192,288},{240,336},{288,384},{... | collective-permute-start | bytes 1179656 | tf_op jit(solution)/shard_map/ppermute | solution.py:88
  234.0 1.8 fusion.15
  235.8 3.2 %collective-permute-start.9 = (bf16[2,768,128]{2,1,0:T(8,128)(2,1)}, bf16[2,768,128]{2,1,0:T(8,128)(2,1)S(1)}, u32[]{:S(2)}, u32[]{:S(2)}) collective-permute-start(bf16[2,768,128]{2,1,0:T(8,128)(2,1)} %fusion.15), channel_id=1, source_target_pairs={{0,672},{48,720},{96,0},{144,48},{192,96},{240,144},{288,192},{336... | collective-permute-start | bytes 1179656 | tf_op jit(solution)/shard_map/ppermute | solution.py:89
  239.0 0.9 convolution_convert_fusion.3
  239.9 0.9 all-to-all-done.4
  240.8 0.7 reduce_sum.59
  241.5 5.2 %collective-permute-done.5 = bf16[2,768,128]{2,1,0:T(8,128)(2,1)S(1)} collective-permute-done((bf16[2,768,128]{2,1,0:T(8,128)(2,1)}, bf16[2,768,128]{2,1,0:T(8,128)(2,1)S(1)}, u32[]{:S(2)}, u32[]{:S(2)}) %collective-permute-start.5) | collective-permute-done | bytes 393248 | tf_op jit(solution)/shard_map/ppermute | solution.py:88
  246.7 1.2 collective-permute-done.9
  247.9 1.0 fusion.18
  (37 shorter events, 0.4 us)
Async XLA Ops:
  0.6 1.3 copy-start
  0.7 23.3 %copy-start.8 = (s32[480]{0:T(512)}, s32[480]{0:T(512)S(1)}, u32[]{:S(2)}) copy-start(s32[480]{0:T(512)S(1)} %get-tuple-element.23) | copy-start | bytes 5764
  1.9 22.1 %copy-start.6 = (pred[480,48]{0,1:T(8,128)(4,1)}, pred[480,48]{0,1:T(8,128)(4,1)S(1)}, u32[]{:S(2)}) copy-start(pred[480,48]{0,1:T(8,128)(4,1)S(1)} %convolution_compare_fusion) | copy-start | bytes 69124
  3.2 0.6 copy-start.4
  4.9 30.0 %all-to-all-start = ((bf16[48,2,5]{2,1,0:T(2,128)(2,1)}), bf16[48,2,5]{2,1,0:T(2,128)(2,1)}, u32[]{:S(2)}, u32[]{:S(2)}) async-start(bf16[48,2,5]{2,1,0:T(2,128)(2,1)} %convert_element_type.161), calls=%async_computation | async-start | bytes 49152 | tf_op jit(solution)/shard_map/all_to_all | solution.py:47
  35.0 74.3 %all-to-all-start.1 = ((bf16[48,2,5,2048]{3,1,2,0:T(2,128)(2,1)}), bf16[48,2,5,2048]{3,1,2,0:T(2,128)(2,1)S(1)}, u32[]{:S(2)}, u32[]{:S(2)}) async-start(bf16[48,2,5,2048]{3,1,2,0:T(2,128)(2,1)} %copy.65), calls=%async_computation.1 | async-start | bytes 3932160 | tf_op jit(solution)/shard_map/all_to_all | solution.py:44
  109.3 1.3 copy-start.1
  129.1 13.5 %copy-start.2 = (bf16[48,2,5,2048]{3,1,2,0:T(2,128)(2,1)S(1)}, bf16[48,2,5,2048]{3,1,2,0:T(2,128)(2,1)}, u32[]{:S(2)}) copy-start(bf16[48,2,5,2048]{3,1,2,0:T(2,128)(2,1)} %copy-done.1) | copy-start | bytes 5898244
  132.2 10.3 %copy-start.10 = (bf16[1,2,240,768]{3,2,1,0:T(8,128)(2,1)S(1)}, bf16[1,2,240,768]{3,2,1,0:T(8,128)(2,1)}, u32[]{:S(2)}) copy-start(bf16[1,2,240,768]{3,2,1,0:T(8,128)(2,1)} %param.10) | copy-start | bytes 2211844
  134.7 43.5 %collective-permute-start.1 = (bf16[2,240,1024]{2,1,0:T(8,128)(2,1)}, bf16[2,240,1024]{2,1,0:T(8,128)(2,1)}, u32[]{:S(2)}, u32[]{:S(2)}) collective-permute-start(bf16[2,240,1024]{2,1,0:T(8,128)(2,1)} %copy.80), channel_id=1, source_target_pairs={{0,48},{48,0},{96,144},{144,96},{192,240},{240,192},{288,336},{336... | collective-permute-start | bytes 2949128 | tf_op jit(solution)/shard_map/ppermute | solution.py:59
  148.8 29.3 %collective-permute-start = (bf16[2,240,768]{2,1,0:T(8,128)(2,1)}, bf16[2,240,768]{2,1,0:T(8,128)(2,1)}, u32[]{:S(2)}, u32[]{:S(2)}) collective-permute-start(bf16[2,240,768]{2,1,0:T(8,128)(2,1)} %get-tuple-element.16), channel_id=1, source_target_pairs={{0,48},{48,0},{96,144},{144,96},{192,240},{240,192},{288,336},{336... | collective-permute-start | bytes 2211848 | tf_op jit(solution)/shard_map/ppermute | solution.py:60
  151.6 19.0 %all-to-all-start.2 = ((f32[1,2,48,5]{3,1,0,2:T(2,128)}), f32[1,2,48,5]{3,1,0,2:T(2,128)}, u32[]{:S(2)}, u32[]{:S(2)}) async-start(f32[1,2,48,5]{3,1,0,2:T(2,128)} %copy.77), calls=%async_computation.2 | async-start | bytes 98304 | tf_op jit(solution)/shard_map/all_to_all | solution.py:95
  159.8 12.2 %copy-start.3 = (bf16[48,2048]{1,0:T(8,128)(2,1)S(1)}, bf16[48,2048]{1,0:T(8,128)(2,1)}, u32[]{:S(2)}) copy-start(bf16[48,2048]{1,0:T(8,128)(2,1)} %param.6) | copy-start | bytes 589828
  160.1 11.5 %copy-start.5 = (f32[48,96]{1,0:T(8,128)S(1)}, f32[48,96]{1,0:T(8,128)}, u32[]{:S(2)}) copy-start(f32[48,96]{1,0:T(8,128)} %copy-done.4) | copy-start | bytes 55300
  160.1 11.5 %copy-start.7 = (pred[480,48]{0,1:T(8,128)(4,1)S(1)}, pred[480,48]{0,1:T(8,128)(4,1)}, u32[]{:S(2)}) copy-start(pred[480,48]{0,1:T(8,128)(4,1)} %copy-done.6) | copy-start | bytes 69124
  160.1 11.5 %copy-start.9 = (s32[480]{0:T(512)S(1)}, s32[480]{0:T(512)}, u32[]{:S(2)}) copy-start(s32[480]{0:T(512)} %copy-done.8) | copy-start | bytes 5764
  173.6 43.3 %all-to-all-start.3 = ((bf16[48,2,2048]{2,1,0:T(2,128)(2,1)}), bf16[48,2,2048]{2,1,0:T(2,128)(2,1)S(1)}, u32[]{:S(2)}, u32[]{:S(2)}) async-start(bf16[48,2,2048]{2,1,0:T(2,128)(2,1)} %reshape.124), calls=%async_computation.3 | async-start | bytes 786432 | tf_op jit(solution)/shard_map/all_to_all | solution.py:106
  189.2 8.4 %collective-permute-start.2 = (bf16[768,128]{1,0:T(8,128)(2,1)S(1)}, bf16[768,128]{1,0:T(8,128)(2,1)S(1)}, u32[]{:S(2)}, u32[]{:S(2)}) collective-permute-start(bf16[768,128]{1,0:T(8,128)(2,1)S(1)} %get-tuple-element.17), channel_id=1, source_target_pairs={{0,96},{48,144},{96,192},{144,240},{192,288},{240,336},{288,384},{... | collective-permute-start | bytes 589832 | tf_op jit(solution)/shard_map/ppermute | solution.py:78
  192.5 7.2 %collective-permute-start.6 = (bf16[768,128]{1,0:T(8,128)(2,1)S(1)}, bf16[768,128]{1,0:T(8,128)(2,1)S(1)}, u32[]{:S(2)}, u32[]{:S(2)}) collective-permute-start(bf16[768,128]{1,0:T(8,128)(2,1)S(1)} %get-tuple-element.18), channel_id=1, source_target_pairs={{0,672},{48,720},{96,0},{144,48},{192,96},{240,144},{288,192},{336... | collective-permute-start | bytes 589832 | tf_op jit(solution)/shard_map/ppermute | solution.py:79
  197.7 11.1 %collective-permute-start.3 = (bf16[2,768,128]{2,1,0:T(8,128)(2,1)S(1)}, bf16[2,768,128]{2,1,0:T(8,128)(2,1)S(1)}, u32[]{:S(2)}, u32[]{:S(2)}) collective-permute-start(bf16[2,768,128]{2,1,0:T(8,128)(2,1)S(1)} %pad_maximum_fusion), channel_id=1, source_target_pairs={{0,96},{48,144},{96,192},{144,240},{192,288},{240,336},{288,384},{... | collective-permute-start | bytes 1179656 | tf_op jit(solution)/shard_map/ppermute | solution.py:88
  199.8 11.8 %collective-permute-start.7 = (bf16[2,768,128]{2,1,0:T(8,128)(2,1)S(1)}, bf16[2,768,128]{2,1,0:T(8,128)(2,1)S(1)}, u32[]{:S(2)}, u32[]{:S(2)}) collective-permute-start(bf16[2,768,128]{2,1,0:T(8,128)(2,1)S(1)} %pad_maximum_fusion.1), channel_id=1, source_target_pairs={{0,672},{48,720},{96,0},{144,48},{192,96},{240,144},{288,192},{336... | collective-permute-start | bytes 1179656 | tf_op jit(solution)/shard_map/ppermute | solution.py:89
  209.6 19.2 %collective-permute-start.4 = (bf16[2,768,128]{2,1,0:T(8,128)(2,1)}, bf16[2,768,128]{2,1,0:T(8,128)(2,1)}, u32[]{:S(2)}, u32[]{:S(2)}) collective-permute-start(bf16[2,768,128]{2,1,0:T(8,128)(2,1)} %fusion.16), channel_id=1, source_target_pairs={{0,96},{48,144},{96,192},{144,240},{192,288},{240,336},{288,384},{... | collective-permute-start | bytes 1179656 | tf_op jit(solution)/shard_map/ppermute | solution.py:88
  212.4 21.6 %collective-permute-start.8 = (bf16[2,768,128]{2,1,0:T(8,128)(2,1)}, bf16[2,768,128]{2,1,0:T(8,128)(2,1)}, u32[]{:S(2)}, u32[]{:S(2)}) collective-permute-start(bf16[2,768,128]{2,1,0:T(8,128)(2,1)} %fusion.14), channel_id=1, source_target_pairs={{0,672},{48,720},{96,0},{144,48},{192,96},{240,144},{288,192},{336... | collective-permute-start | bytes 1179656 | tf_op jit(solution)/shard_map/ppermute | solution.py:89
  218.1 22.7 %all-to-all-start.4 = ((f32[16,2,2048]{2,1,0:T(2,128)}), f32[16,2,2048]{2,1,0:T(2,128)S(1)}, u32[]{:S(2)}, u32[]{:S(2)}) async-start(f32[16,2,2048]{2,1,0:T(2,128)} %broadcast_in_dim.54), calls=%async_computation.4 | async-start | bytes 524288 | tf_op jit(solution)/shard_map/all_to_all | solution.py:111
  230.7 16.0 %collective-permute-start.5 = (bf16[2,768,128]{2,1,0:T(8,128)(2,1)}, bf16[2,768,128]{2,1,0:T(8,128)(2,1)S(1)}, u32[]{:S(2)}, u32[]{:S(2)}) collective-permute-start(bf16[2,768,128]{2,1,0:T(8,128)(2,1)} %fusion.17), channel_id=1, source_target_pairs={{0,96},{48,144},{96,192},{144,240},{192,288},{240,336},{288,384},{... | collective-permute-start | bytes 1179656 | tf_op jit(solution)/shard_map/ppermute | solution.py:88
  235.8 12.1 %collective-permute-start.9 = (bf16[2,768,128]{2,1,0:T(8,128)(2,1)}, bf16[2,768,128]{2,1,0:T(8,128)(2,1)S(1)}, u32[]{:S(2)}, u32[]{:S(2)}) collective-permute-start(bf16[2,768,128]{2,1,0:T(8,128)(2,1)} %fusion.15), channel_id=1, source_target_pairs={{0,672},{48,720},{96,0},{144,48},{192,96},{240,144},{288,192},{336... | collective-permute-start | bytes 1179656 | tf_op jit(solution)/shard_map/ppermute | solution.py:89

commit v2 on v0

v2 whole, which is shorter than its diff:
```python
import functools

import jax
import jax.numpy as jnp
import numpy as np
from jax import lax
from jax.experimental import pallas as pl
from jax.experimental.pallas import tpu as pltpu
from jax.sharding import PartitionSpec as P

F32 = jnp.float32
BF16 = jnp.bfloat16
LANES = 128
N_X = 4
VMEM_BYTES = 40 * 1024 * 1024


def dot(a, b, dims=((1,), (0,))):
    return lax.dot_general(a, b, (dims, ((), ())), preferred_element_type=F32)


def iota(shape, axis):
    return lax.broadcasted_iota(jnp.int32, shape, axis)


def call(body, out_shape, flops, moved, n_smem=0, **kwargs):
    return pl.pallas_call(
        body,
        out_shape=out_shape,
        compiler_params=pltpu.CompilerParams(vmem_limit_bytes=VMEM_BYTES),
        cost_estimate=pl.CostEstimate(flops=flops, bytes_accessed=moved, transcendentals=0),
        **kwargs,
    )


def whole(n):
    return [pl.BlockSpec(memory_space=pltpu.VMEM)] * n


def route_kernel(x_ref, grad_ref, rw_ref, routes_ref, payload_ref, probs_ref, code_ref):
    experts, width = rw_ref.shape
    top, rows = routes_ref.shape
    ids = iota((experts, rows), 0)
    chosen = ids == routes_ref[0:1, :]
    for k in range(1, top):
        chosen = chosen | (ids == routes_ref[k : k + 1, :])
    logits = dot(rw_ref[...], x_ref[...], ((1,), (1,)))
    highest = jnp.max(jnp.where(chosen, logits, -jnp.inf), axis=0, keepdims=True)
    weights = jnp.where(chosen, jnp.exp(jnp.where(chosen, logits - highest, 0.0)), 0.0)
    probs = weights / jnp.sum(weights, axis=0, keepdims=True)
    earlier = jnp.where(iota((rows, rows), 0) < iota((rows, rows), 1), 1.0, 0.0).astype(BF16)
    position = dot(jnp.where(chosen, 1.0, 0.0).astype(BF16), earlier)
    probs_ref[...] = probs
    code_ref[...] = jnp.where(chosen, position, -1.0)
    marked = jnp.where(chosen, probs, -1.0).astype(BF16)
    turn = jnp.where(iota((experts, LANES), 0) == iota((experts, LANES), 1), 1.0, 0.0).astype(BF16)
    payload_ref[:, :width] = grad_ref[...]
    payload_ref[:, width:] = dot(marked, turn, ((0,), (0,))).astype(BF16)


def pick_kernel(n_blocks, n_z, exp_dev, place_ref, plan_ref, *refs):
    blocks, outs, joined = refs[:n_blocks], refs[n_blocks : n_blocks + N_X], refs[n_blocks + N_X]
    rows, wide = blocks[0].shape
    width = wide - LANES
    total = n_blocks * rows
    for i, block in enumerate(blocks):
        joined[i * rows : (i + 1) * rows, :] = block[...]
    picks = plan_ref.shape[0]
    out_rows = picks // N_X
    shift, local, slot, source = (plan_ref[:, i : i + 1] for i in range(4))
    expert = (((place_ref[0] + shift) & (N_X - 1)) * n_z + place_ref[1]) * exp_dev + local
    wanted = jnp.where(iota((picks, LANES), 1) == expert, 1.0, 0.0).astype(BF16)
    value = dot(wanted, joined[:, width:], ((1,), (1,)))
    here = iota((picks, total), 1)
    base = source * rows
    own = (here >= base) & (here < base + rows)
    chosen = own & (value >= 0.0)
    earlier = jnp.where(iota((total, total), 0) < iota((total, total), 1), 1.0, 0.0).astype(BF16)
    position = dot(jnp.where(chosen, 1.0, 0.0).astype(BF16), earlier)
    picked = chosen & (position == slot.astype(F32))
    gate = jnp.sum(jnp.where(picked, value, 0.0), axis=1, keepdims=True)
    picker = jnp.where(picked, 1.0, 0.0).astype(BF16)
    result = dot(picker, joined[:, :width]).astype(BF16)
    tail = jnp.where(iota((picks, LANES), 1) == 0, gate, 0.0).astype(BF16)
    for i, out in enumerate(outs):
        out[:, :width] = result[i * out_rows : (i + 1) * out_rows]
        out[:, width:] = tail[i * out_rows : (i + 1) * out_rows]


def place_kernel(n_parts, place_ref, target_ref, hidden_ref, *refs):
    parts = refs[:n_parts]
    rows_ref, gate_ref, keep_ref, trade_ref, joined = refs[n_parts:]
    slots, width = rows_ref.shape
    at = 0
    for part in parts:
        joined[at : at + part.shape[0], :] = part[...]
        at += part.shape[0]
    placer = jnp.where(iota((slots, at), 0) == target_ref[...], 1.0, 0.0).astype(BF16)
    gate = dot(placer, joined[:, width:])[:, 0:1]
    gate_ref[...] = gate
    rows_ref[...] = dot(placer, joined[:, :width]).astype(BF16)
    gated = (gate * hidden_ref[...].astype(F32)).astype(BF16)
    n_y = width // (2 * LANES)
    keep_ref[:, width // 2 :] = gated
    trade_ref[:, width // 2 :] = gated
    for k in range(n_y):
        chip = lax.rem(place_ref[2] + k, n_y)
        mine = pl.multiple_of((2 * chip + place_ref[3]) * LANES, LANES)
        other = pl.multiple_of((2 * chip + 1 - place_ref[3]) * LANES, LANES)
        keep_ref[:, k * LANES : (k + 1) * LANES] = rows_ref[:, pl.ds(mine, LANES)]
        trade_ref[:, k * LANES : (k + 1) * LANES] = rows_ref[:, pl.ds(other, LANES)]


def product_kernel(capacity, rows_ref, gate_ref, hidden_ref, weight_ref, grad_ref, back_ref, sums):
    e, f = pl.program_id(0), pl.program_id(1)
    slots = rows_ref.shape[0]
    product = dot(rows_ref[...], weight_ref[0], ((1,), (1,)))
    grad_ref[0, 0] = (gate_ref[...] * product).astype(BF16)
    part = jnp.sum(product * hidden_ref[...].astype(F32), axis=1, keepdims=True)

    @pl.when(f == 0)
    def _():
        sums[...] = part

    @pl.when(f > 0)
    def _():
        sums[...] += part

    @pl.when((e == 0) & (f == 0))
    def _():
        back_ref[...] = jnp.zeros_like(back_ref)

    @pl.when(f == pl.num_programs(1) - 1)
    def _():
        lane = iota((slots, LANES), 1)
        slot = iota((slots, LANES), 0)
        spread = jnp.where(lane == e * capacity + lax.rem(slot, capacity), sums[...], 0.0)
        n_source = back_ref.shape[0]
        first = iota((n_source, slots), 0) * capacity
        slot = iota((n_source, slots), 1)
        group = jnp.where((slot >= first) & (slot < first + capacity), 1.0, 0.0).astype(BF16)
        high = spread.astype(BF16)
        rest = spread - high.astype(F32)
        middle = rest.astype(BF16)
        low = (rest - middle.astype(F32)).astype(BF16)
        back_ref[...] += dot(group, high) + dot(group, middle) + dot(group, low)


def partial_kernel(chunks, mine_ref, got_ref, *outs):
    ff = outs[0].shape[-2]
    half_width = mine_ref.shape[1] - ff
    slots = mine_ref.shape[0]
    exp_dev = 2
    per = slots // exp_dev
    low, high = chunks[0] * LANES, (chunks[-1] + 1) * LANES
    for e in range(exp_dev):
        span = pl.ds(e * per, per)
        total = dot(mine_ref[span, half_width:], mine_ref[span, low:high], ((0,), (0,)))
        total += dot(got_ref[span, half_width:], got_ref[span, low:high], ((0,), (0,)))
        total = total.astype(BF16)
        if len(outs) == exp_dev:
            outs[e][...] = total
        else:
            for i in range(len(chunks)):
                outs[0][i, e] = total[:, i * LANES : (i + 1) * LANES]


def add_kernel(side, blocks_ref, arrived_ref, out_ref):
    if side is None:
        out_ref[...] = (blocks_ref[0].astype(F32) + arrived_ref[...].astype(F32)).astype(BF16)
    else:
        out_ref[side] = (blocks_ref[0, side].astype(F32) + arrived_ref[...].astype(F32)).astype(BF16)
        out_ref[1 - side] = blocks_ref[0, 1 - side]


def router_kernel(capacity, exp_dev, back_ref, probs_ref, code_ref, x_ref, rw_ref, term_ref, grad_ref):
    experts, rows = probs_ref.shape
    n_dev = back_ref.shape[0]
    width = rw_ref.shape[1]
    back = back_ref[...]
    ids = iota((experts, n_dev), 0)
    first = iota((experts, n_dev), 1) * exp_dev
    owner = jnp.where((ids >= first) & (ids < first + exp_dev), 1.0, 0.0).astype(BF16)
    high = back.astype(BF16)
    rest = back - high.astype(F32)
    middle = rest.astype(BF16)
    low = (rest - middle.astype(F32)).astype(BF16)
    spread = dot(owner, high) + dot(owner, middle) + dot(owner, low)
    lane = iota((experts, LANES), 1)
    start = lax.rem(iota((experts, LANES), 0), exp_dev) * capacity
    code = code_ref[...]
    probs = probs_ref[...]
    gate_grad = jnp.zeros((experts, rows), F32)
    for c in range(capacity):
        column = jnp.sum(jnp.where(lane == start + c, spread, 0.0), axis=1, keepdims=True)
        gate_grad += jnp.where(code == c, column, 0.0)
    weighted = jnp.sum(probs * gate_grad, axis=0, keepdims=True)
    logit_grad = probs * (gate_grad - weighted)
    high = logit_grad.astype(BF16)
    low = (logit_grad - high.astype(F32)).astype(BF16)
    grad_ref[...] = dot(high, rw_ref[...], ((0,), (0,))).astype(BF16)
    out_rows, piece = term_ref.shape
    split = width // piece
    row = iota((out_rows, experts), 0)
    first = iota((out_rows, experts), 1) * split
    repeat = jnp.where((row >= first) & (row < first + split), 1.0, 0.0).astype(BF16)
    high = dot(repeat, high).astype(BF16)
    low = dot(repeat, low).astype(BF16)
    quarter = lax.rem(iota((out_rows, 1), 0), split)
    total = jnp.zeros((out_rows, piece), F32)
    for q in range(split):
        x = x_ref[:, q * piece : (q + 1) * piece]
        total += jnp.where(quarter == q, dot(high, x) + dot(low, x), 0.0)
    term_ref[...] = total.astype(BF16)


def batches_of(n_z):
    ahead, back = n_z // 2, (n_z - 1) // 2
    steps = [[0]] + [[s, -s] if s <= back else [s] for s in range(1, ahead + 1)]
    if n_z < 8:
        cuts = [len(steps)]
    else:
        cuts = [len(steps) - 4, len(steps) - 2, len(steps)]
    batches, at = [], 0
    for cut in cuts:
        batches.append([d for step in steps[at:cut] for d in step])
        at = cut
    return batches, ahead, back


def on_device(layer_input, out_grad, router_weight, routes, hidden_act, down_weight):
    n_expert = lax.axis_size("expert")
    n_dp = lax.axis_size("dp")
    n_y, n_z = n_dp // 2, n_expert // N_X
    experts, width = router_weight.shape
    exp_dev = experts // n_expert
    per = hidden_act.shape[2]
    slots = exp_dev * per
    ff = hidden_act.shape[3]
    capacity = per // n_expert
    tok_rows, top_count = routes.shape
    wide = width + LANES
    shape = jax.ShapeDtypeStruct
    dp_index, expert_index = lax.axis_index("dp"), lax.axis_index("expert")
    x_index, z_index = expert_index // n_z, expert_index % n_z
    place = jnp.stack([x_index, z_index, dp_index // 2, dp_index % 2]).astype(jnp.int32)
    smem = pl.BlockSpec(memory_space=pltpu.SMEM)

    payload, probs, code = call(
        route_kernel,
        (shape((tok_rows, wide), BF16), shape((experts, tok_rows), F32), shape((experts, tok_rows), F32)),
        2 * tok_rows * experts * width,
        2 * (2 * tok_rows + experts) * width,
    )(layer_input, out_grad, router_weight, routes.T)

    batches, ahead, behind = batches_of(n_z)
    z_of = lambda shift: [(x * n_z + z, x * n_z + (z + shift) % n_z) for x in range(N_X) for z in range(n_z)]
    x_of = lambda shift: [(x * n_z + z, (x + shift) % N_X * n_z + z) for x in range(N_X) for z in range(n_z)]
    held = {0: payload}
    parts, targets = [], []
    done, due, picked = 0, 0, None
    pick_slots = exp_dev * capacity
    for batch in batches:
        last = max(abs(d) for d in batch)
        while done < last:
            done += 1
            if due == done:
                front, rear = held[done - 1], held[1 - done]
                front, rear, first = lax.optimization_barrier((front, rear, picked[0]))
                held[done - 1], held[1 - done], parts[-N_X] = front, rear, first
            held[done] = lax.ppermute(held[done - 1], "expert", z_of(1))
            if done <= behind:
                held[-done] = lax.ppermute(held[-done + 1], "expert", z_of(-1))
        count = len(batch)
        out_rows = -(-count * pick_slots // 16) * 16
        plan = np.full((N_X, out_rows, 4), -1, np.int32)
        target = np.full((N_X, out_rows, 4), -1, np.int32)
        for shift in range(N_X):
            for i, delta in enumerate(batch):
                for local in range(exp_dev):
                    for c in range(capacity):
                        row = i * pick_slots + local * capacity + c
                        plan[shift, row] = (shift, local, c, i)
                        target[shift, row] = (shift, delta, local, c)
        plan = plan.reshape(N_X * out_rows, 4)
        targets.append(target.reshape(N_X * out_rows, 4))
        picked = call(
            functools.partial(pick_kernel, count, n_z, exp_dev),
            [shape((out_rows, wide), BF16)] * N_X,
            2 * N_X * out_rows * count * tok_rows * width,
            2 * (N_X * out_rows + count * tok_rows) * wide,
            in_specs=[smem] + whole(1 + count),
            out_specs=whole(N_X),
            scratch_shapes=[pltpu.VMEM((count * tok_rows, wide), BF16)],
        )(place, jnp.asarray(plan), *[held[d] for d in batch])
        parts.append(picked[0])
        for shift in range(1, N_X):
            parts.append(lax.ppermute(picked[shift], "expert", x_of(shift)))
        due = last + 2

    table = np.concatenate(targets)
    source = ((x_index - table[:, 0]) % N_X) * n_z + (z_index - table[:, 1]) % n_z
    target = jnp.where(table[:, 2] >= 0, table[:, 2] * per + source * capacity + table[:, 3], -1)
    total_rows = table.shape[0]
    hidden = hidden_act.reshape(slots, ff)
    rows, gate, keep, trade = call(
        functools.partial(place_kernel, len(parts)),
        (
            shape((slots, width), BF16),
            shape((slots, 1), F32),
            shape((slots, width // 2 + ff), BF16),
            shape((slots, width // 2 + ff), BF16),
        ),
        2 * slots * total_rows * wide,
        2 * total_rows * wide + 2 * slots * (2 * width + 3 * ff),
        in_specs=[smem] + whole(2 + len(parts)),
        out_specs=whole(4),
        scratch_shapes=[pltpu.VMEM((total_rows, wide), BF16)],
    )(place, target[None, :].astype(jnp.int32), hidden, *parts)

    got = lax.ppermute(trade, "dp", [(i, i ^ 1) for i in range(n_dp)])

    tile = ff // 2 if ff % 256 == 0 else ff
    hidden_grad, back = call(
        functools.partial(product_kernel, capacity),
        (shape((1, exp_dev, per, ff), BF16), shape((n_expert, LANES), F32)),
        2 * slots * ff * width,
        2 * (slots + exp_dev * ff) * width + 4 * slots * ff,
        grid=(exp_dev, ff // tile),
        in_specs=[
            pl.BlockSpec((per, width), lambda e, f: (e, 0)),
            pl.BlockSpec((per, 1), lambda e, f: (e, 0)),
            pl.BlockSpec((per, tile), lambda e, f: (e, f)),
            pl.BlockSpec((1, tile, width), lambda e, f: (e, f, 0)),
        ],
        out_specs=(
            pl.BlockSpec((1, 1, per, tile), lambda e, f: (0, e, 0, f)),
            pl.BlockSpec((n_expert, LANES), lambda e, f: (0, 0)),
        ),
        scratch_shapes=[pltpu.VMEM((per, 1), F32)],
    )(rows, gate, hidden, down_weight)

    got, back = lax.optimization_barrier((got, back))

    back = lax.all_to_all(back.reshape(n_expert, 1, LANES), "expert", split_axis=0, concat_axis=0, tiled=True)
    piece = exp_dev * width // 8
    term, input_grad = call(
        functools.partial(router_kernel, capacity, exp_dev),
        (shape((n_expert * 8, piece), BF16), shape((tok_rows, width), BF16)),
        2 * tok_rows * width * (experts + 2 * n_expert * 8),
        2 * (2 * tok_rows + 2 * experts) * width,
    )(back.reshape(n_expert, LANES), probs, code, layer_input, router_weight)

    half = n_y // 2
    far_up, far_down = call(
        functools.partial(partial_kernel, [half]),
        [shape((ff, LANES), BF16)] * 2,
        4 * slots * ff * LANES,
        4 * slots * (ff + LANES),
        in_specs=whole(2),
        out_specs=whole(2),
    )(keep, got)
    up = [(i, (i + 2) % n_dp) for i in range(n_dp)]
    down = [(i, (i - 2) % n_dp) for i in range(n_dp)]
    going_up = lax.ppermute(far_up, "dp", up)
    going_down = lax.ppermute(far_down, "dp", down)

    def blocks_of(chunks):
        (blocks,) = call(
            functools.partial(partial_kernel, chunks),
            [shape((len(chunks), exp_dev, ff, LANES), BF16)],
            4 * slots * ff * LANES * len(chunks),
            4 * slots * (ff + LANES * len(chunks)),
            in_specs=whole(2),
            out_specs=whole(1),
        )(keep, got)
        return blocks

    def add_block(blocks, index, arrived):
        side = None if arrived.ndim == 3 else int(blocks is rest)
        size = (1, exp_dev, ff, LANES)
        return call(
            functools.partial(add_kernel, side),
            shape(size[1:], BF16),
            2 * exp_dev * ff * LANES,
            6 * exp_dev * ff * LANES,
            grid=(1,),
            in_specs=[pl.BlockSpec(size, lambda i: (index, 0, 0, 0)), pl.BlockSpec(arrived.shape, lambda i: (0,) * arrived.ndim)],
            out_specs=pl.BlockSpec(size[1:], lambda i: (0, 0, 0)),
        )(blocks, arrived)

    if half > 1:
        near, rest = blocks_of(list(range(half))), blocks_of(list(range(half + 1, n_y)))
    else:
        keep_far = jnp.stack([going_up, going_down])
        both = call(
            functools.partial(partial_kernel, [0]),
            [shape((ff, LANES), BF16)] * 2,
            4 * slots * ff * LANES,
            4 * slots * (ff + LANES),
            in_specs=whole(2),
            out_specs=whole(2),
        )(keep, got)
        down_grad = jnp.stack(both).astype(F32) + keep_far.astype(F32)
    for step in range(half - 1, 0, -1):
        going_up = lax.ppermute(add_block(near, step, going_up), "dp", up)
        going_down = lax.ppermute(add_block(rest, half - 1 - step, going_down), "dp", down)
    if half > 1:
        down_grad = near[0].astype(F32) + going_up.astype(F32) + going_down.astype(F32)

    shares = lax.all_to_all(term.reshape(n_expert, 8, piece), "expert", split_axis=0, concat_axis=0, tiled=True)
    replica_sum = jnp.sum(shares.astype(F32), axis=0)
    copies = jnp.broadcast_to(replica_sum[None], (n_dp, 8, piece))
    gathered = lax.all_to_all(copies, "dp", split_axis=0, concat_axis=0, tiled=True)
    router_grad = jnp.sum(gathered, axis=0).reshape(exp_dev, width)
    return (down_grad, hidden_grad, router_grad, input_grad)


def solution(mesh):
    in_specs = (
        P(("dp", "expert"), None),
        P(("dp", "expert"), None),
        P(),
        P(("dp", "expert"), None),
        P("dp", "expert", None, None),
        P("expert", None, None),
    )
    out_specs = (
        P("expert", None, "dp"),
        P("dp", "expert", None, None),
        P("expert", None),
        P(("dp", "expert"), None),
    )
    return jax.shard_map(
        on_device, mesh=mesh, in_specs=in_specs, out_specs=out_specs, check_vma=False
    )
```

time: 646 us -> 208 us (0.32)
  waiting for transfers between devices: 537 us -> 34.2 us
  starting transfers between devices: 33.3 us -> 126 us
  matrix products: 25.6 us -> 0 us
  Pallas kernels: 0 us -> 17.4 us
  local copies, waits for them, and re-layouts: 26.6 us -> 9.35 us
  blocking collectives: 0 us -> 16 us
  between operations: 15.8 us -> 1.29 us
    psum x1 -> x0, waiting for transfers between devices: 451 us -> none  [on_device(): summed = lax.psum(router_term, ('dp', 'expert'))]
    ppermute x0 -> x29, starting transfers between devices: none -> 112 us  [the longest x5 35.1 us: on_device(): held[-done] = lax.ppermute(held[-done + 1], 'expert', z_of(-1))]
    all_to_all x3 -> x2, waiting for transfers between devices: 86.2 us -> 10.7 us  [the longest x1 10.7 us: on_device(): lax.all_to_all(copies, 'dp', split_axis=0, concat_axis=0, tiled=True)]
    dot_general x7 -> x0, matrix products: 25.6 us -> none  [the longest x1 8.24 us: on_device(): jnp.einsum('esd,efd->esf', scaled, down_weight, preferred_element_type=jn...]
    ppermute x0 -> x29, waiting for transfers between devices: none -> 23.5 us  [the longest x6 8.22 us: on_device(): held[done] = lax.ppermute(held[done - 1], 'expert', z_of(1))]
    all_to_all x3 -> x2, starting transfers between devices: 33 us -> 14 us  [the longest x1 8.69 us: on_device(): lax.all_to_all(copies, 'dp', split_axis=0, concat_axis=0, tiled=True)]
    pallas_call x0 -> x16, Pallas kernels: none -> 17.4 us  [the longest x1 4.64 us: on_device(): call(functools.partial(product_kernel, capacity), (shape((1, exp_dev, per...]
    all_to_all x0 -> x1, blocking collectives: none -> 16 us  [on_device(): lax.all_to_all(back.reshape(n_expert, 1, LANES), 'expert', split_axis=0,...]
  transfers between devices with their start and end apart: 5 -> 31, of which waited for: 4 -> 10; matrix products, arithmetic and copies ran while one was open for 3% -> 1% of each run, Pallas kernels for 0% -> 6%
where the time goes in v2:
time: 208 us; the launch traced here: 207 us
  starting transfers between devices  126 us (61%)
  waiting for transfers between devices  34.2 us (16%)
  Pallas kernels  17.4 us (8%)
  blocking collectives  16 us (8%)
  local copies, waits for them, and re-layouts  9.35 us (4%)
  other arithmetic  2.2 us (1%)
    ppermute x5, starting transfers between devices, on_device(): held[-done] = lax.ppermute(held[-done + 1], 'expert', z_of(-1))  35.1 us
    ppermute x9, starting transfers between devices, on_device(): parts.append(lax.ppermute(picked[shift], 'expert', x_of(shift)))  27.7 us
    all_to_all x1, blocking collectives, on_device(): lax.all_to_all(back.reshape(n_expert, 1, LANES), 'expert', split_axis=0,...  16 us
    ppermute x3, starting transfers between devices, on_device(): lax.ppermute(add_block(rest, half - 1 - step, going_down), 'dp', down)  15.2 us
    ppermute x6, starting transfers between devices, on_device(): held[done] = lax.ppermute(held[done - 1], 'expert', z_of(1))  11.5 us
    all_to_all x1, waiting for transfers between devices, on_device(): lax.all_to_all(copies, 'dp', split_axis=0, concat_axis=0, tiled=True)  10.7 us
    ppermute x1, starting transfers between devices, on_device(): got = lax.ppermute(trade, 'dp', [(i, i ^ 1) for i in range(n_dp)])  9.9 us
    all_to_all x1, starting transfers between devices, on_device(): lax.all_to_all(copies, 'dp', split_axis=0, concat_axis=0, tiled=True)  8.69 us
  transfers between devices with their start and end apart: 31, of which 10 were waited for; matrix products, arithmetic and copies ran while one was open for 1% of the time, Pallas kernels for 6%

profile of v2, /device:TPU:1, one launch (start us, length us, event | category | flops | bytes accessed | tf_op | source)
XLA Modules:
  0.0 206.8 jit_solution(18354525381285518808)
XLA Ops:
  0.6 1.0 copy-done.3
  1.6 0.9 copy-done.5
  2.6 0.9 copy-done.8
  3.5 0.7 copy-done.12
  4.2 0.5 shard_map.165
  4.7 15.1 %collective-permute-start.3 = (bf16[48,2176]{1,0:T(8,128)(2,1)S(1)}, bf16[48,2176]{1,0:T(8,128)(2,1)S(1)}, u32[]{:S(2)}, u32[]{:S(2)}) collective-permute-start(bf16[48,2176]{1,0:T(8,128)(2,1)S(1)} %get-tuple-element.37.refs_0_), channel_id=1, source_target_pairs={{0,11},{1,0},{2,1},{3,2},{4,3},{5,4},{6,5},{7,6},{8,7},{9,8},{10,9... | collective-permute-start | bytes 626696 | tf_op jit(solution)/shard_map/ppermute | solution.py:273
  19.8 1.9 collective-permute-start
  21.8 1.9 collective-permute-done.3.refs_2_
  23.7 5.3 %collective-permute-start.4 = (bf16[48,2176]{1,0:T(8,128)(2,1)S(1)}, bf16[48,2176]{1,0:T(8,128)(2,1)S(1)}, u32[]{:S(2)}, u32[]{:S(2)}) collective-permute-start(bf16[48,2176]{1,0:T(8,128)(2,1)S(1)} %collective-permute-done.3.refs_2_), channel_id=1, source_target_pairs={{0,11},{1,0},{2,1},{3,2},{4,3},{5,4},{6,5},{7,6},{8,7},{9,8},{10,9... | collective-permute-start | bytes 626696 | tf_op jit(solution)/shard_map/ppermute | solution.py:273
  29.0 1.9 collective-permute-start.1
  30.9 0.8 collective-permute-done.4.refs_4_
  31.7 5.5 %collective-permute-start.5 = (bf16[48,2176]{1,0:T(8,128)(2,1)S(1)}, bf16[48,2176]{1,0:T(8,128)(2,1)S(1)}, u32[]{:S(2)}, u32[]{:S(2)}) collective-permute-start(bf16[48,2176]{1,0:T(8,128)(2,1)S(1)} %collective-permute-done.4.refs_4_), channel_id=1, source_target_pairs={{0,11},{1,0},{2,1},{3,2},{4,3},{5,4},{6,5},{7,6},{8,7},{9,8},{10,9... | collective-permute-start | bytes 626696 | tf_op jit(solution)/shard_map/ppermute | solution.py:273
  37.2 1.9 collective-permute-start.2
  39.3 0.9 copy-done.9
  40.2 1.4 shard_map.166
  41.6 3.4 %collective-permute-done.2.refs_0_ = bf16[48,2176]{1,0:T(8,128)(2,1)S(1)} collective-permute-done((bf16[48,2176]{1,0:T(8,128)(2,1)S(1)}, bf16[48,2176]{1,0:T(8,128)(2,1)S(1)}, u32[]{:S(2)}, u32[]{:S(2)}) %collective-permute-start.2) | collective-permute-done | bytes 208928 | tf_op jit(solution)/shard_map/ppermute | solution.py:271
  45.0 1.9 collective-permute-start.9
  46.9 4.6 %collective-permute-start.11 = (bf16[48,2176]{1,0:T(8,128)(2,1)S(1)}, bf16[48,2176]{1,0:T(8,128)(2,1)S(1)}, u32[]{:S(2)}, u32[]{:S(2)}) collective-permute-start(bf16[48,2176]{1,0:T(8,128)(2,1)S(1)} %collective-permute-done.5.refs_1_), channel_id=1, source_target_pairs={{0,11},{1,0},{2,1},{3,2},{4,3},{5,4},{6,5},{7,6},{8,7},{9,8},{10,9... | collective-permute-start | bytes 626696 | tf_op jit(solution)/shard_map/ppermute | solution.py:273
  51.4 1.2 collective-permute-done.9.refs_2_
  52.7 1.9 collective-permute-start.10
  54.6 4.6 %collective-permute-start.12 = (bf16[48,2176]{1,0:T(8,128)(2,1)S(1)}, bf16[48,2176]{1,0:T(8,128)(2,1)S(1)}, u32[]{:S(2)}, u32[]{:S(2)}) collective-permute-start(bf16[48,2176]{1,0:T(8,128)(2,1)S(1)} %collective-permute-done.11.refs_3_), channel_id=1, source_target_pairs={{0,11},{1,0},{2,1},{3,2},{4,3},{5,4},{6,5},{7,6},{8,7},{9,8},{10,9... | collective-permute-start | bytes 626696 | tf_op jit(solution)/shard_map/ppermute | solution.py:273
  59.2 3.1 %collective-permute-start.6 = (bf16[64,2176]{1,0:T(8,128)(2,1)S(1)}, bf16[64,2176]{1,0:T(8,128)(2,1)S(1)}, u32[]{:S(2)}, u32[]{:S(2)}) collective-permute-start(bf16[64,2176]{1,0:T(8,128)(2,1)S(1)} %get-tuple-element.40), channel_id=1, source_target_pairs={{0,12},{1,13},{2,14},{3,15},{4,16},{5,17},{6,18},{7,19},{8,20},{9,... | collective-permute-start | bytes 835592 | tf_op jit(solution)/shard_map/ppermute | solution.py:298
  62.3 4.4 %collective-permute-start.7 = (bf16[64,2176]{1,0:T(8,128)(2,1)S(1)}, bf16[64,2176]{1,0:T(8,128)(2,1)S(1)}, u32[]{:S(2)}, u32[]{:S(2)}) collective-permute-start(bf16[64,2176]{1,0:T(8,128)(2,1)S(1)} %get-tuple-element.41), channel_id=1, source_target_pairs={{0,24},{1,25},{2,26},{3,27},{4,28},{5,29},{6,30},{7,31},{8,32},{9,... | collective-permute-start | bytes 835592 | tf_op jit(solution)/shard_map/ppermute | solution.py:298
  66.7 3.0 %collective-permute-start.8 = (bf16[64,2176]{1,0:T(8,128)(2,1)S(1)}, bf16[64,2176]{1,0:T(8,128)(2,1)S(1)}, u32[]{:S(2)}, u32[]{:S(2)}) collective-permute-start(bf16[64,2176]{1,0:T(8,128)(2,1)S(1)} %get-tuple-element.42), channel_id=1, source_target_pairs={{0,36},{1,37},{2,38},{3,39},{4,40},{5,41},{6,42},{7,43},{8,44},{9,... | collective-permute-start | bytes 835592 | tf_op jit(solution)/shard_map/ppermute | solution.py:298
  69.7 1.3 shard_map.167
  71.1 1.9 collective-permute-start.16
  73.0 2.2 %collective-permute-start.13 = (bf16[48,2176]{1,0:T(8,128)(2,1)S(1)}, bf16[48,2176]{1,0:T(8,128)(2,1)S(1)}, u32[]{:S(2)}, u32[]{:S(2)}) collective-permute-start(bf16[48,2176]{1,0:T(8,128)(2,1)S(1)} %get-tuple-element.47), channel_id=1, source_target_pairs={{0,12},{1,13},{2,14},{3,15},{4,16},{5,17},{6,18},{7,19},{8,20},{9,... | collective-permute-start | bytes 626696 | tf_op jit(solution)/shard_map/ppermute | solution.py:298
  75.3 3.6 %collective-permute-done.16.refs_2_ = bf16[48,2176]{1,0:T(8,128)(2,1)S(1)} collective-permute-done((bf16[48,2176]{1,0:T(8,128)(2,1)S(1)}, bf16[48,2176]{1,0:T(8,128)(2,1)S(1)}, u32[]{:S(2)}, u32[]{:S(2)}) %collective-permute-start.16) | collective-permute-done | bytes 208928 | tf_op jit(solution)/shard_map/ppermute | solution.py:271
  78.8 2.3 %collective-permute-start.14 = (bf16[48,2176]{1,0:T(8,128)(2,1)S(1)}, bf16[48,2176]{1,0:T(8,128)(2,1)S(1)}, u32[]{:S(2)}, u32[]{:S(2)}) collective-permute-start(bf16[48,2176]{1,0:T(8,128)(2,1)S(1)} %get-tuple-element.48), channel_id=1, source_target_pairs={{0,24},{1,25},{2,26},{3,27},{4,28},{5,29},{6,30},{7,31},{8,32},{9,... | collective-permute-start | bytes 626696 | tf_op jit(solution)/shard_map/ppermute | solution.py:298
  81.2 0.8 copy-done.11
  82.0 1.2 shard_map.168
  83.2 4.2 %collective-permute-start.15 = (bf16[48,2176]{1,0:T(8,128)(2,1)S(1)}, bf16[48,2176]{1,0:T(8,128)(2,1)S(1)}, u32[]{:S(2)}, u32[]{:S(2)}) collective-permute-start(bf16[48,2176]{1,0:T(8,128)(2,1)S(1)} %get-tuple-element.49), channel_id=1, source_target_pairs={{0,36},{1,37},{2,38},{3,39},{4,40},{5,41},{6,42},{7,43},{8,44},{9,... | collective-permute-start | bytes 626696 | tf_op jit(solution)/shard_map/ppermute | solution.py:298
  87.5 1.9 collective-permute-start.17
  89.4 3.6 %collective-permute-start.18 = (bf16[32,2176]{1,0:T(8,128)(2,1)S(1)}, bf16[32,2176]{1,0:T(8,128)(2,1)S(1)}, u32[]{:S(2)}, u32[]{:S(2)}) collective-permute-start(bf16[32,2176]{1,0:T(8,128)(2,1)S(1)} %get-tuple-element.54), channel_id=1, source_target_pairs={{0,24},{1,25},{2,26},{3,27},{4,28},{5,29},{6,30},{7,31},{8,32},{9,... | collective-permute-start | bytes 417800 | tf_op jit(solution)/shard_map/ppermute | solution.py:298
  93.0 2.9 %collective-permute-start.19 = (bf16[32,2176]{1,0:T(8,128)(2,1)S(1)}, bf16[32,2176]{1,0:T(8,128)(2,1)S(1)}, u32[]{:S(2)}, u32[]{:S(2)}) collective-permute-start(bf16[32,2176]{1,0:T(8,128)(2,1)S(1)} %get-tuple-element.55), channel_id=1, source_target_pairs={{0,36},{1,37},{2,38},{3,39},{4,40},{5,41},{6,42},{7,43},{8,44},{9,... | collective-permute-start | bytes 417800 | tf_op jit(solution)/shard_map/ppermute | solution.py:298
  96.0 2.0 collective-permute-done.17.refs_9_
  98.0 2.7 %collective-permute-done.19.refs_11_ = bf16[32,2176]{1,0:T(8,128)(2,1)S(1)} collective-permute-done((bf16[32,2176]{1,0:T(8,128)(2,1)S(1)}, bf16[32,2176]{1,0:T(8,128)(2,1)S(1)}, u32[]{:S(2)}, u32[]{:S(2)}) %collective-permute-start.19) | collective-permute-done | bytes 139296 | tf_op jit(solution)/shard_map/ppermute | solution.py:298
  100.7 3.0 %shard_map.169 = (bf16[480,2048]{1,0:T(8,128)(2,1)S(1)}, f32[480,1]{1,0:T(8,128)S(1)}, bf16[480,1792]{1,0:T(8,128)(2,1)S(1)}, bf16[480,1792]{1,0:T(8,128)(2,1)S(1)}) custom-call(s32[4]{0:T(128)S(1)} %pad_add_fusion.place_ref, s32[1,576]{1,0:T(1,128)S(1)} %broadcast_in_dim.14.target_ref, bf16[480,768]{1,0:T(8,128)(2,1)S(1)} %bitcast.16, ...), custom_call_target="tpu_custom_call" | custom-call | flops 1203240960 | bytes 8650752 | tf_op jit(solution)/shard_map/pallas_call | solution.py:306
  103.7 9.9 %collective-permute-start.20 = (bf16[480,1792]{1,0:T(8,128)(2,1)S(1)}, bf16[480,1792]{1,0:T(8,128)(2,1)S(1)}, u32[]{:S(2)}, u32[]{:S(2)}) collective-permute-start(bf16[480,1792]{1,0:T(8,128)(2,1)S(1)} %get-tuple-element.57), channel_id=1, source_target_pairs={{0,48},{48,0},{96,144},{144,96},{192,240},{240,192},{288,336},{336... | collective-permute-start | bytes 5160968 | tf_op jit(solution)/shard_map/ppermute | solution.py:321
  113.6 4.6 %shard_map.170 = (bf16[1,2,240,768]{3,2,1,0:T(8,128)(2,1)}, f32[48,128]{1,0:T(8,128)S(1)}) custom-call(bf16[480,2048]{1,0:T(8,128)(2,1)S(1)} %get-tuple-element.58.rows_ref, f32[480,1]{1,0:T(8,128)S(1)} %get-tuple-element.59.gate_ref, bf16[480,768]{1,0:T(8,128)(2,1)S(1)} %bitcast.17, bf16[2,768,2048]{2,1,0:T(8,128)(2,1)S(1)} %copy-done.2), custom_call_target="tpu_custom_call" | custom-call | flops 1509949440 | bytes 9732096 | tf_op jit(solution)/shard_map/pallas_call | solution.py:324
  118.3 1.2 copy-done
  119.5 16.0 %all_to_all.15 = f32[48,1,128]{2,1,0:T(1,128)S(1)} all-to-all(f32[48,1,128]{2,1,0:T(1,128)S(1)} %bitcast.19), channel_id=1, replica_groups=mesh['dp'=16,'expert'=48] {'expert'}, dimensions={0} | all-to-all | bytes 49152 | tf_op jit(solution)/shard_map/all_to_all | solution.py:345
  135.4 2.2 %shard_map.180 = (bf16[384,512]{1,0:T(8,128)(2,1)}, bf16[48,2048]{1,0:T(8,128)(2,1)}) custom-call(f32[48,128]{1,0:T(8,128)S(1)} %bitcast.18, f32[96,48]{1,0:T(8,128)S(1)} %get-tuple-element.66.probs_ref, f32[96,48]{1,0:T(8,128)S(1)} %get-tuple-element.67.code_ref, bf16[48,2048]{1,0:T(8,128)(2,1)S(1)} %copy-done.6, bf16[96,2048]{1,0:T(8,128)(2,1)S(1)} %copy-done.4), custom_call_target="tpu_custom_call" | custom-call | flops 169869312 | bytes 1179648 | tf_op jit(solution)/shard_map/pallas_call | solution.py:347
  137.7 5.3 %all-to-all-start.1 = ((bf16[48,8,512]{2,1,0:T(8,128)(2,1)}), bf16[48,8,512]{2,1,0:T(8,128)(2,1)}, u32[]{:S(2)}, u32[]{:S(2)}) async-start(bf16[48,8,512]{2,1,0:T(8,128)(2,1)} %bitcast.10), calls=%async_computation.1 | async-start | bytes 786432 | tf_op jit(solution)/shard_map/all_to_all | solution.py:411
  143.0 1.5 copy-done.1
  144.5 0.6 shard_map.172
  145.1 5.1 %collective-permute-start.25 = (bf16[768,128]{1,0:T(8,128)(2,1)S(1)}, bf16[768,128]{1,0:T(8,128)(2,1)S(1)}, u32[]{:S(2)}, u32[]{:S(2)}) collective-permute-start(bf16[768,128]{1,0:T(8,128)(2,1)S(1)} %get-tuple-element.63), channel_id=1, source_target_pairs={{0,672},{48,720},{96,0},{144,48},{192,96},{240,144},{288,192},{336... | collective-permute-start | bytes 589832 | tf_op jit(solution)/shard_map/ppermute | solution.py:366
  150.3 2.1 %collective-permute-start.21 = (bf16[768,128]{1,0:T(8,128)(2,1)S(1)}, bf16[768,128]{1,0:T(8,128)(2,1)S(1)}, u32[]{:S(2)}, u32[]{:S(2)}) collective-permute-start(bf16[768,128]{1,0:T(8,128)(2,1)S(1)} %get-tuple-element.62), channel_id=1, source_target_pairs={{0,96},{48,144},{96,192},{144,240},{192,288},{240,336},{288,384},{... | collective-permute-start | bytes 589832 | tf_op jit(solution)/shard_map/ppermute | solution.py:365
  152.4 1.0 shard_map.176.blocks_ref
  153.4 1.0 shard_map.171.blocks_ref
  154.5 4.6 %collective-permute-start.26 = (bf16[2,768,128]{2,1,0:T(8,128)(2,1)S(1)}, bf16[2,768,128]{2,1,0:T(8,128)(2,1)S(1)}, u32[]{:S(2)}, u32[]{:S(2)}) collective-permute-start(bf16[2,768,128]{2,1,0:T(8,128)(2,1)S(1)} %shard_map.177), channel_id=1, source_target_pairs={{0,672},{48,720},{96,0},{144,48},{192,96},{240,144},{288,192},{336... | collective-permute-start | bytes 1179656 | tf_op jit(solution)/shard_map/ppermute | solution.py:407
  159.2 1.9 collective-permute-start.22
  161.1 4.4 %collective-permute-done.26.arrived_ref = bf16[2,768,128]{2,1,0:T(8,128)(2,1)S(1)} collective-permute-done((bf16[2,768,128]{2,1,0:T(8,128)(2,1)S(1)}, bf16[2,768,128]{2,1,0:T(8,128)(2,1)S(1)}, u32[]{:S(2)}, u32[]{:S(2)}) %collective-permute-start.26) | collective-permute-done | bytes 393248 | tf_op jit(solution)/shard_map/ppermute | solution.py:407
  165.6 5.3 %collective-permute-start.27 = (bf16[2,768,128]{2,1,0:T(8,128)(2,1)S(1)}, bf16[2,768,128]{2,1,0:T(8,128)(2,1)S(1)}, u32[]{:S(2)}, u32[]{:S(2)}) collective-permute-start(bf16[2,768,128]{2,1,0:T(8,128)(2,1)S(1)} %shard_map.178), channel_id=1, source_target_pairs={{0,672},{48,720},{96,0},{144,48},{192,96},{240,144},{288,192},{336... | collective-permute-start | bytes 1179656 | tf_op jit(solution)/shard_map/ppermute | solution.py:407
  171.1 1.9 collective-permute-start.23
  173.0 3.5 %collective-permute-done.27.arrived_ref = bf16[2,768,128]{2,1,0:T(8,128)(2,1)S(1)} collective-permute-done((bf16[2,768,128]{2,1,0:T(8,128)(2,1)S(1)}, bf16[2,768,128]{2,1,0:T(8,128)(2,1)S(1)}, u32[]{:S(2)}, u32[]{:S(2)}) %collective-permute-start.27) | collective-permute-done | bytes 393248 | tf_op jit(solution)/shard_map/ppermute | solution.py:407
  176.5 5.3 %collective-permute-start.28 = (bf16[2,768,128]{2,1,0:T(8,128)(2,1)S(1)}, bf16[2,768,128]{2,1,0:T(8,128)(2,1)S(1)}, u32[]{:S(2)}, u32[]{:S(2)}) collective-permute-start(bf16[2,768,128]{2,1,0:T(8,128)(2,1)S(1)} %shard_map.179), channel_id=1, source_target_pairs={{0,672},{48,720},{96,0},{144,48},{192,96},{240,144},{288,192},{336... | collective-permute-start | bytes 1179656 | tf_op jit(solution)/shard_map/ppermute | solution.py:407
  182.0 1.9 collective-permute-start.24
  183.9 1.1 convert_reduce_fusion
  185.0 0.7 broadcast_in_dim.15
  185.7 8.7 %all-to-all-start.2 = ((f32[16,8,512]{2,1,0:T(8,128)}), f32[16,8,512]{2,1,0:T(8,128)S(1)}, u32[]{:S(2)}, u32[]{:S(2)}) async-start(f32[16,8,512]{2,1,0:T(8,128)} %broadcast_in_dim.15), calls=%async_computation.2 | async-start | bytes 524288 | tf_op jit(solution)/shard_map/all_to_all | solution.py:414
  194.4 1.0 fusion
  195.4 10.7 %all-to-all-done.2 = f32[16,8,512]{2,1,0:T(8,128)S(1)} async-done(((f32[16,8,512]{2,1,0:T(8,128)}), f32[16,8,512]{2,1,0:T(8,128)S(1)}, u32[]{:S(2)}, u32[]{:S(2)}) %all-to-all-start.2) | async-done | bytes 262176 | tf_op jit(solution)/shard_map/all_to_all | solution.py:414
  206.1 0.6 reshape.30
  (57 shorter events, 0.7 us)
Async XLA Ops:
  0.6 1.0 copy-start.3
  1.6 0.9 copy-start.5
  2.6 0.9 copy-start.8
  3.5 0.7 copy-start.12
  4.2 65.6 %copy-start.10 = (s32[192,4]{1,0:T(8,128)S(1)}, s32[192,4]{1,0:T(8,128)}, u32[]{:S(2)}) copy-start(s32[192,4]{1,0:T(8,128)} %constant.81.clone.plan_ref) | copy-start | bytes 9220
  4.2 91.7 %copy-start.13 = (s32[576]{0:T(1024)S(1)}, s32[576]{0:T(1024)}, u32[]{:S(2)}) copy-start(s32[576]{0:T(1024)} %constant.95) | copy-start | bytes 6916
  4.2 91.8 %copy-start.14 = (s32[576]{0:T(1024)S(1)}, s32[576]{0:T(1024)}, u32[]{:S(2)}) copy-start(s32[576]{0:T(1024)} %constant.94) | copy-start | bytes 6916
  4.2 91.8 %copy-start.15 = (s32[576]{0:T(1024)S(1)}, s32[576]{0:T(1024)}, u32[]{:S(2)}) copy-start(s32[576]{0:T(1024)} %constant.93) | copy-start | bytes 6916
  4.2 91.8 %copy-start.16 = (pred[576]{0:T(1024)(128)(4,1)S(1)}, pred[576]{0:T(1024)(128)(4,1)}, u32[]{:S(2)}) copy-start(pred[576]{0:T(1024)(128)(4,1)} %constant.87.clone) | copy-start | bytes 1732
  4.2 96.5 %copy-start.7 = (bf16[1,2,240,768]{3,2,1,0:T(8,128)(2,1)S(1)}, bf16[1,2,240,768]{3,2,1,0:T(8,128)(2,1)}, u32[]{:S(2)}) copy-start(bf16[1,2,240,768]{3,2,1,0:T(8,128)(2,1)} %param.18) | copy-start | bytes 2211844
  4.7 19.0 %collective-permute-start.3 = (bf16[48,2176]{1,0:T(8,128)(2,1)S(1)}, bf16[48,2176]{1,0:T(8,128)(2,1)S(1)}, u32[]{:S(2)}, u32[]{:S(2)}) collective-permute-start(bf16[48,2176]{1,0:T(8,128)(2,1)S(1)} %get-tuple-element.37.refs_0_), channel_id=1, source_target_pairs={{0,11},{1,0},{2,1},{3,2},{4,3},{5,4},{6,5},{7,6},{8,7},{9,8},{10,9... | collective-permute-start | bytes 626696 | tf_op jit(solution)/shard_map/ppermute | solution.py:273
  19.8 9.1 %collective-permute-start = (bf16[48,2176]{1,0:T(8,128)(2,1)S(1)}, bf16[48,2176]{1,0:T(8,128)(2,1)S(1)}, u32[]{:S(2)}, u32[]{:S(2)}) collective-permute-start(bf16[48,2176]{1,0:T(8,128)(2,1)S(1)} %get-tuple-element.37.refs_0_), channel_id=1, source_target_pairs={{0,1},{1,2},{2,3},{3,4},{4,5},{5,6},{6,7},{7,8},{8,9},{9,10},{10,1... | collective-permute-start | bytes 626696 | tf_op jit(solution)/shard_map/ppermute | solution.py:271
  23.7 8.0 %collective-permute-start.4 = (bf16[48,2176]{1,0:T(8,128)(2,1)S(1)}, bf16[48,2176]{1,0:T(8,128)(2,1)S(1)}, u32[]{:S(2)}, u32[]{:S(2)}) collective-permute-start(bf16[48,2176]{1,0:T(8,128)(2,1)S(1)} %collective-permute-done.3.refs_2_), channel_id=1, source_target_pairs={{0,11},{1,0},{2,1},{3,2},{4,3},{5,4},{6,5},{7,6},{8,7},{9,8},{10,9... | collective-permute-start | bytes 626696 | tf_op jit(solution)/shard_map/ppermute | solution.py:273
  29.0 8.2 %collective-permute-start.1 = (bf16[48,2176]{1,0:T(8,128)(2,1)S(1)}, bf16[48,2176]{1,0:T(8,128)(2,1)S(1)}, u32[]{:S(2)}, u32[]{:S(2)}) collective-permute-start(bf16[48,2176]{1,0:T(8,128)(2,1)S(1)} %collective-permute-done.refs_1_), channel_id=1, source_target_pairs={{0,1},{1,2},{2,3},{3,4},{4,5},{5,6},{6,7},{7,8},{8,9},{9,10},{10,1... | collective-permute-start | bytes 626696 | tf_op jit(solution)/shard_map/ppermute | solution.py:271
  31.7 9.9 %collective-permute-start.5 = (bf16[48,2176]{1,0:T(8,128)(2,1)S(1)}, bf16[48,2176]{1,0:T(8,128)(2,1)S(1)}, u32[]{:S(2)}, u32[]{:S(2)}) collective-permute-start(bf16[48,2176]{1,0:T(8,128)(2,1)S(1)} %collective-permute-done.4.refs_4_), channel_id=1, source_target_pairs={{0,11},{1,0},{2,1},{3,2},{4,3},{5,4},{6,5},{7,6},{8,7},{9,8},{10,9... | collective-permute-start | bytes 626696 | tf_op jit(solution)/shard_map/ppermute | solution.py:273
  37.2 7.8 %collective-permute-start.2 = (bf16[48,2176]{1,0:T(8,128)(2,1)S(1)}, bf16[48,2176]{1,0:T(8,128)(2,1)S(1)}, u32[]{:S(2)}, u32[]{:S(2)}) collective-permute-start(bf16[48,2176]{1,0:T(8,128)(2,1)S(1)} %collective-permute-done.1.refs_3_), channel_id=1, source_target_pairs={{0,1},{1,2},{2,3},{3,4},{4,5},{5,6},{6,7},{7,8},{8,9},{9,10},{10,1... | collective-permute-start | bytes 626696 | tf_op jit(solution)/shard_map/ppermute | solution.py:271
  39.3 0.9 copy-start.9
  40.2 73.4 %copy-start.2 = (bf16[2,768,2048]{2,1,0:T(8,128)(2,1)S(1)}, bf16[2,768,2048]{2,1,0:T(8,128)(2,1)}, u32[]{:S(2)}) copy-start(bf16[2,768,2048]{2,1,0:T(8,128)(2,1)} %weight_ref.1) | copy-start | bytes 18874372
  45.0 7.7 %collective-permute-start.9 = (bf16[48,2176]{1,0:T(8,128)(2,1)S(1)}, bf16[48,2176]{1,0:T(8,128)(2,1)S(1)}, u32[]{:S(2)}, u32[]{:S(2)}) collective-permute-start(bf16[48,2176]{1,0:T(8,128)(2,1)S(1)} %collective-permute-done.2.refs_0_), channel_id=1, source_target_pairs={{0,1},{1,2},{2,3},{3,4},{4,5},{5,6},{6,7},{7,8},{8,9},{9,10},{10,1... | collective-permute-start | bytes 626696 | tf_op jit(solution)/shard_map/ppermute | solution.py:271
  46.9 7.7 %collective-permute-start.11 = (bf16[48,2176]{1,0:T(8,128)(2,1)S(1)}, bf16[48,2176]{1,0:T(8,128)(2,1)S(1)}, u32[]{:S(2)}, u32[]{:S(2)}) collective-permute-start(bf16[48,2176]{1,0:T(8,128)(2,1)S(1)} %collective-permute-done.5.refs_1_), channel_id=1, source_target_pairs={{0,11},{1,0},{2,1},{3,2},{4,3},{5,4},{6,5},{7,6},{8,7},{9,8},{10,9... | collective-permute-start | bytes 626696 | tf_op jit(solution)/shard_map/ppermute | solution.py:273
  52.7 18.4 %collective-permute-start.10 = (bf16[48,2176]{1,0:T(8,128)(2,1)S(1)}, bf16[48,2176]{1,0:T(8,128)(2,1)S(1)}, u32[]{:S(2)}, u32[]{:S(2)}) collective-permute-start(bf16[48,2176]{1,0:T(8,128)(2,1)S(1)} %collective-permute-done.9.refs_2_), channel_id=1, source_target_pairs={{0,1},{1,2},{2,3},{3,4},{4,5},{5,6},{6,7},{7,8},{8,9},{9,10},{10,1... | collective-permute-start | bytes 626696 | tf_op jit(solution)/shard_map/ppermute | solution.py:271
  54.6 16.4 %collective-permute-start.12 = (bf16[48,2176]{1,0:T(8,128)(2,1)S(1)}, bf16[48,2176]{1,0:T(8,128)(2,1)S(1)}, u32[]{:S(2)}, u32[]{:S(2)}) collective-permute-start(bf16[48,2176]{1,0:T(8,128)(2,1)S(1)} %collective-permute-done.11.refs_3_), channel_id=1, source_target_pairs={{0,11},{1,0},{2,1},{3,2},{4,3},{5,4},{6,5},{7,6},{8,7},{9,8},{10,9... | collective-permute-start | bytes 626696 | tf_op jit(solution)/shard_map/ppermute | solution.py:273
  59.2 24.0 %collective-permute-start.6 = (bf16[64,2176]{1,0:T(8,128)(2,1)S(1)}, bf16[64,2176]{1,0:T(8,128)(2,1)S(1)}, u32[]{:S(2)}, u32[]{:S(2)}) collective-permute-start(bf16[64,2176]{1,0:T(8,128)(2,1)S(1)} %get-tuple-element.40), channel_id=1, source_target_pairs={{0,12},{1,13},{2,14},{3,15},{4,16},{5,17},{6,18},{7,19},{8,20},{9,... | collective-permute-start | bytes 835592 | tf_op jit(solution)/shard_map/ppermute | solution.py:298
  62.3 25.1 %collective-permute-start.7 = (bf16[64,2176]{1,0:T(8,128)(2,1)S(1)}, bf16[64,2176]{1,0:T(8,128)(2,1)S(1)}, u32[]{:S(2)}, u32[]{:S(2)}) collective-permute-start(bf16[64,2176]{1,0:T(8,128)(2,1)S(1)} %get-tuple-element.41), channel_id=1, source_target_pairs={{0,24},{1,25},{2,26},{3,27},{4,28},{5,29},{6,30},{7,31},{8,32},{9,... | collective-permute-start | bytes 835592 | tf_op jit(solution)/shard_map/ppermute | solution.py:298
  66.7 22.7 %collective-permute-start.8 = (bf16[64,2176]{1,0:T(8,128)(2,1)S(1)}, bf16[64,2176]{1,0:T(8,128)(2,1)S(1)}, u32[]{:S(2)}, u32[]{:S(2)}) collective-permute-start(bf16[64,2176]{1,0:T(8,128)(2,1)S(1)} %get-tuple-element.42), channel_id=1, source_target_pairs={{0,36},{1,37},{2,38},{3,39},{4,40},{5,41},{6,42},{7,43},{8,44},{9,... | collective-permute-start | bytes 835592 | tf_op jit(solution)/shard_map/ppermute | solution.py:298
  71.1 7.8 %collective-permute-start.16 = (bf16[48,2176]{1,0:T(8,128)(2,1)S(1)}, bf16[48,2176]{1,0:T(8,128)(2,1)S(1)}, u32[]{:S(2)}, u32[]{:S(2)}) collective-permute-start(bf16[48,2176]{1,0:T(8,128)(2,1)S(1)} %collective-permute-done.10.refs_0_), channel_id=1, source_target_pairs={{0,1},{1,2},{2,3},{3,4},{4,5},{5,6},{6,7},{7,8},{8,9},{9,10},{10,1... | collective-permute-start | bytes 626696 | tf_op jit(solution)/shard_map/ppermute | solution.py:271
  73.0 20.0 %collective-permute-start.13 = (bf16[48,2176]{1,0:T(8,128)(2,1)S(1)}, bf16[48,2176]{1,0:T(8,128)(2,1)S(1)}, u32[]{:S(2)}, u32[]{:S(2)}) collective-permute-start(bf16[48,2176]{1,0:T(8,128)(2,1)S(1)} %get-tuple-element.47), channel_id=1, source_target_pairs={{0,12},{1,13},{2,14},{3,15},{4,16},{5,17},{6,18},{7,19},{8,20},{9,... | collective-permute-start | bytes 626696 | tf_op jit(solution)/shard_map/ppermute | solution.py:298
  78.8 17.2 %collective-permute-start.14 = (bf16[48,2176]{1,0:T(8,128)(2,1)S(1)}, bf16[48,2176]{1,0:T(8,128)(2,1)S(1)}, u32[]{:S(2)}, u32[]{:S(2)}) collective-permute-start(bf16[48,2176]{1,0:T(8,128)(2,1)S(1)} %get-tuple-element.48), channel_id=1, source_target_pairs={{0,24},{1,25},{2,26},{3,27},{4,28},{5,29},{6,30},{7,31},{8,32},{9,... | collective-permute-start | bytes 626696 | tf_op jit(solution)/shard_map/ppermute | solution.py:298
  81.1 0.8 copy-start.11
  83.2 12.8 %collective-permute-start.15 = (bf16[48,2176]{1,0:T(8,128)(2,1)S(1)}, bf16[48,2176]{1,0:T(8,128)(2,1)S(1)}, u32[]{:S(2)}, u32[]{:S(2)}) collective-permute-start(bf16[48,2176]{1,0:T(8,128)(2,1)S(1)} %get-tuple-element.49), channel_id=1, source_target_pairs={{0,36},{1,37},{2,38},{3,39},{4,40},{5,41},{6,42},{7,43},{8,44},{9,... | collective-permute-start | bytes 626696 | tf_op jit(solution)/shard_map/ppermute | solution.py:298
  87.5 10.6 %collective-permute-start.17 = (bf16[32,2176]{1,0:T(8,128)(2,1)S(1)}, bf16[32,2176]{1,0:T(8,128)(2,1)S(1)}, u32[]{:S(2)}, u32[]{:S(2)}) collective-permute-start(bf16[32,2176]{1,0:T(8,128)(2,1)S(1)} %get-tuple-element.53), channel_id=1, source_target_pairs={{0,12},{1,13},{2,14},{3,15},{4,16},{5,17},{6,18},{7,19},{8,20},{9,... | collective-permute-start | bytes 417800 | tf_op jit(solution)/shard_map/ppermute | solution.py:298
  89.4 8.6 %collective-permute-start.18 = (bf16[32,2176]{1,0:T(8,128)(2,1)S(1)}, bf16[32,2176]{1,0:T(8,128)(2,1)S(1)}, u32[]{:S(2)}, u32[]{:S(2)}) collective-permute-start(bf16[32,2176]{1,0:T(8,128)(2,1)S(1)} %get-tuple-element.54), channel_id=1, source_target_pairs={{0,24},{1,25},{2,26},{3,27},{4,28},{5,29},{6,30},{7,31},{8,32},{9,... | collective-permute-start | bytes 417800 | tf_op jit(solution)/shard_map/ppermute | solution.py:298
  93.0 7.7 %collective-permute-start.19 = (bf16[32,2176]{1,0:T(8,128)(2,1)S(1)}, bf16[32,2176]{1,0:T(8,128)(2,1)S(1)}, u32[]{:S(2)}, u32[]{:S(2)}) collective-permute-start(bf16[32,2176]{1,0:T(8,128)(2,1)S(1)} %get-tuple-element.55), channel_id=1, source_target_pairs={{0,36},{1,37},{2,38},{3,39},{4,40},{5,41},{6,42},{7,43},{8,44},{9,... | collective-permute-start | bytes 417800 | tf_op jit(solution)/shard_map/ppermute | solution.py:298
  103.7 14.6 %collective-permute-start.20 = (bf16[480,1792]{1,0:T(8,128)(2,1)S(1)}, bf16[480,1792]{1,0:T(8,128)(2,1)S(1)}, u32[]{:S(2)}, u32[]{:S(2)}) collective-permute-start(bf16[480,1792]{1,0:T(8,128)(2,1)S(1)} %get-tuple-element.57), channel_id=1, source_target_pairs={{0,48},{48,0},{96,144},{144,96},{192,240},{240,192},{288,336},{336... | collective-permute-start | bytes 5160968 | tf_op jit(solution)/shard_map/ppermute | solution.py:321
  113.6 21.9 %copy-start.4 = (bf16[96,2048]{1,0:T(8,128)(2,1)S(1)}, bf16[96,2048]{1,0:T(8,128)(2,1)}, u32[]{:S(2)}) copy-start(bf16[96,2048]{1,0:T(8,128)(2,1)} %rw_ref.3) | copy-start | bytes 1179652
  113.6 21.8 %copy-start.6 = (bf16[48,2048]{1,0:T(8,128)(2,1)S(1)}, bf16[48,2048]{1,0:T(8,128)(2,1)}, u32[]{:S(2)}) copy-start(bf16[48,2048]{1,0:T(8,128)(2,1)} %x_ref.3) | copy-start | bytes 589828
  118.3 1.2 copy-start
  137.7 46.2 %all-to-all-start.1 = ((bf16[48,8,512]{2,1,0:T(8,128)(2,1)}), bf16[48,8,512]{2,1,0:T(8,128)(2,1)}, u32[]{:S(2)}, u32[]{:S(2)}) async-start(bf16[48,8,512]{2,1,0:T(8,128)(2,1)} %bitcast.10), calls=%async_computation.1 | async-start | bytes 786432 | tf_op jit(solution)/shard_map/all_to_all | solution.py:411
  143.0 1.5 copy-start.1
  145.1 9.3 %collective-permute-start.25 = (bf16[768,128]{1,0:T(8,128)(2,1)S(1)}, bf16[768,128]{1,0:T(8,128)(2,1)S(1)}, u32[]{:S(2)}, u32[]{:S(2)}) collective-permute-start(bf16[768,128]{1,0:T(8,128)(2,1)S(1)} %get-tuple-element.63), channel_id=1, source_target_pairs={{0,672},{48,720},{96,0},{144,48},{192,96},{240,144},{288,192},{336... | collective-permute-start | bytes 589832 | tf_op jit(solution)/shard_map/ppermute | solution.py:366
  150.3 8.8 %collective-permute-start.21 = (bf16[768,128]{1,0:T(8,128)(2,1)S(1)}, bf16[768,128]{1,0:T(8,128)(2,1)S(1)}, u32[]{:S(2)}, u32[]{:S(2)}) collective-permute-start(bf16[768,128]{1,0:T(8,128)(2,1)S(1)} %get-tuple-element.62), channel_id=1, source_target_pairs={{0,96},{48,144},{96,192},{144,240},{192,288},{240,336},{288,384},{... | collective-permute-start | bytes 589832 | tf_op jit(solution)/shard_map/ppermute | solution.py:365
  154.5 11.0 %collective-permute-start.26 = (bf16[2,768,128]{2,1,0:T(8,128)(2,1)S(1)}, bf16[2,768,128]{2,1,0:T(8,128)(2,1)S(1)}, u32[]{:S(2)}, u32[]{:S(2)}) collective-permute-start(bf16[2,768,128]{2,1,0:T(8,128)(2,1)S(1)} %shard_map.177), channel_id=1, source_target_pairs={{0,672},{48,720},{96,0},{144,48},{192,96},{240,144},{288,192},{336... | collective-permute-start | bytes 1179656 | tf_op jit(solution)/shard_map/ppermute | solution.py:407
  159.2 11.8 %collective-permute-start.22 = (bf16[2,768,128]{2,1,0:T(8,128)(2,1)S(1)}, bf16[2,768,128]{2,1,0:T(8,128)(2,1)S(1)}, u32[]{:S(2)}, u32[]{:S(2)}) collective-permute-start(bf16[2,768,128]{2,1,0:T(8,128)(2,1)S(1)} %shard_map.173), channel_id=1, source_target_pairs={{0,96},{48,144},{96,192},{144,240},{192,288},{240,336},{288,384},{... | collective-permute-start | bytes 1179656 | tf_op jit(solution)/shard_map/ppermute | solution.py:406
  165.6 10.8 %collective-permute-start.27 = (bf16[2,768,128]{2,1,0:T(8,128)(2,1)S(1)}, bf16[2,768,128]{2,1,0:T(8,128)(2,1)S(1)}, u32[]{:S(2)}, u32[]{:S(2)}) collective-permute-start(bf16[2,768,128]{2,1,0:T(8,128)(2,1)S(1)} %shard_map.178), channel_id=1, source_target_pairs={{0,672},{48,720},{96,0},{144,48},{192,96},{240,144},{288,192},{336... | collective-permute-start | bytes 1179656 | tf_op jit(solution)/shard_map/ppermute | solution.py:407
  171.1 10.8 %collective-permute-start.23 = (bf16[2,768,128]{2,1,0:T(8,128)(2,1)S(1)}, bf16[2,768,128]{2,1,0:T(8,128)(2,1)S(1)}, u32[]{:S(2)}, u32[]{:S(2)}) collective-permute-start(bf16[2,768,128]{2,1,0:T(8,128)(2,1)S(1)} %shard_map.174), channel_id=1, source_target_pairs={{0,96},{48,144},{96,192},{144,240},{192,288},{240,336},{288,384},{... | collective-permute-start | bytes 1179656 | tf_op jit(solution)/shard_map/ppermute | solution.py:406
  176.5 17.9 %collective-permute-start.28 = (bf16[2,768,128]{2,1,0:T(8,128)(2,1)S(1)}, bf16[2,768,128]{2,1,0:T(8,128)(2,1)S(1)}, u32[]{:S(2)}, u32[]{:S(2)}) collective-permute-start(bf16[2,768,128]{2,1,0:T(8,128)(2,1)S(1)} %shard_map.179), channel_id=1, source_target_pairs={{0,672},{48,720},{96,0},{144,48},{192,96},{240,144},{288,192},{336... | collective-permute-start | bytes 1179656 | tf_op jit(solution)/shard_map/ppermute | solution.py:407
  182.0 12.4 %collective-permute-start.24 = (bf16[2,768,128]{2,1,0:T(8,128)(2,1)S(1)}, bf16[2,768,128]{2,1,0:T(8,128)(2,1)S(1)}, u32[]{:S(2)}, u32[]{:S(2)}) collective-permute-start(bf16[2,768,128]{2,1,0:T(8,128)(2,1)S(1)} %shard_map.175), channel_id=1, source_target_pairs={{0,96},{48,144},{96,192},{144,240},{192,288},{240,336},{288,384},{... | collective-permute-start | bytes 1179656 | tf_op jit(solution)/shard_map/ppermute | solution.py:406
  185.7 20.4 %all-to-all-start.2 = ((f32[16,8,512]{2,1,0:T(8,128)}), f32[16,8,512]{2,1,0:T(8,128)S(1)}, u32[]{:S(2)}, u32[]{:S(2)}) async-start(f32[16,8,512]{2,1,0:T(8,128)} %broadcast_in_dim.15), calls=%async_computation.2 | async-start | bytes 524288 | tf_op jit(solution)/shard_map/all_to_all | solution.py:414

commit v3 on v2

v3 whole, which is shorter than its diff:
```python
import functools

import jax
import jax.numpy as jnp
import numpy as np
from jax import lax
from jax.experimental import pallas as pl
from jax.experimental.pallas import tpu as pltpu
from jax.sharding import PartitionSpec as P

F32 = jnp.float32
BF16 = jnp.bfloat16
LANES = 128
N_X = 4
VMEM_BYTES = 40 * 1024 * 1024


def dot(a, b, dims=((1,), (0,))):
    return lax.dot_general(a, b, (dims, ((), ())), preferred_element_type=F32)


def iota(shape, axis):
    return lax.broadcasted_iota(jnp.int32, shape, axis)


def call(body, out_shape, flops, moved, n_smem=0, **kwargs):
    return pl.pallas_call(
        body,
        out_shape=out_shape,
        compiler_params=pltpu.CompilerParams(vmem_limit_bytes=VMEM_BYTES),
        cost_estimate=pl.CostEstimate(flops=flops, bytes_accessed=moved, transcendentals=0),
        **kwargs,
    )


def whole(n):
    return [pl.BlockSpec(memory_space=pltpu.VMEM)] * n


def route_kernel(x_ref, grad_ref, rw_ref, routes_ref, first_ref, second_ref, probs_ref, code_ref):
    experts, width = rw_ref.shape
    top, rows = routes_ref.shape
    ids = iota((experts, rows), 0)
    chosen = ids == routes_ref[0:1, :]
    for k in range(1, top):
        chosen = chosen | (ids == routes_ref[k : k + 1, :])
    logits = dot(rw_ref[...], x_ref[...], ((1,), (1,)))
    highest = jnp.max(jnp.where(chosen, logits, -jnp.inf), axis=0, keepdims=True)
    weights = jnp.where(chosen, jnp.exp(jnp.where(chosen, logits - highest, 0.0)), 0.0)
    probs = weights / jnp.sum(weights, axis=0, keepdims=True)
    earlier = jnp.where(iota((rows, rows), 0) < iota((rows, rows), 1), 1.0, 0.0).astype(BF16)
    position = dot(jnp.where(chosen, 1.0, 0.0).astype(BF16), earlier)
    probs_ref[...] = probs
    code_ref[...] = jnp.where(chosen, position, -1.0)
    marked = jnp.where(chosen, probs, -1.0).astype(BF16)
    turn = jnp.where(iota((experts, LANES), 0) == iota((experts, LANES), 1), 1.0, 0.0).astype(BF16)
    marks = dot(marked, turn, ((0,), (0,))).astype(BF16)
    half = width // 2
    for i, ref in enumerate((first_ref, second_ref)):
        ref[:, :half] = grad_ref[:, i * half : (i + 1) * half]
        ref[:, half:] = marks


def pick_kernel(n_pairs, rows, n_z, exp_dev, place_ref, plan_ref, *refs):
    outs, joined = refs[2 * n_pairs : 2 * n_pairs + N_X], refs[2 * n_pairs + N_X]
    half = joined.shape[1] - LANES
    total = joined.shape[0]
    picks = plan_ref.shape[0]
    out_rows = picks // N_X
    shift, local, slot, source = (plan_ref[:, i : i + 1] for i in range(4))
    expert = ((place_ref[0] ^ shift) * n_z + place_ref[1]) * exp_dev + local
    wanted = jnp.where(iota((picks, LANES), 1) == expert, 1.0, 0.0).astype(BF16)
    here = iota((picks, total), 1)
    base = source * rows
    own = (here >= base) & (here < base + rows)
    earlier = jnp.where(iota((total, total), 0) < iota((total, total), 1), 1.0, 0.0).astype(BF16)
    for side in range(2):
        for i, pair in enumerate(refs[side * n_pairs : (side + 1) * n_pairs]):
            joined[2 * i * rows : 2 * (i + 1) * rows, :] = pair[...]
        value = dot(wanted, joined[:, half:], ((1,), (1,)))
        chosen = own & (value >= 0.0)
        position = dot(jnp.where(chosen, 1.0, 0.0).astype(BF16), earlier)
        picked = chosen & (position == slot.astype(F32))
        result = dot(jnp.where(picked, 1.0, 0.0).astype(BF16), joined[:, :half]).astype(BF16)
        at = side * (half + LANES)
        for i, out in enumerate(outs):
            out[:, at : at + half] = result[i * out_rows : (i + 1) * out_rows]
        if side == 0:
            gate = jnp.sum(jnp.where(picked, value, 0.0), axis=1, keepdims=True)
            tail = jnp.where(iota((picks, LANES), 1) == 0, gate, 0.0).astype(BF16)
            for i, out in enumerate(outs):
                out[:, half : half + LANES] = tail[i * out_rows : (i + 1) * out_rows]


def place_kernel(n_parts, order, place_ref, target_ref, hidden_ref, *refs):
    parts = refs[:n_parts]
    rows_ref, gate_ref, keep_ref, trade_ref, joined = refs[n_parts:]
    slots, width = rows_ref.shape
    half = width // 2
    at = 0
    for part in parts:
        joined[at : at + part.shape[0], :] = part[...]
        at += part.shape[0]
    ids = iota((slots, at), 0)
    placer = jnp.where(ids == target_ref[0:1, :], 1.0, 0.0).astype(BF16)
    gate = dot(placer, joined[:, half : half + LANES])[:, 0:1]
    gate_ref[...] = gate
    rows_ref[:, :half] = dot(placer, joined[:, :half]).astype(BF16)
    placer = jnp.where(ids == target_ref[1:2, :], 1.0, 0.0).astype(BF16)
    rows_ref[:, half:] = dot(placer, joined[:, half + LANES :]).astype(BF16)
    gated = (gate * hidden_ref[...].astype(F32)).astype(BF16)
    keep_ref[:, half:] = gated
    trade_ref[:, half:] = gated
    n_y = len(order[0])
    per = slots // len(order)
    for e, deltas in enumerate(order):
        for k, delta in enumerate(deltas):
            chip = lax.rem(place_ref[2] + place_ref[4] * delta + n_y, n_y)
            mine = pl.multiple_of((2 * chip + place_ref[3]) * LANES, LANES)
            other = pl.multiple_of((2 * chip + 1 - place_ref[3]) * LANES, LANES)
            span, column = slice(e * per, (e + 1) * per), slice(k * LANES, (k + 1) * LANES)
            keep_ref[span, column] = rows_ref[span, pl.ds(mine, LANES)]
            trade_ref[span, column] = rows_ref[span, pl.ds(other, LANES)]


def product_kernel(capacity, rows_ref, gate_ref, hidden_ref, weight_ref, grad_ref, back_ref, sums):
    e, f = pl.program_id(0), pl.program_id(1)
    slots = rows_ref.shape[0]
    product = dot(rows_ref[...], weight_ref[0], ((1,), (1,)))
    grad_ref[0, 0] = (gate_ref[...] * product).astype(BF16)
    part = jnp.sum(product * hidden_ref[...].astype(F32), axis=1, keepdims=True)

    @pl.when(f == 0)
    def _():
        sums[...] = part

    @pl.when(f > 0)
    def _():
        sums[...] += part

    @pl.when((e == 0) & (f == 0))
    def _():
        back_ref[...] = jnp.zeros_like(back_ref)

    @pl.when(f == pl.num_programs(1) - 1)
    def _():
        lane = iota((slots, LANES), 1)
        slot = iota((slots, LANES), 0)
        spread = jnp.where(lane == e * capacity + lax.rem(slot, capacity), sums[...], 0.0)
        n_source = back_ref.shape[0]
        first = iota((n_source, slots), 0) * capacity
        slot = iota((n_source, slots), 1)
        group = jnp.where((slot >= first) & (slot < first + capacity), 1.0, 0.0).astype(BF16)
        high = spread.astype(BF16)
        rest = spread - high.astype(F32)
        middle = rest.astype(BF16)
        low = (rest - middle.astype(F32)).astype(BF16)
        back_ref[...] += dot(group, high) + dot(group, middle) + dot(group, low)


def partial_kernel(first, exp_dev, mine_ref, got_ref, *outs):
    ff, wide = outs[0].shape
    half = mine_ref.shape[1] - ff
    per = mine_ref.shape[0] // exp_dev
    groups = len(outs) // exp_dev
    for e in range(exp_dev):
        span = slice(e * per, (e + 1) * per)
        mine, got = mine_ref[span, half:], got_ref[span, half:]
        for g in range(groups):
            column = slice((first + g) * wide, (first + g + 1) * wide)
            total = dot(mine, mine_ref[span, column], ((0,), (0,)))
            total += dot(got, got_ref[span, column], ((0,), (0,)))
            outs[g * exp_dev + e][...] = total.astype(BF16)


def router_kernel(capacity, exp_dev, back_ref, probs_ref, code_ref, x_ref, rw_ref, term_ref, grad_ref):
    experts, rows = probs_ref.shape
    n_dev = back_ref.shape[0]
    width = rw_ref.shape[1]
    back = back_ref[...]
    ids = iota((experts, n_dev), 0)
    first = iota((experts, n_dev), 1) * exp_dev
    owner = jnp.where((ids >= first) & (ids < first + exp_dev), 1.0, 0.0).astype(BF16)
    high = back.astype(BF16)
    rest = back - high.astype(F32)
    middle = rest.astype(BF16)
    low = (rest - middle.astype(F32)).astype(BF16)
    spread = dot(owner, high) + dot(owner, middle) + dot(owner, low)
    lane = iota((experts, LANES), 1)
    start = lax.rem(iota((experts, LANES), 0), exp_dev) * capacity
    code = code_ref[...]
    probs = probs_ref[...]
    gate_grad = jnp.zeros((experts, rows), F32)
    for c in range(capacity):
        column = jnp.sum(jnp.where(lane == start + c, spread, 0.0), axis=1, keepdims=True)
        gate_grad += jnp.where(code == c, column, 0.0)
    weighted = jnp.sum(probs * gate_grad, axis=0, keepdims=True)
    logit_grad = probs * (gate_grad - weighted)
    high = logit_grad.astype(BF16)
    low = (logit_grad - high.astype(F32)).astype(BF16)
    grad_ref[...] = dot(high, rw_ref[...], ((0,), (0,))).astype(BF16)
    out_rows, piece = term_ref.shape
    split = width // piece
    row = iota((out_rows, experts), 0)
    first = iota((out_rows, experts), 1) * split
    repeat = jnp.where((row >= first) & (row < first + split), 1.0, 0.0).astype(BF16)
    high = dot(repeat, high).astype(BF16)
    low = dot(repeat, low).astype(BF16)
    quarter = lax.rem(iota((out_rows, 1), 0), split)
    total = jnp.zeros((out_rows, piece), F32)
    for q in range(split):
        x = x_ref[:, q * piece : (q + 1) * piece]
        total += jnp.where(quarter == q, dot(high, x) + dot(low, x), 0.0)
    term_ref[...] = total.astype(BF16)


def exchange_order(n):
    pairs = [[0, 1]]
    for step in range(1, n // 2):
        pairs.append([-step, -step - 1] if step % 2 else [step, step + 1])
    return pairs


def on_device(layer_input, out_grad, router_weight, routes, hidden_act, down_weight):
    n_expert = lax.axis_size("expert")
    n_dp = lax.axis_size("dp")
    n_y, n_z = n_dp // 2, n_expert // N_X
    experts, width = router_weight.shape
    exp_dev = experts // n_expert
    per = hidden_act.shape[2]
    slots = exp_dev * per
    ff = hidden_act.shape[3]
    capacity = per // n_expert
    tok_rows, top_count = routes.shape
    wide = width + LANES
    shape = jax.ShapeDtypeStruct
    dp_index, expert_index = lax.axis_index("dp"), lax.axis_index("expert")
    x_index, z_index = expert_index // n_z, expert_index % n_z
    y_index = dp_index // 2
    z_sign, y_sign = 1 - 2 * (z_index % 2), 1 - 2 * (y_index % 2)
    place = jnp.stack([x_index, z_index, y_index, dp_index % 2, y_sign]).astype(jnp.int32)
    smem = pl.BlockSpec(memory_space=pltpu.SMEM)
    half_wide = width // 2 + LANES

    first, second, probs, code = call(
        route_kernel,
        (
            shape((tok_rows, half_wide), BF16),
            shape((tok_rows, half_wide), BF16),
            shape((experts, tok_rows), F32),
            shape((experts, tok_rows), F32),
        ),
        2 * tok_rows * experts * width,
        2 * (2 * tok_rows + experts) * width,
    )(layer_input, out_grad, router_weight, routes.T)

    def z_swap(odd):
        one_way = [(x * n_z + z, x * n_z + (z + 1) % n_z) for x in range(N_X) for z in range(odd, n_z, 2)]
        return one_way + [(b, a) for a, b in one_way]

    def x_swap(mask):
        return [(x * n_z + z, (x ^ mask) * n_z + z) for x in range(N_X) for z in range(n_z)]

    offsets = exchange_order(n_z)
    steps = len(offsets)
    cut = steps - 2 if steps > 3 else steps
    batches = [range(0, cut), range(cut, steps)] if cut < steps else [range(steps)]
    other_first = lax.ppermute(first, "expert", z_swap(0))
    other_second = lax.ppermute(second, "expert", z_swap(1))
    held = [[jnp.concatenate([first, other_first]), jnp.concatenate([second, other_second])]]
    parts, targets = [], []
    pick_slots = exp_dev * capacity
    picked, due = None, 0
    for batch in batches:
        while len(held) <= batch[-1]:
            step = len(held)
            if due == step:
                tied = lax.optimization_barrier((held[-1][0], held[-1][1], picked[0]))
                held[-1], parts[0] = list(tied[:2]), tied[2]
            held.append(
                [lax.ppermute(held[-1][side], "expert", z_swap((step + side) % 2)) for side in range(2)]
            )
        count = 2 * len(batch)
        out_rows = -(-count * pick_slots // 16) * 16
        plan = np.full((N_X, out_rows, 4), -1, np.int32)
        target = np.full((N_X, out_rows, 4), -1, np.int32)
        for mask in range(N_X):
            for i in range(count):
                for local in range(exp_dev):
                    for c in range(capacity):
                        row = i * pick_slots + local * capacity + c
                        plan[mask, row] = (mask, local, c, i)
                        target[mask, row] = (mask, offsets[batch[i // 2]][i % 2], local, c)
            plan[mask, count * pick_slots :, 0] = mask
        plan = plan.reshape(N_X * out_rows, 4)
        picked = call(
            functools.partial(pick_kernel, len(batch), tok_rows, n_z, exp_dev),
            [shape((out_rows, width + LANES), BF16)] * N_X,
            2 * N_X * out_rows * count * tok_rows * width,
            2 * (N_X * out_rows + count * tok_rows) * width,
            in_specs=[smem] + whole(1 + count),
            out_specs=whole(N_X),
            scratch_shapes=[pltpu.VMEM((count * tok_rows, half_wide), BF16)],
        )(place, jnp.asarray(plan), *[held[b][0] for b in batch], *[held[b][1] for b in batch])
        due = batch[-1] + 2
        order = [0, 1, 3, 2]
        for mask in order:
            parts.append(lax.ppermute(picked[mask], "expert", x_swap(mask)) if mask else picked[0])
        targets.append(target[order].reshape(N_X * out_rows, 4))

    table = np.concatenate(targets)
    base = table[:, 2] * per + table[:, 3]
    from_x = (x_index ^ np.maximum(table[:, 0], 0)) * n_z
    both = [
        jnp.where(table[:, 2] >= 0, base + (from_x + (z_index + sign * z_sign * table[:, 1]) % n_z) * capacity, -1)
        for sign in (1, -1)
    ]
    target = jnp.stack(both).astype(jnp.int32)
    total_rows = table.shape[0]
    hidden = hidden_act.reshape(slots, ff)
    y_pairs = exchange_order(n_y)
    order = [d for pair in reversed(y_pairs) for d in pair]
    rows, gate, keep, trade = call(
        functools.partial(place_kernel, len(parts), [order, [-d for d in order]]),
        (
            shape((slots, width), BF16),
            shape((slots, 1), F32),
            shape((slots, width // 2 + ff), BF16),
            shape((slots, width // 2 + ff), BF16),
        ),
        2 * slots * total_rows * width,
        2 * total_rows * width + 2 * slots * (2 * width + 3 * ff),
        in_specs=[smem] + whole(2 + len(parts)),
        out_specs=whole(4),
        scratch_shapes=[pltpu.VMEM((total_rows, width + LANES), BF16)],
    )(place, target, hidden, *parts)

    got = lax.ppermute(trade, "dp", [(i, i ^ 1) for i in range(n_dp)])

    tile = ff // 2 if ff % 256 == 0 else ff
    hidden_grad, back = call(
        functools.partial(product_kernel, capacity),
        (shape((1, exp_dev, per, ff), BF16), shape((n_expert, LANES), F32)),
        2 * slots * ff * width,
        2 * (slots + exp_dev * ff) * width + 4 * slots * ff,
        grid=(exp_dev, ff // tile),
        in_specs=[
            pl.BlockSpec((per, width), lambda e, f: (e, 0)),
            pl.BlockSpec((per, 1), lambda e, f: (e, 0)),
            pl.BlockSpec((per, tile), lambda e, f: (e, f)),
            pl.BlockSpec((1, tile, width), lambda e, f: (e, f, 0)),
        ],
        out_specs=(
            pl.BlockSpec((1, 1, per, tile), lambda e, f: (0, e, 0, f)),
            pl.BlockSpec((n_expert, LANES), lambda e, f: (0, 0)),
        ),
        scratch_shapes=[pltpu.VMEM((per, 1), F32)],
    )(rows, gate, hidden, down_weight)

    got, back = lax.optimization_barrier((got, back))
    groups = len(y_pairs)

    def partials(at, count):
        return call(
            functools.partial(partial_kernel, at, exp_dev),
            [shape((ff, 2 * LANES), BF16)] * (exp_dev * count),
            8 * slots * ff * LANES * count,
            4 * slots * (ff + 2 * LANES * count),
            in_specs=whole(2),
            out_specs=whole(exp_dev * count),
        )(keep, got)

    def y_swap(odd):
        one_way = [(2 * y + c, (2 * y + 2 + c) % n_dp) for y in range(odd, n_y, 2) for c in range(2)]
        return one_way + [(b, a) for a, b in one_way]

    def add(a, b):
        return (a.astype(F32) + b.astype(F32)).astype(BF16)

    sums = partials(0, 1)
    later = []
    if groups > 1:
        later = partials(1, groups - 1)
        tied = lax.optimization_barrier((back, *later))
        back, later = tied[0], list(tied[1:])
    for step in range(groups, 1, -1):
        came = [lax.ppermute(sums[e], "dp", y_swap((step - 1 + e) % 2)) for e in range(exp_dev)]
        mine, later = later[:exp_dev], later[exp_dev:]
        if step > 2:
            sums = [add(a, b) for a, b in zip(mine, came)]
        else:
            away = [add(a[:, LANES:], b[:, LANES:]) for a, b in zip(mine, came)]
            home = [a[:, :LANES].astype(F32) + b[:, :LANES].astype(F32) for a, b in zip(mine, came)]
    if groups == 1:
        away = [a[:, LANES:] for a in sums]
        home = [a[:, :LANES].astype(F32) for a in sums]
    came = [lax.ppermute(away[e], "dp", y_swap(e % 2)) for e in range(exp_dev)]
    down_grad = jnp.stack([a + b.astype(F32) for a, b in zip(home, came)])

    back = lax.all_to_all(back.reshape(n_expert, 1, LANES), "expert", split_axis=0, concat_axis=0, tiled=True)
    piece = exp_dev * width // 8
    term, input_grad = call(
        functools.partial(router_kernel, capacity, exp_dev),
        (shape((n_expert * 8, piece), BF16), shape((tok_rows, width), BF16)),
        2 * tok_rows * width * (experts + 2 * n_expert * 8),
        2 * (2 * tok_rows + 2 * experts) * width,
    )(back.reshape(n_expert, LANES), probs, code, layer_input, router_weight)

    shares = lax.all_to_all(term.reshape(n_expert, 8, piece), "expert", split_axis=0, concat_axis=0, tiled=True)
    replica_sum = jnp.sum(shares.astype(F32), axis=0)
    copies = jnp.broadcast_to(replica_sum[None], (n_dp, 8, piece))
    gathered = lax.all_to_all(copies, "dp", split_axis=0, concat_axis=0, tiled=True)
    router_grad = jnp.sum(gathered, axis=0).reshape(exp_dev, width)
    return (down_grad, hidden_grad, router_grad, input_grad)


def solution(mesh):
    in_specs = (
        P(("dp", "expert"), None),
        P(("dp", "expert"), None),
        P(),
        P(("dp", "expert"), None),
        P("dp", "expert", None, None),
        P("expert", None, None),
    )
    out_specs = (
        P("expert", None, "dp"),
        P("dp", "expert", None, None),
        P("expert", None),
        P(("dp", "expert"), None),
    )
    return jax.shard_map(
        on_device, mesh=mesh, in_specs=in_specs, out_specs=out_specs, check_vma=False
    )
```

time: 208 us -> 205 us (0.986)
  starting transfers between devices: 126 us -> 111 us
  waiting for transfers between devices: 34.2 us -> 40.8 us
  local copies, waits for them, and re-layouts: 9.35 us -> 12.7 us
  blocking collectives: 16 us -> 18.7 us
    ppermute x28 -> x26, starting transfers between devices: 102 us -> 88.2 us  [the longest x10 29.4 us: on_device(): lax.ppermute(held[-1][side], 'expert', z_swap((step + side) % 2))]
    ppermute x28 -> x26, waiting for transfers between devices: 23.5 us -> 30.2 us  [the longest x6 12.4 us: on_device(): lax.ppermute(sums[e], 'dp', y_swap((step - 1 + e) % 2))]
    unnamed x34 -> x42, local copies, waits for them, and re-layouts: 7.99 us -> 11.3 us
    all_to_all x1, blocking collectives: 16 us -> 18.7 us  [on_device(): lax.all_to_all(back.reshape(n_expert, 1, LANES), 'expert', split_axis=0,...]
    pallas_call x14 -> x6, Pallas kernels: 10.5 us -> 9.52 us  [the longest x2 4.48 us: on_device(): call(functools.partial(pick_kernel, len(batch), tok_rows, n_z, exp_dev),...]
  transfers between devices with their start and end apart: 31 -> 29, of which waited for: 10 -> 11; matrix products, arithmetic and copies ran while one was open for 1% -> 2% of each run, Pallas kernels for 6% -> 6%
where the time goes in v3:
time: 205 us; the launch traced here: 204 us
  starting transfers between devices  111 us (54%)
  waiting for transfers between devices  40.8 us (20%)
  blocking collectives  18.7 us (9%)
  Pallas kernels  16.4 us (8%)
  local copies, waits for them, and re-layouts  12.7 us (6%)
  other arithmetic  2.7 us (1%)
    ppermute x10, starting transfers between devices, on_device(): lax.ppermute(held[-1][side], 'expert', z_swap((step + side) % 2))  29.4 us
    all_to_all x1, blocking collectives, on_device(): lax.all_to_all(back.reshape(n_expert, 1, LANES), 'expert', split_axis=0,...  18.7 us
    ppermute x6, starting transfers between devices, on_device(): lax.ppermute(picked[mask], 'expert', x_swap(mask))  18.4 us
    ppermute x6, starting transfers between devices, on_device(): lax.ppermute(sums[e], 'dp', y_swap((step - 1 + e) % 2))  17.4 us
    ppermute x1, starting transfers between devices, on_device(): other_second = lax.ppermute(second, 'expert', z_swap(1))  12.5 us
    ppermute x6, waiting for transfers between devices, on_device(): lax.ppermute(sums[e], 'dp', y_swap((step - 1 + e) % 2))  12.4 us
    unnamed x42, local copies, waits for them, and re-layouts  11.3 us
    all_to_all x1, waiting for transfers between devices, on_device(): lax.all_to_all(copies, 'dp', split_axis=0, concat_axis=0, tiled=True)  10.6 us
  transfers between devices with their start and end apart: 29, of which 11 were waited for; matrix products, arithmetic and copies ran while one was open for 2% of the time, Pallas kernels for 6%

profile of v3, /device:TPU:1, one launch (start us, length us, event | category | flops | bytes accessed | tf_op | source)
XLA Modules:
  0.0 204.0 jit_solution(7572580353733712524)
XLA Ops:
  0.6 1.0 copy-done.1
  1.6 0.9 copy-done.3
  2.6 0.9 copy-done.6
  3.5 0.7 copy-done.9
  4.2 0.5 shard_map.165
  4.7 4.8 %collective-permute-start = (bf16[48,1152]{1,0:T(8,128)(2,1)S(1)}, bf16[48,1152]{1,0:T(8,128)(2,1)S(1)}, u32[]{:S(2)}, u32[]{:S(2)}) collective-permute-start(bf16[48,1152]{1,0:T(8,128)(2,1)S(1)} %get-tuple-element.44), channel_id=1, source_target_pairs={{0,1},{2,3},{4,5},{6,7},{8,9},{10,11},{12,13},{14,15},{16,17},{18,... | collective-permute-start | bytes 331784 | tf_op jit(solution)/shard_map/ppermute | solution.py:268
  9.5 12.5 %collective-permute-start.5 = (bf16[48,1152]{1,0:T(8,128)(2,1)S(1)}, bf16[48,1152]{1,0:T(8,128)(2,1)S(1)}, u32[]{:S(2)}, u32[]{:S(2)}) collective-permute-start(bf16[48,1152]{1,0:T(8,128)(2,1)S(1)} %get-tuple-element.45), channel_id=1, source_target_pairs={{1,2},{3,4},{5,6},{7,8},{9,10},{11,0},{13,14},{15,16},{17,18},{19,... | collective-permute-start | bytes 331784 | tf_op jit(solution)/shard_map/ppermute | solution.py:269
  22.1 2.4 %collective-permute-done.5 = bf16[48,1152]{1,0:T(8,128)(2,1)S(1)} collective-permute-done((bf16[48,1152]{1,0:T(8,128)(2,1)S(1)}, bf16[48,1152]{1,0:T(8,128)(2,1)S(1)}, u32[]{:S(2)}, u32[]{:S(2)}) %collective-permute-start.5) | collective-permute-done | bytes 110624 | tf_op jit(solution)/shard_map/ppermute | solution.py:269
  24.5 1.9 collective-permute-start.6
  26.4 4.2 %collective-permute-start.1 = (bf16[96,1152]{1,0:T(8,128)(2,1)S(1)}, bf16[96,1152]{1,0:T(8,128)(2,1)S(1)}, u32[]{:S(2)}, u32[]{:S(2)}) collective-permute-start(bf16[96,1152]{1,0:T(8,128)(2,1)S(1)} %constant_dynamic-update-slice_fusion.refs_0_), channel_id=1, source_target_pairs={{1,2},{3,4},{5,6},{7,8},{9,10},{11,0},{13,14},{15,16},{17,18},{19,... | collective-permute-start | bytes 663560 | tf_op jit(solution)/shard_map/ppermute | solution.py:281
  30.7 1.1 collective-permute-done.6.refs_5_
  31.7 3.6 %collective-permute-start.7 = (bf16[96,1152]{1,0:T(8,128)(2,1)S(1)}, bf16[96,1152]{1,0:T(8,128)(2,1)S(1)}, u32[]{:S(2)}, u32[]{:S(2)}) collective-permute-start(bf16[96,1152]{1,0:T(8,128)(2,1)S(1)} %collective-permute-done.6.refs_5_), channel_id=1, source_target_pairs={{1,2},{3,4},{5,6},{7,8},{9,10},{11,0},{13,14},{15,16},{17,18},{19,... | collective-permute-start | bytes 663560 | tf_op jit(solution)/shard_map/ppermute | solution.py:281
  35.4 1.9 collective-permute-start.2
  37.3 2.3 %collective-permute-done.7.refs_6_ = bf16[96,1152]{1,0:T(8,128)(2,1)S(1)} collective-permute-done((bf16[96,1152]{1,0:T(8,128)(2,1)S(1)}, bf16[96,1152]{1,0:T(8,128)(2,1)S(1)}, u32[]{:S(2)}, u32[]{:S(2)}) %collective-permute-start.7) | collective-permute-done | bytes 221216 | tf_op jit(solution)/shard_map/ppermute | solution.py:281
  39.6 2.1 %collective-permute-start.8 = (bf16[96,1152]{1,0:T(8,128)(2,1)S(1)}, bf16[96,1152]{1,0:T(8,128)(2,1)S(1)}, u32[]{:S(2)}, u32[]{:S(2)}) collective-permute-start(bf16[96,1152]{1,0:T(8,128)(2,1)S(1)} %collective-permute-done.7.refs_6_), channel_id=1, source_target_pairs={{0,1},{2,3},{4,5},{6,7},{8,9},{10,11},{12,13},{14,15},{16,17},{18,... | collective-permute-start | bytes 663560 | tf_op jit(solution)/shard_map/ppermute | solution.py:281
  41.7 0.6 collective-permute-done.2.refs_2_
  42.4 4.2 %collective-permute-start.3 = (bf16[96,1152]{1,0:T(8,128)(2,1)S(1)}, bf16[96,1152]{1,0:T(8,128)(2,1)S(1)}, u32[]{:S(2)}, u32[]{:S(2)}) collective-permute-start(bf16[96,1152]{1,0:T(8,128)(2,1)S(1)} %collective-permute-done.2.refs_2_), channel_id=1, source_target_pairs={{1,2},{3,4},{5,6},{7,8},{9,10},{11,0},{13,14},{15,16},{17,18},{19,... | collective-permute-start | bytes 663560 | tf_op jit(solution)/shard_map/ppermute | solution.py:281
  46.6 2.4 %collective-permute-done.8.refs_7_ = bf16[96,1152]{1,0:T(8,128)(2,1)S(1)} collective-permute-done((bf16[96,1152]{1,0:T(8,128)(2,1)S(1)}, bf16[96,1152]{1,0:T(8,128)(2,1)S(1)}, u32[]{:S(2)}, u32[]{:S(2)}) %collective-permute-start.8) | collective-permute-done | bytes 221216 | tf_op jit(solution)/shard_map/ppermute | solution.py:281
  48.9 3.2 %collective-permute-start.9 = (bf16[96,1152]{1,0:T(8,128)(2,1)S(1)}, bf16[96,1152]{1,0:T(8,128)(2,1)S(1)}, u32[]{:S(2)}, u32[]{:S(2)}) collective-permute-start(bf16[96,1152]{1,0:T(8,128)(2,1)S(1)} %collective-permute-done.8.refs_7_), channel_id=1, source_target_pairs={{1,2},{3,4},{5,6},{7,8},{9,10},{11,0},{13,14},{15,16},{17,18},{19,... | collective-permute-start | bytes 663560 | tf_op jit(solution)/shard_map/ppermute | solution.py:281
  52.1 1.9 collective-permute-start.4
  54.2 2.9 %shard_map.166 = (bf16[80,2176]{1,0:T(8,128)(2,1)S(1)}, bf16[80,2176]{1,0:T(8,128)(2,1)}, bf16[80,2176]{1,0:T(8,128)(2,1)S(1)}, bf16[80,2176]{1,0:T(8,128)(2,1)S(1)}) custom-call(s32[5]{0:T(128)S(1)} %stack.41.place_ref, s32[320,4]{1,0:T(8,128)S(1)} %copy-done.7, bf16[96,1152]{1,0:T(8,128)(2,1)S(1)} %constant_dynamic-update-slice_fusion.refs_0_, ...), custom_call_target="tpu_custom_call" | custom-call | flops 503316480 | bytes 2883584 | tf_op jit(solution)/shard_map/pallas_call | solution.py:296
  57.1 0.7 copy-done.10
  57.9 0.7 copy-done.14
  58.6 0.7 copy-done.15
  59.3 3.1 %collective-permute-start.10 = (bf16[80,2176]{1,0:T(8,128)(2,1)}, bf16[80,2176]{1,0:T(8,128)(2,1)S(1)}, u32[]{:S(2)}, u32[]{:S(2)}) collective-permute-start(bf16[80,2176]{1,0:T(8,128)(2,1)} %get-tuple-element.48), channel_id=1, source_target_pairs={{0,12},{1,13},{2,14},{3,15},{4,16},{5,17},{6,18},{7,19},{8,20},{9,... | collective-permute-start | bytes 1044488 | tf_op jit(solution)/shard_map/ppermute | solution.py:308
  62.5 4.3 %collective-permute-start.13 = (bf16[96,1152]{1,0:T(8,128)(2,1)S(1)}, bf16[96,1152]{1,0:T(8,128)(2,1)S(1)}, u32[]{:S(2)}, u32[]{:S(2)}) collective-permute-start(bf16[96,1152]{1,0:T(8,128)(2,1)S(1)} %collective-permute-done.4.refs_0_), channel_id=1, source_target_pairs={{1,2},{3,4},{5,6},{7,8},{9,10},{11,0},{13,14},{15,16},{17,18},{19,... | collective-permute-start | bytes 663560 | tf_op jit(solution)/shard_map/ppermute | solution.py:281
  66.8 1.9 collective-permute-start.14
  68.8 3.7 %collective-permute-start.11 = (bf16[80,2176]{1,0:T(8,128)(2,1)}, bf16[80,2176]{1,0:T(8,128)(2,1)S(1)}, u32[]{:S(2)}, u32[]{:S(2)}) collective-permute-start(bf16[80,2176]{1,0:T(8,128)(2,1)} %copy-done.15), channel_id=1, source_target_pairs={{0,36},{1,37},{2,38},{3,39},{4,40},{5,41},{6,42},{7,43},{8,44},{9,... | collective-permute-start | bytes 1044488 | tf_op jit(solution)/shard_map/ppermute | solution.py:308
  72.5 2.6 %collective-permute-start.12 = (bf16[80,2176]{1,0:T(8,128)(2,1)}, bf16[80,2176]{1,0:T(8,128)(2,1)S(1)}, u32[]{:S(2)}, u32[]{:S(2)}) collective-permute-start(bf16[80,2176]{1,0:T(8,128)(2,1)} %copy-done.14), channel_id=1, source_target_pairs={{0,24},{1,25},{2,26},{3,27},{4,28},{5,29},{6,30},{7,31},{8,32},{9,... | collective-permute-start | bytes 1044488 | tf_op jit(solution)/shard_map/ppermute | solution.py:308
  75.1 1.6 shard_map.167
  76.7 2.6 %collective-permute-start.15 = (bf16[48,2176]{1,0:T(8,128)(2,1)S(1)}, bf16[48,2176]{1,0:T(8,128)(2,1)S(1)}, u32[]{:S(2)}, u32[]{:S(2)}) collective-permute-start(bf16[48,2176]{1,0:T(8,128)(2,1)S(1)} %get-tuple-element.54), channel_id=1, source_target_pairs={{0,12},{1,13},{2,14},{3,15},{4,16},{5,17},{6,18},{7,19},{8,20},{9,... | collective-permute-start | bytes 626696 | tf_op jit(solution)/shard_map/ppermute | solution.py:308
  79.4 3.7 %collective-permute-start.16 = (bf16[48,2176]{1,0:T(8,128)(2,1)S(1)}, bf16[48,2176]{1,0:T(8,128)(2,1)S(1)}, u32[]{:S(2)}, u32[]{:S(2)}) collective-permute-start(bf16[48,2176]{1,0:T(8,128)(2,1)S(1)} %get-tuple-element.55), channel_id=1, source_target_pairs={{0,36},{1,37},{2,38},{3,39},{4,40},{5,41},{6,42},{7,43},{8,44},{9,... | collective-permute-start | bytes 626696 | tf_op jit(solution)/shard_map/ppermute | solution.py:308
  83.1 0.7 copy-done.12
  83.8 2.6 %collective-permute-start.17 = (bf16[48,2176]{1,0:T(8,128)(2,1)S(1)}, bf16[48,2176]{1,0:T(8,128)(2,1)S(1)}, u32[]{:S(2)}, u32[]{:S(2)}) collective-permute-start(bf16[48,2176]{1,0:T(8,128)(2,1)S(1)} %get-tuple-element.56), channel_id=1, source_target_pairs={{0,24},{1,25},{2,26},{3,27},{4,28},{5,29},{6,30},{7,31},{8,32},{9,... | collective-permute-start | bytes 626696 | tf_op jit(solution)/shard_map/ppermute | solution.py:308
  86.6 9.1 %collective-permute-done.16.refs_6_ = bf16[48,2176]{1,0:T(8,128)(2,1)S(1)} collective-permute-done((bf16[48,2176]{1,0:T(8,128)(2,1)S(1)}, bf16[48,2176]{1,0:T(8,128)(2,1)S(1)}, u32[]{:S(2)}, u32[]{:S(2)}) %collective-permute-start.16) | collective-permute-done | bytes 208928 | tf_op jit(solution)/shard_map/ppermute | solution.py:308
  95.7 1.0 copy-done.11
  96.7 1.0 copy-done.13
  97.6 2.5 %shard_map.168 = (bf16[480,2048]{1,0:T(8,128)(2,1)S(1)}, f32[480,1]{1,0:T(8,128)S(1)}, bf16[480,1792]{1,0:T(8,128)(2,1)S(1)}, bf16[480,1792]{1,0:T(8,128)(2,1)S(1)}) custom-call(s32[5]{0:T(128)S(1)} %stack.41.place_ref, s32[2,512]{1,0:T(2,128)S(1)} %pad_add_fusion.target_ref, bf16[480,768]{1,0:T(8,128)(2,1)S(1)} %bitcast.18, ...), custom_call_target="tpu_custom_call" | custom-call | flops 1006632960 | bytes 8241152 | tf_op jit(solution)/shard_map/pallas_call | solution.py:323
  100.1 8.2 %collective-permute-start.18 = (bf16[480,1792]{1,0:T(8,128)(2,1)S(1)}, bf16[480,1792]{1,0:T(8,128)(2,1)S(1)}, u32[]{:S(2)}, u32[]{:S(2)}) collective-permute-start(bf16[480,1792]{1,0:T(8,128)(2,1)S(1)} %get-tuple-element.57), channel_id=1, source_target_pairs={{0,48},{48,0},{96,144},{144,96},{192,240},{240,192},{288,336},{336... | collective-permute-start | bytes 5160968 | tf_op jit(solution)/shard_map/ppermute | solution.py:338
  108.4 2.8 %copy-done = bf16[2,768,2048]{2,1,0:T(8,128)(2,1)S(1)} copy-done((bf16[2,768,2048]{2,1,0:T(8,128)(2,1)S(1)}, bf16[2,768,2048]{2,1,0:T(8,128)(2,1)}, u32[]{:S(2)}) %copy-start) | copy-done | bytes 6291480
  111.2 4.6 %shard_map.169 = (bf16[1,2,240,768]{3,2,1,0:T(8,128)(2,1)}, f32[48,128]{1,0:T(8,128)S(1)}) custom-call(bf16[480,2048]{1,0:T(8,128)(2,1)S(1)} %get-tuple-element.58.rows_ref, f32[480,1]{1,0:T(8,128)S(1)} %get-tuple-element.59.gate_ref, bf16[480,768]{1,0:T(8,128)(2,1)S(1)} %bitcast.19, bf16[2,768,2048]{2,1,0:T(8,128)(2,1)S(1)} %copy-done), custom_call_target="tpu_custom_call" | custom-call | flops 1509949440 | bytes 9732096 | tf_op jit(solution)/shard_map/pallas_call | solution.py:341
  115.8 0.6 shard_map.171
  116.4 5.1 %collective-permute-start.19 = (bf16[768,256]{1,0:T(8,128)(2,1)S(1)}, bf16[768,256]{1,0:T(8,128)(2,1)S(1)}, u32[]{:S(2)}, u32[]{:S(2)}) collective-permute-start(bf16[768,256]{1,0:T(8,128)(2,1)S(1)} %get-tuple-element.73), channel_id=1, source_target_pairs={{96,192},{144,240},{288,384},{336,432},{480,576},{528,624},{672,0}... | collective-permute-start | bytes 1179656 | tf_op jit(solution)/shard_map/ppermute | solution.py:387
  121.6 1.9 collective-permute-start.23
  123.5 1.4 shard_map.170
  124.9 6.1 %collective-permute-done.19 = bf16[768,256]{1,0:T(8,128)(2,1)S(1)} collective-permute-done((bf16[768,256]{1,0:T(8,128)(2,1)S(1)}, bf16[768,256]{1,0:T(8,128)(2,1)S(1)}, u32[]{:S(2)}, u32[]{:S(2)}) %collective-permute-start.19) | collective-permute-done | bytes 393248 | tf_op jit(solution)/shard_map/ppermute | solution.py:387
  131.1 1.9 collective-permute-start.20
  133.0 0.8 collective-permute-done.23
  134.0 3.6 %collective-permute-start.24 = (bf16[768,256]{1,0:T(8,128)(2,1)S(1)}, bf16[768,256]{1,0:T(8,128)(2,1)}, u32[]{:S(2)}, u32[]{:S(2)}) collective-permute-start(bf16[768,256]{1,0:T(8,128)(2,1)S(1)} %add_convert_fusion.1), channel_id=1, source_target_pairs={{96,192},{144,240},{288,384},{336,432},{480,576},{528,624},{672,0}... | collective-permute-start | bytes 1179656 | tf_op jit(solution)/shard_map/ppermute | solution.py:387
  137.6 18.7 %all_to_all.15 = f32[48,1,128]{2,1,0:T(1,128)S(1)} all-to-all(f32[48,1,128]{2,1,0:T(1,128)S(1)} %bitcast.21), channel_id=1, replica_groups=mesh['dp'=16,'expert'=48] {'expert'}, dimensions={0} | all-to-all | bytes 49152 | tf_op jit(solution)/shard_map/all_to_all | solution.py:400
  156.2 2.2 %shard_map.172 = (bf16[384,512]{1,0:T(8,128)(2,1)}, bf16[48,2048]{1,0:T(8,128)(2,1)}) custom-call(f32[48,128]{1,0:T(8,128)S(1)} %bitcast.20, f32[96,48]{1,0:T(8,128)S(1)} %get-tuple-element.80.probs_ref, f32[96,48]{1,0:T(8,128)S(1)} %get-tuple-element.81.code_ref, bf16[48,2048]{1,0:T(8,128)(2,1)S(1)} %copy-done.4, bf16[96,2048]{1,0:T(8,128)(2,1)S(1)} %copy-done.2), custom_call_target="tpu_custom_call" | custom-call | flops 169869312 | bytes 1179648 | tf_op jit(solution)/shard_map/pallas_call | solution.py:402
  158.5 4.5 %all-to-all-start.1 = ((bf16[48,8,512]{2,1,0:T(8,128)(2,1)}), bf16[48,8,512]{2,1,0:T(8,128)(2,1)S(1)}, u32[]{:S(2)}, u32[]{:S(2)}) async-start(bf16[48,8,512]{2,1,0:T(8,128)(2,1)} %bitcast.14), calls=%async_computation.1 | async-start | bytes 786432 | tf_op jit(solution)/shard_map/all_to_all | solution.py:409
  163.1 2.9 %collective-permute-start.21 = (bf16[768,256]{1,0:T(8,128)(2,1)S(1)}, bf16[768,256]{1,0:T(8,128)(2,1)S(1)}, u32[]{:S(2)}, u32[]{:S(2)}) collective-permute-start(bf16[768,256]{1,0:T(8,128)(2,1)S(1)} %add_convert_fusion.2), channel_id=1, source_target_pairs={{96,192},{144,240},{288,384},{336,432},{480,576},{528,624},{672,0}... | collective-permute-start | bytes 1179656 | tf_op jit(solution)/shard_map/ppermute | solution.py:387
  166.1 1.1 add_convert_fusion
  167.2 1.9 collective-permute-start.25
  169.1 5.1 %collective-permute-done.21 = bf16[768,256]{1,0:T(8,128)(2,1)S(1)} collective-permute-done((bf16[768,256]{1,0:T(8,128)(2,1)S(1)}, bf16[768,256]{1,0:T(8,128)(2,1)S(1)}, u32[]{:S(2)}, u32[]{:S(2)}) %collective-permute-start.21) | collective-permute-done | bytes 393248 | tf_op jit(solution)/shard_map/ppermute | solution.py:387
  174.3 1.9 collective-permute-start.22
  176.2 0.4 collective-permute-done.25
  176.6 3.8 %collective-permute-start.26 = (bf16[768,128]{1,0:T(8,128)(2,1)S(1)}, bf16[768,128]{1,0:T(8,128)(2,1)S(1)}, u32[]{:S(2)}, u32[]{:S(2)}) collective-permute-start(bf16[768,128]{1,0:T(8,128)(2,1)S(1)} %add_convert_fusion.4), channel_id=1, source_target_pairs={{96,192},{144,240},{288,384},{336,432},{480,576},{528,624},{672,0}... | collective-permute-start | bytes 589832 | tf_op jit(solution)/shard_map/ppermute | solution.py:397
  180.5 0.7 broadcast_in_dim.12
  181.2 10.4 %all-to-all-start.2 = ((f32[16,8,512]{2,1,0:T(8,128)}), f32[16,8,512]{2,1,0:T(8,128)S(1)}, u32[]{:S(2)}, u32[]{:S(2)}) async-start(f32[16,8,512]{2,1,0:T(8,128)} %broadcast_in_dim.12), calls=%async_computation.2 | async-start | bytes 524288 | tf_op jit(solution)/shard_map/all_to_all | solution.py:412
  191.8 0.9 pad_maximum_fusion
  192.8 10.6 %all-to-all-done.2 = f32[16,8,512]{2,1,0:T(8,128)S(1)} async-done(((f32[16,8,512]{2,1,0:T(8,128)}), f32[16,8,512]{2,1,0:T(8,128)S(1)}, u32[]{:S(2)}, u32[]{:S(2)}) %all-to-all-start.2) | async-done | bytes 262176 | tf_op jit(solution)/shard_map/all_to_all | solution.py:412
  203.4 0.6 reshape.28
  (63 shorter events, 0.9 us)
Async XLA Ops:
  0.6 1.0 copy-start.1
  1.6 0.9 copy-start.3
  2.6 0.9 copy-start.6
  3.5 0.7 copy-start.9
  4.2 50.0 %copy-start.7 = (s32[320,4]{1,0:T(8,128)S(1)}, s32[320,4]{1,0:T(8,128)}, u32[]{:S(2)}) copy-start(s32[320,4]{1,0:T(8,128)} %constant.77.clone.plan_ref) | copy-start | bytes 15364
  4.2 70.9 %copy-start.8 = (s32[192,4]{1,0:T(8,128)S(1)}, s32[192,4]{1,0:T(8,128)}, u32[]{:S(2)}) copy-start(s32[192,4]{1,0:T(8,128)} %constant.78.clone.plan_ref) | copy-start | bytes 9220
  4.7 21.7 %collective-permute-start = (bf16[48,1152]{1,0:T(8,128)(2,1)S(1)}, bf16[48,1152]{1,0:T(8,128)(2,1)S(1)}, u32[]{:S(2)}, u32[]{:S(2)}) collective-permute-start(bf16[48,1152]{1,0:T(8,128)(2,1)S(1)} %get-tuple-element.44), channel_id=1, source_target_pairs={{0,1},{2,3},{4,5},{6,7},{8,9},{10,11},{12,13},{14,15},{16,17},{18,... | collective-permute-start | bytes 331784 | tf_op jit(solution)/shard_map/ppermute | solution.py:268
  9.5 14.9 %collective-permute-start.5 = (bf16[48,1152]{1,0:T(8,128)(2,1)S(1)}, bf16[48,1152]{1,0:T(8,128)(2,1)S(1)}, u32[]{:S(2)}, u32[]{:S(2)}) collective-permute-start(bf16[48,1152]{1,0:T(8,128)(2,1)S(1)} %get-tuple-element.45), channel_id=1, source_target_pairs={{1,2},{3,4},{5,6},{7,8},{9,10},{11,0},{13,14},{15,16},{17,18},{19,... | collective-permute-start | bytes 331784 | tf_op jit(solution)/shard_map/ppermute | solution.py:269
  22.0 64.4 %copy-start.16 = (s32[512]{0:T(512)S(1)}, s32[512]{0:T(512)}, u32[]{:S(2)}) copy-start(s32[512]{0:T(512)} %constant.81.clone) | copy-start | bytes 6148
  22.0 64.4 %copy-start.17 = (s32[512]{0:T(512)S(1)}, s32[512]{0:T(512)}, u32[]{:S(2)}) copy-start(s32[512]{0:T(512)} %constant.80.clone) | copy-start | bytes 6148
  22.0 64.4 %copy-start.18 = (s32[512]{0:T(512)S(1)}, s32[512]{0:T(512)}, u32[]{:S(2)}) copy-start(s32[512]{0:T(512)} %constant.79.clone) | copy-start | bytes 6148
  22.1 64.4 %copy-start.19 = (pred[512]{0:T(512)(128)(4,1)S(1)}, pred[512]{0:T(512)(128)(4,1)}, u32[]{:S(2)}) copy-start(pred[512]{0:T(512)(128)(4,1)} %constant.82.clone) | copy-start | bytes 1540
  22.1 73.6 %copy-start.5 = (bf16[1,2,240,768]{3,2,1,0:T(8,128)(2,1)S(1)}, bf16[1,2,240,768]{3,2,1,0:T(8,128)(2,1)}, u32[]{:S(2)}) copy-start(bf16[1,2,240,768]{3,2,1,0:T(8,128)(2,1)} %param.18) | copy-start | bytes 2211844
  24.5 7.3 %collective-permute-start.6 = (bf16[96,1152]{1,0:T(8,128)(2,1)S(1)}, bf16[96,1152]{1,0:T(8,128)(2,1)S(1)}, u32[]{:S(2)}, u32[]{:S(2)}) collective-permute-start(bf16[96,1152]{1,0:T(8,128)(2,1)S(1)} %constant_dynamic-update-slice_fusion.2.refs_4_), channel_id=1, source_target_pairs={{0,1},{2,3},{4,5},{6,7},{8,9},{10,11},{12,13},{14,15},{16,17},{18,... | collective-permute-start | bytes 663560 | tf_op jit(solution)/shard_map/ppermute | solution.py:281
  26.4 9.0 %collective-permute-start.1 = (bf16[96,1152]{1,0:T(8,128)(2,1)S(1)}, bf16[96,1152]{1,0:T(8,128)(2,1)S(1)}, u32[]{:S(2)}, u32[]{:S(2)}) collective-permute-start(bf16[96,1152]{1,0:T(8,128)(2,1)S(1)} %constant_dynamic-update-slice_fusion.refs_0_), channel_id=1, source_target_pairs={{1,2},{3,4},{5,6},{7,8},{9,10},{11,0},{13,14},{15,16},{17,18},{19,... | collective-permute-start | bytes 663560 | tf_op jit(solution)/shard_map/ppermute | solution.py:281
  31.7 7.9 %collective-permute-start.7 = (bf16[96,1152]{1,0:T(8,128)(2,1)S(1)}, bf16[96,1152]{1,0:T(8,128)(2,1)S(1)}, u32[]{:S(2)}, u32[]{:S(2)}) collective-permute-start(bf16[96,1152]{1,0:T(8,128)(2,1)S(1)} %collective-permute-done.6.refs_5_), channel_id=1, source_target_pairs={{1,2},{3,4},{5,6},{7,8},{9,10},{11,0},{13,14},{15,16},{17,18},{19,... | collective-permute-start | bytes 663560 | tf_op jit(solution)/shard_map/ppermute | solution.py:281
  35.4 7.0 %collective-permute-start.2 = (bf16[96,1152]{1,0:T(8,128)(2,1)S(1)}, bf16[96,1152]{1,0:T(8,128)(2,1)S(1)}, u32[]{:S(2)}, u32[]{:S(2)}) collective-permute-start(bf16[96,1152]{1,0:T(8,128)(2,1)S(1)} %collective-permute-done.1.refs_1_), channel_id=1, source_target_pairs={{0,1},{2,3},{4,5},{6,7},{8,9},{10,11},{12,13},{14,15},{16,17},{18,... | collective-permute-start | bytes 663560 | tf_op jit(solution)/shard_map/ppermute | solution.py:281
  39.6 9.3 %collective-permute-start.8 = (bf16[96,1152]{1,0:T(8,128)(2,1)S(1)}, bf16[96,1152]{1,0:T(8,128)(2,1)S(1)}, u32[]{:S(2)}, u32[]{:S(2)}) collective-permute-start(bf16[96,1152]{1,0:T(8,128)(2,1)S(1)} %collective-permute-done.7.refs_6_), channel_id=1, source_target_pairs={{0,1},{2,3},{4,5},{6,7},{8,9},{10,11},{12,13},{14,15},{16,17},{18,... | collective-permute-start | bytes 663560 | tf_op jit(solution)/shard_map/ppermute | solution.py:281
  42.4 9.8 %collective-permute-start.3 = (bf16[96,1152]{1,0:T(8,128)(2,1)S(1)}, bf16[96,1152]{1,0:T(8,128)(2,1)S(1)}, u32[]{:S(2)}, u32[]{:S(2)}) collective-permute-start(bf16[96,1152]{1,0:T(8,128)(2,1)S(1)} %collective-permute-done.2.refs_2_), channel_id=1, source_target_pairs={{1,2},{3,4},{5,6},{7,8},{9,10},{11,0},{13,14},{15,16},{17,18},{19,... | collective-permute-start | bytes 663560 | tf_op jit(solution)/shard_map/ppermute | solution.py:281
  48.9 13.5 %collective-permute-start.9 = (bf16[96,1152]{1,0:T(8,128)(2,1)S(1)}, bf16[96,1152]{1,0:T(8,128)(2,1)S(1)}, u32[]{:S(2)}, u32[]{:S(2)}) collective-permute-start(bf16[96,1152]{1,0:T(8,128)(2,1)S(1)} %collective-permute-done.8.refs_7_), channel_id=1, source_target_pairs={{1,2},{3,4},{5,6},{7,8},{9,10},{11,0},{13,14},{15,16},{17,18},{19,... | collective-permute-start | bytes 663560 | tf_op jit(solution)/shard_map/ppermute | solution.py:281
  52.1 10.3 %collective-permute-start.4 = (bf16[96,1152]{1,0:T(8,128)(2,1)S(1)}, bf16[96,1152]{1,0:T(8,128)(2,1)S(1)}, u32[]{:S(2)}, u32[]{:S(2)}) collective-permute-start(bf16[96,1152]{1,0:T(8,128)(2,1)S(1)} %collective-permute-done.3.refs_3_), channel_id=1, source_target_pairs={{0,1},{2,3},{4,5},{6,7},{8,9},{10,11},{12,13},{14,15},{16,17},{18,... | collective-permute-start | bytes 663560 | tf_op jit(solution)/shard_map/ppermute | solution.py:281
  57.1 0.7 copy-start.10
  57.8 0.7 copy-start.14
  58.6 0.7 copy-start.15
  59.3 23.8 %collective-permute-start.10 = (bf16[80,2176]{1,0:T(8,128)(2,1)}, bf16[80,2176]{1,0:T(8,128)(2,1)S(1)}, u32[]{:S(2)}, u32[]{:S(2)}) collective-permute-start(bf16[80,2176]{1,0:T(8,128)(2,1)} %get-tuple-element.48), channel_id=1, source_target_pairs={{0,12},{1,13},{2,14},{3,15},{4,16},{5,17},{6,18},{7,19},{8,20},{9,... | collective-permute-start | bytes 1044488 | tf_op jit(solution)/shard_map/ppermute | solution.py:308
  62.5 12.6 %collective-permute-start.13 = (bf16[96,1152]{1,0:T(8,128)(2,1)S(1)}, bf16[96,1152]{1,0:T(8,128)(2,1)S(1)}, u32[]{:S(2)}, u32[]{:S(2)}) collective-permute-start(bf16[96,1152]{1,0:T(8,128)(2,1)S(1)} %collective-permute-done.4.refs_0_), channel_id=1, source_target_pairs={{1,2},{3,4},{5,6},{7,8},{9,10},{11,0},{13,14},{15,16},{17,18},{19,... | collective-permute-start | bytes 663560 | tf_op jit(solution)/shard_map/ppermute | solution.py:281
  66.8 8.3 %collective-permute-start.14 = (bf16[96,1152]{1,0:T(8,128)(2,1)S(1)}, bf16[96,1152]{1,0:T(8,128)(2,1)S(1)}, u32[]{:S(2)}, u32[]{:S(2)}) collective-permute-start(bf16[96,1152]{1,0:T(8,128)(2,1)S(1)} %collective-permute-done.9.refs_2_), channel_id=1, source_target_pairs={{0,1},{2,3},{4,5},{6,7},{8,9},{10,11},{12,13},{14,15},{16,17},{18,... | collective-permute-start | bytes 663560 | tf_op jit(solution)/shard_map/ppermute | solution.py:281
  68.8 17.8 %collective-permute-start.11 = (bf16[80,2176]{1,0:T(8,128)(2,1)}, bf16[80,2176]{1,0:T(8,128)(2,1)S(1)}, u32[]{:S(2)}, u32[]{:S(2)}) collective-permute-start(bf16[80,2176]{1,0:T(8,128)(2,1)} %copy-done.15), channel_id=1, source_target_pairs={{0,36},{1,37},{2,38},{3,39},{4,40},{5,41},{6,42},{7,43},{8,44},{9,... | collective-permute-start | bytes 1044488 | tf_op jit(solution)/shard_map/ppermute | solution.py:308
  72.5 14.1 %collective-permute-start.12 = (bf16[80,2176]{1,0:T(8,128)(2,1)}, bf16[80,2176]{1,0:T(8,128)(2,1)S(1)}, u32[]{:S(2)}, u32[]{:S(2)}) collective-permute-start(bf16[80,2176]{1,0:T(8,128)(2,1)} %copy-done.14), channel_id=1, source_target_pairs={{0,24},{1,25},{2,26},{3,27},{4,28},{5,29},{6,30},{7,31},{8,32},{9,... | collective-permute-start | bytes 1044488 | tf_op jit(solution)/shard_map/ppermute | solution.py:308
  76.7 9.8 %collective-permute-start.15 = (bf16[48,2176]{1,0:T(8,128)(2,1)S(1)}, bf16[48,2176]{1,0:T(8,128)(2,1)S(1)}, u32[]{:S(2)}, u32[]{:S(2)}) collective-permute-start(bf16[48,2176]{1,0:T(8,128)(2,1)S(1)} %get-tuple-element.54), channel_id=1, source_target_pairs={{0,12},{1,13},{2,14},{3,15},{4,16},{5,17},{6,18},{7,19},{8,20},{9,... | collective-permute-start | bytes 626696 | tf_op jit(solution)/shard_map/ppermute | solution.py:308
  79.4 16.3 %collective-permute-start.16 = (bf16[48,2176]{1,0:T(8,128)(2,1)S(1)}, bf16[48,2176]{1,0:T(8,128)(2,1)S(1)}, u32[]{:S(2)}, u32[]{:S(2)}) collective-permute-start(bf16[48,2176]{1,0:T(8,128)(2,1)S(1)} %get-tuple-element.55), channel_id=1, source_target_pairs={{0,36},{1,37},{2,38},{3,39},{4,40},{5,41},{6,42},{7,43},{8,44},{9,... | collective-permute-start | bytes 626696 | tf_op jit(solution)/shard_map/ppermute | solution.py:308
  83.1 0.7 copy-start.12
  83.8 11.9 %collective-permute-start.17 = (bf16[48,2176]{1,0:T(8,128)(2,1)S(1)}, bf16[48,2176]{1,0:T(8,128)(2,1)S(1)}, u32[]{:S(2)}, u32[]{:S(2)}) collective-permute-start(bf16[48,2176]{1,0:T(8,128)(2,1)S(1)} %get-tuple-element.56), channel_id=1, source_target_pairs={{0,24},{1,25},{2,26},{3,27},{4,28},{5,29},{6,30},{7,31},{8,32},{9,... | collective-permute-start | bytes 626696 | tf_op jit(solution)/shard_map/ppermute | solution.py:308
  95.7 1.0 copy-start.11
  96.7 1.0 copy-start.13
  100.1 15.7 %collective-permute-start.18 = (bf16[480,1792]{1,0:T(8,128)(2,1)S(1)}, bf16[480,1792]{1,0:T(8,128)(2,1)S(1)}, u32[]{:S(2)}, u32[]{:S(2)}) collective-permute-start(bf16[480,1792]{1,0:T(8,128)(2,1)S(1)} %get-tuple-element.57), channel_id=1, source_target_pairs={{0,48},{48,0},{96,144},{144,96},{192,240},{240,192},{288,336},{336... | collective-permute-start | bytes 5160968 | tf_op jit(solution)/shard_map/ppermute | solution.py:338
  108.4 2.8 %copy-start = (bf16[2,768,2048]{2,1,0:T(8,128)(2,1)S(1)}, bf16[2,768,2048]{2,1,0:T(8,128)(2,1)}, u32[]{:S(2)}) copy-start(bf16[2,768,2048]{2,1,0:T(8,128)(2,1)} %weight_ref.1) | copy-start | bytes 18874372
  116.4 14.6 %collective-permute-start.19 = (bf16[768,256]{1,0:T(8,128)(2,1)S(1)}, bf16[768,256]{1,0:T(8,128)(2,1)S(1)}, u32[]{:S(2)}, u32[]{:S(2)}) collective-permute-start(bf16[768,256]{1,0:T(8,128)(2,1)S(1)} %get-tuple-element.73), channel_id=1, source_target_pairs={{96,192},{144,240},{288,384},{336,432},{480,576},{528,624},{672,0}... | collective-permute-start | bytes 1179656 | tf_op jit(solution)/shard_map/ppermute | solution.py:387
  121.6 12.3 %collective-permute-start.23 = (bf16[768,256]{1,0:T(8,128)(2,1)S(1)}, bf16[768,256]{1,0:T(8,128)(2,1)S(1)}, u32[]{:S(2)}, u32[]{:S(2)}) collective-permute-start(bf16[768,256]{1,0:T(8,128)(2,1)S(1)} %get-tuple-element.77), channel_id=1, source_target_pairs={{0,96},{48,144},{192,288},{240,336},{384,480},{432,528},{576,672},... | collective-permute-start | bytes 1179656 | tf_op jit(solution)/shard_map/ppermute | solution.py:387
  124.9 31.3 %copy-start.2 = (bf16[96,2048]{1,0:T(8,128)(2,1)S(1)}, bf16[96,2048]{1,0:T(8,128)(2,1)}, u32[]{:S(2)}) copy-start(bf16[96,2048]{1,0:T(8,128)(2,1)} %rw_ref.3) | copy-start | bytes 1179652
  124.9 31.3 %copy-start.4 = (bf16[48,2048]{1,0:T(8,128)(2,1)S(1)}, bf16[48,2048]{1,0:T(8,128)(2,1)}, u32[]{:S(2)}) copy-start(bf16[48,2048]{1,0:T(8,128)(2,1)} %x_ref.3) | copy-start | bytes 589828
  131.1 31.9 %collective-permute-start.20 = (bf16[768,256]{1,0:T(8,128)(2,1)S(1)}, bf16[768,256]{1,0:T(8,128)(2,1)S(1)}, u32[]{:S(2)}, u32[]{:S(2)}) collective-permute-start(bf16[768,256]{1,0:T(8,128)(2,1)S(1)} %add_convert_fusion.3), channel_id=1, source_target_pairs={{0,96},{48,144},{192,288},{240,336},{384,480},{432,528},{576,672},... | collective-permute-start | bytes 1179656 | tf_op jit(solution)/shard_map/ppermute | solution.py:387
  134.0 32.1 %collective-permute-start.24 = (bf16[768,256]{1,0:T(8,128)(2,1)S(1)}, bf16[768,256]{1,0:T(8,128)(2,1)}, u32[]{:S(2)}, u32[]{:S(2)}) collective-permute-start(bf16[768,256]{1,0:T(8,128)(2,1)S(1)} %add_convert_fusion.1), channel_id=1, source_target_pairs={{96,192},{144,240},{288,384},{336,432},{480,576},{528,624},{672,0}... | collective-permute-start | bytes 1179656 | tf_op jit(solution)/shard_map/ppermute | solution.py:387
  158.5 21.9 %all-to-all-start.1 = ((bf16[48,8,512]{2,1,0:T(8,128)(2,1)}), bf16[48,8,512]{2,1,0:T(8,128)(2,1)S(1)}, u32[]{:S(2)}, u32[]{:S(2)}) async-start(bf16[48,8,512]{2,1,0:T(8,128)(2,1)} %bitcast.14), calls=%async_computation.1 | async-start | bytes 786432 | tf_op jit(solution)/shard_map/all_to_all | solution.py:409
  163.1 11.1 %collective-permute-start.21 = (bf16[768,256]{1,0:T(8,128)(2,1)S(1)}, bf16[768,256]{1,0:T(8,128)(2,1)S(1)}, u32[]{:S(2)}, u32[]{:S(2)}) collective-permute-start(bf16[768,256]{1,0:T(8,128)(2,1)S(1)} %add_convert_fusion.2), channel_id=1, source_target_pairs={{96,192},{144,240},{288,384},{336,432},{480,576},{528,624},{672,0}... | collective-permute-start | bytes 1179656 | tf_op jit(solution)/shard_map/ppermute | solution.py:387
  167.2 9.4 %collective-permute-start.25 = (bf16[768,256]{1,0:T(8,128)(2,1)S(1)}, bf16[768,256]{1,0:T(8,128)(2,1)S(1)}, u32[]{:S(2)}, u32[]{:S(2)}) collective-permute-start(bf16[768,256]{1,0:T(8,128)(2,1)S(1)} %add_convert_fusion), channel_id=1, source_target_pairs={{0,96},{48,144},{192,288},{240,336},{384,480},{432,528},{576,672},... | collective-permute-start | bytes 1179656 | tf_op jit(solution)/shard_map/ppermute | solution.py:387
  174.3 17.4 %collective-permute-start.22 = (bf16[768,128]{1,0:T(8,128)(2,1)S(1)}, bf16[768,128]{1,0:T(8,128)(2,1)S(1)}, u32[]{:S(2)}, u32[]{:S(2)}) collective-permute-start(bf16[768,128]{1,0:T(8,128)(2,1)S(1)} %add_convert_fusion.5), channel_id=1, source_target_pairs={{0,96},{48,144},{192,288},{240,336},{384,480},{432,528},{576,672},... | collective-permute-start | bytes 589832 | tf_op jit(solution)/shard_map/ppermute | solution.py:397
  176.6 15.1 %collective-permute-start.26 = (bf16[768,128]{1,0:T(8,128)(2,1)S(1)}, bf16[768,128]{1,0:T(8,128)(2,1)S(1)}, u32[]{:S(2)}, u32[]{:S(2)}) collective-permute-start(bf16[768,128]{1,0:T(8,128)(2,1)S(1)} %add_convert_fusion.4), channel_id=1, source_target_pairs={{96,192},{144,240},{288,384},{336,432},{480,576},{528,624},{672,0}... | collective-permute-start | bytes 589832 | tf_op jit(solution)/shard_map/ppermute | solution.py:397
  181.2 22.2 %all-to-all-start.2 = ((f32[16,8,512]{2,1,0:T(8,128)}), f32[16,8,512]{2,1,0:T(8,128)S(1)}, u32[]{:S(2)}, u32[]{:S(2)}) async-start(f32[16,8,512]{2,1,0:T(8,128)} %broadcast_in_dim.12), calls=%async_computation.2 | async-start | bytes 524288 | tf_op jit(solution)/shard_map/all_to_all | solution.py:412

commit v4 on v3

--- a/solution.py
+++ b/solution.py
@@ -2,7 +2,6 @@
 
 import jax
 import jax.numpy as jnp
-import numpy as np
 from jax import lax
 from jax.experimental import pallas as pl
 from jax.experimental.pallas import tpu as pltpu
@@ -61,14 +60,23 @@
         ref[:, half:] = marks
 
 
-def pick_kernel(n_pairs, rows, n_z, exp_dev, place_ref, plan_ref, *refs):
+def split_row(row, exp_dev, capacity):
+    pick_slots = exp_dev * capacity
+    inner = lax.rem(row, pick_slots)
+    return lax.div(row, pick_slots), lax.div(inner, capacity), lax.rem(inner, capacity)
+
+
+def pick_kernel(n_pairs, rows, n_z, exp_dev, capacity, place_ref, *refs):
     outs, joined = refs[2 * n_pairs : 2 * n_pairs + N_X], refs[2 * n_pairs + N_X]
     half = joined.shape[1] - LANES
     total = joined.shape[0]
-    picks = plan_ref.shape[0]
-    out_rows = picks // N_X
-    shift, local, slot, source = (plan_ref[:, i : i + 1] for i in range(4))
-    expert = ((place_ref[0] ^ shift) * n_z + place_ref[1]) * exp_dev + local
+    out_rows = outs[0].shape[0]
+    picks = N_X * out_rows
+    index = iota((picks, 1), 0)
+    row = lax.rem(index, out_rows)
+    source, local, slot = split_row(row, exp_dev, capacity)
+    slot = jnp.where(source < 2 * n_pairs, slot, -1)
+    expert = ((place_ref[0] ^ lax.div(index, out_rows)) * n_z + place_ref[1]) * exp_dev + local
     wanted = jnp.where(iota((picks, LANES), 1) == expert, 1.0, 0.0).astype(BF16)
     here = iota((picks, total), 1)
     base = source * rows
@@ -92,7 +100,7 @@
                 out[:, half : half + LANES] = tail[i * out_rows : (i + 1) * out_rows]
 
 
-def place_kernel(n_parts, order, place_ref, target_ref, hidden_ref, *refs):
+def place_kernel(n_parts, n_pairs, n_z, capacity, order, place_ref, hidden_ref, *refs):
     parts = refs[:n_parts]
     rows_ref, gate_ref, keep_ref, trade_ref, joined = refs[n_parts:]
     slots, width = rows_ref.shape
@@ -101,18 +109,33 @@
     for part in parts:
         joined[at : at + part.shape[0], :] = part[...]
         at += part.shape[0]
+    exp_dev = len(order)
+    per = slots // exp_dev
+    index = iota((1, at), 1)
+    part = lax.div(index, parts[0].shape[0])
+    block, local, slot = split_row(lax.rem(index, parts[0].shape[0]), exp_dev, capacity)
+    turn = lax.rem(part, N_X)
+    from_x = (place_ref[0] ^ turn ^ lax.div(turn, 2)) * n_z
+    pair = lax.div(part, N_X) * n_pairs + lax.div(block, 2)
+    delta = (pair + lax.rem(block, 2)) * (1 - 2 * lax.rem(pair, 2)) * place_ref[5]
+    base = local * per + slot
     ids = iota((slots, at), 0)
-    placer = jnp.where(ids == target_ref[0:1, :], 1.0, 0.0).astype(BF16)
+
+    def placer_of(sign):
+        source = from_x + lax.rem(place_ref[1] + sign * delta + 2 * n_z, n_z)
+        target = jnp.where(block < 2 * n_pairs, base + source * capacity, -1)
+        return jnp.where(ids == target, 1.0, 0.0).astype(BF16)
+
+    placer = placer_of(1)
     gate = dot(placer, joined[:, half : half + LANES])[:, 0:1]
     gate_ref[...] = gate
     rows_ref[:, :half] = dot(placer, joined[:, :half]).astype(BF16)
-    placer = jnp.where(ids == target_ref[1:2, :], 1.0, 0.0).astype(BF16)
+    placer = placer_of(-1)
     rows_ref[:, half:] = dot(placer, joined[:, half + LANES :]).astype(BF16)
     gated = (gate * hidden_ref[...].astype(F32)).astype(BF16)
     keep_ref[:, half:] = gated
     trade_ref[:, half:] = gated
     n_y = len(order[0])
-    per = slots // len(order)
     for e, deltas in enumerate(order):
         for k, delta in enumerate(deltas):
             chip = lax.rem(place_ref[2] + place_ref[4] * delta + n_y, n_y)
@@ -123,7 +146,7 @@
             trade_ref[span, column] = rows_ref[span, pl.ds(other, LANES)]
 
 
-def product_kernel(capacity, rows_ref, gate_ref, hidden_ref, weight_ref, grad_ref, back_ref, sums):
+def product_kernel(capacity, rows_ref, gate_ref, hidden_ref, weight_ref, grad_ref, back_ref, sums, total):
     e, f = pl.program_id(0), pl.program_id(1)
     slots = rows_ref.shape[0]
     product = dot(rows_ref[...], weight_ref[0], ((1,), (1,)))
@@ -140,22 +163,26 @@
 
     @pl.when((e == 0) & (f == 0))
     def _():
-        back_ref[...] = jnp.zeros_like(back_ref)
+        total[...] = jnp.zeros_like(total)
 
     @pl.when(f == pl.num_programs(1) - 1)
     def _():
         lane = iota((slots, LANES), 1)
         slot = iota((slots, LANES), 0)
         spread = jnp.where(lane == e * capacity + lax.rem(slot, capacity), sums[...], 0.0)
-        n_source = back_ref.shape[0]
-        first = iota((n_source, slots), 0) * capacity
-        slot = iota((n_source, slots), 1)
-        group = jnp.where((slot >= first) & (slot < first + capacity), 1.0, 0.0).astype(BF16)
+        row = iota((total.shape[0], slots), 0)
+        source = lax.div(iota((total.shape[0], slots), 1), capacity)
         high = spread.astype(BF16)
         rest = spread - high.astype(F32)
         middle = rest.astype(BF16)
         low = (rest - middle.astype(F32)).astype(BF16)
-        back_ref[...] += dot(group, high) + dot(group, middle) + dot(group, low)
+        for i, piece in enumerate((high, middle, low)):
+            group = jnp.where(row == source * 8 + i, 1.0, 0.0).astype(BF16)
+            total[...] += dot(group, piece)
+
+    @pl.when((e == pl.num_programs(0) - 1) & (f == pl.num_programs(1) - 1))
+    def _():
+        back_ref[...] = total[...].astype(BF16)
 
 
 def partial_kernel(first, exp_dev, mine_ref, got_ref, *outs):
@@ -175,17 +202,12 @@
 
 def router_kernel(capacity, exp_dev, back_ref, probs_ref, code_ref, x_ref, rw_ref, term_ref, grad_ref):
     experts, rows = probs_ref.shape
-    n_dev = back_ref.shape[0]
+    parts = back_ref.shape[0]
     width = rw_ref.shape[1]
-    back = back_ref[...]
-    ids = iota((experts, n_dev), 0)
-    first = iota((experts, n_dev), 1) * exp_dev
-    owner = jnp.where((ids >= first) & (ids < first + exp_dev), 1.0, 0.0).astype(BF16)
-    high = back.astype(BF16)
-    rest = back - high.astype(F32)
-    middle = rest.astype(BF16)
-    low = (rest - middle.astype(F32)).astype(BF16)
-    spread = dot(owner, high) + dot(owner, middle) + dot(owner, low)
+    ids = lax.div(iota((experts, parts), 0), exp_dev)
+    column = iota((experts, parts), 1)
+    owner = jnp.where((lax.div(column, 8) == ids) & (lax.rem(column, 8) < 3), 1.0, 0.0).astype(BF16)
+    spread = dot(owner, back_ref[...])
     lane = iota((experts, LANES), 1)
     start = lax.rem(iota((experts, LANES), 0), exp_dev) * capacity
     code = code_ref[...]
@@ -238,7 +260,7 @@
     x_index, z_index = expert_index // n_z, expert_index % n_z
     y_index = dp_index // 2
     z_sign, y_sign = 1 - 2 * (z_index % 2), 1 - 2 * (y_index % 2)
-    place = jnp.stack([x_index, z_index, y_index, dp_index % 2, y_sign]).astype(jnp.int32)
+    place = jnp.stack([x_index, z_index, y_index, dp_index % 2, y_sign, z_sign]).astype(jnp.int32)
     smem = pl.BlockSpec(memory_space=pltpu.SMEM)
     half_wide = width // 2 + LANES
 
@@ -263,65 +285,51 @@
 
     offsets = exchange_order(n_z)
     steps = len(offsets)
-    cut = steps - 2 if steps > 3 else steps
-    batches = [range(0, cut), range(cut, steps)] if cut < steps else [range(steps)]
+    batches = [range(i, i + 2) for i in range(0, steps, 2)]
     other_first = lax.ppermute(first, "expert", z_swap(0))
     other_second = lax.ppermute(second, "expert", z_swap(1))
     held = [[jnp.concatenate([first, other_first]), jnp.concatenate([second, other_second])]]
-    parts, targets = [], []
+    parts = []
     pick_slots = exp_dev * capacity
     picked, due = None, 0
     for batch in batches:
         while len(held) <= batch[-1]:
             step = len(held)
+            tied_parts = []
             if due == step:
-                tied = lax.optimization_barrier((held[-1][0], held[-1][1], picked[0]))
-                held[-1], parts[0] = list(tied[:2]), tied[2]
+                tied_parts.append(len(parts) - N_X)
+            if step >= 4 and step % 2 == 0:
+                at = (step - 4) // 2 * N_X
+                tied_parts += list(range(at + 1, at + N_X))
+            if tied_parts:
+                tied = lax.optimization_barrier((*held[-1], *[parts[i] for i in tied_parts]))
+                held[-1] = list(tied[:2])
+                for i, part in zip(tied_parts, tied[2:]):
+                    parts[i] = part
             held.append(
                 [lax.ppermute(held[-1][side], "expert", z_swap((step + side) % 2)) for side in range(2)]
             )
         count = 2 * len(batch)
         out_rows = -(-count * pick_slots // 16) * 16
-        plan = np.full((N_X, out_rows, 4), -1, np.int32)
-        target = np.full((N_X, out_rows, 4), -1, np.int32)
-        for mask in range(N_X):
-            for i in range(count):
-                for local in range(exp_dev):
-                    for c in range(capacity):
-                        row = i * pick_slots + local * capacity + c
-                        plan[mask, row] = (mask, local, c, i)
-                        target[mask, row] = (mask, offsets[batch[i // 2]][i % 2], local, c)
-            plan[mask, count * pick_slots :, 0] = mask
-        plan = plan.reshape(N_X * out_rows, 4)
         picked = call(
-            functools.partial(pick_kernel, len(batch), tok_rows, n_z, exp_dev),
+            functools.partial(pick_kernel, len(batch), tok_rows, n_z, exp_dev, capacity),
             [shape((out_rows, width + LANES), BF16)] * N_X,
             2 * N_X * out_rows * count * tok_rows * width,
             2 * (N_X * out_rows + count * tok_rows) * width,
-            in_specs=[smem] + whole(1 + count),
+            in_specs=[smem] + whole(count),
             out_specs=whole(N_X),
             scratch_shapes=[pltpu.VMEM((count * tok_rows, half_wide), BF16)],
-        )(place, jnp.asarray(plan), *[held[b][0] for b in batch], *[held[b][1] for b in batch])
+        )(place, *[held[b][0] for b in batch], *[held[b][1] for b in batch])
         due = batch[-1] + 2
-        order = [0, 1, 3, 2]
-        for mask in order:
+        for mask in (0, 1, 3, 2):
             parts.append(lax.ppermute(picked[mask], "expert", x_swap(mask)) if mask else picked[0])
-        targets.append(target[order].reshape(N_X * out_rows, 4))
-
-    table = np.concatenate(targets)
-    base = table[:, 2] * per + table[:, 3]
-    from_x = (x_index ^ np.maximum(table[:, 0], 0)) * n_z
-    both = [
-        jnp.where(table[:, 2] >= 0, base + (from_x + (z_index + sign * z_sign * table[:, 1]) % n_z) * capacity, -1)
-        for sign in (1, -1)
-    ]
-    target = jnp.stack(both).astype(jnp.int32)
-    total_rows = table.shape[0]
+
+    total_rows = len(parts) * out_rows
     hidden = hidden_act.reshape(slots, ff)
     y_pairs = exchange_order(n_y)
     order = [d for pair in reversed(y_pairs) for d in pair]
     rows, gate, keep, trade = call(
-        functools.partial(place_kernel, len(parts), [order, [-d for d in order]]),
+        functools.partial(place_kernel, len(parts), 2, n_z, capacity, [order, [-d for d in order]]),
         (
             shape((slots, width), BF16),
             shape((slots, 1), F32),
@@ -330,17 +338,17 @@
         ),
         2 * slots * total_rows * width,
         2 * total_rows * width + 2 * slots * (2 * width + 3 * ff),
-        in_specs=[smem] + whole(2 + len(parts)),
+        in_specs=[smem] + whole(1 + len(parts)),
         out_specs=whole(4),
         scratch_shapes=[pltpu.VMEM((total_rows, width + LANES), BF16)],
-    )(place, target, hidden, *parts)
+    )(place, hidden, *parts)
 
     got = lax.ppermute(trade, "dp", [(i, i ^ 1) for i in range(n_dp)])
 
     tile = ff // 2 if ff % 256 == 0 else ff
     hidden_grad, back = call(
         functools.partial(product_kernel, capacity),
-        (shape((1, exp_dev, per, ff), BF16), shape((n_expert, LANES), F32)),
+        (shape((1, exp_dev, per, ff), BF16), shape((n_expert * 8, LANES), BF16)),
         2 * slots * ff * width,
         2 * (slots + exp_dev * ff) * width + 4 * slots * ff,
         grid=(exp_dev, ff // tile),
@@ -352,9 +360,9 @@
         ],
         out_specs=(
             pl.BlockSpec((1, 1, per, tile), lambda e, f: (0, e, 0, f)),
-            pl.BlockSpec((n_expert, LANES), lambda e, f: (0, 0)),
+            pl.BlockSpec((n_expert * 8, LANES), lambda e, f: (0, 0)),
         ),
-        scratch_shapes=[pltpu.VMEM((per, 1), F32)],
+        scratch_shapes=[pltpu.VMEM((per, 1), F32), pltpu.VMEM((n_expert * 8, LANES), F32)],
     )(rows, gate, hidden, down_weight)
 
     got, back = lax.optimization_barrier((got, back))
@@ -397,14 +405,14 @@
     came = [lax.ppermute(away[e], "dp", y_swap(e % 2)) for e in range(exp_dev)]
     down_grad = jnp.stack([a + b.astype(F32) for a, b in zip(home, came)])
 
-    back = lax.all_to_all(back.reshape(n_expert, 1, LANES), "expert", split_axis=0, concat_axis=0, tiled=True)
+    back = lax.all_to_all(back.reshape(n_expert, 8, LANES), "expert", split_axis=0, concat_axis=0, tiled=True)
     piece = exp_dev * width // 8
     term, input_grad = call(
         functools.partial(router_kernel, capacity, exp_dev),
         (shape((n_expert * 8, piece), BF16), shape((tok_rows, width), BF16)),
         2 * tok_rows * width * (experts + 2 * n_expert * 8),
         2 * (2 * tok_rows + 2 * experts) * width,
-    )(back.reshape(n_expert, LANES), probs, code, layer_input, router_weight)
+    )(back.reshape(n_expert * 8, LANES), probs, code, layer_input, router_weight)
 
     shares = lax.all_to_all(term.reshape(n_expert, 8, piece), "expert", split_axis=0, concat_axis=0, tiled=True)
     replica_sum = jnp.sum(shares.astype(F32), axis=0)

time: 205 us -> 209 us (1.020)
  starting transfers between devices: 111 us -> 135 us
  blocking collectives: 18.7 us -> 0 us
  local copies, waits for them, and re-layouts: 12.7 us -> 5.05 us
  waiting for transfers between devices: 40.8 us -> 43.3 us
    all_to_all x1 -> x0, blocking collectives: 18.7 us -> none  [on_device(): lax.all_to_all(back.reshape(n_expert, 1, LANES), 'expert', split_axis=0,...]
    ppermute x6 -> x9, starting transfers between devices: 18.4 us -> 27.3 us  [on_device(): lax.ppermute(picked[mask], 'expert', x_swap(mask))]
    all_to_all x0 -> x1, starting transfers between devices: none -> 8.9 us  [on_device(): lax.all_to_all(back.reshape(n_expert, 8, LANES), 'expert', split_axis=0,...]
    unnamed x42 -> x18, local copies, waits for them, and re-layouts: 11.3 us -> 3.57 us
    ppermute x6, waiting for transfers between devices: 12.4 us -> 6.35 us  [on_device(): lax.ppermute(sums[e], 'dp', y_swap((step - 1 + e) % 2))]
    all_to_all x1, starting transfers between devices: 4.54 us -> 9.1 us  [on_device(): lax.all_to_all(term.reshape(n_expert, 8, piece), 'expert', split_axis=0,...]
    ppermute x6 -> x9, waiting for transfers between devices: 9.14 us -> 12.7 us  [on_device(): lax.ppermute(picked[mask], 'expert', x_swap(mask))]
    all_to_all x0 -> x1, waiting for transfers between devices: none -> 2.82 us  [on_device(): lax.all_to_all(back.reshape(n_expert, 8, LANES), 'expert', split_axis=0,...]
  transfers between devices with their start and end apart: 29 -> 33, of which waited for: 11 -> 13; matrix products, arithmetic and copies ran while one was open for 2% -> 3% of each run, Pallas kernels for 6% -> 6%
where the time goes in v4:
time: 209 us; the launch traced here: 207 us
  starting transfers between devices  135 us (65%)
  waiting for transfers between devices  43.3 us (21%)
  Pallas kernels  18.1 us (9%)
  local copies, waits for them, and re-layouts  5.05 us (2%)
  other arithmetic  4.4 us (2%)
    ppermute x10, starting transfers between devices, on_device(): lax.ppermute(held[-1][side], 'expert', z_swap((step + side) % 2))  27.9 us
    ppermute x9, starting transfers between devices, on_device(): lax.ppermute(picked[mask], 'expert', x_swap(mask))  27.3 us
    ppermute x6, starting transfers between devices, on_device(): lax.ppermute(sums[e], 'dp', y_swap((step - 1 + e) % 2))  19 us
    ppermute x9, waiting for transfers between devices, on_device(): lax.ppermute(picked[mask], 'expert', x_swap(mask))  12.7 us
    ppermute x1, starting transfers between devices, on_device(): other_second = lax.ppermute(second, 'expert', z_swap(1))  12.5 us
    all_to_all x1, waiting for transfers between devices, on_device(): lax.all_to_all(copies, 'dp', split_axis=0, concat_axis=0, tiled=True)  10.6 us
    ppermute x1, starting transfers between devices, on_device(): got = lax.ppermute(trade, 'dp', [(i, i ^ 1) for i in range(n_dp)])  10.4 us
    all_to_all x1, starting transfers between devices, on_device(): lax.all_to_all(copies, 'dp', split_axis=0, concat_axis=0, tiled=True)  10.1 us
  transfers between devices with their start and end apart: 33, of which 13 were waited for; matrix products, arithmetic and copies ran while one was open for 3% of the time, Pallas kernels for 6%

profile of v4, /device:TPU:1, one launch (start us, length us, event | category | flops | bytes accessed | tf_op | source)
XLA Modules:
  0.0 207.4 jit_solution(12055342660125994310)
XLA Ops:
  0.6 1.0 copy-done.1
  1.6 0.9 copy-done.3
  2.6 0.9 copy-done.6
  3.5 0.7 copy-done.7
  4.2 0.5 shard_map.93
  4.7 4.8 %collective-permute-start = (bf16[48,1152]{1,0:T(8,128)(2,1)S(1)}, bf16[48,1152]{1,0:T(8,128)(2,1)S(1)}, u32[]{:S(2)}, u32[]{:S(2)}) collective-permute-start(bf16[48,1152]{1,0:T(8,128)(2,1)S(1)} %get-tuple-element.56), channel_id=1, source_target_pairs={{0,1},{2,3},{4,5},{6,7},{8,9},{10,11},{12,13},{14,15},{16,17},{18,... | collective-permute-start | bytes 331784 | tf_op jit(solution)/shard_map/ppermute | solution.py:289
  9.5 12.5 %collective-permute-start.3 = (bf16[48,1152]{1,0:T(8,128)(2,1)S(1)}, bf16[48,1152]{1,0:T(8,128)(2,1)S(1)}, u32[]{:S(2)}, u32[]{:S(2)}) collective-permute-start(bf16[48,1152]{1,0:T(8,128)(2,1)S(1)} %get-tuple-element.57), channel_id=1, source_target_pairs={{1,2},{3,4},{5,6},{7,8},{9,10},{11,0},{13,14},{15,16},{17,18},{19,... | collective-permute-start | bytes 331784 | tf_op jit(solution)/shard_map/ppermute | solution.py:290
  22.0 2.4 %collective-permute-done.3 = bf16[48,1152]{1,0:T(8,128)(2,1)S(1)} collective-permute-done((bf16[48,1152]{1,0:T(8,128)(2,1)S(1)}, bf16[48,1152]{1,0:T(8,128)(2,1)S(1)}, u32[]{:S(2)}, u32[]{:S(2)}) %collective-permute-start.3) | collective-permute-done | bytes 110624 | tf_op jit(solution)/shard_map/ppermute | solution.py:290
  24.5 1.9 collective-permute-start.4
  26.4 4.2 %collective-permute-start.1 = (bf16[96,1152]{1,0:T(8,128)(2,1)S(1)}, bf16[96,1152]{1,0:T(8,128)(2,1)S(1)}, u32[]{:S(2)}, u32[]{:S(2)}) collective-permute-start(bf16[96,1152]{1,0:T(8,128)(2,1)S(1)} %constant_dynamic-update-slice_fusion.refs_0_), channel_id=1, source_target_pairs={{1,2},{3,4},{5,6},{7,8},{9,10},{11,0},{13,14},{15,16},{17,18},{19,... | collective-permute-start | bytes 663560 | tf_op jit(solution)/shard_map/ppermute | solution.py:310
  30.7 1.1 collective-permute-done.4.refs_3_
  31.7 3.6 %collective-permute-start.5 = (bf16[96,1152]{1,0:T(8,128)(2,1)S(1)}, bf16[96,1152]{1,0:T(8,128)(2,1)S(1)}, u32[]{:S(2)}, u32[]{:S(2)}) collective-permute-start(bf16[96,1152]{1,0:T(8,128)(2,1)S(1)} %collective-permute-done.4.refs_3_), channel_id=1, source_target_pairs={{1,2},{3,4},{5,6},{7,8},{9,10},{11,0},{13,14},{15,16},{17,18},{19,... | collective-permute-start | bytes 663560 | tf_op jit(solution)/shard_map/ppermute | solution.py:310
  35.4 1.9 collective-permute-start.2
  37.5 1.5 shard_map.94
  39.0 0.6 collective-permute-done.5.refs_2_
  39.6 2.7 %collective-permute-done.2.refs_0_ = bf16[96,1152]{1,0:T(8,128)(2,1)S(1)} collective-permute-done((bf16[96,1152]{1,0:T(8,128)(2,1)S(1)}, bf16[96,1152]{1,0:T(8,128)(2,1)S(1)}, u32[]{:S(2)}, u32[]{:S(2)}) %collective-permute-start.2) | collective-permute-done | bytes 221216 | tf_op jit(solution)/shard_map/ppermute | solution.py:310
  42.4 3.1 %collective-permute-start.6 = (bf16[96,1152]{1,0:T(8,128)(2,1)S(1)}, bf16[96,1152]{1,0:T(8,128)(2,1)S(1)}, u32[]{:S(2)}, u32[]{:S(2)}) collective-permute-start(bf16[96,1152]{1,0:T(8,128)(2,1)S(1)} %collective-permute-done.2.refs_0_), channel_id=1, source_target_pairs={{1,2},{3,4},{5,6},{7,8},{9,10},{11,0},{13,14},{15,16},{17,18},{19,... | collective-permute-start | bytes 663560 | tf_op jit(solution)/shard_map/ppermute | solution.py:310
  45.5 1.9 collective-permute-start.7
  47.4 3.1 %collective-permute-start.8 = (bf16[48,2176]{1,0:T(8,128)(2,1)S(1)}, bf16[48,2176]{1,0:T(8,128)(2,1)S(1)}, u32[]{:S(2)}, u32[]{:S(2)}) collective-permute-start(bf16[48,2176]{1,0:T(8,128)(2,1)S(1)} %get-tuple-element.62), channel_id=1, source_target_pairs={{0,12},{1,13},{2,14},{3,15},{4,16},{5,17},{6,18},{7,19},{8,20},{9,... | collective-permute-start | bytes 626696 | tf_op jit(solution)/shard_map/ppermute | solution.py:325
  50.6 3.7 %collective-permute-start.9 = (bf16[48,2176]{1,0:T(8,128)(2,1)S(1)}, bf16[48,2176]{1,0:T(8,128)(2,1)S(1)}, u32[]{:S(2)}, u32[]{:S(2)}) collective-permute-start(bf16[48,2176]{1,0:T(8,128)(2,1)S(1)} %get-tuple-element.63), channel_id=1, source_target_pairs={{0,36},{1,37},{2,38},{3,39},{4,40},{5,41},{6,42},{7,43},{8,44},{9,... | collective-permute-start | bytes 626696 | tf_op jit(solution)/shard_map/ppermute | solution.py:325
  54.3 2.6 %collective-permute-start.10 = (bf16[48,2176]{1,0:T(8,128)(2,1)S(1)}, bf16[48,2176]{1,0:T(8,128)(2,1)S(1)}, u32[]{:S(2)}, u32[]{:S(2)}) collective-permute-start(bf16[48,2176]{1,0:T(8,128)(2,1)S(1)} %get-tuple-element.64), channel_id=1, source_target_pairs={{0,24},{1,25},{2,26},{3,27},{4,28},{5,29},{6,30},{7,31},{8,32},{9,... | collective-permute-start | bytes 626696 | tf_op jit(solution)/shard_map/ppermute | solution.py:325
  56.9 1.5 collective-permute-done.9.refs_2_
  58.3 5.9 %collective-permute-done.10.refs_3_ = bf16[48,2176]{1,0:T(8,128)(2,1)S(1)} collective-permute-done((bf16[48,2176]{1,0:T(8,128)(2,1)S(1)}, bf16[48,2176]{1,0:T(8,128)(2,1)S(1)}, u32[]{:S(2)}, u32[]{:S(2)}) %collective-permute-start.10) | collective-permute-done | bytes 208928 | tf_op jit(solution)/shard_map/ppermute | solution.py:325
  64.2 3.6 %collective-permute-start.11 = (bf16[96,1152]{1,0:T(8,128)(2,1)S(1)}, bf16[96,1152]{1,0:T(8,128)(2,1)S(1)}, u32[]{:S(2)}, u32[]{:S(2)}) collective-permute-start(bf16[96,1152]{1,0:T(8,128)(2,1)S(1)} %collective-permute-done.6.refs_1_), channel_id=1, source_target_pairs={{0,1},{2,3},{4,5},{6,7},{8,9},{10,11},{12,13},{14,15},{16,17},{18,... | collective-permute-start | bytes 663560 | tf_op jit(solution)/shard_map/ppermute | solution.py:310
  67.9 2.8 %collective-permute-start.12 = (bf16[96,1152]{1,0:T(8,128)(2,1)S(1)}, bf16[96,1152]{1,0:T(8,128)(2,1)S(1)}, u32[]{:S(2)}, u32[]{:S(2)}) collective-permute-start(bf16[96,1152]{1,0:T(8,128)(2,1)S(1)} %collective-permute-done.7.refs_3_), channel_id=1, source_target_pairs={{1,2},{3,4},{5,6},{7,8},{9,10},{11,0},{13,14},{15,16},{17,18},{19,... | collective-permute-start | bytes 663560 | tf_op jit(solution)/shard_map/ppermute | solution.py:310
  70.6 1.5 shard_map.95
  72.2 3.6 %collective-permute-done.12.refs_2_ = bf16[96,1152]{1,0:T(8,128)(2,1)S(1)} collective-permute-done((bf16[96,1152]{1,0:T(8,128)(2,1)S(1)}, bf16[96,1152]{1,0:T(8,128)(2,1)S(1)}, u32[]{:S(2)}, u32[]{:S(2)}) %collective-permute-start.12) | collective-permute-done | bytes 221216 | tf_op jit(solution)/shard_map/ppermute | solution.py:310
  75.7 2.8 %collective-permute-start.16 = (bf16[96,1152]{1,0:T(8,128)(2,1)S(1)}, bf16[96,1152]{1,0:T(8,128)(2,1)S(1)}, u32[]{:S(2)}, u32[]{:S(2)}) collective-permute-start(bf16[96,1152]{1,0:T(8,128)(2,1)S(1)} %collective-permute-done.11.refs_0_), channel_id=1, source_target_pairs={{1,2},{3,4},{5,6},{7,8},{9,10},{11,0},{13,14},{15,16},{17,18},{19,... | collective-permute-start | bytes 663560 | tf_op jit(solution)/shard_map/ppermute | solution.py:310
  78.5 1.9 collective-permute-start.17
  80.5 1.9 collective-permute-start.13
  82.4 2.7 %collective-permute-start.14 = (bf16[48,2176]{1,0:T(8,128)(2,1)S(1)}, bf16[48,2176]{1,0:T(8,128)(2,1)S(1)}, u32[]{:S(2)}, u32[]{:S(2)}) collective-permute-start(bf16[48,2176]{1,0:T(8,128)(2,1)S(1)} %get-tuple-element.73), channel_id=1, source_target_pairs={{0,36},{1,37},{2,38},{3,39},{4,40},{5,41},{6,42},{7,43},{8,44},{9,... | collective-permute-start | bytes 626696 | tf_op jit(solution)/shard_map/ppermute | solution.py:325
  85.1 4.4 %collective-permute-start.15 = (bf16[48,2176]{1,0:T(8,128)(2,1)S(1)}, bf16[48,2176]{1,0:T(8,128)(2,1)S(1)}, u32[]{:S(2)}, u32[]{:S(2)}) collective-permute-start(bf16[48,2176]{1,0:T(8,128)(2,1)S(1)} %get-tuple-element.74), channel_id=1, source_target_pairs={{0,24},{1,25},{2,26},{3,27},{4,28},{5,29},{6,30},{7,31},{8,32},{9,... | collective-permute-start | bytes 626696 | tf_op jit(solution)/shard_map/ppermute | solution.py:325
  89.5 1.5 shard_map.96
  91.0 1.9 collective-permute-start.18
  92.9 2.7 %collective-permute-start.19 = (bf16[48,2176]{1,0:T(8,128)(2,1)S(1)}, bf16[48,2176]{1,0:T(8,128)(2,1)S(1)}, u32[]{:S(2)}, u32[]{:S(2)}) collective-permute-start(bf16[48,2176]{1,0:T(8,128)(2,1)S(1)} %get-tuple-element.79), channel_id=1, source_target_pairs={{0,36},{1,37},{2,38},{3,39},{4,40},{5,41},{6,42},{7,43},{8,44},{9,... | collective-permute-start | bytes 626696 | tf_op jit(solution)/shard_map/ppermute | solution.py:325
  95.6 4.4 %collective-permute-start.20 = (bf16[48,2176]{1,0:T(8,128)(2,1)S(1)}, bf16[48,2176]{1,0:T(8,128)(2,1)S(1)}, u32[]{:S(2)}, u32[]{:S(2)}) collective-permute-start(bf16[48,2176]{1,0:T(8,128)(2,1)S(1)} %get-tuple-element.80), channel_id=1, source_target_pairs={{0,24},{1,25},{2,26},{3,27},{4,28},{5,29},{6,30},{7,31},{8,32},{9,... | collective-permute-start | bytes 626696 | tf_op jit(solution)/shard_map/ppermute | solution.py:325
  100.0 5.3 %collective-permute-done.19.refs_10_ = bf16[48,2176]{1,0:T(8,128)(2,1)S(1)} collective-permute-done((bf16[48,2176]{1,0:T(8,128)(2,1)S(1)}, bf16[48,2176]{1,0:T(8,128)(2,1)S(1)}, u32[]{:S(2)}, u32[]{:S(2)}) %collective-permute-start.19) | collective-permute-done | bytes 208928 | tf_op jit(solution)/shard_map/ppermute | solution.py:325
  105.3 3.1 %shard_map.97 = (bf16[480,2048]{1,0:T(8,128)(2,1)S(1)}, f32[480,1]{1,0:T(8,128)S(1)}, bf16[480,1792]{1,0:T(8,128)(2,1)S(1)}, bf16[480,1792]{1,0:T(8,128)(2,1)S(1)}) custom-call(s32[6]{0:T(128)S(1)} %stack.36.place_ref, bf16[480,768]{1,0:T(8,128)(2,1)S(1)} %bitcast.15, bf16[48,2176]{1,0:T(8,128)(2,1)S(1)} %get-tuple-element.59.refs_0_, ...), custom_call_target="tpu_custom_call" | custom-call | flops 1132462080 | bytes 8503296 | tf_op jit(solution)/shard_map/pallas_call | solution.py:331
  108.4 10.4 %collective-permute-start.21 = (bf16[480,1792]{1,0:T(8,128)(2,1)S(1)}, bf16[480,1792]{1,0:T(8,128)(2,1)S(1)}, u32[]{:S(2)}, u32[]{:S(2)}) collective-permute-start(bf16[480,1792]{1,0:T(8,128)(2,1)S(1)} %get-tuple-element.81), channel_id=1, source_target_pairs={{0,48},{48,0},{96,144},{144,96},{192,240},{240,192},{288,336},{336... | collective-permute-start | bytes 5160968 | tf_op jit(solution)/shard_map/ppermute | solution.py:346
  118.8 5.0 %shard_map.98 = (bf16[1,2,240,768]{3,2,1,0:T(8,128)(2,1)}, bf16[384,128]{1,0:T(8,128)(2,1)}) custom-call(bf16[480,2048]{1,0:T(8,128)(2,1)S(1)} %get-tuple-element.82.rows_ref, f32[480,1]{1,0:T(8,128)S(1)} %get-tuple-element.83.gate_ref, bf16[480,768]{1,0:T(8,128)(2,1)S(1)} %bitcast.16, bf16[2,768,2048]{2,1,0:T(8,128)(2,1)S(1)} %copy-done), custom_call_target="tpu_custom_call" | custom-call | flops 1509949440 | bytes 9732096 | tf_op jit(solution)/shard_map/pallas_call | solution.py:349
  123.8 1.4 shard_map.100
  125.2 5.1 %collective-permute-start.22 = (bf16[768,256]{1,0:T(8,128)(2,1)}, bf16[768,256]{1,0:T(8,128)(2,1)}, u32[]{:S(2)}, u32[]{:S(2)}) collective-permute-start(bf16[768,256]{1,0:T(8,128)(2,1)} %get-tuple-element.97), channel_id=1, source_target_pairs={{96,192},{144,240},{288,384},{336,432},{480,576},{528,624},{672,0}... | collective-permute-start | bytes 1179656 | tf_op jit(solution)/shard_map/ppermute | solution.py:395
  130.3 1.9 collective-permute-start.26
  132.2 1.4 shard_map.99
  133.7 8.9 %all-to-all-start = ((bf16[48,8,128]{2,1,0:T(8,128)(2,1)}), bf16[48,8,128]{2,1,0:T(8,128)(2,1)S(1)}, u32[]{:S(2)}, u32[]{:S(2)}) async-start(bf16[48,8,128]{2,1,0:T(8,128)(2,1)} %bitcast.10), calls=%async_computation | async-start | bytes 196608 | tf_op jit(solution)/shard_map/all_to_all | solution.py:408
  142.6 1.8 add_convert_fusion.3
  144.4 3.3 %collective-permute-start.23 = (bf16[768,256]{1,0:T(8,128)(2,1)}, bf16[768,256]{1,0:T(8,128)(2,1)S(1)}, u32[]{:S(2)}, u32[]{:S(2)}) collective-permute-start(bf16[768,256]{1,0:T(8,128)(2,1)} %add_convert_fusion.3), channel_id=1, source_target_pairs={{0,96},{48,144},{192,288},{240,336},{384,480},{432,528},{576,672},... | collective-permute-start | bytes 1179656 | tf_op jit(solution)/shard_map/ppermute | solution.py:395
  147.8 1.1 add_convert_fusion.1
  148.9 2.7 %collective-permute-start.27 = (bf16[768,256]{1,0:T(8,128)(2,1)S(1)}, bf16[768,256]{1,0:T(8,128)(2,1)S(1)}, u32[]{:S(2)}, u32[]{:S(2)}) collective-permute-start(bf16[768,256]{1,0:T(8,128)(2,1)S(1)} %add_convert_fusion.1), channel_id=1, source_target_pairs={{96,192},{144,240},{288,384},{336,432},{480,576},{528,624},{672,0}... | collective-permute-start | bytes 1179656 | tf_op jit(solution)/shard_map/ppermute | solution.py:395
  151.6 2.8 %all-to-all-done = bf16[48,8,128]{2,1,0:T(8,128)(2,1)S(1)} async-done(((bf16[48,8,128]{2,1,0:T(8,128)(2,1)}), bf16[48,8,128]{2,1,0:T(8,128)(2,1)S(1)}, u32[]{:S(2)}, u32[]{:S(2)}) %all-to-all-start) | async-done | bytes 98336 | tf_op jit(solution)/shard_map/all_to_all | solution.py:408
  154.5 2.2 %shard_map.101 = (bf16[384,512]{1,0:T(8,128)(2,1)}, bf16[48,2048]{1,0:T(8,128)(2,1)}) custom-call(bf16[384,128]{1,0:T(8,128)(2,1)S(1)} %bitcast.17, f32[96,48]{1,0:T(8,128)S(1)} %get-tuple-element.104.probs_ref, f32[96,48]{1,0:T(8,128)S(1)} %get-tuple-element.105.code_ref, bf16[48,2048]{1,0:T(8,128)(2,1)S(1)} %copy-done.4, bf16[96,2048]{1,0:T(8,128)(2,1)S(1)} %copy-done.2), custom_call_target="tpu_custom_call" | custom-call | flops 169869312 | bytes 1179648 | tf_op jit(solution)/shard_map/pallas_call | solution.py:410
  156.7 9.1 %all-to-all-start.1 = ((bf16[48,8,512]{2,1,0:T(8,128)(2,1)}), bf16[48,8,512]{2,1,0:T(8,128)(2,1)S(1)}, u32[]{:S(2)}, u32[]{:S(2)}) async-start(bf16[48,8,512]{2,1,0:T(8,128)(2,1)} %bitcast.12), calls=%async_computation.1 | async-start | bytes 786432 | tf_op jit(solution)/shard_map/all_to_all | solution.py:417
  165.9 3.9 %collective-permute-start.24 = (bf16[768,256]{1,0:T(8,128)(2,1)S(1)}, bf16[768,256]{1,0:T(8,128)(2,1)S(1)}, u32[]{:S(2)}, u32[]{:S(2)}) collective-permute-start(bf16[768,256]{1,0:T(8,128)(2,1)S(1)} %add_convert_fusion.2), channel_id=1, source_target_pairs={{96,192},{144,240},{288,384},{336,432},{480,576},{528,624},{672,0}... | collective-permute-start | bytes 1179656 | tf_op jit(solution)/shard_map/ppermute | solution.py:395
  170.0 1.9 collective-permute-start.28
  171.9 6.0 %collective-permute-done.24 = bf16[768,256]{1,0:T(8,128)(2,1)S(1)} collective-permute-done((bf16[768,256]{1,0:T(8,128)(2,1)S(1)}, bf16[768,256]{1,0:T(8,128)(2,1)S(1)}, u32[]{:S(2)}, u32[]{:S(2)}) %collective-permute-start.24) | collective-permute-done | bytes 393248 | tf_op jit(solution)/shard_map/ppermute | solution.py:395
  178.0 1.9 collective-permute-start.25
  179.9 0.3 collective-permute-done.28
  180.3 3.4 %collective-permute-start.29 = (bf16[768,128]{1,0:T(8,128)(2,1)S(1)}, bf16[768,128]{1,0:T(8,128)(2,1)S(1)}, u32[]{:S(2)}, u32[]{:S(2)}) collective-permute-start(bf16[768,128]{1,0:T(8,128)(2,1)S(1)} %add_convert_fusion.4), channel_id=1, source_target_pairs={{96,192},{144,240},{288,384},{336,432},{480,576},{528,624},{672,0}... | collective-permute-start | bytes 589832 | tf_op jit(solution)/shard_map/ppermute | solution.py:405
  183.7 0.4 all-to-all-done.1
  184.2 0.7 broadcast_in_dim.2
  184.9 10.1 %all-to-all-start.2 = ((f32[16,8,512]{2,1,0:T(8,128)}), f32[16,8,512]{2,1,0:T(8,128)S(1)}, u32[]{:S(2)}, u32[]{:S(2)}) async-start(f32[16,8,512]{2,1,0:T(8,128)} %broadcast_in_dim.2), calls=%async_computation.2 | async-start | bytes 524288 | tf_op jit(solution)/shard_map/all_to_all | solution.py:420
  195.2 0.9 pad_maximum_fusion
  196.1 10.6 %all-to-all-done.2 = f32[16,8,512]{2,1,0:T(8,128)S(1)} async-done(((f32[16,8,512]{2,1,0:T(8,128)}), f32[16,8,512]{2,1,0:T(8,128)S(1)}, u32[]{:S(2)}, u32[]{:S(2)}) %all-to-all-start.2) | async-done | bytes 262176 | tf_op jit(solution)/shard_map/all_to_all | solution.py:420
  206.8 0.6 reshape.28
  (45 shorter events, 0.8 us)
Async XLA Ops:
  0.6 1.0 copy-start.1
  1.6 0.9 copy-start.3
  2.6 0.9 copy-start.6
  3.5 0.7 copy-start.7
  4.7 21.7 %collective-permute-start = (bf16[48,1152]{1,0:T(8,128)(2,1)S(1)}, bf16[48,1152]{1,0:T(8,128)(2,1)S(1)}, u32[]{:S(2)}, u32[]{:S(2)}) collective-permute-start(bf16[48,1152]{1,0:T(8,128)(2,1)S(1)} %get-tuple-element.56), channel_id=1, source_target_pairs={{0,1},{2,3},{4,5},{6,7},{8,9},{10,11},{12,13},{14,15},{16,17},{18,... | collective-permute-start | bytes 331784 | tf_op jit(solution)/shard_map/ppermute | solution.py:289
  9.5 15.0 %collective-permute-start.3 = (bf16[48,1152]{1,0:T(8,128)(2,1)S(1)}, bf16[48,1152]{1,0:T(8,128)(2,1)S(1)}, u32[]{:S(2)}, u32[]{:S(2)}) collective-permute-start(bf16[48,1152]{1,0:T(8,128)(2,1)S(1)} %get-tuple-element.57), channel_id=1, source_target_pairs={{1,2},{3,4},{5,6},{7,8},{9,10},{11,0},{13,14},{15,16},{17,18},{19,... | collective-permute-start | bytes 331784 | tf_op jit(solution)/shard_map/ppermute | solution.py:290
  22.0 83.3 %copy-start.5 = (bf16[1,2,240,768]{3,2,1,0:T(8,128)(2,1)S(1)}, bf16[1,2,240,768]{3,2,1,0:T(8,128)(2,1)}, u32[]{:S(2)}) copy-start(bf16[1,2,240,768]{3,2,1,0:T(8,128)(2,1)} %param.10) | copy-start | bytes 2211844
  24.5 7.3 %collective-permute-start.4 = (bf16[96,1152]{1,0:T(8,128)(2,1)S(1)}, bf16[96,1152]{1,0:T(8,128)(2,1)S(1)}, u32[]{:S(2)}, u32[]{:S(2)}) collective-permute-start(bf16[96,1152]{1,0:T(8,128)(2,1)S(1)} %constant_dynamic-update-slice_fusion.2.refs_2_), channel_id=1, source_target_pairs={{0,1},{2,3},{4,5},{6,7},{8,9},{10,11},{12,13},{14,15},{16,17},{18,... | collective-permute-start | bytes 663560 | tf_op jit(solution)/shard_map/ppermute | solution.py:310
  26.4 9.0 %collective-permute-start.1 = (bf16[96,1152]{1,0:T(8,128)(2,1)S(1)}, bf16[96,1152]{1,0:T(8,128)(2,1)S(1)}, u32[]{:S(2)}, u32[]{:S(2)}) collective-permute-start(bf16[96,1152]{1,0:T(8,128)(2,1)S(1)} %constant_dynamic-update-slice_fusion.refs_0_), channel_id=1, source_target_pairs={{1,2},{3,4},{5,6},{7,8},{9,10},{11,0},{13,14},{15,16},{17,18},{19,... | collective-permute-start | bytes 663560 | tf_op jit(solution)/shard_map/ppermute | solution.py:310
  31.7 7.9 %collective-permute-start.5 = (bf16[96,1152]{1,0:T(8,128)(2,1)S(1)}, bf16[96,1152]{1,0:T(8,128)(2,1)S(1)}, u32[]{:S(2)}, u32[]{:S(2)}) collective-permute-start(bf16[96,1152]{1,0:T(8,128)(2,1)S(1)} %collective-permute-done.4.refs_3_), channel_id=1, source_target_pairs={{1,2},{3,4},{5,6},{7,8},{9,10},{11,0},{13,14},{15,16},{17,18},{19,... | collective-permute-start | bytes 663560 | tf_op jit(solution)/shard_map/ppermute | solution.py:310
  35.4 7.0 %collective-permute-start.2 = (bf16[96,1152]{1,0:T(8,128)(2,1)S(1)}, bf16[96,1152]{1,0:T(8,128)(2,1)S(1)}, u32[]{:S(2)}, u32[]{:S(2)}) collective-permute-start(bf16[96,1152]{1,0:T(8,128)(2,1)S(1)} %collective-permute-done.1.refs_1_), channel_id=1, source_target_pairs={{0,1},{2,3},{4,5},{6,7},{8,9},{10,11},{12,13},{14,15},{16,17},{18,... | collective-permute-start | bytes 663560 | tf_op jit(solution)/shard_map/ppermute | solution.py:310
  37.5 81.3 %copy-start = (bf16[2,768,2048]{2,1,0:T(8,128)(2,1)S(1)}, bf16[2,768,2048]{2,1,0:T(8,128)(2,1)}, u32[]{:S(2)}) copy-start(bf16[2,768,2048]{2,1,0:T(8,128)(2,1)} %weight_ref.1) | copy-start | bytes 18874372
  42.4 21.9 %collective-permute-start.6 = (bf16[96,1152]{1,0:T(8,128)(2,1)S(1)}, bf16[96,1152]{1,0:T(8,128)(2,1)S(1)}, u32[]{:S(2)}, u32[]{:S(2)}) collective-permute-start(bf16[96,1152]{1,0:T(8,128)(2,1)S(1)} %collective-permute-done.2.refs_0_), channel_id=1, source_target_pairs={{1,2},{3,4},{5,6},{7,8},{9,10},{11,0},{13,14},{15,16},{17,18},{19,... | collective-permute-start | bytes 663560 | tf_op jit(solution)/shard_map/ppermute | solution.py:310
  45.5 18.7 %collective-permute-start.7 = (bf16[96,1152]{1,0:T(8,128)(2,1)S(1)}, bf16[96,1152]{1,0:T(8,128)(2,1)S(1)}, u32[]{:S(2)}, u32[]{:S(2)}) collective-permute-start(bf16[96,1152]{1,0:T(8,128)(2,1)S(1)} %collective-permute-done.5.refs_2_), channel_id=1, source_target_pairs={{0,1},{2,3},{4,5},{6,7},{8,9},{10,11},{12,13},{14,15},{16,17},{18,... | collective-permute-start | bytes 663560 | tf_op jit(solution)/shard_map/ppermute | solution.py:310
  47.4 9.4 %collective-permute-start.8 = (bf16[48,2176]{1,0:T(8,128)(2,1)S(1)}, bf16[48,2176]{1,0:T(8,128)(2,1)S(1)}, u32[]{:S(2)}, u32[]{:S(2)}) collective-permute-start(bf16[48,2176]{1,0:T(8,128)(2,1)S(1)} %get-tuple-element.62), channel_id=1, source_target_pairs={{0,12},{1,13},{2,14},{3,15},{4,16},{5,17},{6,18},{7,19},{8,20},{9,... | collective-permute-start | bytes 626696 | tf_op jit(solution)/shard_map/ppermute | solution.py:325
  50.6 7.8 %collective-permute-start.9 = (bf16[48,2176]{1,0:T(8,128)(2,1)S(1)}, bf16[48,2176]{1,0:T(8,128)(2,1)S(1)}, u32[]{:S(2)}, u32[]{:S(2)}) collective-permute-start(bf16[48,2176]{1,0:T(8,128)(2,1)S(1)} %get-tuple-element.63), channel_id=1, source_target_pairs={{0,36},{1,37},{2,38},{3,39},{4,40},{5,41},{6,42},{7,43},{8,44},{9,... | collective-permute-start | bytes 626696 | tf_op jit(solution)/shard_map/ppermute | solution.py:325
  54.3 9.9 %collective-permute-start.10 = (bf16[48,2176]{1,0:T(8,128)(2,1)S(1)}, bf16[48,2176]{1,0:T(8,128)(2,1)S(1)}, u32[]{:S(2)}, u32[]{:S(2)}) collective-permute-start(bf16[48,2176]{1,0:T(8,128)(2,1)S(1)} %get-tuple-element.64), channel_id=1, source_target_pairs={{0,24},{1,25},{2,26},{3,27},{4,28},{5,29},{6,30},{7,31},{8,32},{9,... | collective-permute-start | bytes 626696 | tf_op jit(solution)/shard_map/ppermute | solution.py:325
  64.2 7.9 %collective-permute-start.11 = (bf16[96,1152]{1,0:T(8,128)(2,1)S(1)}, bf16[96,1152]{1,0:T(8,128)(2,1)S(1)}, u32[]{:S(2)}, u32[]{:S(2)}) collective-permute-start(bf16[96,1152]{1,0:T(8,128)(2,1)S(1)} %collective-permute-done.6.refs_1_), channel_id=1, source_target_pairs={{0,1},{2,3},{4,5},{6,7},{8,9},{10,11},{12,13},{14,15},{16,17},{18,... | collective-permute-start | bytes 663560 | tf_op jit(solution)/shard_map/ppermute | solution.py:310
  67.9 7.9 %collective-permute-start.12 = (bf16[96,1152]{1,0:T(8,128)(2,1)S(1)}, bf16[96,1152]{1,0:T(8,128)(2,1)S(1)}, u32[]{:S(2)}, u32[]{:S(2)}) collective-permute-start(bf16[96,1152]{1,0:T(8,128)(2,1)S(1)} %collective-permute-done.7.refs_3_), channel_id=1, source_target_pairs={{1,2},{3,4},{5,6},{7,8},{9,10},{11,0},{13,14},{15,16},{17,18},{19,... | collective-permute-start | bytes 663560 | tf_op jit(solution)/shard_map/ppermute | solution.py:310
  75.7 13.7 %collective-permute-start.16 = (bf16[96,1152]{1,0:T(8,128)(2,1)S(1)}, bf16[96,1152]{1,0:T(8,128)(2,1)S(1)}, u32[]{:S(2)}, u32[]{:S(2)}) collective-permute-start(bf16[96,1152]{1,0:T(8,128)(2,1)S(1)} %collective-permute-done.11.refs_0_), channel_id=1, source_target_pairs={{1,2},{3,4},{5,6},{7,8},{9,10},{11,0},{13,14},{15,16},{17,18},{19,... | collective-permute-start | bytes 663560 | tf_op jit(solution)/shard_map/ppermute | solution.py:310
  78.5 10.9 %collective-permute-start.17 = (bf16[96,1152]{1,0:T(8,128)(2,1)S(1)}, bf16[96,1152]{1,0:T(8,128)(2,1)S(1)}, u32[]{:S(2)}, u32[]{:S(2)}) collective-permute-start(bf16[96,1152]{1,0:T(8,128)(2,1)S(1)} %collective-permute-done.12.refs_2_), channel_id=1, source_target_pairs={{0,1},{2,3},{4,5},{6,7},{8,9},{10,11},{12,13},{14,15},{16,17},{18,... | collective-permute-start | bytes 663560 | tf_op jit(solution)/shard_map/ppermute | solution.py:310
  80.5 15.2 %collective-permute-start.13 = (bf16[48,2176]{1,0:T(8,128)(2,1)S(1)}, bf16[48,2176]{1,0:T(8,128)(2,1)S(1)}, u32[]{:S(2)}, u32[]{:S(2)}) collective-permute-start(bf16[48,2176]{1,0:T(8,128)(2,1)S(1)} %get-tuple-element.72), channel_id=1, source_target_pairs={{0,12},{1,13},{2,14},{3,15},{4,16},{5,17},{6,18},{7,19},{8,20},{9,... | collective-permute-start | bytes 626696 | tf_op jit(solution)/shard_map/ppermute | solution.py:325
  82.4 17.6 %collective-permute-start.14 = (bf16[48,2176]{1,0:T(8,128)(2,1)S(1)}, bf16[48,2176]{1,0:T(8,128)(2,1)S(1)}, u32[]{:S(2)}, u32[]{:S(2)}) collective-permute-start(bf16[48,2176]{1,0:T(8,128)(2,1)S(1)} %get-tuple-element.73), channel_id=1, source_target_pairs={{0,36},{1,37},{2,38},{3,39},{4,40},{5,41},{6,42},{7,43},{8,44},{9,... | collective-permute-start | bytes 626696 | tf_op jit(solution)/shard_map/ppermute | solution.py:325
  85.1 14.9 %collective-permute-start.15 = (bf16[48,2176]{1,0:T(8,128)(2,1)S(1)}, bf16[48,2176]{1,0:T(8,128)(2,1)S(1)}, u32[]{:S(2)}, u32[]{:S(2)}) collective-permute-start(bf16[48,2176]{1,0:T(8,128)(2,1)S(1)} %get-tuple-element.74), channel_id=1, source_target_pairs={{0,24},{1,25},{2,26},{3,27},{4,28},{5,29},{6,30},{7,31},{8,32},{9,... | collective-permute-start | bytes 626696 | tf_op jit(solution)/shard_map/ppermute | solution.py:325
  91.0 9.0 %collective-permute-start.18 = (bf16[48,2176]{1,0:T(8,128)(2,1)S(1)}, bf16[48,2176]{1,0:T(8,128)(2,1)S(1)}, u32[]{:S(2)}, u32[]{:S(2)}) collective-permute-start(bf16[48,2176]{1,0:T(8,128)(2,1)S(1)} %get-tuple-element.78), channel_id=1, source_target_pairs={{0,12},{1,13},{2,14},{3,15},{4,16},{5,17},{6,18},{7,19},{8,20},{9,... | collective-permute-start | bytes 626696 | tf_op jit(solution)/shard_map/ppermute | solution.py:325
  92.9 12.4 %collective-permute-start.19 = (bf16[48,2176]{1,0:T(8,128)(2,1)S(1)}, bf16[48,2176]{1,0:T(8,128)(2,1)S(1)}, u32[]{:S(2)}, u32[]{:S(2)}) collective-permute-start(bf16[48,2176]{1,0:T(8,128)(2,1)S(1)} %get-tuple-element.79), channel_id=1, source_target_pairs={{0,36},{1,37},{2,38},{3,39},{4,40},{5,41},{6,42},{7,43},{8,44},{9,... | collective-permute-start | bytes 626696 | tf_op jit(solution)/shard_map/ppermute | solution.py:325
  95.6 9.7 %collective-permute-start.20 = (bf16[48,2176]{1,0:T(8,128)(2,1)S(1)}, bf16[48,2176]{1,0:T(8,128)(2,1)S(1)}, u32[]{:S(2)}, u32[]{:S(2)}) collective-permute-start(bf16[48,2176]{1,0:T(8,128)(2,1)S(1)} %get-tuple-element.80), channel_id=1, source_target_pairs={{0,24},{1,25},{2,26},{3,27},{4,28},{5,29},{6,30},{7,31},{8,32},{9,... | collective-permute-start | bytes 626696 | tf_op jit(solution)/shard_map/ppermute | solution.py:325
  108.4 15.4 %collective-permute-start.21 = (bf16[480,1792]{1,0:T(8,128)(2,1)S(1)}, bf16[480,1792]{1,0:T(8,128)(2,1)S(1)}, u32[]{:S(2)}, u32[]{:S(2)}) collective-permute-start(bf16[480,1792]{1,0:T(8,128)(2,1)S(1)} %get-tuple-element.81), channel_id=1, source_target_pairs={{0,48},{48,0},{96,144},{144,96},{192,240},{240,192},{288,336},{336... | collective-permute-start | bytes 5160968 | tf_op jit(solution)/shard_map/ppermute | solution.py:346
  125.2 17.4 %collective-permute-start.22 = (bf16[768,256]{1,0:T(8,128)(2,1)}, bf16[768,256]{1,0:T(8,128)(2,1)}, u32[]{:S(2)}, u32[]{:S(2)}) collective-permute-start(bf16[768,256]{1,0:T(8,128)(2,1)} %get-tuple-element.97), channel_id=1, source_target_pairs={{96,192},{144,240},{288,384},{336,432},{480,576},{528,624},{672,0}... | collective-permute-start | bytes 1179656 | tf_op jit(solution)/shard_map/ppermute | solution.py:395
  130.3 17.5 %collective-permute-start.26 = (bf16[768,256]{1,0:T(8,128)(2,1)S(1)}, bf16[768,256]{1,0:T(8,128)(2,1)}, u32[]{:S(2)}, u32[]{:S(2)}) collective-permute-start(bf16[768,256]{1,0:T(8,128)(2,1)S(1)} %get-tuple-element.101), channel_id=1, source_target_pairs={{0,96},{48,144},{192,288},{240,336},{384,480},{432,528},{576,672},... | collective-permute-start | bytes 1179656 | tf_op jit(solution)/shard_map/ppermute | solution.py:395
  133.6 20.8 %copy-start.2 = (bf16[96,2048]{1,0:T(8,128)(2,1)S(1)}, bf16[96,2048]{1,0:T(8,128)(2,1)}, u32[]{:S(2)}) copy-start(bf16[96,2048]{1,0:T(8,128)(2,1)} %rw_ref.3) | copy-start | bytes 1179652
  133.7 20.8 %copy-start.4 = (bf16[48,2048]{1,0:T(8,128)(2,1)S(1)}, bf16[48,2048]{1,0:T(8,128)(2,1)}, u32[]{:S(2)}) copy-start(bf16[48,2048]{1,0:T(8,128)(2,1)} %x_ref.3) | copy-start | bytes 589828
  133.7 20.8 %all-to-all-start = ((bf16[48,8,128]{2,1,0:T(8,128)(2,1)}), bf16[48,8,128]{2,1,0:T(8,128)(2,1)S(1)}, u32[]{:S(2)}, u32[]{:S(2)}) async-start(bf16[48,8,128]{2,1,0:T(8,128)(2,1)} %bitcast.10), calls=%async_computation | async-start | bytes 196608 | tf_op jit(solution)/shard_map/all_to_all | solution.py:408
  144.4 21.4 %collective-permute-start.23 = (bf16[768,256]{1,0:T(8,128)(2,1)}, bf16[768,256]{1,0:T(8,128)(2,1)S(1)}, u32[]{:S(2)}, u32[]{:S(2)}) collective-permute-start(bf16[768,256]{1,0:T(8,128)(2,1)} %add_convert_fusion.3), channel_id=1, source_target_pairs={{0,96},{48,144},{192,288},{240,336},{384,480},{432,528},{576,672},... | collective-permute-start | bytes 1179656 | tf_op jit(solution)/shard_map/ppermute | solution.py:395
  148.9 21.0 %collective-permute-start.27 = (bf16[768,256]{1,0:T(8,128)(2,1)S(1)}, bf16[768,256]{1,0:T(8,128)(2,1)S(1)}, u32[]{:S(2)}, u32[]{:S(2)}) collective-permute-start(bf16[768,256]{1,0:T(8,128)(2,1)S(1)} %add_convert_fusion.1), channel_id=1, source_target_pairs={{96,192},{144,240},{288,384},{336,432},{480,576},{528,624},{672,0}... | collective-permute-start | bytes 1179656 | tf_op jit(solution)/shard_map/ppermute | solution.py:395
  156.7 27.4 %all-to-all-start.1 = ((bf16[48,8,512]{2,1,0:T(8,128)(2,1)}), bf16[48,8,512]{2,1,0:T(8,128)(2,1)S(1)}, u32[]{:S(2)}, u32[]{:S(2)}) async-start(bf16[48,8,512]{2,1,0:T(8,128)(2,1)} %bitcast.12), calls=%async_computation.1 | async-start | bytes 786432 | tf_op jit(solution)/shard_map/all_to_all | solution.py:417
  165.9 12.0 %collective-permute-start.24 = (bf16[768,256]{1,0:T(8,128)(2,1)S(1)}, bf16[768,256]{1,0:T(8,128)(2,1)S(1)}, u32[]{:S(2)}, u32[]{:S(2)}) collective-permute-start(bf16[768,256]{1,0:T(8,128)(2,1)S(1)} %add_convert_fusion.2), channel_id=1, source_target_pairs={{96,192},{144,240},{288,384},{336,432},{480,576},{528,624},{672,0}... | collective-permute-start | bytes 1179656 | tf_op jit(solution)/shard_map/ppermute | solution.py:395
  170.0 10.3 %collective-permute-start.28 = (bf16[768,256]{1,0:T(8,128)(2,1)S(1)}, bf16[768,256]{1,0:T(8,128)(2,1)S(1)}, u32[]{:S(2)}, u32[]{:S(2)}) collective-permute-start(bf16[768,256]{1,0:T(8,128)(2,1)S(1)} %add_convert_fusion), channel_id=1, source_target_pairs={{0,96},{48,144},{192,288},{240,336},{384,480},{432,528},{576,672},... | collective-permute-start | bytes 1179656 | tf_op jit(solution)/shard_map/ppermute | solution.py:395
  178.0 17.0 %collective-permute-start.25 = (bf16[768,128]{1,0:T(8,128)(2,1)S(1)}, bf16[768,128]{1,0:T(8,128)(2,1)S(1)}, u32[]{:S(2)}, u32[]{:S(2)}) collective-permute-start(bf16[768,128]{1,0:T(8,128)(2,1)S(1)} %add_convert_fusion.5), channel_id=1, source_target_pairs={{0,96},{48,144},{192,288},{240,336},{384,480},{432,528},{576,672},... | collective-permute-start | bytes 589832 | tf_op jit(solution)/shard_map/ppermute | solution.py:405
  180.3 14.8 %collective-permute-start.29 = (bf16[768,128]{1,0:T(8,128)(2,1)S(1)}, bf16[768,128]{1,0:T(8,128)(2,1)S(1)}, u32[]{:S(2)}, u32[]{:S(2)}) collective-permute-start(bf16[768,128]{1,0:T(8,128)(2,1)S(1)} %add_convert_fusion.4), channel_id=1, source_target_pairs={{96,192},{144,240},{288,384},{336,432},{480,576},{528,624},{672,0}... | collective-permute-start | bytes 589832 | tf_op jit(solution)/shard_map/ppermute | solution.py:405
  184.9 21.8 %all-to-all-start.2 = ((f32[16,8,512]{2,1,0:T(8,128)}), f32[16,8,512]{2,1,0:T(8,128)S(1)}, u32[]{:S(2)}, u32[]{:S(2)}) async-start(f32[16,8,512]{2,1,0:T(8,128)} %broadcast_in_dim.2), calls=%async_computation.2 | async-start | bytes 524288 | tf_op jit(solution)/shard_map/all_to_all | solution.py:420

commit v5 on v0

v5 whole, which is shorter than its diff:
```python
import functools

import jax
import jax.numpy as jnp
from jax import lax
from jax.experimental import pallas as pl
from jax.experimental.pallas import tpu as pltpu
from jax.sharding import PartitionSpec as P

F32 = jnp.float32
BF16 = jnp.bfloat16
LANES = 128
VMEM_BYTES = 40 * 1024 * 1024


def dot(a, b, dims=((1,), (0,))):
    return lax.dot_general(a, b, (dims, ((), ())), preferred_element_type=F32)


def iota(shape, axis):
    return lax.broadcasted_iota(jnp.int32, shape, axis)


def call(body, out_shape, flops, moved, n_smem=0, **kwargs):
    return pl.pallas_call(
        body,
        out_shape=out_shape,
        compiler_params=pltpu.CompilerParams(vmem_limit_bytes=VMEM_BYTES),
        cost_estimate=pl.CostEstimate(flops=flops, bytes_accessed=moved, transcendentals=0),
        **kwargs,
    )


def whole(n):
    return [pl.BlockSpec(memory_space=pltpu.VMEM)] * n


def narrow(tiles, out_ref):
    for k in range(tiles.shape[0]):
        out_ref[:, k * LANES : (k + 1) * LANES] = tiles[k].astype(BF16)


def pack(e, exp_dev, capacity, code, grad_ref, buffer):
    experts, rows = code.shape
    n_dev = experts // exp_dev
    piece = grad_ref.shape[1] // 8
    owner = jnp.where(iota((n_dev, experts), 1) == iota((n_dev, experts), 0) * exp_dev + e, 1.0, 0.0).astype(BF16)
    own = dot(owner, code.astype(BF16))
    select = [jnp.where(own == c, 1.0, 0.0) for c in range(capacity)]
    picked = dot(jnp.concatenate(select, axis=0).astype(BF16), grad_ref[...])
    tiles = piece // LANES
    for c in range(capacity):
        for p in range(8):
            for j in range(tiles):
                column = p * piece + j * LANES
                buffer.at[c * tiles + j][pl.ds(p, n_dev, stride=8), :] = picked[
                    c * n_dev : (c + 1) * n_dev, column : column + LANES
                ]
    return owner, select


def route_kernel(exp_dev, capacity, x_ref, grad_ref, rw_ref, routes_ref, chunk_ref, probs_ref, code_ref, buffer):
    experts = rw_ref.shape[0]
    top, rows = routes_ref.shape
    ids = iota((experts, rows), 0)
    chosen = ids == routes_ref[0:1, :]
    for k in range(1, top):
        chosen = chosen | (ids == routes_ref[k : k + 1, :])
    logits = dot(rw_ref[...], x_ref[...], ((1,), (1,)))
    highest = jnp.max(jnp.where(chosen, logits, -jnp.inf), axis=0, keepdims=True)
    weights = jnp.where(chosen, jnp.exp(jnp.where(chosen, logits - highest, 0.0)), 0.0)
    probs = weights / jnp.sum(weights, axis=0, keepdims=True)
    earlier = jnp.where(iota((rows, rows), 0) < iota((rows, rows), 1), 1.0, 0.0).astype(BF16)
    position = dot(jnp.where(chosen, 1.0, 0.0).astype(BF16), earlier)
    code = jnp.where(chosen, position, -1.0)
    probs_ref[...] = probs
    code_ref[...] = code
    n_dev = experts // exp_dev
    lane = iota((n_dev, LANES), 1)
    gates = jnp.zeros((n_dev, LANES), F32)
    for e in reversed(range(exp_dev)):
        if e == 0:
            owner, select = pack(0, exp_dev, capacity, code, grad_ref, buffer)
        else:
            owner = jnp.where(iota((n_dev, experts), 1) == iota((n_dev, experts), 0) * exp_dev + e, 1.0, 0.0)
            owner = owner.astype(BF16)
            own = dot(owner, code.astype(BF16))
            select = [jnp.where(own == c, 1.0, 0.0) for c in range(capacity)]
        own_probs = dot(owner, probs.astype(BF16))
        for c in range(capacity):
            gate = jnp.sum(select[c] * own_probs, axis=1, keepdims=True)
            gates = jnp.where(lane == e * capacity + c, gate, gates)
    for p in range(8):
        buffer.at[buffer.shape[0] - 1][pl.ds(p, n_dev, stride=8), :] = gates
    narrow(buffer, chunk_ref)


def pack_kernel(e, exp_dev, capacity, code_ref, grad_ref, chunk_ref, buffer):
    pack(e, exp_dev, capacity, code_ref[...], grad_ref, buffer)
    narrow(buffer, chunk_ref)


def place_kernel(e, capacity, order, place_ref, hidden_ref, *refs):
    chunk_ref, gates_ref = refs[0], refs[e]
    rows_ref, gate_ref, keep_ref, trade_ref, buffer, wide = refs[1 + e :]
    slots, width = rows_ref.shape
    n_source = slots // capacity
    piece, half = width // 8, width // 2
    tiles = piece // LANES
    for k in range(capacity * tiles):
        buffer[k] = chunk_ref[:, k * LANES : (k + 1) * LANES].astype(F32)
    for c in range(capacity):
        for p in range(8):
            for j in range(tiles):
                wide.at[p * tiles + j][pl.ds(c, n_source, stride=capacity), :] = buffer.at[c * tiles + j][
                    pl.ds(p, n_source, stride=8), :
                ]
    narrow(wide, rows_ref)
    spread = jnp.where(
        iota((slots, n_source * 8), 1) == lax.div(iota((slots, n_source * 8), 0), capacity) * 8, 1.0, 0.0
    ).astype(BF16)
    gates = dot(spread, gates_ref[:, gates_ref.shape[1] - LANES :])
    lane = e * capacity + lax.rem(iota((slots, LANES), 0), capacity)
    gate = jnp.sum(jnp.where(iota((slots, LANES), 1) == lane, gates, 0.0), axis=1, keepdims=True)
    gate_ref[...] = gate
    gated = (gate * hidden_ref[...].astype(F32)).astype(BF16)
    keep_ref[:, half:] = gated
    trade_ref[:, half:] = gated
    n_y = len(order)
    for k, delta in enumerate(order):
        chip = lax.rem(place_ref[0] + place_ref[2] * delta + n_y, n_y)
        mine = pl.multiple_of((2 * chip + place_ref[1]) * LANES, LANES)
        other = pl.multiple_of((2 * chip + 1 - place_ref[1]) * LANES, LANES)
        column = slice(k * LANES, (k + 1) * LANES)
        keep_ref[:, column] = rows_ref[:, pl.ds(mine, LANES)]
        trade_ref[:, column] = rows_ref[:, pl.ds(other, LANES)]


def product_kernel(e, capacity, rows_ref, gate_ref, hidden_ref, weight_ref, *refs):
    if e > 0:
        earlier_ref = refs[0]
        refs = refs[2:]
    grad_ref, back_ref, sums = refs
    f = pl.program_id(0)
    slots = rows_ref.shape[0]
    product = dot(rows_ref[...], weight_ref[0], ((1,), (1,)))
    grad_ref[0, 0] = (gate_ref[...] * product).astype(BF16)
    part = jnp.sum(product * hidden_ref[...].astype(F32), axis=1, keepdims=True)

    @pl.when(f == 0)
    def _():
        sums[...] = part

    @pl.when(f > 0)
    def _():
        sums[...] += part

    @pl.when(f == pl.num_programs(0) - 1)
    def _():
        lane = iota((slots, LANES), 1)
        slot = iota((slots, LANES), 0)
        spread = jnp.where(lane == e * capacity + lax.rem(slot, capacity), sums[...], 0.0)
        row = iota((back_ref.shape[0], slots), 0)
        source = lax.div(iota((back_ref.shape[0], slots), 1), capacity)
        high = spread.astype(BF16)
        rest = spread - high.astype(F32)
        middle = rest.astype(BF16)
        low = (rest - middle.astype(F32)).astype(BF16)
        total = jnp.zeros(back_ref.shape, F32) if e == 0 else earlier_ref[...].astype(F32)
        for i, piece in enumerate((high, middle, low)):
            group = jnp.where(row == source * 8 + i, 1.0, 0.0).astype(BF16)
            total += dot(group, piece)
        back_ref[...] = total.astype(BF16)


def partial_kernel(columns, mine_ref, got_ref, *outs):
    half = mine_ref.shape[1] - outs[0].shape[0] * 2
    for out, (part, blocks) in zip(outs, columns):
        span = slice(half + part * out.shape[0], half + (part + 1) * out.shape[0])
        total = jnp.zeros(out.shape, F32)
        for ref in (mine_ref, got_ref):
            wide = jnp.concatenate([ref[:, b * LANES : (b + 1) * LANES] for b in blocks], axis=1)
            total += dot(ref[:, span], wide, ((0,), (0,)))
        out[...] = total.astype(BF16)


def router_kernel(capacity, exp_dev, back_ref, probs_ref, code_ref, x_ref, rw_ref, term_ref, grad_ref):
    experts, rows = probs_ref.shape
    parts = back_ref.shape[0]
    width = rw_ref.shape[1]
    ids = lax.div(iota((experts, parts), 0), exp_dev)
    column = iota((experts, parts), 1)
    owner = jnp.where((lax.div(column, 8) == ids) & (lax.rem(column, 8) < 3), 1.0, 0.0).astype(BF16)
    spread = dot(owner, back_ref[...])
    lane = iota((experts, LANES), 1)
    start = lax.rem(iota((experts, LANES), 0), exp_dev) * capacity
    code = code_ref[...]
    probs = probs_ref[...]
    gate_grad = jnp.zeros((experts, rows), F32)
    for c in range(capacity):
        column = jnp.sum(jnp.where(lane == start + c, spread, 0.0), axis=1, keepdims=True)
        gate_grad += jnp.where(code == c, column, 0.0)
    weighted = jnp.sum(probs * gate_grad, axis=0, keepdims=True)
    logit_grad = probs * (gate_grad - weighted)
    high = logit_grad.astype(BF16)
    low = (logit_grad - high.astype(F32)).astype(BF16)
    grad_ref[...] = dot(high, rw_ref[...], ((0,), (0,))).astype(BF16)
    out_rows, piece = term_ref.shape
    split = width // piece
    row = iota((out_rows, experts), 0)
    first = iota((out_rows, experts), 1) * split
    repeat = jnp.where((row >= first) & (row < first + split), 1.0, 0.0).astype(BF16)
    high = dot(repeat, high).astype(BF16)
    low = dot(repeat, low).astype(BF16)
    quarter = lax.rem(iota((out_rows, 1), 0), split)
    total = jnp.zeros((out_rows, piece), F32)
    for q in range(split):
        x = x_ref[:, q * piece : (q + 1) * piece]
        total += jnp.where(quarter == q, dot(high, x) + dot(low, x), 0.0)
    term_ref[...] = total.astype(BF16)


def exchange_order(n):
    pairs = [[0, 1]]
    for step in range(1, n // 2):
        pairs.append([-step, -step - 1] if step % 2 else [step, step + 1])
    return pairs


def on_device(layer_input, out_grad, router_weight, routes, hidden_act, down_weight):
    n_expert = lax.axis_size("expert")
    n_dp = lax.axis_size("dp")
    n_y = n_dp // 2
    experts, width = router_weight.shape
    exp_dev = experts // n_expert
    per = hidden_act.shape[2]
    slots = exp_dev * per
    ff = hidden_act.shape[3]
    capacity = per // n_expert
    tok_rows, top_count = routes.shape
    shape = jax.ShapeDtypeStruct
    dp_index, expert_index = lax.axis_index("dp"), lax.axis_index("expert")
    y_index = dp_index // 2
    place = jnp.stack([y_index, dp_index % 2, 1 - 2 * (y_index % 2)]).astype(jnp.int32)
    smem = pl.BlockSpec(memory_space=pltpu.SMEM)
    chunk_rows, chunk_wide = n_expert * 8, capacity * width // 8

    chunk, probs, code = call(
        functools.partial(route_kernel, exp_dev, capacity),
        (
            shape((chunk_rows, chunk_wide + LANES), BF16),
            shape((experts, tok_rows), F32),
            shape((experts, tok_rows), F32),
        ),
        2 * tok_rows * experts * width,
        2 * (2 * tok_rows + experts) * width,
        scratch_shapes=[pltpu.VMEM((chunk_wide // LANES + 1, chunk_rows, LANES), F32)],
    )(layer_input, out_grad, router_weight, routes.T)

    def dispatch(chunk):
        chunk = chunk.reshape(n_expert, 8, chunk.shape[1])
        chunk = lax.all_to_all(chunk, "expert", split_axis=0, concat_axis=0, tiled=True)
        return chunk.reshape(chunk_rows, chunk.shape[2])

    arrived = [dispatch(chunk)]
    for e in range(1, exp_dev):
        chunk = call(
            functools.partial(pack_kernel, e, exp_dev, capacity),
            shape((chunk_rows, chunk_wide), BF16),
            2 * chunk_rows * tok_rows * width,
            2 * chunk_rows * chunk_wide,
            scratch_shapes=[pltpu.VMEM((chunk_wide // LANES, chunk_rows, LANES), F32)],
        )(code, out_grad)
        arrived.append(dispatch(chunk))

    hidden = hidden_act.reshape(slots, ff)
    y_pairs = exchange_order(n_y)
    groups = len(y_pairs)
    order = [d for pair in y_pairs for d in pair]
    block_of = {d % n_y: k for k, d in enumerate(order)}
    tile = ff // 2

    def y_swap(odd):
        one_way = [(2 * y + c, (2 * y + 2 + c) % n_dp) for y in range(odd, n_y, 2) for c in range(2)]
        return one_way + [(b, a) for a, b in one_way]

    def add(a, b):
        return (a.astype(F32) + b.astype(F32)).astype(BF16)

    hidden_grad, back, paced = None, None, None
    down_parts = []
    for e in range(exp_dev):
        if e > 0:
            arrived[e], _ = lax.optimization_barrier((arrived[e], paced))
        inputs = [arrived[e]] + ([arrived[0]] if e else [])
        rows, gate, keep, trade = call(
            functools.partial(place_kernel, e, capacity, order),
            (
                shape((per, width), BF16),
                shape((per, 1), F32),
                shape((per, width // 2 + ff), BF16),
                shape((per, width // 2 + ff), BF16),
            ),
            2 * per * chunk_rows * LANES,
            2 * per * (4 * width + 3 * ff),
            in_specs=[smem, pl.BlockSpec((per, ff), lambda i: (e, 0))] + whole(len(inputs)),
            out_specs=whole(4),
            grid=(1,),
            scratch_shapes=[
                pltpu.VMEM((chunk_wide // LANES, chunk_rows, LANES), F32),
                pltpu.VMEM((width // LANES, per, LANES), F32),
            ],
        )(place, hidden, *inputs)

        got = lax.ppermute(trade, "dp", [(i, i ^ 1) for i in range(n_dp)])

        more, specs, alias = [], [], {}
        if e > 0:
            more = [back, hidden_grad]
            specs = [pl.BlockSpec((chunk_rows, LANES), lambda f: (0, 0)), pl.BlockSpec(memory_space=pl.ANY)]
            alias = {5: 0}
        hidden_grad, back = call(
            functools.partial(product_kernel, e, capacity),
            (shape((1, exp_dev, per, ff), BF16), shape((chunk_rows, LANES), BF16)),
            2 * per * ff * width,
            2 * (per + ff) * width + 4 * per * ff,
            grid=(ff // tile,),
            in_specs=[
                pl.BlockSpec((per, width), lambda f: (0, 0)),
                pl.BlockSpec((per, 1), lambda f: (0, 0)),
                pl.BlockSpec((per, tile), lambda f: (e, f)),
                pl.BlockSpec((1, tile, width), lambda f: (e, f, 0)),
                *specs,
            ],
            out_specs=(
                pl.BlockSpec((1, 1, per, tile), lambda f: (0, e, 0, f)),
                pl.BlockSpec((chunk_rows, LANES), lambda f: (0, 0)),
            ),
            scratch_shapes=[pltpu.VMEM((per, 1), F32)],
            input_output_aliases=alias,
        )(rows, gate, hidden, down_weight, *more)
        got, back = lax.optimization_barrier((got, back))

        def partials(which):
            columns = [
                (half, [block_of[(1 - 2 * half) * d % n_y] for d in y_pairs[g]]) for g in which for half in range(2)
            ]
            return call(
                functools.partial(partial_kernel, columns),
                [shape((tile, 2 * LANES), BF16)] * len(columns),
                4 * per * ff * 2 * LANES * len(which),
                4 * per * (ff + 2 * LANES * len(which)),
                in_specs=whole(2),
                out_specs=whole(len(columns)),
            )(keep, got)

        sums = partials([groups - 1])
        later = list(partials(list(range(groups - 2, -1, -1)))) if groups > 1 else []
        if e == exp_dev - 1:
            back, *later = lax.optimization_barrier((back, *later))
        paced = sums[0]
        for step in range(groups, 1, -1):
            came = [lax.ppermute(sums[h], "dp", y_swap((step - 1 + h) % 2)) for h in range(2)]
            mine, later = later[:2], later[2:]
            if step > 2:
                sums = [add(a, b) for a, b in zip(mine, came)]
                paced = sums[0]
            else:
                away = [add(a[:, LANES:], b[:, LANES:]) for a, b in zip(mine, came)]
                home = [a[:, :LANES].astype(F32) + b[:, :LANES].astype(F32) for a, b in zip(mine, came)]
        if groups == 1:
            away = [a[:, LANES:] for a in sums]
            home = [a[:, :LANES].astype(F32) for a in sums]
        came = [lax.ppermute(away[h], "dp", y_swap(h)) for h in range(2)]
        down_parts += [a + b.astype(F32) for a, b in zip(home, came)]
    down_grad = jnp.concatenate(down_parts).reshape(exp_dev, ff, LANES)

    back = lax.all_to_all(back.reshape(n_expert, 8, LANES), "expert", split_axis=0, concat_axis=0, tiled=True)
    piece = exp_dev * width // 8
    term, input_grad = call(
        functools.partial(router_kernel, capacity, exp_dev),
        (shape((n_expert * 8, piece), BF16), shape((tok_rows, width), BF16)),
        2 * tok_rows * width * (experts + 2 * n_expert * 8),
        2 * (2 * tok_rows + 2 * experts) * width,
    )(back.reshape(n_expert * 8, LANES), probs, code, layer_input, router_weight)

    shares = lax.all_to_all(term.reshape(n_expert, 8, piece), "expert", split_axis=0, concat_axis=0, tiled=True)
    replica_sum = jnp.sum(shares.astype(F32), axis=0)
    copies = jnp.broadcast_to(replica_sum[None], (n_dp, 8, piece))
    gathered = lax.all_to_all(copies, "dp", split_axis=0, concat_axis=0, tiled=True)
    router_grad = jnp.sum(gathered, axis=0).reshape(exp_dev, width)
    return (down_grad, hidden_grad, router_grad, input_grad)


def solution(mesh):
    in_specs = (
        P(("dp", "expert"), None),
        P(("dp", "expert"), None),
        P(),
        P(("dp", "expert"), None),
        P("dp", "expert", None, None),
        P("expert", None, None),
    )
    out_specs = (
        P("expert", None, "dp"),
        P("dp", "expert", None, None),
        P("expert", None),
        P(("dp", "expert"), None),
    )
    return jax.shard_map(
        on_device, mesh=mesh, in_specs=in_specs, out_specs=out_specs, check_vma=False
    )
```

time: 646 us -> 214 us (0.33)
  waiting for transfers between devices: 537 us -> 63.7 us
  starting transfers between devices: 33.3 us -> 113 us
  matrix products: 25.6 us -> 0 us
  Pallas kernels: 0 us -> 16.9 us
  between operations: 15.8 us -> 1.16 us
  local copies, waits for them, and re-layouts: 26.6 us -> 12 us
    psum x1 -> x0, waiting for transfers between devices: 451 us -> none  [on_device(): summed = lax.psum(router_term, ('dp', 'expert'))]
    ppermute x0 -> x18, starting transfers between devices: none -> 58.8 us  [the longest x12 37 us: on_device(): lax.ppermute(sums[h], 'dp', y_swap((step - 1 + h) % 2))]
    all_to_all x3 -> x5, waiting for transfers between devices: 86.2 us -> 55.4 us  [the longest x2 38.3 us: dispatch(): lax.all_to_all(chunk, 'expert', split_axis=0, concat_axis=0, tiled=True)]
    dot_general x7 -> x0, matrix products: 25.6 us -> none  [the longest x1 8.24 us: on_device(): jnp.einsum('esd,efd->esf', scaled, down_weight, preferred_element_type=jn...]
    all_to_all x3 -> x5, starting transfers between devices: 33 us -> 54.2 us  [the longest x2 30.1 us: dispatch(): lax.all_to_all(chunk, 'expert', split_axis=0, concat_axis=0, tiled=True)]
    pallas_call x0 -> x11, Pallas kernels: none -> 16.9 us  [the longest x2 5.59 us: on_device(): call(functools.partial(product_kernel, e, capacity), (shape((1, exp_dev,...]
    ppermute x0 -> x18, waiting for transfers between devices: none -> 8.28 us  [the longest x12 8.26 us: on_device(): lax.ppermute(sums[h], 'dp', y_swap((step - 1 + h) % 2))]
    gather x3 -> x0, local copies, waits for them, and re-layouts: 7.74 us -> none  [the longest x2 4.94 us: on_device(): out_grad[jnp.maximum(slot_token, 0)]]
  transfers between devices with their start and end apart: 5 -> 23, of which waited for: 4 -> 9; matrix products, arithmetic and copies ran while one was open for 3% -> 3% of each run, Pallas kernels for 0% -> 7%
where the time goes in v5:
time: 214 us; the launch traced here: 213 us
  starting transfers between devices  113 us (53%)
  waiting for transfers between devices  63.7 us (30%)
  Pallas kernels  16.9 us (8%)
  local copies, waits for them, and re-layouts  12 us (6%)
  other arithmetic  5.82 us (3%)
    all_to_all x2, waiting for transfers between devices, dispatch(): lax.all_to_all(chunk, 'expert', split_axis=0, concat_axis=0, tiled=True)  38.3 us
    ppermute x12, starting transfers between devices, on_device(): lax.ppermute(sums[h], 'dp', y_swap((step - 1 + h) % 2))  37 us
    all_to_all x2, starting transfers between devices, dispatch(): lax.all_to_all(chunk, 'expert', split_axis=0, concat_axis=0, tiled=True)  30.1 us
    ppermute x4, starting transfers between devices, on_device(): came = [lax.ppermute(away[h], 'dp', y_swap(h)) for h in range(2)]  12.3 us
    all_to_all x1, starting transfers between devices, on_device(): lax.all_to_all(copies, 'dp', split_axis=0, concat_axis=0, tiled=True)  12 us
    unnamed x26, local copies, waits for them, and re-layouts  10.7 us
    all_to_all x1, waiting for transfers between devices, on_device(): lax.all_to_all(copies, 'dp', split_axis=0, concat_axis=0, tiled=True)  10.7 us
    ppermute x2, starting transfers between devices, on_device(): got = lax.ppermute(trade, 'dp', [(i, i ^ 1) for i in range(n_dp)])  9.44 us
  transfers between devices with their start and end apart: 23, of which 9 were waited for; matrix products, arithmetic and copies ran while one was open for 3% of the time, Pallas kernels for 7%

profile of v5, /device:TPU:1, one launch (start us, length us, event | category | flops | bytes accessed | tf_op | source)
XLA Modules:
  0.0 212.6 jit_solution(10698956666396984265)
XLA Ops:
  0.6 0.0 copy-start.4
  0.6 1.0 copy-done.4
  1.6 0.9 copy-done.6
  2.6 0.9 copy-done.8
  3.5 0.7 copy-done.12
  4.2 2.3 %shard_map.93 = (bf16[384,1408]{1,0:T(8,128)(2,1)}, f32[96,48]{1,0:T(8,128)S(1)}, f32[96,48]{1,0:T(8,128)S(1)}) custom-call(bf16[48,2048]{1,0:T(8,128)(2,1)S(1)} %copy-done.8, bf16[48,2048]{1,0:T(8,128)(2,1)S(1)} %copy-done.6, bf16[96,2048]{1,0:T(8,128)(2,1)S(1)} %copy-done.4, s32[8,48]{1,0:T(8,128)S(1)} %bitcast.22), custom_call_target="tpu_custom_call" | custom-call | flops 18874368 | bytes 786432 | tf_op jit(solution)/shard_map/pallas_call | solution.py:248
  6.5 0.6 copy-done.10
  7.1 19.0 %all-to-all-start = ((bf16[48,8,1408]{2,1,0:T(8,128)(2,1)}), bf16[48,8,1408]{2,1,0:T(8,128)(2,1)S(1)}, u32[]{:S(2)}, u32[]{:S(2)}) async-start(bf16[48,8,1408]{2,1,0:T(8,128)(2,1)} %bitcast.5), calls=%async_computation | async-start | bytes 2162688 | tf_op jit(solution)/shard_map/all_to_all | solution.py:262
  26.1 0.8 shard_map.98
  26.9 0.9 copy-done.3
  27.8 36.6 %all-to-all-done = bf16[48,8,1408]{2,1,0:T(8,128)(2,1)S(1)} async-done(((bf16[48,8,1408]{2,1,0:T(8,128)(2,1)}), bf16[48,8,1408]{2,1,0:T(8,128)(2,1)S(1)}, u32[]{:S(2)}, u32[]{:S(2)}) %all-to-all-start) | async-done | bytes 1081376 | tf_op jit(solution)/shard_map/all_to_all | solution.py:262
  64.4 11.2 %all-to-all-start.1 = ((bf16[48,8,1280]{2,1,0:T(8,128)(2,1)}), bf16[48,8,1280]{2,1,0:T(8,128)(2,1)S(1)}, u32[]{:S(2)}, u32[]{:S(2)}) async-start(bf16[48,8,1280]{2,1,0:T(8,128)(2,1)} %bitcast.20), calls=%async_computation.1 | async-start | bytes 1966080 | tf_op jit(solution)/shard_map/all_to_all | solution.py:262
  75.6 0.1 pad_add_fusion.place_ref
  75.7 1.8 shard_map.94
  77.4 2.7 %collective-permute-start = (bf16[240,1792]{1,0:T(8,128)(2,1)S(1)}, bf16[240,1792]{1,0:T(8,128)(2,1)S(1)}, u32[]{:S(2)}, u32[]{:S(2)}) collective-permute-start(bf16[240,1792]{1,0:T(8,128)(2,1)S(1)} %get-tuple-element.51), channel_id=1, source_target_pairs={{0,48},{48,0},{96,144},{144,96},{192,240},{240,192},{288,336},{336... | collective-permute-start | bytes 2580488 | tf_op jit(solution)/shard_map/ppermute | solution.py:315
  80.1 2.8 %copy-done = bf16[2,768,2048]{2,1,0:T(8,128)(2,1)S(1)} copy-done((bf16[2,768,2048]{2,1,0:T(8,128)(2,1)S(1)}, bf16[2,768,2048]{2,1,0:T(8,128)(2,1)}, u32[]{:S(2)}) %copy-start) | copy-done | bytes 6291480
  82.9 2.8 %shard_map.95 = (bf16[1,2,240,768]{3,2,1,0:T(8,128)(2,1)}, bf16[384,128]{1,0:T(8,128)(2,1)S(1)}) custom-call(bf16[240,2048]{1,0:T(8,128)(2,1)S(1)} %get-tuple-element.52.rows_ref, f32[240,1]{1,0:T(8,128)S(1)} %get-tuple-element.53.gate_ref, bf16[480,768]{1,0:T(8,128)(2,1)S(1)} %bitcast.14, bf16[2,768,2048]{2,1,0:T(8,128)(2,1)S(1)} %copy-done), custom_call_target="tpu_custom_call" | custom-call | flops 754974720 | bytes 4866048 | tf_op jit(solution)/shard_map/pallas_call | solution.py:322
  85.7 0.4 shard_map.97
  86.1 5.1 %collective-permute-start.1 = (bf16[384,256]{1,0:T(8,128)(2,1)S(1)}, bf16[384,256]{1,0:T(8,128)(2,1)S(1)}, u32[]{:S(2)}, u32[]{:S(2)}) collective-permute-start(bf16[384,256]{1,0:T(8,128)(2,1)S(1)} %get-tuple-element.59), channel_id=1, source_target_pairs={{96,192},{144,240},{288,384},{336,432},{480,576},{528,624},{672,0}... | collective-permute-start | bytes 589832 | tf_op jit(solution)/shard_map/ppermute | solution.py:363
  91.2 1.9 collective-permute-start.5
  93.1 0.8 shard_map.96
  94.0 2.5 %collective-permute-done.1 = bf16[384,256]{1,0:T(8,128)(2,1)S(1)} collective-permute-done((bf16[384,256]{1,0:T(8,128)(2,1)S(1)}, bf16[384,256]{1,0:T(8,128)(2,1)S(1)}, u32[]{:S(2)}, u32[]{:S(2)}) %collective-permute-start.1) | collective-permute-done | bytes 196640 | tf_op jit(solution)/shard_map/ppermute | solution.py:363
  96.5 1.9 collective-permute-start.2
  98.4 0.9 collective-permute-done.5
  99.3 0.7 add_convert_fusion.5
  100.0 3.5 %collective-permute-start.6 = (bf16[384,256]{1,0:T(8,128)(2,1)}, bf16[384,256]{1,0:T(8,128)(2,1)}, u32[]{:S(2)}, u32[]{:S(2)}) collective-permute-start(bf16[384,256]{1,0:T(8,128)(2,1)} %add_convert_fusion.5), channel_id=1, source_target_pairs={{96,192},{144,240},{288,384},{336,432},{480,576},{528,624},{672,0}... | collective-permute-start | bytes 589832 | tf_op jit(solution)/shard_map/ppermute | solution.py:363
  103.5 0.7 collective-permute-done.2
  104.3 0.7 add_convert_fusion.6
  105.0 4.1 %collective-permute-start.3 = (bf16[384,256]{1,0:T(8,128)(2,1)}, bf16[384,256]{1,0:T(8,128)(2,1)}, u32[]{:S(2)}, u32[]{:S(2)}) collective-permute-start(bf16[384,256]{1,0:T(8,128)(2,1)} %add_convert_fusion.6), channel_id=1, source_target_pairs={{96,192},{144,240},{288,384},{336,432},{480,576},{528,624},{672,0}... | collective-permute-start | bytes 589832 | tf_op jit(solution)/shard_map/ppermute | solution.py:363
  109.1 1.7 all-to-all-done.1
  110.9 1.7 shard_map.99
  112.6 6.8 %collective-permute-start.9 = (bf16[240,1792]{1,0:T(8,128)(2,1)S(1)}, bf16[240,1792]{1,0:T(8,128)(2,1)S(1)}, u32[]{:S(2)}, u32[]{:S(2)}) collective-permute-start(bf16[240,1792]{1,0:T(8,128)(2,1)S(1)} %get-tuple-element.66), channel_id=1, source_target_pairs={{0,48},{48,0},{96,144},{144,96},{192,240},{240,192},{288,336},{336... | collective-permute-start | bytes 2580488 | tf_op jit(solution)/shard_map/ppermute | solution.py:315
  119.4 1.0 add_convert_fusion.4
  120.4 3.2 %collective-permute-start.7 = (bf16[384,256]{1,0:T(8,128)(2,1)S(1)}, bf16[384,256]{1,0:T(8,128)(2,1)S(1)}, u32[]{:S(2)}, u32[]{:S(2)}) collective-permute-start(bf16[384,256]{1,0:T(8,128)(2,1)S(1)} %add_convert_fusion.4), channel_id=1, source_target_pairs={{0,96},{48,144},{192,288},{240,336},{384,480},{432,528},{576,672},... | collective-permute-start | bytes 589832 | tf_op jit(solution)/shard_map/ppermute | solution.py:363
  123.6 2.8 %copy-done.1 = bf16[2,768,2048]{2,1,0:T(8,128)(2,1)S(1)} copy-done((bf16[2,768,2048]{2,1,0:T(8,128)(2,1)S(1)}, bf16[2,768,2048]{2,1,0:T(8,128)(2,1)}, u32[]{:S(2)}) %copy-start.1) | copy-done | bytes 6291480
  126.4 2.8 %shard_map.100 = (bf16[1,2,240,768]{3,2,1,0:T(8,128)(2,1)}, bf16[384,128]{1,0:T(8,128)(2,1)}) custom-call(bf16[240,2048]{1,0:T(8,128)(2,1)S(1)} %get-tuple-element.67.rows_ref, f32[240,1]{1,0:T(8,128)S(1)} %get-tuple-element.68.gate_ref, bf16[480,768]{1,0:T(8,128)(2,1)S(1)} %bitcast.16, ...), custom_call_target="tpu_custom_call", output_to_operand_aliasing={{0}: (5, {})} | custom-call | flops 754974720 | bytes 4866048 | tf_op jit(solution)/shard_map/pallas_call | solution.py:322
  129.2 0.9 add_convert_fusion.11
  130.1 2.1 collective-permute-start.4
  132.3 5.1 %collective-permute-start.8 = (bf16[384,128]{1,0:T(8,128)(2,1)S(1)}, bf16[384,128]{1,0:T(8,128)(2,1)S(1)}, u32[]{:S(2)}, u32[]{:S(2)}) collective-permute-start(bf16[384,128]{1,0:T(8,128)(2,1)S(1)} %add_convert_fusion.10), channel_id=1, source_target_pairs={{96,192},{144,240},{288,384},{336,432},{480,576},{528,624},{672,0}... | collective-permute-start | bytes 294920 | tf_op jit(solution)/shard_map/ppermute | solution.py:374
  137.4 0.9 convert_add_fusion.3
  138.3 0.8 shard_map.101
  139.2 0.0 copy-start.5
  139.2 0.0 copy-start.9
  139.2 0.4 shard_map.102
  139.6 3.6 %collective-permute-start.10 = (bf16[384,256]{1,0:T(8,128)(2,1)S(1)}, bf16[384,256]{1,0:T(8,128)(2,1)S(1)}, u32[]{:S(2)}, u32[]{:S(2)}) collective-permute-start(bf16[384,256]{1,0:T(8,128)(2,1)S(1)} %get-tuple-element.84), channel_id=1, source_target_pairs={{96,192},{144,240},{288,384},{336,432},{480,576},{528,624},{672,0}... | collective-permute-start | bytes 589832 | tf_op jit(solution)/shard_map/ppermute | solution.py:363
  143.2 6.5 %all-to-all-start.2 = ((bf16[48,8,128]{2,1,0:T(8,128)(2,1)}), bf16[48,8,128]{2,1,0:T(8,128)(2,1)S(1)}, u32[]{:S(2)}, u32[]{:S(2)}) async-start(bf16[48,8,128]{2,1,0:T(8,128)(2,1)} %bitcast.10), calls=%async_computation.2 | async-start | bytes 196608 | tf_op jit(solution)/shard_map/all_to_all | solution.py:378
  149.8 1.9 collective-permute-start.14
  151.8 3.4 %collective-permute-start.11 = (bf16[384,256]{1,0:T(8,128)(2,1)S(1)}, bf16[384,256]{1,0:T(8,128)(2,1)S(1)}, u32[]{:S(2)}, u32[]{:S(2)}) collective-permute-start(bf16[384,256]{1,0:T(8,128)(2,1)S(1)} %add_convert_fusion.3), channel_id=1, source_target_pairs={{0,96},{48,144},{192,288},{240,336},{384,480},{432,528},{576,672},... | collective-permute-start | bytes 589832 | tf_op jit(solution)/shard_map/ppermute | solution.py:363
  155.2 6.4 %all-to-all-done.2 = bf16[48,8,128]{2,1,0:T(8,128)(2,1)S(1)} async-done(((bf16[48,8,128]{2,1,0:T(8,128)(2,1)}), bf16[48,8,128]{2,1,0:T(8,128)(2,1)S(1)}, u32[]{:S(2)}, u32[]{:S(2)}) %all-to-all-start.2) | async-done | bytes 98336 | tf_op jit(solution)/shard_map/all_to_all | solution.py:378
  161.6 2.2 %shard_map.103 = (bf16[384,512]{1,0:T(8,128)(2,1)}, bf16[48,2048]{1,0:T(8,128)(2,1)}) custom-call(bf16[384,128]{1,0:T(8,128)(2,1)S(1)} %bitcast.21, f32[96,48]{1,0:T(8,128)S(1)} %copy-done.11, f32[96,48]{1,0:T(8,128)S(1)} %get-tuple-element.64.code_ref, bf16[48,2048]{1,0:T(8,128)(2,1)S(1)} %copy-done.9, bf16[96,2048]{1,0:T(8,128)(2,1)S(1)} %copy-done.5), custom_call_target="tpu_custom_call" | custom-call | flops 169869312 | bytes 1179648 | tf_op jit(solution)/shard_map/pallas_call | solution.py:380
  163.9 5.5 %all-to-all-start.3 = ((bf16[48,8,512]{2,1,0:T(8,128)(2,1)}), bf16[48,8,512]{2,1,0:T(8,128)(2,1)S(1)}, u32[]{:S(2)}, u32[]{:S(2)}) async-start(bf16[48,8,512]{2,1,0:T(8,128)(2,1)} %bitcast.12), calls=%async_computation.3 | async-start | bytes 786432 | tf_op jit(solution)/shard_map/all_to_all | solution.py:387
  169.5 2.9 %collective-permute-start.15 = (bf16[384,256]{1,0:T(8,128)(2,1)S(1)}, bf16[384,256]{1,0:T(8,128)(2,1)S(1)}, u32[]{:S(2)}, u32[]{:S(2)}) collective-permute-start(bf16[384,256]{1,0:T(8,128)(2,1)S(1)} %add_convert_fusion.1), channel_id=1, source_target_pairs={{96,192},{144,240},{288,384},{336,432},{480,576},{528,624},{672,0}... | collective-permute-start | bytes 589832 | tf_op jit(solution)/shard_map/ppermute | solution.py:363
  172.4 3.6 %collective-permute-start.12 = (bf16[384,256]{1,0:T(8,128)(2,1)S(1)}, bf16[384,256]{1,0:T(8,128)(2,1)S(1)}, u32[]{:S(2)}, u32[]{:S(2)}) collective-permute-start(bf16[384,256]{1,0:T(8,128)(2,1)S(1)} %add_convert_fusion.2), channel_id=1, source_target_pairs={{96,192},{144,240},{288,384},{336,432},{480,576},{528,624},{672,0}... | collective-permute-start | bytes 589832 | tf_op jit(solution)/shard_map/ppermute | solution.py:363
  176.0 1.0 collective-permute-done.15
  177.1 1.9 collective-permute-start.16
  179.1 3.1 %collective-permute-done.12 = bf16[384,256]{1,0:T(8,128)(2,1)S(1)} collective-permute-done((bf16[384,256]{1,0:T(8,128)(2,1)S(1)}, bf16[384,256]{1,0:T(8,128)(2,1)S(1)}, u32[]{:S(2)}, u32[]{:S(2)}) %collective-permute-start.12) | collective-permute-done | bytes 196640 | tf_op jit(solution)/shard_map/ppermute | solution.py:363
  182.2 1.9 collective-permute-start.13
  184.2 3.2 %collective-permute-start.17 = (bf16[384,128]{1,0:T(8,128)(2,1)S(1)}, bf16[384,128]{1,0:T(8,128)(2,1)S(1)}, u32[]{:S(2)}, u32[]{:S(2)}) collective-permute-start(bf16[384,128]{1,0:T(8,128)(2,1)S(1)} %add_convert_fusion.8), channel_id=1, source_target_pairs={{96,192},{144,240},{288,384},{336,432},{480,576},{528,624},{672,0}... | collective-permute-start | bytes 294920 | tf_op jit(solution)/shard_map/ppermute | solution.py:374
  187.4 0.1 convert_reduce_fusion
  187.5 0.7 broadcast_in_dim.2
  188.2 12.0 %all-to-all-start.4 = ((f32[16,8,512]{2,1,0:T(8,128)}), f32[16,8,512]{2,1,0:T(8,128)S(1)}, u32[]{:S(2)}, u32[]{:S(2)}) async-start(f32[16,8,512]{2,1,0:T(8,128)} %broadcast_in_dim.2), calls=%async_computation.4 | async-start | bytes 524288 | tf_op jit(solution)/shard_map/all_to_all | solution.py:390
  200.3 0.9 pad_maximum_fusion
  201.2 10.7 %all-to-all-done.4 = f32[16,8,512]{2,1,0:T(8,128)S(1)} async-done(((f32[16,8,512]{2,1,0:T(8,128)}), f32[16,8,512]{2,1,0:T(8,128)S(1)}, u32[]{:S(2)}, u32[]{:S(2)}) %all-to-all-start.4) | async-done | bytes 262176 | tf_op jit(solution)/shard_map/all_to_all | solution.py:390
  211.9 0.6 reshape.48
  (41 shorter events, 0.5 us)
Async XLA Ops:
  0.6 1.0 copy-start.4
  1.6 0.9 copy-start.6
  2.6 0.9 copy-start.8
  3.5 0.7 copy-start.12
  6.5 0.6 copy-start.10
  7.1 19.0 %copy-start.7 = (bf16[48,2048]{1,0:T(8,128)(2,1)S(1)}, bf16[48,2048]{1,0:T(8,128)(2,1)}, u32[]{:S(2)}) copy-start(bf16[48,2048]{1,0:T(8,128)(2,1)} %grad_ref.3) | copy-start | bytes 589828
  7.1 57.3 %all-to-all-start = ((bf16[48,8,1408]{2,1,0:T(8,128)(2,1)}), bf16[48,8,1408]{2,1,0:T(8,128)(2,1)S(1)}, u32[]{:S(2)}, u32[]{:S(2)}) async-start(bf16[48,8,1408]{2,1,0:T(8,128)(2,1)} %bitcast.5), calls=%async_computation | async-start | bytes 2162688 | tf_op jit(solution)/shard_map/all_to_all | solution.py:262
  26.9 1.0 copy-start.3
  27.8 47.8 %copy-start.2 = (bf16[1,2,240,768]{3,2,1,0:T(8,128)(2,1)S(1)}, bf16[1,2,240,768]{3,2,1,0:T(8,128)(2,1)}, u32[]{:S(2)}) copy-start(bf16[1,2,240,768]{3,2,1,0:T(8,128)(2,1)} %param.10) | copy-start | bytes 2211844
  64.4 46.5 %all-to-all-start.1 = ((bf16[48,8,1280]{2,1,0:T(8,128)(2,1)}), bf16[48,8,1280]{2,1,0:T(8,128)(2,1)S(1)}, u32[]{:S(2)}, u32[]{:S(2)}) async-start(bf16[48,8,1280]{2,1,0:T(8,128)(2,1)} %bitcast.20), calls=%async_computation.1 | async-start | bytes 1966080 | tf_op jit(solution)/shard_map/all_to_all | solution.py:262
  77.4 8.3 %collective-permute-start = (bf16[240,1792]{1,0:T(8,128)(2,1)S(1)}, bf16[240,1792]{1,0:T(8,128)(2,1)S(1)}, u32[]{:S(2)}, u32[]{:S(2)}) collective-permute-start(bf16[240,1792]{1,0:T(8,128)(2,1)S(1)} %get-tuple-element.51), channel_id=1, source_target_pairs={{0,48},{48,0},{96,144},{144,96},{192,240},{240,192},{288,336},{336... | collective-permute-start | bytes 2580488 | tf_op jit(solution)/shard_map/ppermute | solution.py:315
  80.1 2.8 %copy-start = (bf16[2,768,2048]{2,1,0:T(8,128)(2,1)S(1)}, bf16[2,768,2048]{2,1,0:T(8,128)(2,1)}, u32[]{:S(2)}) copy-start(bf16[2,768,2048]{2,1,0:T(8,128)(2,1)} %weight_ref.3) | copy-start | bytes 18874372
  86.1 10.3 %collective-permute-start.1 = (bf16[384,256]{1,0:T(8,128)(2,1)S(1)}, bf16[384,256]{1,0:T(8,128)(2,1)S(1)}, u32[]{:S(2)}, u32[]{:S(2)}) collective-permute-start(bf16[384,256]{1,0:T(8,128)(2,1)S(1)} %get-tuple-element.59), channel_id=1, source_target_pairs={{96,192},{144,240},{288,384},{336,432},{480,576},{528,624},{672,0}... | collective-permute-start | bytes 589832 | tf_op jit(solution)/shard_map/ppermute | solution.py:363
  91.2 8.1 %collective-permute-start.5 = (bf16[384,256]{1,0:T(8,128)(2,1)S(1)}, bf16[384,256]{1,0:T(8,128)(2,1)S(1)}, u32[]{:S(2)}, u32[]{:S(2)}) collective-permute-start(bf16[384,256]{1,0:T(8,128)(2,1)S(1)} %get-tuple-element.63), channel_id=1, source_target_pairs={{0,96},{48,144},{192,288},{240,336},{384,480},{432,528},{576,672},... | collective-permute-start | bytes 589832 | tf_op jit(solution)/shard_map/ppermute | solution.py:363
  96.5 7.8 %collective-permute-start.2 = (bf16[384,256]{1,0:T(8,128)(2,1)S(1)}, bf16[384,256]{1,0:T(8,128)(2,1)S(1)}, u32[]{:S(2)}, u32[]{:S(2)}) collective-permute-start(bf16[384,256]{1,0:T(8,128)(2,1)S(1)} %add_convert_fusion.7), channel_id=1, source_target_pairs={{0,96},{48,144},{192,288},{240,336},{384,480},{432,528},{576,672},... | collective-permute-start | bytes 589832 | tf_op jit(solution)/shard_map/ppermute | solution.py:363
  100.0 19.4 %collective-permute-start.6 = (bf16[384,256]{1,0:T(8,128)(2,1)}, bf16[384,256]{1,0:T(8,128)(2,1)}, u32[]{:S(2)}, u32[]{:S(2)}) collective-permute-start(bf16[384,256]{1,0:T(8,128)(2,1)} %add_convert_fusion.5), channel_id=1, source_target_pairs={{96,192},{144,240},{288,384},{336,432},{480,576},{528,624},{672,0}... | collective-permute-start | bytes 589832 | tf_op jit(solution)/shard_map/ppermute | solution.py:363
  105.0 24.2 %collective-permute-start.3 = (bf16[384,256]{1,0:T(8,128)(2,1)}, bf16[384,256]{1,0:T(8,128)(2,1)}, u32[]{:S(2)}, u32[]{:S(2)}) collective-permute-start(bf16[384,256]{1,0:T(8,128)(2,1)} %add_convert_fusion.6), channel_id=1, source_target_pairs={{96,192},{144,240},{288,384},{336,432},{480,576},{528,624},{672,0}... | collective-permute-start | bytes 589832 | tf_op jit(solution)/shard_map/ppermute | solution.py:363
  112.6 25.7 %collective-permute-start.9 = (bf16[240,1792]{1,0:T(8,128)(2,1)S(1)}, bf16[240,1792]{1,0:T(8,128)(2,1)S(1)}, u32[]{:S(2)}, u32[]{:S(2)}) collective-permute-start(bf16[240,1792]{1,0:T(8,128)(2,1)S(1)} %get-tuple-element.66), channel_id=1, source_target_pairs={{0,48},{48,0},{96,144},{144,96},{192,240},{240,192},{288,336},{336... | collective-permute-start | bytes 2580488 | tf_op jit(solution)/shard_map/ppermute | solution.py:315
  120.4 11.8 %collective-permute-start.7 = (bf16[384,256]{1,0:T(8,128)(2,1)S(1)}, bf16[384,256]{1,0:T(8,128)(2,1)S(1)}, u32[]{:S(2)}, u32[]{:S(2)}) collective-permute-start(bf16[384,256]{1,0:T(8,128)(2,1)S(1)} %add_convert_fusion.4), channel_id=1, source_target_pairs={{0,96},{48,144},{192,288},{240,336},{384,480},{432,528},{576,672},... | collective-permute-start | bytes 589832 | tf_op jit(solution)/shard_map/ppermute | solution.py:363
  123.6 2.8 %copy-start.1 = (bf16[2,768,2048]{2,1,0:T(8,128)(2,1)S(1)}, bf16[2,768,2048]{2,1,0:T(8,128)(2,1)}, u32[]{:S(2)}) copy-start(bf16[2,768,2048]{2,1,0:T(8,128)(2,1)} %weight_ref.3) | copy-start | bytes 18874372
  130.1 7.2 %collective-permute-start.4 = (bf16[384,128]{1,0:T(8,128)(2,1)S(1)}, bf16[384,128]{1,0:T(8,128)(2,1)S(1)}, u32[]{:S(2)}, u32[]{:S(2)}) collective-permute-start(bf16[384,128]{1,0:T(8,128)(2,1)S(1)} %add_convert_fusion.11), channel_id=1, source_target_pairs={{0,96},{48,144},{192,288},{240,336},{384,480},{432,528},{576,672},... | collective-permute-start | bytes 294920 | tf_op jit(solution)/shard_map/ppermute | solution.py:374
  132.3 17.5 %collective-permute-start.8 = (bf16[384,128]{1,0:T(8,128)(2,1)S(1)}, bf16[384,128]{1,0:T(8,128)(2,1)S(1)}, u32[]{:S(2)}, u32[]{:S(2)}) collective-permute-start(bf16[384,128]{1,0:T(8,128)(2,1)S(1)} %add_convert_fusion.10), channel_id=1, source_target_pairs={{96,192},{144,240},{288,384},{336,432},{480,576},{528,624},{672,0}... | collective-permute-start | bytes 294920 | tf_op jit(solution)/shard_map/ppermute | solution.py:374
  139.2 22.5 %copy-start.5 = (bf16[96,2048]{1,0:T(8,128)(2,1)S(1)}, bf16[96,2048]{1,0:T(8,128)(2,1)}, u32[]{:S(2)}) copy-start(bf16[96,2048]{1,0:T(8,128)(2,1)} %rw_ref.3) | copy-start | bytes 1179652
  139.2 22.5 %copy-start.9 = (bf16[48,2048]{1,0:T(8,128)(2,1)S(1)}, bf16[48,2048]{1,0:T(8,128)(2,1)}, u32[]{:S(2)}) copy-start(bf16[48,2048]{1,0:T(8,128)(2,1)} %x_ref.3) | copy-start | bytes 589828
  139.2 22.5 %copy-start.11 = (f32[96,48]{1,0:T(8,128)S(1)}, f32[96,48]{1,0:T(8,128)}, u32[]{:S(2)}) copy-start(f32[96,48]{1,0:T(8,128)} %copy-done.10) | copy-start | bytes 55300
  139.6 12.1 %collective-permute-start.10 = (bf16[384,256]{1,0:T(8,128)(2,1)S(1)}, bf16[384,256]{1,0:T(8,128)(2,1)S(1)}, u32[]{:S(2)}, u32[]{:S(2)}) collective-permute-start(bf16[384,256]{1,0:T(8,128)(2,1)S(1)} %get-tuple-element.84), channel_id=1, source_target_pairs={{96,192},{144,240},{288,384},{336,432},{480,576},{528,624},{672,0}... | collective-permute-start | bytes 589832 | tf_op jit(solution)/shard_map/ppermute | solution.py:363
  143.2 18.4 %all-to-all-start.2 = ((bf16[48,8,128]{2,1,0:T(8,128)(2,1)}), bf16[48,8,128]{2,1,0:T(8,128)(2,1)S(1)}, u32[]{:S(2)}, u32[]{:S(2)}) async-start(bf16[48,8,128]{2,1,0:T(8,128)(2,1)} %bitcast.10), calls=%async_computation.2 | async-start | bytes 196608 | tf_op jit(solution)/shard_map/all_to_all | solution.py:378
  149.8 19.6 %collective-permute-start.14 = (bf16[384,256]{1,0:T(8,128)(2,1)S(1)}, bf16[384,256]{1,0:T(8,128)(2,1)S(1)}, u32[]{:S(2)}, u32[]{:S(2)}) collective-permute-start(bf16[384,256]{1,0:T(8,128)(2,1)S(1)} %get-tuple-element.88), channel_id=1, source_target_pairs={{0,96},{48,144},{192,288},{240,336},{384,480},{432,528},{576,672},... | collective-permute-start | bytes 589832 | tf_op jit(solution)/shard_map/ppermute | solution.py:363
  151.8 20.6 %collective-permute-start.11 = (bf16[384,256]{1,0:T(8,128)(2,1)S(1)}, bf16[384,256]{1,0:T(8,128)(2,1)S(1)}, u32[]{:S(2)}, u32[]{:S(2)}) collective-permute-start(bf16[384,256]{1,0:T(8,128)(2,1)S(1)} %add_convert_fusion.3), channel_id=1, source_target_pairs={{0,96},{48,144},{192,288},{240,336},{384,480},{432,528},{576,672},... | collective-permute-start | bytes 589832 | tf_op jit(solution)/shard_map/ppermute | solution.py:363
  163.9 23.5 %all-to-all-start.3 = ((bf16[48,8,512]{2,1,0:T(8,128)(2,1)}), bf16[48,8,512]{2,1,0:T(8,128)(2,1)S(1)}, u32[]{:S(2)}, u32[]{:S(2)}) async-start(bf16[48,8,512]{2,1,0:T(8,128)(2,1)} %bitcast.12), calls=%async_computation.3 | async-start | bytes 786432 | tf_op jit(solution)/shard_map/all_to_all | solution.py:387
  169.5 7.6 %collective-permute-start.15 = (bf16[384,256]{1,0:T(8,128)(2,1)S(1)}, bf16[384,256]{1,0:T(8,128)(2,1)S(1)}, u32[]{:S(2)}, u32[]{:S(2)}) collective-permute-start(bf16[384,256]{1,0:T(8,128)(2,1)S(1)} %add_convert_fusion.1), channel_id=1, source_target_pairs={{96,192},{144,240},{288,384},{336,432},{480,576},{528,624},{672,0}... | collective-permute-start | bytes 589832 | tf_op jit(solution)/shard_map/ppermute | solution.py:363
  172.4 9.8 %collective-permute-start.12 = (bf16[384,256]{1,0:T(8,128)(2,1)S(1)}, bf16[384,256]{1,0:T(8,128)(2,1)S(1)}, u32[]{:S(2)}, u32[]{:S(2)}) collective-permute-start(bf16[384,256]{1,0:T(8,128)(2,1)S(1)} %add_convert_fusion.2), channel_id=1, source_target_pairs={{96,192},{144,240},{288,384},{336,432},{480,576},{528,624},{672,0}... | collective-permute-start | bytes 589832 | tf_op jit(solution)/shard_map/ppermute | solution.py:363
  177.1 7.0 %collective-permute-start.16 = (bf16[384,256]{1,0:T(8,128)(2,1)S(1)}, bf16[384,256]{1,0:T(8,128)(2,1)S(1)}, u32[]{:S(2)}, u32[]{:S(2)}) collective-permute-start(bf16[384,256]{1,0:T(8,128)(2,1)S(1)} %add_convert_fusion), channel_id=1, source_target_pairs={{0,96},{48,144},{192,288},{240,336},{384,480},{432,528},{576,672},... | collective-permute-start | bytes 589832 | tf_op jit(solution)/shard_map/ppermute | solution.py:363
  182.2 18.0 %collective-permute-start.13 = (bf16[384,128]{1,0:T(8,128)(2,1)S(1)}, bf16[384,128]{1,0:T(8,128)(2,1)S(1)}, u32[]{:S(2)}, u32[]{:S(2)}) collective-permute-start(bf16[384,128]{1,0:T(8,128)(2,1)S(1)} %add_convert_fusion.9), channel_id=1, source_target_pairs={{0,96},{48,144},{192,288},{240,336},{384,480},{432,528},{576,672},... | collective-permute-start | bytes 294920 | tf_op jit(solution)/shard_map/ppermute | solution.py:374
  184.2 16.1 %collective-permute-start.17 = (bf16[384,128]{1,0:T(8,128)(2,1)S(1)}, bf16[384,128]{1,0:T(8,128)(2,1)S(1)}, u32[]{:S(2)}, u32[]{:S(2)}) collective-permute-start(bf16[384,128]{1,0:T(8,128)(2,1)S(1)} %add_convert_fusion.8), channel_id=1, source_target_pairs={{96,192},{144,240},{288,384},{336,432},{480,576},{528,624},{672,0}... | collective-permute-start | bytes 294920 | tf_op jit(solution)/shard_map/ppermute | solution.py:374
  188.2 23.7 %all-to-all-start.4 = ((f32[16,8,512]{2,1,0:T(8,128)}), f32[16,8,512]{2,1,0:T(8,128)S(1)}, u32[]{:S(2)}, u32[]{:S(2)}) async-start(f32[16,8,512]{2,1,0:T(8,128)} %broadcast_in_dim.2), calls=%async_computation.4 | async-start | bytes 524288 | tf_op jit(solution)/shard_map/all_to_all | solution.py:390

commit v6 on v4

v6 whole, which is shorter than its diff:
```python
import functools

import jax
import jax.numpy as jnp
from jax import lax
from jax.experimental import pallas as pl
from jax.experimental.pallas import tpu as pltpu
from jax.sharding import PartitionSpec as P

F32 = jnp.float32
BF16 = jnp.bfloat16
LANES = 128
VMEM_BYTES = 28 * 1024 * 1024


def dot(a, b, dims=((1,), (0,))):
    return lax.dot_general(a, b, (dims, ((), ())), preferred_element_type=F32)


def iota(shape, axis):
    return lax.broadcasted_iota(jnp.int32, shape, axis)


def call(body, out_shape, flops, moved, n_smem=0, **kwargs):
    return pl.pallas_call(
        body,
        out_shape=out_shape,
        compiler_params=pltpu.CompilerParams(vmem_limit_bytes=VMEM_BYTES),
        cost_estimate=pl.CostEstimate(flops=flops, bytes_accessed=moved, transcendentals=0),
        **kwargs,
    )


def whole(n):
    return [pl.BlockSpec(memory_space=pltpu.VMEM)] * n


def narrow(tiles, out_ref):
    for k in range(tiles.shape[0]):
        out_ref[:, k * LANES : (k + 1) * LANES] = tiles[k].astype(BF16)


def route_kernel(exp_dev, capacity, x_ref, grad_ref, rw_ref, routes_ref, chunk_ref, probs_ref, code_ref, buffer):
    experts = rw_ref.shape[0]
    top, rows = routes_ref.shape
    ids = iota((experts, rows), 0)
    chosen = ids == routes_ref[0:1, :]
    for k in range(1, top):
        chosen = chosen | (ids == routes_ref[k : k + 1, :])
    logits = dot(rw_ref[...], x_ref[...], ((1,), (1,)))
    highest = jnp.max(jnp.where(chosen, logits, -jnp.inf), axis=0, keepdims=True)
    weights = jnp.where(chosen, jnp.exp(jnp.where(chosen, logits - highest, 0.0)), 0.0)
    probs = weights / jnp.sum(weights, axis=0, keepdims=True)
    earlier = jnp.where(iota((rows, rows), 0) < iota((rows, rows), 1), 1.0, 0.0).astype(BF16)
    position = dot(jnp.where(chosen, 1.0, 0.0).astype(BF16), earlier)
    code = jnp.where(chosen, position, -1.0)
    probs_ref[...] = probs
    code_ref[...] = code
    n_dev = experts // exp_dev
    lane = iota((n_dev, LANES), 1)
    gates = jnp.zeros((n_dev, LANES), F32)
    piece = grad_ref.shape[1] // 8
    tiles = piece // LANES
    for e in range(exp_dev):
        owner = jnp.where(iota((n_dev, experts), 1) == iota((n_dev, experts), 0) * exp_dev + e, 1.0, 0.0).astype(BF16)
        own = dot(owner, code.astype(BF16))
        own_probs = dot(owner, probs.astype(BF16))
        select = [jnp.where(own == c, 1.0, 0.0) for c in range(capacity)]
        picked = dot(jnp.concatenate(select, axis=0).astype(BF16), grad_ref[...])
        for c in range(capacity):
            gate = jnp.sum(select[c] * own_probs, axis=1, keepdims=True)
            gates = jnp.where(lane == e * capacity + c, gate, gates)
            for p in range(8):
                for j in range(tiles):
                    column = p * piece + j * LANES
                    buffer.at[(e * capacity + c) * tiles + j][pl.ds(p, n_dev, stride=8), :] = picked[
                        c * n_dev : (c + 1) * n_dev, column : column + LANES
                    ]
    for p in range(8):
        buffer.at[buffer.shape[0] - 1][pl.ds(p, n_dev, stride=8), :] = gates
    narrow(buffer, chunk_ref)


def place_kernel(capacity, order, place_ref, hidden_ref, chunk_ref, rows_ref, gate_ref, keep_ref, trade_ref, buffer, wide):
    slots, width = rows_ref.shape
    exp_dev = len(order)
    per = slots // exp_dev
    n_source = per // capacity
    piece, half = width // 8, width // 2
    tiles = piece // LANES
    spread = jnp.where(
        iota((per, n_source * 8), 1) == lax.div(iota((per, n_source * 8), 0), capacity) * 8, 1.0, 0.0
    ).astype(BF16)
    gates = dot(spread, chunk_ref[:, chunk_ref.shape[1] - LANES :])
    n_y = len(order[0])
    for e in range(exp_dev):
        span = slice(e * per, (e + 1) * per)
        for k in range(capacity * tiles):
            at = e * capacity * tiles + k
            buffer[k] = chunk_ref[:, at * LANES : (at + 1) * LANES].astype(F32)
        for c in range(capacity):
            for p in range(8):
                for j in range(tiles):
                    wide.at[p * tiles + j][pl.ds(c, n_source, stride=capacity), :] = buffer.at[c * tiles + j][
                        pl.ds(p, n_source, stride=8), :
                    ]
        for k in range(width // LANES):
            rows_ref[span, k * LANES : (k + 1) * LANES] = wide[k].astype(BF16)
        lane = e * capacity + lax.rem(iota((per, LANES), 0), capacity)
        gate = jnp.sum(jnp.where(iota((per, LANES), 1) == lane, gates, 0.0), axis=1, keepdims=True)
        gate_ref[span, :] = gate
        gated = (gate * hidden_ref[span, :].astype(F32)).astype(BF16)
        keep_ref[span, half:] = gated
        trade_ref[span, half:] = gated
        for k, delta in enumerate(order[e]):
            chip = lax.rem(place_ref[0] + place_ref[2] * delta + n_y, n_y)
            mine = pl.multiple_of((2 * chip + place_ref[1]) * LANES, LANES)
            other = pl.multiple_of((2 * chip + 1 - place_ref[1]) * LANES, LANES)
            column = slice(k * LANES, (k + 1) * LANES)
            keep_ref[span, column] = rows_ref[span, pl.ds(mine, LANES)]
            trade_ref[span, column] = rows_ref[span, pl.ds(other, LANES)]


def product_kernel(capacity, rows_ref, gate_ref, hidden_ref, weight_ref, grad_ref, back_ref, sums, total):
    e, f = pl.program_id(0), pl.program_id(1)
    slots = rows_ref.shape[0]
    product = dot(rows_ref[...], weight_ref[0], ((1,), (1,)))
    grad_ref[0, 0] = (gate_ref[...] * product).astype(BF16)
    part = jnp.sum(product * hidden_ref[...].astype(F32), axis=1, keepdims=True)

    @pl.when(f == 0)
    def _():
        sums[...] = part

    @pl.when(f > 0)
    def _():
        sums[...] += part

    @pl.when((e == 0) & (f == 0))
    def _():
        total[...] = jnp.zeros_like(total)

    @pl.when(f == pl.num_programs(1) - 1)
    def _():
        lane = iota((slots, LANES), 1)
        slot = iota((slots, LANES), 0)
        spread = jnp.where(lane == e * capacity + lax.rem(slot, capacity), sums[...], 0.0)
        row = iota((total.shape[0], slots), 0)
        source = lax.div(iota((total.shape[0], slots), 1), capacity)
        high = spread.astype(BF16)
        rest = spread - high.astype(F32)
        middle = rest.astype(BF16)
        low = (rest - middle.astype(F32)).astype(BF16)
        for i, piece in enumerate((high, middle, low)):
            group = jnp.where(row == source * 8 + i, 1.0, 0.0).astype(BF16)
            total[...] += dot(group, piece)

    @pl.when((e == pl.num_programs(0) - 1) & (f == pl.num_programs(1) - 1))
    def _():
        back_ref[...] = total[...].astype(BF16)


def partial_kernel(first, exp_dev, mine_ref, got_ref, *outs):
    ff, wide = outs[0].shape
    half = mine_ref.shape[1] - ff
    per = mine_ref.shape[0] // exp_dev
    groups = len(outs) // exp_dev
    for e in range(exp_dev):
        span = slice(e * per, (e + 1) * per)
        mine, got = mine_ref[span, half:], got_ref[span, half:]
        for g in range(groups):
            column = slice((first + g) * wide, (first + g + 1) * wide)
            total = dot(mine, mine_ref[span, column], ((0,), (0,)))
            total += dot(got, got_ref[span, column], ((0,), (0,)))
            outs[g * exp_dev + e][...] = total.astype(BF16)


def router_kernel(capacity, exp_dev, back_ref, probs_ref, code_ref, x_ref, rw_ref, term_ref, grad_ref):
    experts, rows = probs_ref.shape
    parts = back_ref.shape[0]
    width = rw_ref.shape[1]
    ids = lax.div(iota((experts, parts), 0), exp_dev)
    column = iota((experts, parts), 1)
    owner = jnp.where((lax.div(column, 8) == ids) & (lax.rem(column, 8) < 3), 1.0, 0.0).astype(BF16)
    spread = dot(owner, back_ref[...])
    lane = iota((experts, LANES), 1)
    start = lax.rem(iota((experts, LANES), 0), exp_dev) * capacity
    code = code_ref[...]
    probs = probs_ref[...]
    gate_grad = jnp.zeros((experts, rows), F32)
    for c in range(capacity):
        column = jnp.sum(jnp.where(lane == start + c, spread, 0.0), axis=1, keepdims=True)
        gate_grad += jnp.where(code == c, column, 0.0)
    weighted = jnp.sum(probs * gate_grad, axis=0, keepdims=True)
    logit_grad = probs * (gate_grad - weighted)
    high = logit_grad.astype(BF16)
    low = (logit_grad - high.astype(F32)).astype(BF16)
    grad_ref[...] = dot(high, rw_ref[...], ((0,), (0,))).astype(BF16)
    out_rows, piece = term_ref.shape
    split = width // piece
    row = iota((out_rows, experts), 0)
    first = iota((out_rows, experts), 1) * split
    repeat = jnp.where((row >= first) & (row < first + split), 1.0, 0.0).astype(BF16)
    high = dot(repeat, high).astype(BF16)
    low = dot(repeat, low).astype(BF16)
    quarter = lax.rem(iota((out_rows, 1), 0), split)
    total = jnp.zeros((out_rows, piece), F32)
    for q in range(split):
        x = x_ref[:, q * piece : (q + 1) * piece]
        total += jnp.where(quarter == q, dot(high, x) + dot(low, x), 0.0)
    term_ref[...] = total.astype(BF16)


def exchange_order(n):
    pairs = [[0, 1]]
    for step in range(1, n // 2):
        pairs.append([-step, -step - 1] if step % 2 else [step, step + 1])
    return pairs


def on_device(layer_input, out_grad, router_weight, routes, hidden_act, down_weight):
    n_expert = lax.axis_size("expert")
    n_dp = lax.axis_size("dp")
    n_y = n_dp // 2
    experts, width = router_weight.shape
    exp_dev = experts // n_expert
    per = hidden_act.shape[2]
    slots = exp_dev * per
    ff = hidden_act.shape[3]
    capacity = per // n_expert
    tok_rows, top_count = routes.shape
    shape = jax.ShapeDtypeStruct
    dp_index, expert_index = lax.axis_index("dp"), lax.axis_index("expert")
    y_index = dp_index // 2
    place = jnp.stack([y_index, dp_index % 2, 1 - 2 * (y_index % 2)]).astype(jnp.int32)
    smem = pl.BlockSpec(memory_space=pltpu.SMEM)
    chunk_rows, chunk_wide = n_expert * 8, exp_dev * capacity * width // 8

    chunk, probs, code = call(
        functools.partial(route_kernel, exp_dev, capacity),
        (
            shape((chunk_rows, chunk_wide + LANES), BF16),
            shape((experts, tok_rows), F32),
            shape((experts, tok_rows), F32),
        ),
        2 * tok_rows * experts * width,
        2 * (2 * tok_rows + experts) * width,
        scratch_shapes=[pltpu.VMEM((chunk_wide // LANES + 1, chunk_rows, LANES), F32)],
    )(layer_input, out_grad, router_weight, routes.T)

    chunk = lax.all_to_all(chunk.reshape(n_expert, 8, -1), "expert", split_axis=0, concat_axis=0, tiled=True)
    chunk = chunk.reshape(chunk_rows, -1)

    hidden = hidden_act.reshape(slots, ff)
    y_pairs = exchange_order(n_y)
    groups = len(y_pairs)
    order = [d for pair in reversed(y_pairs) for d in pair]
    def y_swap(odd):
        one_way = [(2 * y + c, (2 * y + 2 + c) % n_dp) for y in range(odd, n_y, 2) for c in range(2)]
        return one_way + [(b, a) for a, b in one_way]

    def add(a, b):
        return (a.astype(F32) + b.astype(F32)).astype(BF16)

    rows, gate, keep, trade = call(
        functools.partial(place_kernel, capacity, [order, [-d for d in order]]),
        (
            shape((slots, width), BF16),
            shape((slots, 1), F32),
            shape((slots, width // 2 + ff), BF16),
            shape((slots, width // 2 + ff), BF16),
        ),
        2 * slots * chunk_rows * LANES,
        2 * slots * (4 * width + 3 * ff),
        in_specs=[smem] + whole(2),
        out_specs=whole(4),
        scratch_shapes=[
            pltpu.VMEM((chunk_wide // LANES // exp_dev, chunk_rows, LANES), F32),
            pltpu.VMEM((width // LANES, per, LANES), F32),
        ],
    )(place, hidden, chunk)

    got = lax.ppermute(trade, "dp", [(i, i ^ 1) for i in range(n_dp)])

    tile = ff // 2 if ff % 256 == 0 else ff
    hidden_grad, back = call(
        functools.partial(product_kernel, capacity),
        (shape((1, exp_dev, per, ff), BF16), shape((n_expert * 8, LANES), BF16)),
        2 * slots * ff * width,
        2 * (slots + exp_dev * ff) * width + 4 * slots * ff,
        grid=(exp_dev, ff // tile),
        in_specs=[
            pl.BlockSpec((per, width), lambda e, f: (e, 0)),
            pl.BlockSpec((per, 1), lambda e, f: (e, 0)),
            pl.BlockSpec((per, tile), lambda e, f: (e, f)),
            pl.BlockSpec((1, tile, width), lambda e, f: (e, f, 0)),
        ],
        out_specs=(
            pl.BlockSpec((1, 1, per, tile), lambda e, f: (0, e, 0, f)),
            pl.BlockSpec((n_expert * 8, LANES), lambda e, f: (0, 0)),
        ),
        scratch_shapes=[pltpu.VMEM((per, 1), F32), pltpu.VMEM((n_expert * 8, LANES), F32)],
    )(rows, gate, hidden, down_weight)

    got, back = lax.optimization_barrier((got, back))
    back = lax.all_to_all(back.reshape(n_expert, 8, LANES), "expert", split_axis=0, concat_axis=0, tiled=True)

    def partials(at, count):
        return call(
            functools.partial(partial_kernel, at, exp_dev),
            [shape((ff, 2 * LANES), BF16)] * (exp_dev * count),
            8 * slots * ff * LANES * count,
            4 * slots * (ff + 2 * LANES * count),
            in_specs=whole(2),
            out_specs=whole(exp_dev * count),
        )(keep, got)

    sums = partials(0, 1)
    later = []
    if groups > 1:
        later = partials(1, groups - 1)
        back = lax.optimization_barrier((back, *later))[0]
    for step in range(groups, 1, -1):
        came = [lax.ppermute(sums[e], "dp", y_swap((step - 1 + e) % 2)) for e in range(exp_dev)]
        mine, later = later[:exp_dev], later[exp_dev:]
        if step > 2:
            sums = [add(a, b) for a, b in zip(mine, came)]
        else:
            away = [add(a[:, LANES:], b[:, LANES:]) for a, b in zip(mine, came)]
            home = [a[:, :LANES].astype(F32) + b[:, :LANES].astype(F32) for a, b in zip(mine, came)]
    if groups == 1:
        away = [a[:, LANES:] for a in sums]
        home = [a[:, :LANES].astype(F32) for a in sums]
    came = [lax.ppermute(away[e], "dp", y_swap(e % 2)) for e in range(exp_dev)]
    down_grad = jnp.stack([a + b.astype(F32) for a, b in zip(home, came)])

    piece = exp_dev * width // 8
    term, input_grad = call(
        functools.partial(router_kernel, capacity, exp_dev),
        (shape((n_expert * 8, piece), BF16), shape((tok_rows, width), BF16)),
        2 * tok_rows * width * (experts + 2 * n_expert * 8),
        2 * (2 * tok_rows + 2 * experts) * width,
    )(back.reshape(n_expert * 8, LANES), probs, code, layer_input, router_weight)

    shares = lax.all_to_all(term.reshape(n_expert, 8, piece), "expert", split_axis=0, concat_axis=0, tiled=True)
    replica_sum = jnp.sum(shares.astype(F32), axis=0)
    copies = jnp.broadcast_to(replica_sum[None], (n_dp, 8, piece))
    gathered = lax.all_to_all(copies, "dp", split_axis=0, concat_axis=0, tiled=True)
    router_grad = jnp.sum(gathered, axis=0).reshape(exp_dev, width)
    return (down_grad, hidden_grad, router_grad, input_grad)


def solution(mesh):
    in_specs = (
        P(("dp", "expert"), None),
        P(("dp", "expert"), None),
        P(),
        P(("dp", "expert"), None),
        P("dp", "expert", None, None),
        P("expert", None, None),
    )
    out_specs = (
        P("expert", None, "dp"),
        P("dp", "expert", None, None),
        P("expert", None),
        P(("dp", "expert"), None),
    )
    return jax.shard_map(
        on_device, mesh=mesh, in_specs=in_specs, out_specs=out_specs, check_vma=False
    )
```

time: 209 us -> 198 us (0.947)
  starting transfers between devices: 135 us -> 79.5 us
  waiting for transfers between devices: 43.3 us -> 85.9 us
  local copies, waits for them, and re-layouts: 5.05 us -> 10.5 us
  Pallas kernels: 18.1 us -> 14.6 us
    ppermute x21 -> x0, starting transfers between devices: 72.5 us -> none  [the longest x10 27.9 us: on_device(): lax.ppermute(held[-1][side], 'expert', z_swap((step + side) % 2))]
    all_to_all x0 -> x1, waiting for transfers between devices: none -> 68.9 us  [on_device(): lax.all_to_all(chunk.reshape(n_expert, 8, -1), 'expert', split_axis=0, co...]
    ppermute x21 -> x0, waiting for transfers between devices: 23.1 us -> none  [the longest x9 12.7 us: on_device(): lax.ppermute(picked[mask], 'expert', x_swap(mask))]
    all_to_all x0 -> x1, starting transfers between devices: none -> 19 us  [on_device(): lax.all_to_all(chunk.reshape(n_expert, 8, -1), 'expert', split_axis=0, co...]
    unnamed x18 -> x30, local copies, waits for them, and re-layouts: 3.57 us -> 9.13 us
    ppermute x1, starting transfers between devices: 10.4 us -> 5.65 us  [on_device(): got = lax.ppermute(trade, 'dp', [(i, i ^ 1) for i in range(n_dp)])]
    pallas_call x5 -> x2, Pallas kernels: 8.04 us -> 4.44 us  [the longest x1 2.86 us: on_device(): call(functools.partial(place_kernel, capacity, [order, [-d for d in order...]
    all_to_all x1, starting transfers between devices: 9.1 us -> 12 us  [on_device(): lax.all_to_all(term.reshape(n_expert, 8, piece), 'expert', split_axis=0,...]
  transfers between devices with their start and end apart: 33 -> 13, of which waited for: 13 -> 4; matrix products, arithmetic and copies ran while one was open for 3% -> 3% of each run, Pallas kernels for 6% -> 4%
where the time goes in v6:
time: 198 us; the launch traced here: 197 us
  waiting for transfers between devices  85.9 us (43%)
  starting transfers between devices  79.5 us (40%)
  Pallas kernels  14.6 us (7%)
  local copies, waits for them, and re-layouts  10.5 us (5%)
  other arithmetic  5.77 us (3%)
    all_to_all x1, waiting for transfers between devices, on_device(): lax.all_to_all(chunk.reshape(n_expert, 8, -1), 'expert', split_axis=0, co...  68.9 us
    all_to_all x1, starting transfers between devices, on_device(): lax.all_to_all(chunk.reshape(n_expert, 8, -1), 'expert', split_axis=0, co...  19 us
    ppermute x6, starting transfers between devices, on_device(): lax.ppermute(sums[e], 'dp', y_swap((step - 1 + e) % 2))  18.8 us
    all_to_all x1, starting transfers between devices, on_device(): lax.all_to_all(term.reshape(n_expert, 8, piece), 'expert', split_axis=0,...  12 us
    all_to_all x1, starting transfers between devices, on_device(): lax.all_to_all(copies, 'dp', split_axis=0, concat_axis=0, tiled=True)  11.2 us
    all_to_all x1, waiting for transfers between devices, on_device(): lax.all_to_all(copies, 'dp', split_axis=0, concat_axis=0, tiled=True)  10.6 us
    unnamed x30, local copies, waits for them, and re-layouts  9.13 us
    all_to_all x1, starting transfers between devices, on_device(): lax.all_to_all(back.reshape(n_expert, 8, LANES), 'expert', split_axis=0,...  8.07 us
  transfers between devices with their start and end apart: 13, of which 4 were waited for; matrix products, arithmetic and copies ran while one was open for 3% of the time, Pallas kernels for 4%

profile of v6, /device:TPU:1, one launch (start us, length us, event | category | flops | bytes accessed | tf_op | source)
XLA Modules:
  0.0 197.3 jit_solution(5442744471406643052)
XLA Ops:
  0.6 0.0 copy-start.5
  0.6 1.0 copy-done.5
  1.6 0.9 copy-done.7
  2.6 0.9 copy-done.13
  3.5 0.7 copy-done.14
  4.2 1.6 shard_map.93
  5.8 0.0 copy-start.2
  5.8 1.3 copy-done.2
  7.1 19.0 %all-to-all-start = ((bf16[48,8,2688]{2,1,0:T(8,128)(2,1)}), bf16[48,8,2688]{2,1,0:T(8,128)(2,1)S(1)}, u32[]{:S(2)}, u32[]{:S(2)}) async-start(bf16[48,8,2688]{2,1,0:T(8,128)(2,1)} %bitcast.17), calls=%async_computation | async-start | bytes 4128768 | tf_op jit(solution)/shard_map/all_to_all | solution.py:251
  26.1 0.1 pad_add_fusion.place_ref
  26.2 68.9 %all-to-all-done = bf16[48,8,2688]{2,1,0:T(8,128)(2,1)S(1)} async-done(((bf16[48,8,2688]{2,1,0:T(8,128)(2,1)}), bf16[48,8,2688]{2,1,0:T(8,128)(2,1)S(1)}, u32[]{:S(2)}, u32[]{:S(2)}) %all-to-all-start) | async-done | bytes 2064416 | tf_op jit(solution)/shard_map/all_to_all | solution.py:251
  95.1 0.0 copy-done.1
  95.1 2.9 %shard_map.94 = (bf16[480,2048]{1,0:T(8,128)(2,1)S(1)}, f32[480,1]{1,0:T(8,128)S(1)}, bf16[480,1792]{1,0:T(8,128)(2,1)S(1)}, bf16[480,1792]{1,0:T(8,128)(2,1)S(1)}) custom-call(s32[3]{0:T(128)S(1)} %pad_add_fusion.place_ref, bf16[480,768]{1,0:T(8,128)(2,1)S(1)} %bitcast.15, bf16[384,2688]{1,0:T(8,128)(2,1)S(1)} %bitcast.14), custom_call_target="tpu_custom_call" | custom-call | flops 47185920 | bytes 10076160 | tf_op jit(solution)/shard_map/pallas_call | solution.py:265
  98.0 0.0 copy-start.3
  98.0 5.6 %collective-permute-start = (bf16[480,1792]{1,0:T(8,128)(2,1)S(1)}, bf16[480,1792]{1,0:T(8,128)(2,1)S(1)}, u32[]{:S(2)}, u32[]{:S(2)}) collective-permute-start(bf16[480,1792]{1,0:T(8,128)(2,1)S(1)} %get-tuple-element.28), channel_id=1, source_target_pairs={{0,48},{48,0},{96,144},{144,96},{192,240},{240,192},{288,336},{336... | collective-permute-start | bytes 5160968 | tf_op jit(solution)/shard_map/ppermute | solution.py:283
  103.7 0.0 copy-start
  103.7 2.8 %copy-done = bf16[2,768,2048]{2,1,0:T(8,128)(2,1)S(1)} copy-done((bf16[2,768,2048]{2,1,0:T(8,128)(2,1)S(1)}, bf16[2,768,2048]{2,1,0:T(8,128)(2,1)}, u32[]{:S(2)}) %copy-start) | copy-done | bytes 6291480
  106.5 5.0 %shard_map.95 = (bf16[1,2,240,768]{3,2,1,0:T(8,128)(2,1)}, bf16[384,128]{1,0:T(8,128)(2,1)}) custom-call(bf16[480,2048]{1,0:T(8,128)(2,1)S(1)} %get-tuple-element.29.rows_ref, f32[480,1]{1,0:T(8,128)S(1)} %get-tuple-element.30.gate_ref, bf16[480,768]{1,0:T(8,128)(2,1)S(1)} %bitcast.16, bf16[2,768,2048]{2,1,0:T(8,128)(2,1)S(1)} %copy-done), custom_call_target="tpu_custom_call" | custom-call | flops 1509949440 | bytes 9732096 | tf_op jit(solution)/shard_map/pallas_call | solution.py:286
  111.4 0.0 collective-permute-done.got_ref
  111.4 0.0 copy-done.3
  111.4 1.5 shard_map.97
  113.0 5.1 %collective-permute-start.1 = (bf16[768,256]{1,0:T(8,128)(2,1)}, bf16[768,256]{1,0:T(8,128)(2,1)}, u32[]{:S(2)}, u32[]{:S(2)}) collective-permute-start(bf16[768,256]{1,0:T(8,128)(2,1)} %get-tuple-element.36), channel_id=1, source_target_pairs={{96,192},{144,240},{288,384},{336,432},{480,576},{528,624},{672,0}... | collective-permute-start | bytes 1179656 | tf_op jit(solution)/shard_map/ppermute | solution.py:324
  118.1 1.9 collective-permute-start.5
  120.0 8.1 %all-to-all-start.1 = ((bf16[48,8,128]{2,1,0:T(8,128)(2,1)}), bf16[48,8,128]{2,1,0:T(8,128)(2,1)S(1)}, u32[]{:S(2)}, u32[]{:S(2)}) async-start(bf16[48,8,128]{2,1,0:T(8,128)(2,1)} %bitcast.9), calls=%async_computation.1 | async-start | bytes 196608 | tf_op jit(solution)/shard_map/all_to_all | solution.py:306
  128.1 0.0 copy-start.4
  128.1 1.5 copy-done.4
  129.5 1.4 shard_map.96
  131.0 0.0 copy-start.9
  131.0 0.0 copy-start.11
  131.0 0.0 copy-start.6
  131.0 0.0 copy-start.8
  131.0 0.0 collective-permute-done.1
  131.0 1.4 add_convert_fusion.3
  132.4 3.4 %collective-permute-start.2 = (bf16[768,256]{1,0:T(8,128)(2,1)S(1)}, bf16[768,256]{1,0:T(8,128)(2,1)S(1)}, u32[]{:S(2)}, u32[]{:S(2)}) collective-permute-start(bf16[768,256]{1,0:T(8,128)(2,1)S(1)} %add_convert_fusion.3), channel_id=1, source_target_pairs={{0,96},{48,144},{192,288},{240,336},{384,480},{432,528},{576,672},... | collective-permute-start | bytes 1179656 | tf_op jit(solution)/shard_map/ppermute | solution.py:324
  135.8 0.0 collective-permute-done.5
  135.8 1.8 add_convert_fusion.1
  137.6 0.0 copy-done.9
  137.6 2.6 %collective-permute-start.6 = (bf16[768,256]{1,0:T(8,128)(2,1)}, bf16[768,256]{1,0:T(8,128)(2,1)}, u32[]{:S(2)}, u32[]{:S(2)}) collective-permute-start(bf16[768,256]{1,0:T(8,128)(2,1)} %add_convert_fusion.1), channel_id=1, source_target_pairs={{96,192},{144,240},{288,384},{336,432},{480,576},{528,624},{672,0}... | collective-permute-start | bytes 1179656 | tf_op jit(solution)/shard_map/ppermute | solution.py:324
  140.2 0.0 all-to-all-done.1
  140.3 2.3 %shard_map.98 = (bf16[384,512]{1,0:T(8,128)(2,1)}, bf16[48,2048]{1,0:T(8,128)(2,1)}) custom-call(bf16[384,128]{1,0:T(8,128)(2,1)S(1)} %bitcast.18, f32[96,48]{1,0:T(8,128)S(1)} %get-tuple-element.44.probs_ref, f32[96,48]{1,0:T(8,128)S(1)} %get-tuple-element.45.code_ref, bf16[48,2048]{1,0:T(8,128)(2,1)S(1)} %copy-done.8, bf16[96,2048]{1,0:T(8,128)(2,1)S(1)} %copy-done.6), custom_call_target="tpu_custom_call" | custom-call | flops 169869312 | bytes 1179648 | tf_op jit(solution)/shard_map/pallas_call | solution.py:338
  142.5 12.0 %all-to-all-start.2 = ((bf16[48,8,512]{2,1,0:T(8,128)(2,1)}), bf16[48,8,512]{2,1,0:T(8,128)(2,1)S(1)}, u32[]{:S(2)}, u32[]{:S(2)}) async-start(bf16[48,8,512]{2,1,0:T(8,128)(2,1)} %bitcast.11), calls=%async_computation.2 | async-start | bytes 786432 | tf_op jit(solution)/shard_map/all_to_all | solution.py:345
  154.6 0.0 collective-permute-done.2
  154.6 0.1 add_convert_fusion.2
  154.7 3.9 %collective-permute-start.3 = (bf16[768,256]{1,0:T(8,128)(2,1)S(1)}, bf16[768,256]{1,0:T(8,128)(2,1)S(1)}, u32[]{:S(2)}, u32[]{:S(2)}) collective-permute-start(bf16[768,256]{1,0:T(8,128)(2,1)S(1)} %add_convert_fusion.2), channel_id=1, source_target_pairs={{96,192},{144,240},{288,384},{336,432},{480,576},{528,624},{672,0}... | collective-permute-start | bytes 1179656 | tf_op jit(solution)/shard_map/ppermute | solution.py:324
  158.6 0.0 collective-permute-done.6
  158.6 1.1 add_convert_fusion
  159.7 1.9 collective-permute-start.7
  161.6 5.1 %collective-permute-done.3 = bf16[768,256]{1,0:T(8,128)(2,1)S(1)} collective-permute-done((bf16[768,256]{1,0:T(8,128)(2,1)S(1)}, bf16[768,256]{1,0:T(8,128)(2,1)S(1)}, u32[]{:S(2)}, u32[]{:S(2)}) %collective-permute-start.3) | collective-permute-done | bytes 393248 | tf_op jit(solution)/shard_map/ppermute | solution.py:324
  166.7 0.1 add_convert_fusion.5
  166.8 1.9 collective-permute-start.4
  168.7 1.2 collective-permute-done.7
  169.9 0.1 add_convert_fusion.4
  170.0 2.9 %collective-permute-start.8 = (bf16[768,128]{1,0:T(8,128)(2,1)S(1)}, bf16[768,128]{1,0:T(8,128)(2,1)S(1)}, u32[]{:S(2)}, u32[]{:S(2)}) collective-permute-start(bf16[768,128]{1,0:T(8,128)(2,1)S(1)} %add_convert_fusion.4), channel_id=1, source_target_pairs={{96,192},{144,240},{288,384},{336,432},{480,576},{528,624},{672,0}... | collective-permute-start | bytes 589832 | tf_op jit(solution)/shard_map/ppermute | solution.py:334
  172.9 0.0 all-to-all-done.2
  172.9 0.1 convert_reduce_fusion
  173.0 0.7 broadcast_in_dim.2
  173.7 11.2 %all-to-all-start.3 = ((f32[16,8,512]{2,1,0:T(8,128)}), f32[16,8,512]{2,1,0:T(8,128)S(1)}, u32[]{:S(2)}, u32[]{:S(2)}) async-start(f32[16,8,512]{2,1,0:T(8,128)} %broadcast_in_dim.2), calls=%async_computation.3 | async-start | bytes 524288 | tf_op jit(solution)/shard_map/all_to_all | solution.py:348
  184.9 0.0 collective-permute-done.4
  184.9 0.1 add_bitcast_fusion.1
  185.0 0.0 collective-permute-done.8
  185.0 0.1 add_bitcast_fusion
  185.1 0.9 pad_maximum_fusion
  186.0 10.6 %all-to-all-done.3 = f32[16,8,512]{2,1,0:T(8,128)S(1)} async-done(((f32[16,8,512]{2,1,0:T(8,128)}), f32[16,8,512]{2,1,0:T(8,128)S(1)}, u32[]{:S(2)}, u32[]{:S(2)}) %all-to-all-start.3) | async-done | bytes 262176 | tf_op jit(solution)/shard_map/all_to_all | solution.py:348
  196.6 0.6 reshape.36
  (12 shorter events, 0.0 us)
Async XLA Ops:
  0.6 1.0 copy-start.5
  1.6 0.9 copy-start.7
  2.6 0.9 copy-start.13
  3.5 0.7 copy-start.14
  5.8 1.3 copy-start.2
  7.1 88.0 %copy-start.1 = (bf16[1,2,240,768]{3,2,1,0:T(8,128)(2,1)S(1)}, bf16[1,2,240,768]{3,2,1,0:T(8,128)(2,1)}, u32[]{:S(2)}) copy-start(bf16[1,2,240,768]{3,2,1,0:T(8,128)(2,1)} %param.10) | copy-start | bytes 2211844
  7.1 88.0 %all-to-all-start = ((bf16[48,8,2688]{2,1,0:T(8,128)(2,1)}), bf16[48,8,2688]{2,1,0:T(8,128)(2,1)S(1)}, u32[]{:S(2)}, u32[]{:S(2)}) async-start(bf16[48,8,2688]{2,1,0:T(8,128)(2,1)} %bitcast.17), calls=%async_computation | async-start | bytes 4128768 | tf_op jit(solution)/shard_map/all_to_all | solution.py:251
  98.0 13.4 %copy-start.3 = (bf16[480,1792]{1,0:T(8,128)(2,1)}, bf16[480,1792]{1,0:T(8,128)(2,1)S(1)}, u32[]{:S(2)}) copy-start(bf16[480,1792]{1,0:T(8,128)(2,1)S(1)} %get-tuple-element.27.mine_ref) | copy-start | bytes 5160964
  98.0 13.4 %collective-permute-start = (bf16[480,1792]{1,0:T(8,128)(2,1)S(1)}, bf16[480,1792]{1,0:T(8,128)(2,1)S(1)}, u32[]{:S(2)}, u32[]{:S(2)}) collective-permute-start(bf16[480,1792]{1,0:T(8,128)(2,1)S(1)} %get-tuple-element.28), channel_id=1, source_target_pairs={{0,48},{48,0},{96,144},{144,96},{192,240},{240,192},{288,336},{336... | collective-permute-start | bytes 5160968 | tf_op jit(solution)/shard_map/ppermute | solution.py:283
  103.7 2.8 %copy-start = (bf16[2,768,2048]{2,1,0:T(8,128)(2,1)S(1)}, bf16[2,768,2048]{2,1,0:T(8,128)(2,1)}, u32[]{:S(2)}) copy-start(bf16[2,768,2048]{2,1,0:T(8,128)(2,1)} %weight_ref.1) | copy-start | bytes 18874372
  113.0 18.0 %collective-permute-start.1 = (bf16[768,256]{1,0:T(8,128)(2,1)}, bf16[768,256]{1,0:T(8,128)(2,1)}, u32[]{:S(2)}, u32[]{:S(2)}) collective-permute-start(bf16[768,256]{1,0:T(8,128)(2,1)} %get-tuple-element.36), channel_id=1, source_target_pairs={{96,192},{144,240},{288,384},{336,432},{480,576},{528,624},{672,0}... | collective-permute-start | bytes 1179656 | tf_op jit(solution)/shard_map/ppermute | solution.py:324
  118.1 17.7 %collective-permute-start.5 = (bf16[768,256]{1,0:T(8,128)(2,1)}, bf16[768,256]{1,0:T(8,128)(2,1)}, u32[]{:S(2)}, u32[]{:S(2)}) collective-permute-start(bf16[768,256]{1,0:T(8,128)(2,1)} %get-tuple-element.40), channel_id=1, source_target_pairs={{0,96},{48,144},{192,288},{240,336},{384,480},{432,528},{576,672},... | collective-permute-start | bytes 1179656 | tf_op jit(solution)/shard_map/ppermute | solution.py:324
  120.0 20.3 %all-to-all-start.1 = ((bf16[48,8,128]{2,1,0:T(8,128)(2,1)}), bf16[48,8,128]{2,1,0:T(8,128)(2,1)S(1)}, u32[]{:S(2)}, u32[]{:S(2)}) async-start(bf16[48,8,128]{2,1,0:T(8,128)(2,1)} %bitcast.9), calls=%async_computation.1 | async-start | bytes 196608 | tf_op jit(solution)/shard_map/all_to_all | solution.py:306
  128.1 1.5 copy-start.4
  131.0 6.7 %copy-start.9 = (bf16[768,256]{1,0:T(8,128)(2,1)}, bf16[768,256]{1,0:T(8,128)(2,1)S(1)}, u32[]{:S(2)}) copy-start(bf16[768,256]{1,0:T(8,128)(2,1)S(1)} %get-tuple-element.37) | copy-start | bytes 1179652
  131.0 6.7 %copy-start.11 = (bf16[768,256]{1,0:T(8,128)(2,1)}, bf16[768,256]{1,0:T(8,128)(2,1)S(1)}, u32[]{:S(2)}) copy-start(bf16[768,256]{1,0:T(8,128)(2,1)S(1)} %get-tuple-element.33) | copy-start | bytes 1179652
  131.0 9.3 %copy-start.6 = (bf16[96,2048]{1,0:T(8,128)(2,1)S(1)}, bf16[96,2048]{1,0:T(8,128)(2,1)}, u32[]{:S(2)}) copy-start(bf16[96,2048]{1,0:T(8,128)(2,1)} %rw_ref.3) | copy-start | bytes 1179652
  131.0 9.3 %copy-start.8 = (bf16[48,2048]{1,0:T(8,128)(2,1)S(1)}, bf16[48,2048]{1,0:T(8,128)(2,1)}, u32[]{:S(2)}) copy-start(bf16[48,2048]{1,0:T(8,128)(2,1)} %x_ref.3) | copy-start | bytes 589828
  132.4 22.2 %collective-permute-start.2 = (bf16[768,256]{1,0:T(8,128)(2,1)S(1)}, bf16[768,256]{1,0:T(8,128)(2,1)S(1)}, u32[]{:S(2)}, u32[]{:S(2)}) collective-permute-start(bf16[768,256]{1,0:T(8,128)(2,1)S(1)} %add_convert_fusion.3), channel_id=1, source_target_pairs={{0,96},{48,144},{192,288},{240,336},{384,480},{432,528},{576,672},... | collective-permute-start | bytes 1179656 | tf_op jit(solution)/shard_map/ppermute | solution.py:324
  137.6 21.0 %collective-permute-start.6 = (bf16[768,256]{1,0:T(8,128)(2,1)}, bf16[768,256]{1,0:T(8,128)(2,1)}, u32[]{:S(2)}, u32[]{:S(2)}) collective-permute-start(bf16[768,256]{1,0:T(8,128)(2,1)} %add_convert_fusion.1), channel_id=1, source_target_pairs={{96,192},{144,240},{288,384},{336,432},{480,576},{528,624},{672,0}... | collective-permute-start | bytes 1179656 | tf_op jit(solution)/shard_map/ppermute | solution.py:324
  140.3 26.4 %copy-start.12 = (bf16[768,256]{1,0:T(8,128)(2,1)S(1)}, bf16[768,256]{1,0:T(8,128)(2,1)}, u32[]{:S(2)}) copy-start(bf16[768,256]{1,0:T(8,128)(2,1)} %copy-done.11) | copy-start | bytes 1179652
  142.5 27.4 %copy-start.10 = (bf16[768,256]{1,0:T(8,128)(2,1)S(1)}, bf16[768,256]{1,0:T(8,128)(2,1)}, u32[]{:S(2)}) copy-start(bf16[768,256]{1,0:T(8,128)(2,1)} %copy-done.9) | copy-start | bytes 1179652
  142.5 30.4 %all-to-all-start.2 = ((bf16[48,8,512]{2,1,0:T(8,128)(2,1)}), bf16[48,8,512]{2,1,0:T(8,128)(2,1)S(1)}, u32[]{:S(2)}, u32[]{:S(2)}) async-start(bf16[48,8,512]{2,1,0:T(8,128)(2,1)} %bitcast.11), calls=%async_computation.2 | async-start | bytes 786432 | tf_op jit(solution)/shard_map/all_to_all | solution.py:345
  154.7 12.0 %collective-permute-start.3 = (bf16[768,256]{1,0:T(8,128)(2,1)S(1)}, bf16[768,256]{1,0:T(8,128)(2,1)S(1)}, u32[]{:S(2)}, u32[]{:S(2)}) collective-permute-start(bf16[768,256]{1,0:T(8,128)(2,1)S(1)} %add_convert_fusion.2), channel_id=1, source_target_pairs={{96,192},{144,240},{288,384},{336,432},{480,576},{528,624},{672,0}... | collective-permute-start | bytes 1179656 | tf_op jit(solution)/shard_map/ppermute | solution.py:324
  159.7 10.2 %collective-permute-start.7 = (bf16[768,256]{1,0:T(8,128)(2,1)S(1)}, bf16[768,256]{1,0:T(8,128)(2,1)S(1)}, u32[]{:S(2)}, u32[]{:S(2)}) collective-permute-start(bf16[768,256]{1,0:T(8,128)(2,1)S(1)} %add_convert_fusion), channel_id=1, source_target_pairs={{0,96},{48,144},{192,288},{240,336},{384,480},{432,528},{576,672},... | collective-permute-start | bytes 1179656 | tf_op jit(solution)/shard_map/ppermute | solution.py:324
  166.8 18.1 %collective-permute-start.4 = (bf16[768,128]{1,0:T(8,128)(2,1)S(1)}, bf16[768,128]{1,0:T(8,128)(2,1)S(1)}, u32[]{:S(2)}, u32[]{:S(2)}) collective-permute-start(bf16[768,128]{1,0:T(8,128)(2,1)S(1)} %add_convert_fusion.5), channel_id=1, source_target_pairs={{0,96},{48,144},{192,288},{240,336},{384,480},{432,528},{576,672},... | collective-permute-start | bytes 589832 | tf_op jit(solution)/shard_map/ppermute | solution.py:334
  170.0 15.0 %collective-permute-start.8 = (bf16[768,128]{1,0:T(8,128)(2,1)S(1)}, bf16[768,128]{1,0:T(8,128)(2,1)S(1)}, u32[]{:S(2)}, u32[]{:S(2)}) collective-permute-start(bf16[768,128]{1,0:T(8,128)(2,1)S(1)} %add_convert_fusion.4), channel_id=1, source_target_pairs={{96,192},{144,240},{288,384},{336,432},{480,576},{528,624},{672,0}... | collective-permute-start | bytes 589832 | tf_op jit(solution)/shard_map/ppermute | solution.py:334
  173.7 22.9 %all-to-all-start.3 = ((f32[16,8,512]{2,1,0:T(8,128)}), f32[16,8,512]{2,1,0:T(8,128)S(1)}, u32[]{:S(2)}, u32[]{:S(2)}) async-start(f32[16,8,512]{2,1,0:T(8,128)} %broadcast_in_dim.2), calls=%async_computation.3 | async-start | bytes 524288 | tf_op jit(solution)/shard_map/all_to_all | solution.py:348

commit v7 on v6

--- a/solution.py
+++ b/solution.py
@@ -10,7 +10,7 @@
 F32 = jnp.float32
 BF16 = jnp.bfloat16
 LANES = 128
-VMEM_BYTES = 28 * 1024 * 1024
+VMEM_BYTES = 18 * 1024 * 1024
 
 
 def dot(a, b, dims=((1,), (0,))):
@@ -121,43 +121,27 @@
             trade_ref[span, column] = rows_ref[span, pl.ds(other, LANES)]
 
 
-def product_kernel(capacity, rows_ref, gate_ref, hidden_ref, weight_ref, grad_ref, back_ref, sums, total):
-    e, f = pl.program_id(0), pl.program_id(1)
-    slots = rows_ref.shape[0]
-    product = dot(rows_ref[...], weight_ref[0], ((1,), (1,)))
-    grad_ref[0, 0] = (gate_ref[...] * product).astype(BF16)
-    part = jnp.sum(product * hidden_ref[...].astype(F32), axis=1, keepdims=True)
-
-    @pl.when(f == 0)
-    def _():
-        sums[...] = part
-
-    @pl.when(f > 0)
-    def _():
-        sums[...] += part
-
-    @pl.when((e == 0) & (f == 0))
-    def _():
-        total[...] = jnp.zeros_like(total)
-
-    @pl.when(f == pl.num_programs(1) - 1)
-    def _():
-        lane = iota((slots, LANES), 1)
-        slot = iota((slots, LANES), 0)
-        spread = jnp.where(lane == e * capacity + lax.rem(slot, capacity), sums[...], 0.0)
-        row = iota((total.shape[0], slots), 0)
-        source = lax.div(iota((total.shape[0], slots), 1), capacity)
+def product_kernel(capacity, rows_ref, gate_ref, hidden_ref, weight_ref, grad_ref, back_ref):
+    exp_dev = weight_ref.shape[0]
+    slots = rows_ref.shape[0] // exp_dev
+    lane = iota((slots, LANES), 1)
+    place = lax.rem(iota((slots, LANES), 0), capacity)
+    row = iota((back_ref.shape[0], slots), 0)
+    source = lax.div(iota((back_ref.shape[0], slots), 1), capacity) * 8
+    total = jnp.zeros(back_ref.shape, F32)
+    for e in range(exp_dev):
+        span = slice(e * slots, (e + 1) * slots)
+        product = dot(rows_ref[span, :], weight_ref[e], ((1,), (1,)))
+        grad_ref[0, e] = (gate_ref[span, :] * product).astype(BF16)
+        sums = jnp.sum(product * hidden_ref[span, :].astype(F32), axis=1, keepdims=True)
+        spread = jnp.where(lane == e * capacity + place, sums, 0.0)
         high = spread.astype(BF16)
         rest = spread - high.astype(F32)
         middle = rest.astype(BF16)
         low = (rest - middle.astype(F32)).astype(BF16)
         for i, piece in enumerate((high, middle, low)):
-            group = jnp.where(row == source * 8 + i, 1.0, 0.0).astype(BF16)
-            total[...] += dot(group, piece)
-
-    @pl.when((e == pl.num_programs(0) - 1) & (f == pl.num_programs(1) - 1))
-    def _():
-        back_ref[...] = total[...].astype(BF16)
+            total += dot(jnp.where(row == source + i, 1.0, 0.0).astype(BF16), piece)
+    back_ref[...] = total.astype(BF16)
 
 
 def partial_kernel(first, exp_dev, mine_ref, got_ref, *outs):
@@ -280,29 +264,18 @@
         ],
     )(place, hidden, chunk)
 
-    got = lax.ppermute(trade, "dp", [(i, i ^ 1) for i in range(n_dp)])
-
-    tile = ff // 2 if ff % 256 == 0 else ff
     hidden_grad, back = call(
         functools.partial(product_kernel, capacity),
-        (shape((1, exp_dev, per, ff), BF16), shape((n_expert * 8, LANES), BF16)),
+        (shape((1, exp_dev, per, ff), BF16), shape((chunk_rows, LANES), BF16)),
         2 * slots * ff * width,
         2 * (slots + exp_dev * ff) * width + 4 * slots * ff,
-        grid=(exp_dev, ff // tile),
-        in_specs=[
-            pl.BlockSpec((per, width), lambda e, f: (e, 0)),
-            pl.BlockSpec((per, 1), lambda e, f: (e, 0)),
-            pl.BlockSpec((per, tile), lambda e, f: (e, f)),
-            pl.BlockSpec((1, tile, width), lambda e, f: (e, f, 0)),
-        ],
-        out_specs=(
-            pl.BlockSpec((1, 1, per, tile), lambda e, f: (0, e, 0, f)),
-            pl.BlockSpec((n_expert * 8, LANES), lambda e, f: (0, 0)),
-        ),
-        scratch_shapes=[pltpu.VMEM((per, 1), F32), pltpu.VMEM((n_expert * 8, LANES), F32)],
+        in_specs=whole(4),
+        out_specs=whole(2),
     )(rows, gate, hidden, down_weight)
 
-    got, back = lax.optimization_barrier((got, back))
+    trade, back = lax.optimization_barrier((trade, back))
+    got = lax.ppermute(trade, "dp", [(i, i ^ 1) for i in range(n_dp)])
+
     back = lax.all_to_all(back.reshape(n_expert, 8, LANES), "expert", split_axis=0, concat_axis=0, tiled=True)
 
     def partials(at, count):
@@ -320,9 +293,22 @@
     if groups > 1:
         later = partials(1, groups - 1)
         back = lax.optimization_barrier((back, *later))[0]
+    piece = exp_dev * width // 8
+    term, input_grad = call(
+        functools.partial(router_kernel, capacity, exp_dev),
+        (shape((n_expert * 8, piece), BF16), shape((tok_rows, width), BF16)),
+        2 * tok_rows * width * (experts + 2 * n_expert * 8),
+        2 * (2 * tok_rows + 2 * experts) * width,
+    )(back.reshape(n_expert * 8, LANES), probs, code, layer_input, router_weight)
+
+    shares = lax.all_to_all(term.reshape(n_expert, 8, piece), "expert", split_axis=0, concat_axis=0, tiled=True)
+    replica_sum = jnp.sum(shares.astype(F32), axis=0)
+    copies = jnp.broadcast_to(replica_sum[None], (n_dp, 8, piece))
     for step in range(groups, 1, -1):
         came = [lax.ppermute(sums[e], "dp", y_swap((step - 1 + e) % 2)) for e in range(exp_dev)]
         mine, later = later[:exp_dev], later[exp_dev:]
+        if step == 2:
+            copies, *came = lax.optimization_barrier((copies, *came))
         if step > 2:
             sums = [add(a, b) for a, b in zip(mine, came)]
         else:
@@ -334,17 +320,6 @@
     came = [lax.ppermute(away[e], "dp", y_swap(e % 2)) for e in range(exp_dev)]
     down_grad = jnp.stack([a + b.astype(F32) for a, b in zip(home, came)])
 
-    piece = exp_dev * width // 8
-    term, input_grad = call(
-        functools.partial(router_kernel, capacity, exp_dev),
-        (shape((n_expert * 8, piece), BF16), shape((tok_rows, width), BF16)),
-        2 * tok_rows * width * (experts + 2 * n_expert * 8),
-        2 * (2 * tok_rows + 2 * experts) * width,
-    )(back.reshape(n_expert * 8, LANES), probs, code, layer_input, router_weight)
-
-    shares = lax.all_to_all(term.reshape(n_expert, 8, piece), "expert", split_axis=0, concat_axis=0, tiled=True)
-    replica_sum = jnp.sum(shares.astype(F32), axis=0)
-    copies = jnp.broadcast_to(replica_sum[None], (n_dp, 8, piece))
     gathered = lax.all_to_all(copies, "dp", split_axis=0, concat_axis=0, tiled=True)
     router_grad = jnp.sum(gathered, axis=0).reshape(exp_dev, width)
     return (down_grad, hidden_grad, router_grad, input_grad)

time: 198 us -> 204 us (1.030)
  waiting for transfers between devices: 85.9 us -> 95.2 us
  starting transfers between devices: 79.5 us -> 75.5 us
  local copies, waits for them, and re-layouts: 10.5 us -> 14.2 us
    all_to_all x1, waiting for transfers between devices: 10.6 us -> 0.01 us  [on_device(): lax.all_to_all(copies, 'dp', split_axis=0, concat_axis=0, tiled=True)]
    ppermute x2, waiting for transfers between devices: 0.01 us -> 6.82 us  [on_device(): came = [lax.ppermute(away[e], 'dp', y_swap(e % 2)) for e in range(exp_dev)]]
    ppermute x6, waiting for transfers between devices: 6.33 us -> 12.2 us  [on_device(): lax.ppermute(sums[e], 'dp', y_swap((step - 1 + e) % 2))]
    all_to_all x1, starting transfers between devices: 12 us -> 7.92 us  [on_device(): lax.all_to_all(term.reshape(n_expert, 8, piece), 'expert', split_axis=0,...]
    all_to_all x1, waiting for transfers between devices: 0.01 us -> 3.99 us  [on_device(): lax.all_to_all(back.reshape(n_expert, 8, LANES), 'expert', split_axis=0,...]
    unnamed x30 -> x36, local copies, waits for them, and re-layouts: 9.13 us -> 12.8 us
    ppermute x1, waiting for transfers between devices: 0.01 us -> 3.23 us  [on_device(): got = lax.ppermute(trade, 'dp', [(i, i ^ 1) for i in range(n_dp)])]
  transfers between devices with their start and end apart: 13 -> 13, of which waited for: 4 -> 7; matrix products, arithmetic and copies ran while one was open for 3% -> 2% of each run, Pallas kernels for 4% -> 2%
where the time goes in v7:
time: 204 us; the launch traced here: 203 us
  waiting for transfers between devices  95.2 us (47%)
  starting transfers between devices  75.5 us (37%)
  local copies, waits for them, and re-layouts  14.2 us (7%)
  Pallas kernels  13.4 us (7%)
  other arithmetic  3.86 us (2%)
    all_to_all x1, waiting for transfers between devices, on_device(): lax.all_to_all(chunk.reshape(n_expert, 8, -1), 'expert', split_axis=0, co...  68.9 us
    all_to_all x1, starting transfers between devices, on_device(): lax.all_to_all(chunk.reshape(n_expert, 8, -1), 'expert', split_axis=0, co...  19 us
    ppermute x6, starting transfers between devices, on_device(): lax.ppermute(sums[e], 'dp', y_swap((step - 1 + e) % 2))  18.7 us
    unnamed x36, local copies, waits for them, and re-layouts  12.8 us
    ppermute x6, waiting for transfers between devices, on_device(): lax.ppermute(sums[e], 'dp', y_swap((step - 1 + e) % 2))  12.2 us
    all_to_all x1, starting transfers between devices, on_device(): lax.all_to_all(copies, 'dp', split_axis=0, concat_axis=0, tiled=True)  9.74 us
    all_to_all x1, starting transfers between devices, on_device(): lax.all_to_all(back.reshape(n_expert, 8, LANES), 'expert', split_axis=0,...  8.08 us
    all_to_all x1, starting transfers between devices, on_device(): lax.all_to_all(term.reshape(n_expert, 8, piece), 'expert', split_axis=0,...  7.92 us
  transfers between devices with their start and end apart: 13, of which 7 were waited for; matrix products, arithmetic and copies ran while one was open for 2% of the time, Pallas kernels for 2%

profile of v7, /device:TPU:1, one launch (start us, length us, event | category | flops | bytes accessed | tf_op | source)
XLA Modules:
  0.0 203.1 jit_solution(10273476213875235314)
XLA Ops:
  0.6 0.0 copy-start.5
  0.6 1.0 copy-done.5
  1.6 0.9 copy-done.7
  2.6 0.9 copy-done.16
  3.5 0.7 copy-done.17
  4.2 1.6 shard_map.93
  5.8 0.0 copy-start.2
  5.8 1.3 copy-done.2
  7.1 19.0 %all-to-all-start = ((bf16[48,8,2688]{2,1,0:T(8,128)(2,1)}), bf16[48,8,2688]{2,1,0:T(8,128)(2,1)S(1)}, u32[]{:S(2)}, u32[]{:S(2)}) async-start(bf16[48,8,2688]{2,1,0:T(8,128)(2,1)} %bitcast.17), calls=%async_computation | async-start | bytes 4128768 | tf_op jit(solution)/shard_map/all_to_all | solution.py:235
  26.1 0.1 pad_add_fusion.place_ref
  26.2 68.9 %all-to-all-done = bf16[48,8,2688]{2,1,0:T(8,128)(2,1)S(1)} async-done(((bf16[48,8,2688]{2,1,0:T(8,128)(2,1)}), bf16[48,8,2688]{2,1,0:T(8,128)(2,1)S(1)}, u32[]{:S(2)}, u32[]{:S(2)}) %all-to-all-start) | async-done | bytes 2064416 | tf_op jit(solution)/shard_map/all_to_all | solution.py:235
  95.1 0.0 copy-done.1
  95.1 2.9 %shard_map.94 = (bf16[480,2048]{1,0:T(8,128)(2,1)S(1)}, f32[480,1]{1,0:T(8,128)S(1)}, bf16[480,1792]{1,0:T(8,128)(2,1)S(1)}, bf16[480,1792]{1,0:T(8,128)(2,1)S(1)}) custom-call(s32[3]{0:T(128)S(1)} %pad_add_fusion.place_ref, bf16[480,768]{1,0:T(8,128)(2,1)S(1)} %bitcast.15, bf16[384,2688]{1,0:T(8,128)(2,1)S(1)} %bitcast.14), custom_call_target="tpu_custom_call" | custom-call | flops 47185920 | bytes 10076160 | tf_op jit(solution)/shard_map/pallas_call | solution.py:249
  98.0 0.0 copy-start.3
  98.0 0.0 copy-start
  98.0 3.4 %copy-done = bf16[2,768,2048]{2,1,0:T(8,128)(2,1)S(1)} copy-done((bf16[2,768,2048]{2,1,0:T(8,128)(2,1)S(1)}, bf16[2,768,2048]{2,1,0:T(8,128)(2,1)}, u32[]{:S(2)}) %copy-start) | copy-done | bytes 6291480
  101.4 3.8 %shard_map.95 = (bf16[1,2,240,768]{3,2,1,0:T(8,128)(2,1)}, bf16[384,128]{1,0:T(8,128)(2,1)}) custom-call(bf16[480,2048]{1,0:T(8,128)(2,1)S(1)} %get-tuple-element.32.rows_ref, f32[480,1]{1,0:T(8,128)S(1)} %get-tuple-element.33.gate_ref, bf16[480,768]{1,0:T(8,128)(2,1)S(1)} %bitcast.16, bf16[2,768,2048]{2,1,0:T(8,128)(2,1)S(1)} %copy-done), custom_call_target="tpu_custom_call" | custom-call | flops 1509949440 | bytes 9732096 | tf_op jit(solution)/shard_map/pallas_call | solution.py:267
  105.2 5.6 %collective-permute-start = (bf16[480,1792]{1,0:T(8,128)(2,1)S(1)}, bf16[480,1792]{1,0:T(8,128)(2,1)S(1)}, u32[]{:S(2)}, u32[]{:S(2)}) collective-permute-start(bf16[480,1792]{1,0:T(8,128)(2,1)S(1)} %get-tuple-element.35), channel_id=1, source_target_pairs={{0,48},{48,0},{96,144},{144,96},{192,240},{240,192},{288,336},{336... | collective-permute-start | bytes 5160968 | tf_op jit(solution)/shard_map/ppermute | solution.py:277
  110.9 3.2 %collective-permute-done.got_ref = bf16[480,1792]{1,0:T(8,128)(2,1)S(1)} collective-permute-done((bf16[480,1792]{1,0:T(8,128)(2,1)S(1)}, bf16[480,1792]{1,0:T(8,128)(2,1)S(1)}, u32[]{:S(2)}, u32[]{:S(2)}) %collective-permute-start) | collective-permute-done | bytes 1720352 | tf_op jit(solution)/shard_map/ppermute | solution.py:277
  114.1 0.0 copy-done.3
  114.1 1.5 shard_map.98
  115.6 5.1 %collective-permute-start.1 = (bf16[768,256]{1,0:T(8,128)(2,1)}, bf16[768,256]{1,0:T(8,128)(2,1)}, u32[]{:S(2)}, u32[]{:S(2)}) collective-permute-start(bf16[768,256]{1,0:T(8,128)(2,1)} %get-tuple-element.47), channel_id=1, source_target_pairs={{96,192},{144,240},{288,384},{336,432},{480,576},{528,624},{672,0}... | collective-permute-start | bytes 1179656 | tf_op jit(solution)/shard_map/ppermute | solution.py:308
  120.7 8.1 %all-to-all-start.1 = ((bf16[48,8,128]{2,1,0:T(8,128)(2,1)}), bf16[48,8,128]{2,1,0:T(8,128)(2,1)S(1)}, u32[]{:S(2)}, u32[]{:S(2)}) async-start(bf16[48,8,128]{2,1,0:T(8,128)(2,1)} %bitcast.7), calls=%async_computation.1 | async-start | bytes 196608 | tf_op jit(solution)/shard_map/all_to_all | solution.py:279
  128.8 1.9 collective-permute-start.4
  130.7 0.0 copy-start.4
  130.7 1.5 copy-done.4
  132.2 1.4 shard_map.96
  133.6 0.8 copy-done.9
  134.4 0.8 copy-done.11
  135.2 0.7 copy-done.12
  135.9 0.8 copy-done.14
  136.7 4.0 %all-to-all-done.1 = bf16[48,8,128]{2,1,0:T(8,128)(2,1)S(1)} async-done(((bf16[48,8,128]{2,1,0:T(8,128)(2,1)}), bf16[48,8,128]{2,1,0:T(8,128)(2,1)S(1)}, u32[]{:S(2)}, u32[]{:S(2)}) %all-to-all-start.1) | async-done | bytes 98336 | tf_op jit(solution)/shard_map/all_to_all | solution.py:279
  140.7 0.0 copy-done.6
  140.7 2.2 %shard_map.97 = (bf16[384,512]{1,0:T(8,128)(2,1)}, bf16[48,2048]{1,0:T(8,128)(2,1)}) custom-call(bf16[384,128]{1,0:T(8,128)(2,1)S(1)} %bitcast.18, f32[96,48]{1,0:T(8,128)S(1)} %get-tuple-element.44.probs_ref, f32[96,48]{1,0:T(8,128)S(1)} %get-tuple-element.45.code_ref, bf16[48,2048]{1,0:T(8,128)(2,1)S(1)} %copy-done.8, bf16[96,2048]{1,0:T(8,128)(2,1)S(1)} %copy-done.6), custom_call_target="tpu_custom_call" | custom-call | flops 169869312 | bytes 1179648 | tf_op jit(solution)/shard_map/pallas_call | solution.py:297
  142.9 7.9 %all-to-all-start.2 = ((bf16[48,8,512]{2,1,0:T(8,128)(2,1)}), bf16[48,8,512]{2,1,0:T(8,128)(2,1)S(1)}, u32[]{:S(2)}, u32[]{:S(2)}) async-start(bf16[48,8,512]{2,1,0:T(8,128)(2,1)} %bitcast.9), calls=%async_computation.2 | async-start | bytes 786432 | tf_op jit(solution)/shard_map/all_to_all | solution.py:304
  150.8 0.0 collective-permute-done.1
  150.8 1.2 add_convert_fusion.3
  152.1 3.4 %collective-permute-start.2 = (bf16[768,256]{1,0:T(8,128)(2,1)S(1)}, bf16[768,256]{1,0:T(8,128)(2,1)S(1)}, u32[]{:S(2)}, u32[]{:S(2)}) collective-permute-start(bf16[768,256]{1,0:T(8,128)(2,1)S(1)} %add_convert_fusion.3), channel_id=1, source_target_pairs={{0,96},{48,144},{192,288},{240,336},{384,480},{432,528},{576,672},... | collective-permute-start | bytes 1179656 | tf_op jit(solution)/shard_map/ppermute | solution.py:308
  155.4 0.0 collective-permute-done.4
  155.4 1.1 add_convert_fusion.1
  156.6 2.7 %collective-permute-start.5 = (bf16[768,256]{1,0:T(8,128)(2,1)S(1)}, bf16[768,256]{1,0:T(8,128)(2,1)S(1)}, u32[]{:S(2)}, u32[]{:S(2)}) collective-permute-start(bf16[768,256]{1,0:T(8,128)(2,1)S(1)} %add_convert_fusion.1), channel_id=1, source_target_pairs={{96,192},{144,240},{288,384},{336,432},{480,576},{528,624},{672,0}... | collective-permute-start | bytes 1179656 | tf_op jit(solution)/shard_map/ppermute | solution.py:308
  159.3 3.8 %collective-permute-done.2 = bf16[768,256]{1,0:T(8,128)(2,1)S(1)} collective-permute-done((bf16[768,256]{1,0:T(8,128)(2,1)S(1)}, bf16[768,256]{1,0:T(8,128)(2,1)S(1)}, u32[]{:S(2)}, u32[]{:S(2)}) %collective-permute-start.2) | collective-permute-done | bytes 393248 | tf_op jit(solution)/shard_map/ppermute | solution.py:308
  163.1 0.1 add_convert_fusion.2
  163.2 3.8 %collective-permute-start.3 = (bf16[768,256]{1,0:T(8,128)(2,1)S(1)}, bf16[768,256]{1,0:T(8,128)(2,1)S(1)}, u32[]{:S(2)}, u32[]{:S(2)}) collective-permute-start(bf16[768,256]{1,0:T(8,128)(2,1)S(1)} %add_convert_fusion.2), channel_id=1, source_target_pairs={{96,192},{144,240},{288,384},{336,432},{480,576},{528,624},{672,0}... | collective-permute-start | bytes 1179656 | tf_op jit(solution)/shard_map/ppermute | solution.py:308
  166.9 1.4 collective-permute-done.5
  168.4 0.1 add_convert_fusion
  168.5 1.9 collective-permute-start.6
  170.4 0.0 all-to-all-done.2
  170.4 0.1 convert_reduce_fusion
  170.5 7.0 %collective-permute-done.3 = bf16[768,256]{1,0:T(8,128)(2,1)S(1)} collective-permute-done((bf16[768,256]{1,0:T(8,128)(2,1)S(1)}, bf16[768,256]{1,0:T(8,128)(2,1)S(1)}, u32[]{:S(2)}, u32[]{:S(2)}) %collective-permute-start.3) | collective-permute-done | bytes 393248 | tf_op jit(solution)/shard_map/ppermute | solution.py:308
  177.5 0.0 collective-permute-done.6
  177.5 0.7 broadcast_in_dim.2
  178.2 9.7 %all-to-all-start.3 = ((f32[16,8,512]{2,1,0:T(8,128)}), f32[16,8,512]{2,1,0:T(8,128)S(1)}, u32[]{:S(2)}, u32[]{:S(2)}) async-start(f32[16,8,512]{2,1,0:T(8,128)} %broadcast_in_dim.2), calls=%async_computation.3 | async-start | bytes 524288 | tf_op jit(solution)/shard_map/all_to_all | solution.py:323
  188.0 0.1 add_convert_fusion.4
  188.0 4.5 %collective-permute-start.8 = (bf16[768,128]{1,0:T(8,128)(2,1)S(1)}, bf16[768,128]{1,0:T(8,128)(2,1)S(1)}, u32[]{:S(2)}, u32[]{:S(2)}) collective-permute-start(bf16[768,128]{1,0:T(8,128)(2,1)S(1)} %add_convert_fusion.4), channel_id=1, source_target_pairs={{96,192},{144,240},{288,384},{336,432},{480,576},{528,624},{672,0}... | collective-permute-start | bytes 589832 | tf_op jit(solution)/shard_map/ppermute | solution.py:320
  192.5 0.1 add_convert_fusion.5
  192.6 1.9 collective-permute-start.7
  194.5 6.8 %collective-permute-done.8 = bf16[768,128]{1,0:T(8,128)(2,1)S(1)} collective-permute-done((bf16[768,128]{1,0:T(8,128)(2,1)S(1)}, bf16[768,128]{1,0:T(8,128)(2,1)S(1)}, u32[]{:S(2)}, u32[]{:S(2)}) %collective-permute-start.8) | collective-permute-done | bytes 196640 | tf_op jit(solution)/shard_map/ppermute | solution.py:320
  201.4 0.1 add_bitcast_fusion
  201.4 0.0 collective-permute-done.7
  201.4 0.1 add_bitcast_fusion.1
  201.5 0.9 pad_maximum_fusion
  202.4 0.0 all-to-all-done.3
  202.5 0.6 reshape.36
  (18 shorter events, 0.1 us)
Async XLA Ops:
  0.6 1.0 copy-start.5
  1.6 0.9 copy-start.7
  2.6 0.9 copy-start.16
  3.5 0.7 copy-start.17
  5.8 1.3 copy-start.2
  7.1 88.0 %copy-start.1 = (bf16[1,2,240,768]{3,2,1,0:T(8,128)(2,1)S(1)}, bf16[1,2,240,768]{3,2,1,0:T(8,128)(2,1)}, u32[]{:S(2)}) copy-start(bf16[1,2,240,768]{3,2,1,0:T(8,128)(2,1)} %param.10) | copy-start | bytes 2211844
  7.1 88.0 %all-to-all-start = ((bf16[48,8,2688]{2,1,0:T(8,128)(2,1)}), bf16[48,8,2688]{2,1,0:T(8,128)(2,1)S(1)}, u32[]{:S(2)}, u32[]{:S(2)}) async-start(bf16[48,8,2688]{2,1,0:T(8,128)(2,1)} %bitcast.17), calls=%async_computation | async-start | bytes 4128768 | tf_op jit(solution)/shard_map/all_to_all | solution.py:235
  98.0 16.1 %copy-start.3 = (bf16[480,1792]{1,0:T(8,128)(2,1)}, bf16[480,1792]{1,0:T(8,128)(2,1)S(1)}, u32[]{:S(2)}) copy-start(bf16[480,1792]{1,0:T(8,128)(2,1)S(1)} %get-tuple-element.30.mine_ref) | copy-start | bytes 5160964
  98.0 3.4 %copy-start = (bf16[2,768,2048]{2,1,0:T(8,128)(2,1)S(1)}, bf16[2,768,2048]{2,1,0:T(8,128)(2,1)}, u32[]{:S(2)}) copy-start(bf16[2,768,2048]{2,1,0:T(8,128)(2,1)} %weight_ref.1) | copy-start | bytes 18874372
  105.2 8.9 %collective-permute-start = (bf16[480,1792]{1,0:T(8,128)(2,1)S(1)}, bf16[480,1792]{1,0:T(8,128)(2,1)S(1)}, u32[]{:S(2)}, u32[]{:S(2)}) collective-permute-start(bf16[480,1792]{1,0:T(8,128)(2,1)S(1)} %get-tuple-element.35), channel_id=1, source_target_pairs={{0,48},{48,0},{96,144},{144,96},{192,240},{240,192},{288,336},{336... | collective-permute-start | bytes 5160968 | tf_op jit(solution)/shard_map/ppermute | solution.py:277
  115.6 35.2 %collective-permute-start.1 = (bf16[768,256]{1,0:T(8,128)(2,1)}, bf16[768,256]{1,0:T(8,128)(2,1)}, u32[]{:S(2)}, u32[]{:S(2)}) collective-permute-start(bf16[768,256]{1,0:T(8,128)(2,1)} %get-tuple-element.47), channel_id=1, source_target_pairs={{96,192},{144,240},{288,384},{336,432},{480,576},{528,624},{672,0}... | collective-permute-start | bytes 1179656 | tf_op jit(solution)/shard_map/ppermute | solution.py:308
  120.7 20.0 %all-to-all-start.1 = ((bf16[48,8,128]{2,1,0:T(8,128)(2,1)}), bf16[48,8,128]{2,1,0:T(8,128)(2,1)S(1)}, u32[]{:S(2)}, u32[]{:S(2)}) async-start(bf16[48,8,128]{2,1,0:T(8,128)(2,1)} %bitcast.7), calls=%async_computation.1 | async-start | bytes 196608 | tf_op jit(solution)/shard_map/all_to_all | solution.py:279
  128.8 26.6 %collective-permute-start.4 = (bf16[768,256]{1,0:T(8,128)(2,1)}, bf16[768,256]{1,0:T(8,128)(2,1)}, u32[]{:S(2)}, u32[]{:S(2)}) collective-permute-start(bf16[768,256]{1,0:T(8,128)(2,1)} %get-tuple-element.48), channel_id=1, source_target_pairs={{0,96},{48,144},{192,288},{240,336},{384,480},{432,528},{576,672},... | collective-permute-start | bytes 1179656 | tf_op jit(solution)/shard_map/ppermute | solution.py:308
  130.7 1.5 copy-start.4
  132.2 8.5 %copy-start.6 = (bf16[96,2048]{1,0:T(8,128)(2,1)S(1)}, bf16[96,2048]{1,0:T(8,128)(2,1)}, u32[]{:S(2)}) copy-start(bf16[96,2048]{1,0:T(8,128)(2,1)} %rw_ref.3) | copy-start | bytes 1179652
  132.2 8.5 %copy-start.8 = (bf16[48,2048]{1,0:T(8,128)(2,1)S(1)}, bf16[48,2048]{1,0:T(8,128)(2,1)}, u32[]{:S(2)}) copy-start(bf16[48,2048]{1,0:T(8,128)(2,1)} %x_ref.3) | copy-start | bytes 589828
  133.6 0.8 copy-start.9
  134.4 0.8 copy-start.11
  135.2 0.7 copy-start.12
  135.9 0.8 copy-start.14
  140.7 14.8 %copy-start.10 = (bf16[768,256]{1,0:T(8,128)(2,1)S(1)}, bf16[768,256]{1,0:T(8,128)(2,1)}, u32[]{:S(2)}) copy-start(bf16[768,256]{1,0:T(8,128)(2,1)} %copy-done.9) | copy-start | bytes 1179652
  142.9 27.5 %all-to-all-start.2 = ((bf16[48,8,512]{2,1,0:T(8,128)(2,1)}), bf16[48,8,512]{2,1,0:T(8,128)(2,1)S(1)}, u32[]{:S(2)}, u32[]{:S(2)}) async-start(bf16[48,8,512]{2,1,0:T(8,128)(2,1)} %bitcast.9), calls=%async_computation.2 | async-start | bytes 786432 | tf_op jit(solution)/shard_map/all_to_all | solution.py:304
  152.1 11.0 %collective-permute-start.2 = (bf16[768,256]{1,0:T(8,128)(2,1)S(1)}, bf16[768,256]{1,0:T(8,128)(2,1)S(1)}, u32[]{:S(2)}, u32[]{:S(2)}) collective-permute-start(bf16[768,256]{1,0:T(8,128)(2,1)S(1)} %add_convert_fusion.3), channel_id=1, source_target_pairs={{0,96},{48,144},{192,288},{240,336},{384,480},{432,528},{576,672},... | collective-permute-start | bytes 1179656 | tf_op jit(solution)/shard_map/ppermute | solution.py:308
  156.5 31.4 %copy-start.15 = (bf16[768,256]{1,0:T(8,128)(2,1)S(1)}, bf16[768,256]{1,0:T(8,128)(2,1)}, u32[]{:S(2)}) copy-start(bf16[768,256]{1,0:T(8,128)(2,1)} %copy-done.14) | copy-start | bytes 1179652
  156.6 36.0 %copy-start.13 = (bf16[768,256]{1,0:T(8,128)(2,1)S(1)}, bf16[768,256]{1,0:T(8,128)(2,1)}, u32[]{:S(2)}) copy-start(bf16[768,256]{1,0:T(8,128)(2,1)} %copy-done.12) | copy-start | bytes 1179652
  156.6 11.8 %collective-permute-start.5 = (bf16[768,256]{1,0:T(8,128)(2,1)S(1)}, bf16[768,256]{1,0:T(8,128)(2,1)S(1)}, u32[]{:S(2)}, u32[]{:S(2)}) collective-permute-start(bf16[768,256]{1,0:T(8,128)(2,1)S(1)} %add_convert_fusion.1), channel_id=1, source_target_pairs={{96,192},{144,240},{288,384},{336,432},{480,576},{528,624},{672,0}... | collective-permute-start | bytes 1179656 | tf_op jit(solution)/shard_map/ppermute | solution.py:308
  163.2 14.3 %collective-permute-start.3 = (bf16[768,256]{1,0:T(8,128)(2,1)S(1)}, bf16[768,256]{1,0:T(8,128)(2,1)S(1)}, u32[]{:S(2)}, u32[]{:S(2)}) collective-permute-start(bf16[768,256]{1,0:T(8,128)(2,1)S(1)} %add_convert_fusion.2), channel_id=1, source_target_pairs={{96,192},{144,240},{288,384},{336,432},{480,576},{528,624},{672,0}... | collective-permute-start | bytes 1179656 | tf_op jit(solution)/shard_map/ppermute | solution.py:308
  168.5 9.0 %collective-permute-start.6 = (bf16[768,256]{1,0:T(8,128)(2,1)S(1)}, bf16[768,256]{1,0:T(8,128)(2,1)S(1)}, u32[]{:S(2)}, u32[]{:S(2)}) collective-permute-start(bf16[768,256]{1,0:T(8,128)(2,1)S(1)} %add_convert_fusion), channel_id=1, source_target_pairs={{0,96},{48,144},{192,288},{240,336},{384,480},{432,528},{576,672},... | collective-permute-start | bytes 1179656 | tf_op jit(solution)/shard_map/ppermute | solution.py:308
  178.2 24.2 %all-to-all-start.3 = ((f32[16,8,512]{2,1,0:T(8,128)}), f32[16,8,512]{2,1,0:T(8,128)S(1)}, u32[]{:S(2)}, u32[]{:S(2)}) async-start(f32[16,8,512]{2,1,0:T(8,128)} %broadcast_in_dim.2), calls=%async_computation.3 | async-start | bytes 524288 | tf_op jit(solution)/shard_map/all_to_all | solution.py:323
  188.0 13.3 %collective-permute-start.8 = (bf16[768,128]{1,0:T(8,128)(2,1)S(1)}, bf16[768,128]{1,0:T(8,128)(2,1)S(1)}, u32[]{:S(2)}, u32[]{:S(2)}) collective-permute-start(bf16[768,128]{1,0:T(8,128)(2,1)S(1)} %add_convert_fusion.4), channel_id=1, source_target_pairs={{96,192},{144,240},{288,384},{336,432},{480,576},{528,624},{672,0}... | collective-permute-start | bytes 589832 | tf_op jit(solution)/shard_map/ppermute | solution.py:320
  192.6 8.8 %collective-permute-start.7 = (bf16[768,128]{1,0:T(8,128)(2,1)S(1)}, bf16[768,128]{1,0:T(8,128)(2,1)S(1)}, u32[]{:S(2)}, u32[]{:S(2)}) collective-permute-start(bf16[768,128]{1,0:T(8,128)(2,1)S(1)} %add_convert_fusion.5), channel_id=1, source_target_pairs={{0,96},{48,144},{192,288},{240,336},{384,480},{432,528},{576,672},... | collective-permute-start | bytes 589832 | tf_op jit(solution)/shard_map/ppermute | solution.py:320

commit v8 on v6

--- a/solution.py
+++ b/solution.py
@@ -81,18 +81,16 @@
     narrow(buffer, chunk_ref)
 
 
-def place_kernel(capacity, order, place_ref, hidden_ref, chunk_ref, rows_ref, gate_ref, keep_ref, trade_ref, buffer, wide):
+def place_kernel(capacity, exp_dev, hidden_ref, chunk_ref, rows_ref, gate_ref, gated_ref, buffer, wide):
     slots, width = rows_ref.shape
-    exp_dev = len(order)
     per = slots // exp_dev
     n_source = per // capacity
-    piece, half = width // 8, width // 2
+    piece = width // 8
     tiles = piece // LANES
     spread = jnp.where(
         iota((per, n_source * 8), 1) == lax.div(iota((per, n_source * 8), 0), capacity) * 8, 1.0, 0.0
     ).astype(BF16)
     gates = dot(spread, chunk_ref[:, chunk_ref.shape[1] - LANES :])
-    n_y = len(order[0])
     for e in range(exp_dev):
         span = slice(e * per, (e + 1) * per)
         for k in range(capacity * tiles):
@@ -109,16 +107,7 @@
         lane = e * capacity + lax.rem(iota((per, LANES), 0), capacity)
         gate = jnp.sum(jnp.where(iota((per, LANES), 1) == lane, gates, 0.0), axis=1, keepdims=True)
         gate_ref[span, :] = gate
-        gated = (gate * hidden_ref[span, :].astype(F32)).astype(BF16)
-        keep_ref[span, half:] = gated
-        trade_ref[span, half:] = gated
-        for k, delta in enumerate(order[e]):
-            chip = lax.rem(place_ref[0] + place_ref[2] * delta + n_y, n_y)
-            mine = pl.multiple_of((2 * chip + place_ref[1]) * LANES, LANES)
-            other = pl.multiple_of((2 * chip + 1 - place_ref[1]) * LANES, LANES)
-            column = slice(k * LANES, (k + 1) * LANES)
-            keep_ref[span, column] = rows_ref[span, pl.ds(mine, LANES)]
-            trade_ref[span, column] = rows_ref[span, pl.ds(other, LANES)]
+        gated_ref[span, :] = (gate * hidden_ref[span, :].astype(F32)).astype(BF16)
 
 
 def product_kernel(capacity, rows_ref, gate_ref, hidden_ref, weight_ref, grad_ref, back_ref, sums, total):
@@ -160,19 +149,14 @@
         back_ref[...] = total[...].astype(BF16)
 
 
-def partial_kernel(first, exp_dev, mine_ref, got_ref, *outs):
-    ff, wide = outs[0].shape
-    half = mine_ref.shape[1] - ff
-    per = mine_ref.shape[0] // exp_dev
-    groups = len(outs) // exp_dev
+def partial_kernel(exp_dev, gated_ref, rows_ref, out_ref):
+    ff = gated_ref.shape[1]
+    per = gated_ref.shape[0] // exp_dev
     for e in range(exp_dev):
         span = slice(e * per, (e + 1) * per)
-        mine, got = mine_ref[span, half:], got_ref[span, half:]
-        for g in range(groups):
-            column = slice((first + g) * wide, (first + g + 1) * wide)
-            total = dot(mine, mine_ref[span, column], ((0,), (0,)))
-            total += dot(got, got_ref[span, column], ((0,), (0,)))
-            outs[g * exp_dev + e][...] = total.astype(BF16)
+        total = dot(gated_ref[span, :], rows_ref[span, :], ((0,), (0,))).astype(BF16)
+        for i in range(out_ref.shape[0]):
+            out_ref[i, e * ff : (e + 1) * ff, :] = total[:, i * LANES : (i + 1) * LANES]
 
 
 def router_kernel(capacity, exp_dev, back_ref, probs_ref, code_ref, x_ref, rw_ref, term_ref, grad_ref):
@@ -211,17 +195,9 @@
     term_ref[...] = total.astype(BF16)
 
 
-def exchange_order(n):
-    pairs = [[0, 1]]
-    for step in range(1, n // 2):
-        pairs.append([-step, -step - 1] if step % 2 else [step, step + 1])
-    return pairs
-
-
 def on_device(layer_input, out_grad, router_weight, routes, hidden_act, down_weight):
     n_expert = lax.axis_size("expert")
     n_dp = lax.axis_size("dp")
-    n_y = n_dp // 2
     experts, width = router_weight.shape
     exp_dev = experts // n_expert
     per = hidden_act.shape[2]
@@ -230,10 +206,6 @@
     capacity = per // n_expert
     tok_rows, top_count = routes.shape
     shape = jax.ShapeDtypeStruct
-    dp_index, expert_index = lax.axis_index("dp"), lax.axis_index("expert")
-    y_index = dp_index // 2
-    place = jnp.stack([y_index, dp_index % 2, 1 - 2 * (y_index % 2)]).astype(jnp.int32)
-    smem = pl.BlockSpec(memory_space=pltpu.SMEM)
     chunk_rows, chunk_wide = n_expert * 8, exp_dev * capacity * width // 8
 
     chunk, probs, code = call(
@@ -252,35 +224,34 @@
     chunk = chunk.reshape(chunk_rows, -1)
 
     hidden = hidden_act.reshape(slots, ff)
-    y_pairs = exchange_order(n_y)
-    groups = len(y_pairs)
-    order = [d for pair in reversed(y_pairs) for d in pair]
-    def y_swap(odd):
-        one_way = [(2 * y + c, (2 * y + 2 + c) % n_dp) for y in range(odd, n_y, 2) for c in range(2)]
-        return one_way + [(b, a) for a, b in one_way]
-
-    def add(a, b):
-        return (a.astype(F32) + b.astype(F32)).astype(BF16)
-
-    rows, gate, keep, trade = call(
-        functools.partial(place_kernel, capacity, [order, [-d for d in order]]),
-        (
-            shape((slots, width), BF16),
-            shape((slots, 1), F32),
-            shape((slots, width // 2 + ff), BF16),
-            shape((slots, width // 2 + ff), BF16),
-        ),
+    rows, gate, gated = call(
+        functools.partial(place_kernel, capacity, exp_dev),
+        (shape((slots, width), BF16), shape((slots, 1), F32), shape((slots, ff), BF16)),
         2 * slots * chunk_rows * LANES,
-        2 * slots * (4 * width + 3 * ff),
-        in_specs=[smem] + whole(2),
-        out_specs=whole(4),
+        2 * slots * (4 * width + 2 * ff),
+        in_specs=whole(2),
+        out_specs=whole(3),
         scratch_shapes=[
             pltpu.VMEM((chunk_wide // LANES // exp_dev, chunk_rows, LANES), F32),
             pltpu.VMEM((width // LANES, per, LANES), F32),
         ],
-    )(place, hidden, chunk)
-
-    got = lax.ppermute(trade, "dp", [(i, i ^ 1) for i in range(n_dp)])
+    )(hidden, chunk)
+
+    partial_grad = call(
+        functools.partial(partial_kernel, exp_dev),
+        shape((n_dp, exp_dev * ff, LANES), BF16),
+        2 * slots * ff * width,
+        2 * (slots * (ff + width) + exp_dev * ff * width),
+        grid=(n_dp // 2,),
+        in_specs=[
+            pl.BlockSpec((slots, ff), lambda k: (0, 0)),
+            pl.BlockSpec((slots, 2 * LANES), lambda k: (0, k)),
+        ],
+        out_specs=pl.BlockSpec((2, exp_dev * ff, LANES), lambda k: (k, 0, 0)),
+    )(gated, rows)
+    rows, partial_grad = lax.optimization_barrier((rows, partial_grad))
+    down_grad = lax.psum_scatter(partial_grad, "dp", scatter_dimension=0, tiled=True)
+    down_grad = down_grad.astype(F32).reshape(exp_dev, ff, LANES)
 
     tile = ff // 2 if ff % 256 == 0 else ff
     hidden_grad, back = call(
@@ -302,37 +273,7 @@
         scratch_shapes=[pltpu.VMEM((per, 1), F32), pltpu.VMEM((n_expert * 8, LANES), F32)],
     )(rows, gate, hidden, down_weight)
 
-    got, back = lax.optimization_barrier((got, back))
     back = lax.all_to_all(back.reshape(n_expert, 8, LANES), "expert", split_axis=0, concat_axis=0, tiled=True)
-
-    def partials(at, count):
-        return call(
-            functools.partial(partial_kernel, at, exp_dev),
-            [shape((ff, 2 * LANES), BF16)] * (exp_dev * count),
-            8 * slots * ff * LANES * count,
-            4 * slots * (ff + 2 * LANES * count),
-            in_specs=whole(2),
-            out_specs=whole(exp_dev * count),
-        )(keep, got)
-
-    sums = partials(0, 1)
-    later = []
-    if groups > 1:
-        later = partials(1, groups - 1)
-        back = lax.optimization_barrier((back, *later))[0]
-    for step in range(groups, 1, -1):
-        came = [lax.ppermute(sums[e], "dp", y_swap((step - 1 + e) % 2)) for e in range(exp_dev)]
-        mine, later = later[:exp_dev], later[exp_dev:]
-        if step > 2:
-            sums = [add(a, b) for a, b in zip(mine, came)]
-        else:
-            away = [add(a[:, LANES:], b[:, LANES:]) for a, b in zip(mine, came)]
-            home = [a[:, :LANES].astype(F32) + b[:, :LANES].astype(F32) for a, b in zip(mine, came)]
-    if groups == 1:
-        away = [a[:, LANES:] for a in sums]
-        home = [a[:, :LANES].astype(F32) for a in sums]
-    came = [lax.ppermute(away[e], "dp", y_swap(e % 2)) for e in range(exp_dev)]
-    down_grad = jnp.stack([a + b.astype(F32) for a, b in zip(home, came)])
 
     piece = exp_dev * width // 8
     term, input_grad = call(

time: 198 us -> 196 us (0.990)
  blocking collectives: 0 us -> 156 us
  waiting for transfers between devices: 85.9 us -> 0.02 us
  starting transfers between devices: 79.5 us -> 0.04 us
  between operations: 1 us -> 14.1 us
  other arithmetic: 5.77 us -> 2.02 us
    all_to_all x0 -> x4, blocking collectives: none -> 156 us  [the longest x1 89.2 us: on_device(): lax.all_to_all(chunk.reshape(n_expert, 8, -1), 'expert', split_axis=0, co...]
    all_to_all x4 -> x0, waiting for transfers between devices: 79.6 us -> none  [the longest x1 68.9 us: on_device(): lax.all_to_all(chunk.reshape(n_expert, 8, -1), 'expert', split_axis=0, co...]
    all_to_all x4 -> x0, starting transfers between devices: 50.3 us -> none  [the longest x1 19 us: on_device(): lax.all_to_all(chunk.reshape(n_expert, 8, -1), 'expert', split_axis=0, co...]
    ppermute x9 -> x0, starting transfers between devices: 29.2 us -> none  [the longest x6 18.8 us: on_device(): lax.ppermute(sums[e], 'dp', y_swap((step - 1 + e) % 2))]
    ppermute x9 -> x0, waiting for transfers between devices: 6.34 us -> none  [the longest x6 6.33 us: on_device(): lax.ppermute(sums[e], 'dp', y_swap((step - 1 + e) % 2))]
    convert_element_type x6 -> x0, other arithmetic: 4.53 us -> none  [add(): return (a.astype(F32) + b.astype(F32)).astype(BF16)]
    pallas_call x3 -> x2, Pallas kernels: 5.8 us -> 5.55 us  [the longest x1 3.74 us: on_device(): call(functools.partial(partial_kernel, exp_dev), shape((n_dp, exp_dev * f...]
    unnamed x30 -> x18, local copies, waits for them, and re-layouts: 9.13 us -> 8.97 us
  transfers between devices with their start and end apart: 13 -> 1, of which waited for: 4 -> 0; matrix products, arithmetic and copies ran while one was open for 3% -> 0% of each run, Pallas kernels for 4% -> 3%
where the time goes in v8:
time: 196 us; the launch traced here: 195 us
  blocking collectives  156 us (80%)
  between operations  14.1 us (7%)
  Pallas kernels  13.6 us (7%)
  local copies, waits for them, and re-layouts  9.62 us (5%)
  other arithmetic  2.02 us (1%)
    all_to_all x1, blocking collectives, on_device(): lax.all_to_all(chunk.reshape(n_expert, 8, -1), 'expert', split_axis=0, co...  89.2 us
    all_to_all x1, blocking collectives, on_device(): lax.all_to_all(term.reshape(n_expert, 8, piece), 'expert', split_axis=0,...  23.2 us
    all_to_all x1, blocking collectives, on_device(): lax.all_to_all(back.reshape(n_expert, 8, LANES), 'expert', split_axis=0,...  22.2 us
    all_to_all x1, blocking collectives, on_device(): lax.all_to_all(copies, 'dp', split_axis=0, concat_axis=0, tiled=True)  21.3 us
    unnamed x18, local copies, waits for them, and re-layouts  8.97 us
    pallas_call x1, Pallas kernels, on_device(): call(functools.partial(product_kernel, capacity), (shape((1, exp_dev, per...  4.95 us
  transfers between devices with their start and end apart: 1, of which 0 were waited for; matrix products, arithmetic and copies ran while one was open for 0% of the time, Pallas kernels for 3%

profile of v8, /device:TPU:1, one launch (start us, length us, event | category | flops | bytes accessed | tf_op | source)
XLA Modules:
  0.0 195.3 jit_solution(947821605666125222)
XLA Ops:
  7.2 0.0 reduce-scatter.2.cloned.1.call-start
  7.2 0.0 copy-start.3
  7.2 1.0 copy-done.3
  8.2 0.0 copy-start.5
  8.2 0.9 copy-done.5
  9.1 0.0 copy-start.7
  9.1 0.9 copy-done.7
  10.1 0.0 copy-start.8
  10.1 0.7 copy-done.8
  10.8 1.6 shard_map.93
  12.3 0.0 copy-start.2
  12.4 89.2 %all_to_all.20 = bf16[48,8,2688]{2,1,0:T(8,128)(2,1)S(1)} all-to-all(bf16[48,8,2688]{2,1,0:T(8,128)(2,1)S(1)} %bitcast.12), channel_id=1, replica_groups=mesh['dp'=16,'expert'=48] {'expert'}, dimensions={0} | all-to-all | bytes 4128768 | tf_op jit(solution)/shard_map/all_to_all | solution.py:223
  101.5 0.0 copy-done.2
  101.5 1.8 shard_map.94
  103.4 3.7 %shard_map.95 = bf16[16,1536,128]{2,1,0:T(8,128)(2,1)S(1)} custom-call(bf16[480,768]{1,0:T(8,128)(2,1)S(1)} %get-tuple-element.18.gated_ref, bf16[480,2048]{1,0:T(8,128)(2,1)S(1)} %get-tuple-element.20.rows_ref), custom_call_target="tpu_custom_call" | custom-call | flops 1509949440 | bytes 8994816 | tf_op jit(solution)/shard_map/pallas_call | solution.py:240
  107.1 0.0 copy-start
  107.1 2.6 %copy-done = bf16[16,1536,128]{2,1,0:T(8,128)(2,1)} copy-done((bf16[16,1536,128]{2,1,0:T(8,128)(2,1)}, bf16[16,1536,128]{2,1,0:T(8,128)(2,1)S(1)}, u32[]{:S(2)}) %copy-start) | copy-done | bytes 6291480
  109.8 0.0 reduce-scatter.2.cloned.1.call-update
  109.8 0.0 copy-start.1
  109.8 2.8 %copy-done.1 = bf16[2,768,2048]{2,1,0:T(8,128)(2,1)S(1)} copy-done((bf16[2,768,2048]{2,1,0:T(8,128)(2,1)S(1)}, bf16[2,768,2048]{2,1,0:T(8,128)(2,1)}, u32[]{:S(2)}) %copy-start.1) | copy-done | bytes 6291480
  112.6 0.0 copy-start.4
  112.6 0.0 copy-start.6
  112.6 4.9 %shard_map.96 = (bf16[1,2,240,768]{3,2,1,0:T(8,128)(2,1)}, bf16[384,128]{1,0:T(8,128)(2,1)S(1)}) custom-call(bf16[480,2048]{1,0:T(8,128)(2,1)S(1)} %get-tuple-element.20.rows_ref, f32[480,1]{1,0:T(8,128)S(1)} %get-tuple-element.21.gate_ref, bf16[480,768]{1,0:T(8,128)(2,1)S(1)} %bitcast.11, bf16[2,768,2048]{2,1,0:T(8,128)(2,1)S(1)} %copy-done.1), custom_call_target="tpu_custom_call" | custom-call | flops 1509949440 | bytes 9732096 | tf_op jit(solution)/shard_map/pallas_call | solution.py:257
  117.5 22.2 %all_to_all.21 = bf16[48,8,128]{2,1,0:T(8,128)(2,1)S(1)} all-to-all(bf16[48,8,128]{2,1,0:T(8,128)(2,1)S(1)} %bitcast.15), channel_id=1, replica_groups=mesh['dp'=16,'expert'=48] {'expert'}, dimensions={0} | all-to-all | bytes 196608 | tf_op jit(solution)/shard_map/all_to_all | solution.py:276
  139.7 0.0 copy-done.4
  139.7 0.0 copy-done.6
  139.8 1.5 shard_map.97
  141.2 23.2 %all_to_all.22 = bf16[48,8,512]{2,1,0:T(8,128)(2,1)S(1)} all-to-all(bf16[48,8,512]{2,1,0:T(8,128)(2,1)S(1)} %bitcast.13), channel_id=1, replica_groups=mesh['dp'=16,'expert'=48] {'expert'}, dimensions={0} | all-to-all | bytes 786432 | tf_op jit(solution)/shard_map/all_to_all | solution.py:286
  164.4 0.1 convert_reduce_fusion
  164.5 21.3 %all_to_all.23 = f32[16,8,512]{2,1,0:T(8,128)S(1)} all-to-all(f32[16,8,512]{2,1,0:T(8,128)S(1)} %broadcast_in_dim.2), channel_id=1, replica_groups=mesh['dp'=16,'expert'=48] {'dp'}, dimensions={0} | all-to-all | bytes 524288 | tf_op jit(solution)/shard_map/all_to_all | solution.py:289
  185.9 0.6 reshape.44
  186.5 0.0 reduce-scatter.2.cloned.1.call-done
  186.5 1.9 convert.1
  (2 shorter events, 0.0 us)
Async XLA Ops:
  7.2 179.3 %reduce-scatter.2.cloned.1.call-start = ((), (), s32[]{:S(2)}) async-start(), calls=%async_computation.5 | async-start | bytes 6684672 | tf_op jit(solution)/shard_map/reduce_scatter | solution.py:253
  7.2 1.0 copy-start.3
  8.2 0.9 copy-start.5
  9.1 0.9 copy-start.7
  10.1 0.7 copy-start.8
  12.3 89.2 %copy-start.2 = (bf16[1,2,240,768]{3,2,1,0:T(8,128)(2,1)S(1)}, bf16[1,2,240,768]{3,2,1,0:T(8,128)(2,1)}, u32[]{:S(2)}) copy-start(bf16[1,2,240,768]{3,2,1,0:T(8,128)(2,1)} %param.10) | copy-start | bytes 2211844
  107.1 2.7 %copy-start = (bf16[16,1536,128]{2,1,0:T(8,128)(2,1)}, bf16[16,1536,128]{2,1,0:T(8,128)(2,1)S(1)}, u32[]{:S(2)}) copy-start(bf16[16,1536,128]{2,1,0:T(8,128)(2,1)S(1)} %shard_map.95) | copy-start | bytes 18874372
  109.8 2.8 %copy-start.1 = (bf16[2,768,2048]{2,1,0:T(8,128)(2,1)S(1)}, bf16[2,768,2048]{2,1,0:T(8,128)(2,1)}, u32[]{:S(2)}) copy-start(bf16[2,768,2048]{2,1,0:T(8,128)(2,1)} %weight_ref.1) | copy-start | bytes 18874372
  112.6 27.2 %copy-start.4 = (bf16[96,2048]{1,0:T(8,128)(2,1)S(1)}, bf16[96,2048]{1,0:T(8,128)(2,1)}, u32[]{:S(2)}) copy-start(bf16[96,2048]{1,0:T(8,128)(2,1)} %rw_ref.3) | copy-start | bytes 1179652
  112.6 27.2 %copy-start.6 = (bf16[48,2048]{1,0:T(8,128)(2,1)S(1)}, bf16[48,2048]{1,0:T(8,128)(2,1)}, u32[]{:S(2)}) copy-start(bf16[48,2048]{1,0:T(8,128)(2,1)} %x_ref.3) | copy-start | bytes 589828
Sparse Core Ops, SparseCore 0:
  109.9 69.8 reduce-scatter.1
